TPU v7x, 32 devices: a whole 2x2x4 slice. The times are simulated.
32 devices in a mesh: grp: 2 (over y), dev: 16 (over z, x, core).
Axes of the slice: x: 2, y: 2, z: 4, core: 2. Of those that a mesh axis runs over, the one named last changes fastest.
Arguments:
- embeddings: bfloat16 [12288, 768], P(('grp', 'dev')), may hold values from -6 to 6
- labels: bfloat16 [12288, 896], P(('grp', 'dev')), may hold values from -6 to 6
- cluster_rows: int32 [32], P(('grp', 'dev')), may hold values from 96 to 384, as said below
Outputs:
- propagated: bfloat16 [12288, 896], P(('grp', 'dev'))
Inputs may be any that keep to these rules, and one draw needn't show every extreme that they name: `cluster_rows`: some cluster has all 384 slots filled and some has 96.
All inputs are finite; a program needn't handle non-finite values.
Results may differ from a plain program's by a relative error of at most 0.006.
Values may be sent and summed in bfloat16 or wider, within the bound.
No kernel may reach another device: no remote copies, remote signals or barrier semaphores. Data moves between devices by JAX's collectives and lax.ppermute only.
A program may use at most 64 MiB of HBM per device.

v0:
```python
import math

import jax
import jax.numpy as jnp
from jax import lax
from jax.sharding import PartitionSpec as P

INNER = 4


sharpness = 25.0
keep_share = 0.8


def passed_along(block, axis, distance):
    devices = range(lax.axis_size(axis))
    route = [((i - distance) % len(devices), i) for i in devices]
    return lax.ppermute(block, axis, route)


def unit_rows(embeddings):
    values = embeddings.astype(jnp.float32)
    scaled = values * lax.rsqrt(jnp.mean(values * values, axis=-1, keepdims=True) + 1e-06)
    return (scaled / math.sqrt(values.shape[-1])).astype(jnp.bfloat16)


def raw_affinity(left_unit, right_unit):
    cosine = lax.dot_general(
        left_unit, right_unit, (((1,), (1,)), ((), ())), preferred_element_type=jnp.float32
    )
    return jnp.exp(sharpness * cosine)


def backward_terms(pair_tile, own_labels):
    return lax.dot_general(
        pair_tile, own_labels, (((0,), (0,)), ((), ())), preferred_element_type=jnp.float32
    )


def body(embeddings, labels, cluster_rows):
    places = lax.iota(jnp.int32, embeddings.shape[0])
    row_valid = (places < cluster_rows[0]).astype(jnp.float32)[:, None]
    unit_vectors = unit_rows(embeddings)
    seed_labels = labels * row_valid.astype(jnp.bfloat16)
    offdiag = (places[:, None] != places[None, :]).astype(jnp.float32)
    current = seed_labels
    pair_tiles = []
    for sweep_index in range(2):
        fetched = [
            passed_along((unit_vectors, current), "dev", -offset) for offset in range(1, INNER + 1)
        ]
        cross_unit, cross_labels = passed_along((unit_vectors, current), "grp", -1)
        far_labels = [received[1] for received in fetched]
        pair_tiles = [
            raw_affinity(unit_vectors, received[0]).astype(jnp.bfloat16) for received in fetched
        ]
        pair_tiles.append(raw_affinity(unit_vectors, cross_unit).astype(jnp.bfloat16))
        pair_tiles.append((raw_affinity(unit_vectors, unit_vectors) * offdiag).astype(jnp.bfloat16))
        summed = jnp.dot(pair_tiles[INNER + 1], current, preferred_element_type=jnp.float32)
        summed = summed + jnp.dot(
            pair_tiles[INNER], cross_labels, preferred_element_type=jnp.float32
        )
        summed = summed + passed_along(
            backward_terms(pair_tiles[INNER], current).astype(jnp.bfloat16), "grp", 1
        ).astype(jnp.float32)
        returned = []
        for offset in range(INNER):
            summed = summed + jnp.dot(
                pair_tiles[offset], far_labels[offset], preferred_element_type=jnp.float32
            )
            returned.append(backward_terms(pair_tiles[offset], current))
        for offset in range(1, INNER + 1):
            summed = summed + passed_along(
                returned[offset - 1].astype(jnp.bfloat16), "dev", offset
            ).astype(jnp.float32)
        factor = lax.rsqrt(jnp.mean(summed * summed, axis=-1, keepdims=True) + 1e-06)
        mixed = keep_share * summed * factor + (1.0 - keep_share) * seed_labels.astype(jnp.float32)
        current = (mixed * row_valid).astype(jnp.bfloat16)
    return current


def solution(mesh):
    placed = (P(("grp", "dev"), None), P(("grp", "dev"), None), P(("grp", "dev")))
    return jax.shard_map(
        body, mesh=mesh, in_specs=placed, out_specs=P(("grp", "dev"), None), check_vma=False
    )
```

profile of v0, /device:TPU:10, one launch (start us, length us, event | category | flops | bytes accessed | tf_op | source)
XLA Modules:
  0.0 229.7 jit_solution(1969144734777712751)
XLA Ops:
  0.0 1.3 fusion.25
  1.3 1.3 fusion.27
  3.1 2.8 %collective-permute-start.7 = (bf16[384,768]{1,0:T(8,128)(2,1)S(1)}, bf16[384,768]{1,0:T(8,128)(2,1)S(1)}, u32[]{:S(2)}, u32[]{:S(2)}) collective-permute-start(bf16[384,768]{1,0:T(8,128)(2,1)S(1)} %fusion.27), channel_id=1, source_target_pairs={{3,0},{4,1},{5,2},{6,3},{7,4},{8,5},{9,6},{10,7},{11,8},{12,9},{13... | collective-permute-start | bytes 1769480 | tf_op jit(solution)/shard_map/ppermute | solution.py:18
  6.4 1.7 collective-permute-start.3
  8.1 1.5 collective-permute-start
  11.5 6.2 %collective-permute-done.9 = bf16[384,768]{1,0:T(8,128)(2,1)S(1)} collective-permute-done((bf16[384,768]{1,0:T(8,128)(2,1)S(1)}, bf16[384,768]{1,0:T(8,128)(2,1)S(1)}, u32[]{:S(2)}, u32[]{:S(2)}) %collective-permute-start.9) | collective-permute-done | bytes 589856 | tf_op jit(solution)/shard_map/ppermute | solution.py:18
  17.7 1.6 collective-permute-start.10
  19.8 9.4 %collective-permute-done.7 = bf16[384,768]{1,0:T(8,128)(2,1)S(1)} collective-permute-done((bf16[384,768]{1,0:T(8,128)(2,1)S(1)}, bf16[384,768]{1,0:T(8,128)(2,1)S(1)}, u32[]{:S(2)}, u32[]{:S(2)}) %collective-permute-start.7) | collective-permute-done | bytes 589856 | tf_op jit(solution)/shard_map/ppermute | solution.py:18
  29.6 14.4 %collective-permute-done.5 = bf16[384,768]{1,0:T(8,128)(2,1)S(1)} collective-permute-done((bf16[384,768]{1,0:T(8,128)(2,1)S(1)}, bf16[384,768]{1,0:T(8,128)(2,1)S(1)}, u32[]{:S(2)}, u32[]{:S(2)}) %collective-permute-start.5) | collective-permute-done | bytes 589856 | tf_op jit(solution)/shard_map/ppermute | solution.py:18
  47.5 1.6 collective-permute-start.1
  51.3 20.0 %collective-permute-done.8 = bf16[384,896]{1,0:T(8,128)(2,1)S(1)} collective-permute-done((bf16[384,896]{1,0:T(8,128)(2,1)S(1)}, bf16[384,896]{1,0:T(8,128)(2,1)S(1)}, u32[]{:S(2)}, u32[]{:S(2)}) %collective-permute-start.8) | collective-permute-done | bytes 688160 | tf_op jit(solution)/shard_map/ppermute | solution.py:18
  71.3 22.3 %collective-permute-done.6 = bf16[384,896]{1,0:T(8,128)(2,1)S(1)} collective-permute-done((bf16[384,896]{1,0:T(8,128)(2,1)S(1)}, bf16[384,896]{1,0:T(8,128)(2,1)S(1)}, u32[]{:S(2)}, u32[]{:S(2)}) %collective-permute-start.6) | collective-permute-done | bytes 688160 | tf_op jit(solution)/shard_map/ppermute | solution.py:18
  93.6 1.6 collective-permute-start.14
  96.9 18.6 %collective-permute-done.11 = bf16[384,896]{1,0:T(8,128)(2,1)S(1)} collective-permute-done((bf16[384,896]{1,0:T(8,128)(2,1)S(1)}, bf16[384,896]{1,0:T(8,128)(2,1)S(1)}, u32[]{:S(2)}, u32[]{:S(2)}) %collective-permute-start.11) | collective-permute-done | bytes 688160 | tf_op jit(solution)/shard_map/ppermute | solution.py:18
  115.7 8.5 %collective-permute-done.13 = bf16[384,896]{1,0:T(8,128)(2,1)S(1)} collective-permute-done((bf16[384,896]{1,0:T(8,128)(2,1)S(1)}, bf16[384,896]{1,0:T(8,128)(2,1)S(1)}, u32[]{:S(2)}, u32[]{:S(2)}) %collective-permute-start.13) | collective-permute-done | bytes 688160 | tf_op jit(solution)/shard_map/ppermute | solution.py:18
  124.2 14.1 %collective-permute-done.14 = bf16[384,896]{1,0:T(8,128)(2,1)S(1)} collective-permute-done((bf16[384,896]{1,0:T(8,128)(2,1)S(1)}, bf16[384,896]{1,0:T(8,128)(2,1)S(1)}, u32[]{:S(2)}, u32[]{:S(2)}) %collective-permute-start.14) | collective-permute-done | bytes 688160 | tf_op jit(solution)/shard_map/ppermute | solution.py:18
  138.3 1.2 multiply_reduce_fusion.1
  141.7 5.8 %collective-permute-start.20 = (bf16[384,896]{1,0:T(8,128)(2,1)S(1)}, bf16[384,896]{1,0:T(8,128)(2,1)S(1)}, u32[]{:S(2)}, u32[]{:S(2)}) collective-permute-start(bf16[384,896]{1,0:T(8,128)(2,1)S(1)} %multiply_convert_fusion.1), channel_id=1, source_target_pairs={{4,0},{5,1},{6,2},{7,3},{8,4},{9,5},{10,6},{11,7},{12,8},{13,9},{1... | collective-permute-start | bytes 2064392 | tf_op jit(solution)/shard_map/ppermute | solution.py:18
  147.5 1.3 collective-permute-start.17
  148.8 1.5 collective-permute-start.16
  152.0 9.3 %collective-permute-done.20 = bf16[384,896]{1,0:T(8,128)(2,1)S(1)} collective-permute-done((bf16[384,896]{1,0:T(8,128)(2,1)S(1)}, bf16[384,896]{1,0:T(8,128)(2,1)S(1)}, u32[]{:S(2)}, u32[]{:S(2)}) %collective-permute-start.20) | collective-permute-done | bytes 688160 | tf_op jit(solution)/shard_map/ppermute | solution.py:18
  161.3 1.5 collective-permute-start.15
  163.3 3.7 %collective-permute-done.16 = bf16[384,896]{1,0:T(8,128)(2,1)S(1)} collective-permute-done((bf16[384,896]{1,0:T(8,128)(2,1)S(1)}, bf16[384,896]{1,0:T(8,128)(2,1)S(1)}, u32[]{:S(2)}, u32[]{:S(2)}) %collective-permute-start.16) | collective-permute-done | bytes 688160 | tf_op jit(solution)/shard_map/ppermute | solution.py:18
  167.1 1.6 collective-permute-done.19
  169.8 8.6 %collective-permute-done.18 = bf16[384,896]{1,0:T(8,128)(2,1)S(1)} collective-permute-done((bf16[384,896]{1,0:T(8,128)(2,1)S(1)}, bf16[384,896]{1,0:T(8,128)(2,1)S(1)}, u32[]{:S(2)}, u32[]{:S(2)}) %collective-permute-start.18) | collective-permute-done | bytes 688160 | tf_op jit(solution)/shard_map/ppermute | solution.py:18
  178.4 1.9 collective-permute-start.23
  180.2 17.9 %collective-permute-done.17 = bf16[384,896]{1,0:T(8,128)(2,1)S(1)} collective-permute-done((bf16[384,896]{1,0:T(8,128)(2,1)S(1)}, bf16[384,896]{1,0:T(8,128)(2,1)S(1)}, u32[]{:S(2)}, u32[]{:S(2)}) %collective-permute-start.17) | collective-permute-done | bytes 688160 | tf_op jit(solution)/shard_map/ppermute | solution.py:18
  198.1 3.9 %collective-permute-start.24 = (bf16[384,896]{1,0:T(8,128)(2,1)S(1)}, bf16[384,896]{1,0:T(8,128)(2,1)S(1)}, u32[]{:S(2)}, u32[]{:S(2)}) collective-permute-start(bf16[384,896]{1,0:T(8,128)(2,1)S(1)} %convolution_convert_fusion), channel_id=1, source_target_pairs={{12,0},{13,1},{14,2},{15,3},{0,4},{1,5},{2,6},{3,7},{4,8},{5,9},{6... | collective-permute-start | bytes 2064392 | tf_op jit(solution)/shard_map/ppermute | solution.py:18
  203.7 5.1 %collective-permute-done.23 = bf16[384,896]{1,0:T(8,128)(2,1)S(1)} collective-permute-done((bf16[384,896]{1,0:T(8,128)(2,1)S(1)}, bf16[384,896]{1,0:T(8,128)(2,1)S(1)}, u32[]{:S(2)}, u32[]{:S(2)}) %collective-permute-start.23) | collective-permute-done | bytes 688160 | tf_op jit(solution)/shard_map/ppermute | solution.py:18
  208.8 18.2 %collective-permute-done.24 = bf16[384,896]{1,0:T(8,128)(2,1)S(1)} collective-permute-done((bf16[384,896]{1,0:T(8,128)(2,1)S(1)}, bf16[384,896]{1,0:T(8,128)(2,1)S(1)}, u32[]{:S(2)}, u32[]{:S(2)}) %collective-permute-start.24) | collective-permute-done | bytes 688160 | tf_op jit(solution)/shard_map/ppermute | solution.py:18
  227.0 1.2 multiply_reduce_fusion
  228.2 1.4 multiply_convert_fusion
  (58 shorter events, 17.7 us)
Async XLA Ops:
  2.5 8.2 %copy-start = (bf16[384,896]{1,0:T(8,128)(2,1)S(1)}, bf16[384,896]{1,0:T(8,128)(2,1)}, u32[]{:S(2)}) copy-start(bf16[384,896]{1,0:T(8,128)(2,1)} %param.4) | copy-start | bytes 2064388
  2.6 15.1 %collective-permute-start.9 = (bf16[384,768]{1,0:T(8,128)(2,1)S(1)}, bf16[384,768]{1,0:T(8,128)(2,1)S(1)}, u32[]{:S(2)}, u32[]{:S(2)}) collective-permute-start(bf16[384,768]{1,0:T(8,128)(2,1)S(1)} %fusion.27), channel_id=1, source_target_pairs={{4,0},{5,1},{6,2},{7,3},{8,4},{9,5},{10,6},{11,7},{12,8},{13,9},{1... | collective-permute-start | bytes 1769480 | tf_op jit(solution)/shard_map/ppermute | solution.py:18
  3.1 26.1 %collective-permute-start.7 = (bf16[384,768]{1,0:T(8,128)(2,1)S(1)}, bf16[384,768]{1,0:T(8,128)(2,1)S(1)}, u32[]{:S(2)}, u32[]{:S(2)}) collective-permute-start(bf16[384,768]{1,0:T(8,128)(2,1)S(1)} %fusion.27), channel_id=1, source_target_pairs={{3,0},{4,1},{5,2},{6,3},{7,4},{8,5},{9,6},{10,7},{11,8},{12,9},{13... | collective-permute-start | bytes 1769480 | tf_op jit(solution)/shard_map/ppermute | solution.py:18
  5.8 38.3 %collective-permute-start.5 = (bf16[384,768]{1,0:T(8,128)(2,1)S(1)}, bf16[384,768]{1,0:T(8,128)(2,1)S(1)}, u32[]{:S(2)}, u32[]{:S(2)}) collective-permute-start(bf16[384,768]{1,0:T(8,128)(2,1)S(1)} %fusion.27), channel_id=1, source_target_pairs={{2,0},{3,1},{4,2},{5,3},{6,4},{7,5},{8,6},{9,7},{10,8},{11,9},{12,... | collective-permute-start | bytes 1769480 | tf_op jit(solution)/shard_map/ppermute | solution.py:18
  6.4 39.4 %collective-permute-start.3 = (bf16[384,768]{1,0:T(8,128)(2,1)S(1)}, bf16[384,768]{1,0:T(8,128)(2,1)S(1)}, u32[]{:S(2)}, u32[]{:S(2)}) collective-permute-start(bf16[384,768]{1,0:T(8,128)(2,1)S(1)} %fusion.27), channel_id=1, source_target_pairs={{1,0},{2,1},{3,2},{4,3},{5,4},{6,5},{7,6},{8,7},{9,8},{10,9},{11,1... | collective-permute-start | bytes 1769480 | tf_op jit(solution)/shard_map/ppermute | solution.py:18
  8.1 39.4 %collective-permute-start = (bf16[384,768]{1,0:T(8,128)(2,1)S(1)}, bf16[384,768]{1,0:T(8,128)(2,1)S(1)}, u32[]{:S(2)}, u32[]{:S(2)}) collective-permute-start(bf16[384,768]{1,0:T(8,128)(2,1)S(1)} %fusion.27), channel_id=1, source_target_pairs={{16,0},{0,16},{17,1},{1,17},{18,2},{2,18},{19,3},{3,19},{20,4},{4,... | collective-permute-start | bytes 1769480 | tf_op jit(solution)/shard_map/ppermute | solution.py:18
  17.7 32.5 %collective-permute-start.10 = (bf16[384,896]{1,0:T(8,128)(2,1)S(1)}, bf16[384,896]{1,0:T(8,128)(2,1)S(1)}, u32[]{:S(2)}, u32[]{:S(2)}) collective-permute-start(bf16[384,896]{1,0:T(8,128)(2,1)S(1)} %broadcast_multiply_fusion), channel_id=1, source_target_pairs={{4,0},{5,1},{6,2},{7,3},{8,4},{9,5},{10,6},{11,7},{12,8},{13,9},{1... | collective-permute-start | bytes 2064392 | tf_op jit(solution)/shard_map/ppermute | solution.py:18
  29.1 42.1 %collective-permute-start.8 = (bf16[384,896]{1,0:T(8,128)(2,1)S(1)}, bf16[384,896]{1,0:T(8,128)(2,1)S(1)}, u32[]{:S(2)}, u32[]{:S(2)}) collective-permute-start(bf16[384,896]{1,0:T(8,128)(2,1)S(1)} %broadcast_multiply_fusion), channel_id=1, source_target_pairs={{3,0},{4,1},{5,2},{6,3},{7,4},{8,5},{9,6},{10,7},{11,8},{12,9},{13... | collective-permute-start | bytes 2064392 | tf_op jit(solution)/shard_map/ppermute | solution.py:18
  44.1 49.5 %collective-permute-start.6 = (bf16[384,896]{1,0:T(8,128)(2,1)S(1)}, bf16[384,896]{1,0:T(8,128)(2,1)S(1)}, u32[]{:S(2)}, u32[]{:S(2)}) collective-permute-start(bf16[384,896]{1,0:T(8,128)(2,1)S(1)} %broadcast_multiply_fusion), channel_id=1, source_target_pairs={{2,0},{3,1},{4,2},{5,3},{6,4},{7,5},{8,6},{9,7},{10,8},{11,9},{12,... | collective-permute-start | bytes 2064392 | tf_op jit(solution)/shard_map/ppermute | solution.py:18
  45.8 47.8 %collective-permute-start.4 = (bf16[384,896]{1,0:T(8,128)(2,1)S(1)}, bf16[384,896]{1,0:T(8,128)(2,1)S(1)}, u32[]{:S(2)}, u32[]{:S(2)}) collective-permute-start(bf16[384,896]{1,0:T(8,128)(2,1)S(1)} %broadcast_multiply_fusion), channel_id=1, source_target_pairs={{1,0},{2,1},{3,2},{4,3},{5,4},{6,5},{7,6},{8,7},{9,8},{10,9},{11,1... | collective-permute-start | bytes 2064392 | tf_op jit(solution)/shard_map/ppermute | solution.py:18
  47.5 46.1 %collective-permute-start.1 = (bf16[384,896]{1,0:T(8,128)(2,1)S(1)}, bf16[384,896]{1,0:T(8,128)(2,1)S(1)}, u32[]{:S(2)}, u32[]{:S(2)}) collective-permute-start(bf16[384,896]{1,0:T(8,128)(2,1)S(1)} %broadcast_multiply_fusion), channel_id=1, source_target_pairs={{16,0},{0,16},{17,1},{1,17},{18,2},{2,18},{19,3},{3,19},{20,4},{4,... | collective-permute-start | bytes 2064392 | tf_op jit(solution)/shard_map/ppermute | solution.py:18
  50.2 46.7 %collective-permute-start.2 = (bf16[384,896]{1,0:T(8,128)(2,1)S(1)}, bf16[384,896]{1,0:T(8,128)(2,1)S(1)}, u32[]{:S(2)}, u32[]{:S(2)}) collective-permute-start(bf16[384,896]{1,0:T(8,128)(2,1)S(1)} %convolution_convert_fusion.9), channel_id=1, source_target_pairs={{16,0},{0,16},{17,1},{1,17},{18,2},{2,18},{19,3},{3,19},{20,4},{4,... | collective-permute-start | bytes 2064392 | tf_op jit(solution)/shard_map/ppermute | solution.py:18
  71.3 44.2 %collective-permute-start.11 = (bf16[384,896]{1,0:T(8,128)(2,1)S(1)}, bf16[384,896]{1,0:T(8,128)(2,1)S(1)}, u32[]{:S(2)}, u32[]{:S(2)}) collective-permute-start(bf16[384,896]{1,0:T(8,128)(2,1)S(1)} %convolution_convert_fusion.8), channel_id=1, source_target_pairs={{15,0},{0,1},{1,2},{2,3},{3,4},{4,5},{5,6},{6,7},{7,8},{8,9},{9,10... | collective-permute-start | bytes 2064392 | tf_op jit(solution)/shard_map/ppermute | solution.py:18
  93.6 22.1 %collective-permute-start.12 = (bf16[384,896]{1,0:T(8,128)(2,1)S(1)}, bf16[384,896]{1,0:T(8,128)(2,1)S(1)}, u32[]{:S(2)}, u32[]{:S(2)}) collective-permute-start(bf16[384,896]{1,0:T(8,128)(2,1)S(1)} %convolution_convert_fusion.7), channel_id=1, source_target_pairs={{14,0},{15,1},{0,2},{1,3},{2,4},{3,5},{4,6},{5,7},{6,8},{7,9},{8,1... | collective-permute-start | bytes 2064392 | tf_op jit(solution)/shard_map/ppermute | solution.py:18
  93.6 30.6 %collective-permute-start.13 = (bf16[384,896]{1,0:T(8,128)(2,1)S(1)}, bf16[384,896]{1,0:T(8,128)(2,1)S(1)}, u32[]{:S(2)}, u32[]{:S(2)}) collective-permute-start(bf16[384,896]{1,0:T(8,128)(2,1)S(1)} %convolution_convert_fusion.6), channel_id=1, source_target_pairs={{13,0},{14,1},{15,2},{0,3},{1,4},{2,5},{3,6},{4,7},{5,8},{6,9},{7,... | collective-permute-start | bytes 2064392 | tf_op jit(solution)/shard_map/ppermute | solution.py:18
  93.6 44.7 %collective-permute-start.14 = (bf16[384,896]{1,0:T(8,128)(2,1)S(1)}, bf16[384,896]{1,0:T(8,128)(2,1)S(1)}, u32[]{:S(2)}, u32[]{:S(2)}) collective-permute-start(bf16[384,896]{1,0:T(8,128)(2,1)S(1)} %convolution_convert_fusion.5), channel_id=1, source_target_pairs={{12,0},{13,1},{14,2},{15,3},{0,4},{1,5},{2,6},{3,7},{4,8},{5,9},{6... | collective-permute-start | bytes 2064392 | tf_op jit(solution)/shard_map/ppermute | solution.py:18
  141.7 19.6 %collective-permute-start.20 = (bf16[384,896]{1,0:T(8,128)(2,1)S(1)}, bf16[384,896]{1,0:T(8,128)(2,1)S(1)}, u32[]{:S(2)}, u32[]{:S(2)}) collective-permute-start(bf16[384,896]{1,0:T(8,128)(2,1)S(1)} %multiply_convert_fusion.1), channel_id=1, source_target_pairs={{4,0},{5,1},{6,2},{7,3},{8,4},{9,5},{10,6},{11,7},{12,8},{13,9},{1... | collective-permute-start | bytes 2064392 | tf_op jit(solution)/shard_map/ppermute | solution.py:18
  147.5 21.1 %collective-permute-start.19 = (bf16[384,896]{1,0:T(8,128)(2,1)S(1)}, bf16[384,896]{1,0:T(8,128)(2,1)S(1)}, u32[]{:S(2)}, u32[]{:S(2)}) collective-permute-start(bf16[384,896]{1,0:T(8,128)(2,1)S(1)} %multiply_convert_fusion.1), channel_id=1, source_target_pairs={{3,0},{4,1},{5,2},{6,3},{7,4},{8,5},{9,6},{10,7},{11,8},{12,9},{13... | collective-permute-start | bytes 2064392 | tf_op jit(solution)/shard_map/ppermute | solution.py:18
  147.5 30.9 %collective-permute-start.18 = (bf16[384,896]{1,0:T(8,128)(2,1)S(1)}, bf16[384,896]{1,0:T(8,128)(2,1)S(1)}, u32[]{:S(2)}, u32[]{:S(2)}) collective-permute-start(bf16[384,896]{1,0:T(8,128)(2,1)S(1)} %multiply_convert_fusion.1), channel_id=1, source_target_pairs={{2,0},{3,1},{4,2},{5,3},{6,4},{7,5},{8,6},{9,7},{10,8},{11,9},{12,... | collective-permute-start | bytes 2064392 | tf_op jit(solution)/shard_map/ppermute | solution.py:18
  147.5 50.6 %collective-permute-start.17 = (bf16[384,896]{1,0:T(8,128)(2,1)S(1)}, bf16[384,896]{1,0:T(8,128)(2,1)S(1)}, u32[]{:S(2)}, u32[]{:S(2)}) collective-permute-start(bf16[384,896]{1,0:T(8,128)(2,1)S(1)} %multiply_convert_fusion.1), channel_id=1, source_target_pairs={{1,0},{2,1},{3,2},{4,3},{5,4},{6,5},{7,6},{8,7},{9,8},{10,9},{11,1... | collective-permute-start | bytes 2064392 | tf_op jit(solution)/shard_map/ppermute | solution.py:18
  148.8 18.3 %collective-permute-start.16 = (bf16[384,896]{1,0:T(8,128)(2,1)S(1)}, bf16[384,896]{1,0:T(8,128)(2,1)S(1)}, u32[]{:S(2)}, u32[]{:S(2)}) collective-permute-start(bf16[384,896]{1,0:T(8,128)(2,1)S(1)} %convolution_convert_fusion.4), channel_id=1, source_target_pairs={{16,0},{0,16},{17,1},{1,17},{18,2},{2,18},{19,3},{3,19},{20,4},{4,... | collective-permute-start | bytes 2064392 | tf_op jit(solution)/shard_map/ppermute | solution.py:18
  161.3 65.8 %collective-permute-start.15 = (bf16[384,896]{1,0:T(8,128)(2,1)S(1)}, bf16[384,896]{1,0:T(8,128)(2,1)S(1)}, u32[]{:S(2)}, u32[]{:S(2)}) collective-permute-start(bf16[384,896]{1,0:T(8,128)(2,1)S(1)} %multiply_convert_fusion.1), channel_id=1, source_target_pairs={{16,0},{0,16},{17,1},{1,17},{18,2},{2,18},{19,3},{3,19},{20,4},{4,... | collective-permute-start | bytes 2064392 | tf_op jit(solution)/shard_map/ppermute | solution.py:18
  167.1 36.6 %collective-permute-start.21 = (bf16[384,896]{1,0:T(8,128)(2,1)S(1)}, bf16[384,896]{1,0:T(8,128)(2,1)S(1)}, u32[]{:S(2)}, u32[]{:S(2)}) collective-permute-start(bf16[384,896]{1,0:T(8,128)(2,1)S(1)} %convolution_convert_fusion.3), channel_id=1, source_target_pairs={{15,0},{0,1},{1,2},{2,3},{3,4},{4,5},{5,6},{6,7},{7,8},{8,9},{9,10... | collective-permute-start | bytes 2064392 | tf_op jit(solution)/shard_map/ppermute | solution.py:18
  168.6 35.1 %collective-permute-start.22 = (bf16[384,896]{1,0:T(8,128)(2,1)S(1)}, bf16[384,896]{1,0:T(8,128)(2,1)S(1)}, u32[]{:S(2)}, u32[]{:S(2)}) collective-permute-start(bf16[384,896]{1,0:T(8,128)(2,1)S(1)} %convolution_convert_fusion.2), channel_id=1, source_target_pairs={{14,0},{15,1},{0,2},{1,3},{2,4},{3,5},{4,6},{5,7},{6,8},{7,9},{8,1... | collective-permute-start | bytes 2064392 | tf_op jit(solution)/shard_map/ppermute | solution.py:18
  178.4 30.5 %collective-permute-start.23 = (bf16[384,896]{1,0:T(8,128)(2,1)S(1)}, bf16[384,896]{1,0:T(8,128)(2,1)S(1)}, u32[]{:S(2)}, u32[]{:S(2)}) collective-permute-start(bf16[384,896]{1,0:T(8,128)(2,1)S(1)} %convolution_convert_fusion.1), channel_id=1, source_target_pairs={{13,0},{14,1},{15,2},{0,3},{1,4},{2,5},{3,6},{4,7},{5,8},{6,9},{7,... | collective-permute-start | bytes 2064392 | tf_op jit(solution)/shard_map/ppermute | solution.py:18
  198.1 28.9 %collective-permute-start.24 = (bf16[384,896]{1,0:T(8,128)(2,1)S(1)}, bf16[384,896]{1,0:T(8,128)(2,1)S(1)}, u32[]{:S(2)}, u32[]{:S(2)}) collective-permute-start(bf16[384,896]{1,0:T(8,128)(2,1)S(1)} %convolution_convert_fusion), channel_id=1, source_target_pairs={{12,0},{13,1},{14,2},{15,3},{0,4},{1,5},{2,6},{3,7},{4,8},{5,9},{6... | collective-permute-start | bytes 2064392 | tf_op jit(solution)/shard_map/ppermute | solution.py:18
where the time goes:
time: 230 us
  waiting for transfers between devices  178 us (77%)
  starting transfers between devices  29.6 us (13%)
  matrix products  16.5 us (7%)
  other arithmetic  4.51 us (2%)
    ppermute x25, waiting for transfers between devices, passed_along(): return lax.ppermute(block, axis, route)  178 us
    ppermute x25, starting transfers between devices, passed_along(): return lax.ppermute(block, axis, route)  29.6 us
    dot_general x10, matrix products, backward_terms(): lax.dot_general(pair_tile, own_labels, (((0,), (0,)), ((), ())), preferre...  5.74 us
  transfers between devices with their start and end apart: 25, of which 16 were waited for; matrix products, arithmetic and copies ran while one was open for 5% of the time, Pallas kernels for 0%

commit v1 on v0

v1 whole, which is shorter than its diff:
```python
import functools
import math

import jax
import jax.numpy as jnp
from jax import lax
from jax.experimental import pallas as pl
from jax.experimental.pallas import tpu as pltpu
from jax.sharding import PartitionSpec as P

sharpness = 25.0
keep_share = 0.8
BF16 = jnp.bfloat16
F32 = jnp.float32
QUAD = 4
INVALID = 1e38
MB = 2**20


def along_dev(block, source):
    size = lax.axis_size("dev")
    return lax.ppermute(block, "dev", [(source(i) % size, i) for i in range(size)])


def from_up(block):
    return along_dev(block, lambda i: i + QUAD)


def from_down(block):
    return along_dev(block, lambda i: i - QUAD)


def from_side(block):
    return along_dev(block, lambda i: i ^ 2)


def from_core(block):
    return along_dev(block, lambda i: i ^ 1)


def from_group(block, step):
    size = lax.axis_size("grp")
    return lax.ppermute(block, "grp", [((i + step) % size, i) for i in range(size)])


def after(value, earlier):
    return lax.optimization_barrier((value, earlier))[0]


def exchange(pieces):
    return [along_dev(piece, lambda i, m=m: i ^ m) for m, piece in enumerate(pieces, 1)]


def call(kernel, name, operands, out_shape, scratch=(), limit=24):
    specs = [
        pl.BlockSpec(memory_space=pltpu.SMEM if x.dtype == jnp.int32 else pltpu.VMEM) for x in operands
    ]
    return pl.pallas_call(
        kernel,
        in_specs=specs,
        out_shape=out_shape,
        scratch_shapes=list(scratch),
        compiler_params=pltpu.CompilerParams(vmem_limit_bytes=limit * MB),
        name=name,
    )(*operands)


def like(shape, dtype):
    return jax.ShapeDtypeStruct(tuple(shape), dtype)


def dot(left, right):
    return jnp.dot(left, right, preferred_element_type=F32)


def affinity(left, right):
    cosine = lax.dot_general(left, right, (((1,), (1,)), ((), ())), preferred_element_type=F32)
    return jnp.exp2(cosine * (sharpness * math.log2(math.e)))


def cut(block, place, pieces):
    quarter = block.shape[1] // QUAD
    for k in range(QUAD):
        for m, piece in pieces:

            @pl.when(place ^ m == k)
            def _():
                piece[...] = block[:, k * quarter : (k + 1) * quarter]


def join(place, pieces, out):
    quarter = out.shape[1] // QUAD
    for k in range(QUAD):
        for m, piece in pieces:

            @pl.when(place ^ m == k)
            def _():
                out[:, k * quarter : (k + 1) * quarter] = piece[...]


def unit_kernel(embeddings, unit):
    values = embeddings[...].astype(F32)
    scaled = values * lax.rsqrt(jnp.mean(values * values, axis=-1, keepdims=True) + 1e-06)
    unit[...] = (scaled / math.sqrt(values.shape[-1])).astype(BF16)


def seed_kernel(scalars, labels, seed, *pieces):
    row = lax.broadcasted_iota(jnp.int32, labels.shape, 0)
    seed[...] = jnp.where(row < scalars[1], labels[...].astype(F32), 0.0).astype(BF16)
    cut(seed, scalars[0], list(enumerate(pieces, 1)))


def pack_kernel(scalars, whole, *rest):
    pieces, out = rest[:-1], rest[-1]
    out[...] = whole[...]
    join(scalars[0], list(enumerate(pieces, 1)), out)


def at(cluster, rows):
    return pl.ds(pl.multiple_of(cluster * rows, rows), rows)


def near_kernel(clusters, own, side, core, across, units, near):
    rows = own.shape[0]
    for i, block in enumerate((own, side, core, across)):
        units[at(clusters[i], rows), :] = block[...]
    for k in range(QUAD):
        for pair in range(2):
            span = slice(2 * pair * rows, 2 * (pair + 1) * rows)
            tile = affinity(units[k * rows : (k + 1) * rows, :], units[span, :])
            if k // 2 == pair:
                row = lax.broadcasted_iota(jnp.int32, tile.shape, 0)
                lane = lax.broadcasted_iota(jnp.int32, tile.shape, 1)
                tile = jnp.where(row + (k % 2) * rows == lane, 0.0, tile)
            near[k * rows : (k + 1) * rows, span] = tile.astype(BF16)


def far_kernel(clusters, units, up, side, core, across, own, far, sums, up_units, stack):
    rows = up.shape[0]
    for i, block in enumerate((up, core, side, across)):
        up_units[at(clusters[(0, 2, 1, 3)[i]], rows), :] = block[...]
    unpack(own, stack)
    for k in range(QUAD):
        here = slice(k * rows, (k + 1) * rows)
        for first in range(0, k + 1, 2):
            span = slice(first * rows, min(first + 2, k + 1) * rows)
            far[here, span] = affinity(units[here, :], up_units[span, :]).astype(BF16)
    scatter(far, stack, sums)


def unpack(block, stack):
    rows, quarter = stack.shape[0] // QUAD, stack.shape[1]
    for k in range(QUAD):
        stack[k * rows : (k + 1) * rows, :] = block[:, k * quarter : (k + 1) * quarter]


def scatter(far, stack, out):
    rows, quarter = stack.shape[0] // QUAD, stack.shape[1]
    for k in range(QUAD):
        total = lax.dot_general(
            far[k * rows :, k * rows : (k + 1) * rows],
            stack[k * rows :, :],
            (((0,), (0,)), ((), ())),
            preferred_element_type=F32,
        )
        out[:, k * quarter : (k + 1) * quarter] = total.astype(out.dtype)


def scatter_kernel(scalars, far, own, out, *rest):
    pieces, stack = rest[:-1], rest[-1]
    unpack(own, stack)
    scatter(far, stack, out)
    cut(out, scalars[0], list(enumerate(pieces, 1)))


def cross_kernel(weight, unit, *rest):
    others, out = rest[:-1], rest[-1]
    rows = unit.shape[0]
    for n, other in enumerate(others):
        out[n * rows : (n + 1) * rows, :] = (affinity(unit[...], other[...]) * weight).astype(BF16)


def gather_kernel(crosses, clusters, near, far, t0, t1, t2, t3, own, up, *rest):
    cross, (out, *pieces, stack, total) = rest[:crosses], rest[crosses:]
    rows, quarter = own.shape[0], own.shape[1] // QUAD
    unpack(own, stack)
    for k in range(QUAD):
        here = slice(k * rows, (k + 1) * rows)
        total[here, :] = dot(near[here, :], stack[...])
    for n, block in enumerate(cross):
        unpack(block, stack)
        for i, tile in enumerate((t0, t1, t2, t3)):
            here = at(clusters[i], rows)
            total[here, :] += dot(tile[n * rows : (n + 1) * rows, :], stack[here, :])
    unpack(up, stack)
    for k in range(QUAD):
        here = slice(k * rows, (k + 1) * rows)
        done = total[here, :] + dot(far[here, : (k + 1) * rows], stack[: (k + 1) * rows, :])
        out[:, k * quarter : (k + 1) * quarter] = done.astype(out.dtype)
    cut(out, clusters[0], list(enumerate(pieces, 1)))


def lanes_of(cluster_count, lanes):
    quarter = lanes // QUAD
    row = lax.broadcasted_iota(jnp.int32, (cluster_count, lanes), 0)
    lane = lax.broadcasted_iota(jnp.int32, (cluster_count, lanes), 1)
    return ((lane >= row * quarter) & (lane < (row + 1) * quarter)).astype(F32)


def combine_kernel(scalars, kept, sent, summed, squares):
    total = kept[...] + sent[...].astype(F32)
    summed[...] = total
    sums = lax.dot_general(
        lanes_of(8, total.shape[1]),
        total * total,
        (((1,), (1,)), ((), ())),
        precision=lax.Precision.HIGHEST,
        preferred_element_type=F32,
    )
    row = lax.broadcasted_iota(jnp.int32, sums.shape, 0)
    lane = lax.broadcasted_iota(jnp.int32, sums.shape, 1)
    squares[...] = sums + jnp.where((row == scalars[0]) & (lane >= scalars[1]), INVALID, 0.0)


def mix_kernel(summed, s0, s1, s2, s3, seed, out):
    total = (s0[...] + s1[...]) + (s2[...] + s3[...])
    factor = jnp.where(total > INVALID / 10, 0.0, lax.rsqrt(total / summed.shape[1] + 1e-06))
    spread = lax.dot_general(
        factor,
        lanes_of(8, summed.shape[1]),
        (((0,), (0,)), ((), ())),
        precision=lax.Precision.HIGHEST,
        preferred_element_type=F32,
    )
    out[...] = (keep_share * summed[...] * spread + (1.0 - keep_share) * seed[...].astype(F32)).astype(BF16)


def finish_kernel(scalars, kept, k1, k2, k3, sent, seed, out, whole):
    whole[...] = kept[...]
    join(scalars[0], [(1, k1), (2, k2), (3, k3)], whole)
    summed = whole[...].astype(F32) + sent[...].astype(F32)
    factor = lax.rsqrt(jnp.mean(summed * summed, axis=-1, keepdims=True) + 1e-06)
    result = keep_share * summed * factor + (1.0 - keep_share) * seed[...].astype(F32)
    row = lax.broadcasted_iota(jnp.int32, summed.shape, 0)
    out[...] = jnp.where(row < scalars[1], result, 0.0).astype(BF16)


def body(embeddings, labels, cluster_rows):
    rows, classes = labels.shape
    depth = embeddings.shape[1]
    groups = lax.axis_size("grp")
    steps, weight = ([1], 2.0) if groups == 2 else ([1, -1], 1.0)
    place = (lax.axis_index("dev") % QUAD).astype(jnp.int32)
    clusters = jnp.stack([place, place ^ 2, place ^ 1, place ^ 3])
    scalars = jnp.stack([place, cluster_rows[0]])
    stack = pltpu.VMEM((QUAD * rows, classes // QUAD), BF16)
    total = pltpu.VMEM((QUAD * rows, classes // QUAD), F32)
    packed = like(labels.shape, BF16)
    piece = like((rows, classes // QUAD), BF16)
    matrix = like((QUAD * rows, QUAD * rows), BF16)

    unit = call(unit_kernel, "unit", (embeddings,), like(embeddings.shape, BF16))
    unit_up = from_up(unit)
    seed, *pieces = call(seed_kernel, "seed", (scalars, labels), (packed, piece, piece, piece))
    received = exchange(pieces)
    unit_side, unit_core = from_side(unit), from_core(unit)
    cross_unit = [from_group(unit, step) for step in steps]
    received[0] = after(received[0], unit_up)
    packed_seed = call(pack_kernel, "pack", (scalars, seed, *received), packed)
    seed_up = from_up(packed_seed)
    seed_cross = [from_group(packed_seed, step) for step in steps]
    up_side, up_core = from_side(unit_up), from_core(unit_up)
    cross0 = call(
        functools.partial(cross_kernel, weight), "cross", (unit, *cross_unit), like((len(steps) * rows, rows), BF16)
    )
    unit_side = after(unit_side, packed_seed)
    unit_across = from_core(unit_side)
    unit_side = after(unit_side, cross0)
    units, near = call(
        near_kernel,
        "near",
        (clusters, unit, unit_side, unit_core, unit_across),
        (like((QUAD * rows, depth), BF16), matrix),
    )
    up_side = after(up_side, units)
    up_across = from_core(up_side)
    cross0 = after(cross0, up_side)
    cross1, cross2 = from_side(cross0), from_core(cross0)
    cross3 = from_core(cross1)
    up_core = after(up_core, seed_up)
    far, sums = call(
        far_kernel,
        "far",
        (clusters, units, unit_up, up_side, up_core, up_across, packed_seed),
        (matrix, packed),
        [pltpu.VMEM((QUAD * rows, depth), BF16), stack],
        limit=28,
    )

    def gather(own, up, cross, out):
        return call(
            functools.partial(gather_kernel, len(cross)),
            "gather",
            (clusters, near, far, cross0, cross1, cross2, cross3, own, up, *cross),
            out,
            [stack, total],
        )

    sent = from_down(sums)
    kept = gather(packed_seed, seed_up, seed_cross, like(labels.shape, F32))
    summed, squares = call(
        combine_kernel, "combine", (scalars, kept, sent), (like(labels.shape, F32), like((8, rows), F32))
    )
    current = call(mix_kernel, "mix", (summed, squares, *exchange([squares] * 3), packed_seed), packed)

    current_up = from_up(current)
    current_cross = [from_group(current, step) for step in steps]
    sums, *pieces = call(
        scatter_kernel, "scatter", (scalars, far, current), (packed, piece, piece, piece), [stack]
    )
    sums = call(pack_kernel, "pack", (scalars, sums, *exchange(pieces)), packed)
    sent = from_down(sums)
    current_up = after(current_up, sums)
    kept, *pieces = gather(current, current_up, current_cross, (packed, piece, piece, piece))
    return call(
        finish_kernel, "finish", (scalars, kept, *exchange(pieces), sent, seed), packed, [pltpu.VMEM(labels.shape, BF16)]
    )


def solution(mesh):
    placed = (P(("grp", "dev"), None), P(("grp", "dev"), None), P(("grp", "dev")))
    return jax.shard_map(
        body, mesh=mesh, in_specs=placed, out_specs=P(("grp", "dev"), None), check_vma=False
    )
```

time: 230 us -> 119 us (0.52)
  the two profiles are of different devices: /device:TPU:10 before, /device:TPU:0 now
where the time goes in v1:
time: 119 us
  waiting for transfers between devices  60.6 us (51%)
  Pallas kernels  30.1 us (25%)
  starting transfers between devices  24.7 us (21%)
  local copies, waits for them, and re-layouts  2.17 us (2%)
    ppermute x26, waiting for transfers between devices, along_dev(): lax.ppermute(block, 'dev', [(source(i) % size, i) for i in range(size)])  57.4 us
    pallas_call x13, Pallas kernels, call(): pl.pallas_call(kernel, in_specs=specs, out_shape=out_shape, scratch_shape...  30.1 us
    ppermute x26, starting transfers between devices, along_dev(): lax.ppermute(block, 'dev', [(source(i) % size, i) for i in range(size)])  20.1 us
    ppermute x3, starting transfers between devices, from_group(): lax.ppermute(block, 'grp', [((i + step) % size, i) for i in range(size)])  4.63 us
    ppermute x3, waiting for transfers between devices, from_group(): lax.ppermute(block, 'grp', [((i + step) % size, i) for i in range(size)])  3.13 us
  transfers between devices with their start and end apart: 29, of which 17 were waited for; matrix products, arithmetic and copies ran while one was open for 0% of the time, Pallas kernels for 21%

profile of v1, /device:TPU:0, one launch (start us, length us, event | category | flops | bytes accessed | tf_op | source)
XLA Modules:
  0.0 118.6 jit_solution(11918577696680130597)
XLA Ops:
  1.3 5.1 %collective-permute-start.2 = (bf16[384,768]{1,0:T(8,128)(2,1)S(1)}, bf16[384,768]{1,0:T(8,128)(2,1)S(1)}, u32[]{:S(2)}, u32[]{:S(2)}) collective-permute-start(bf16[384,768]{1,0:T(8,128)(2,1)S(1)} %unit.1.own), channel_id=1, source_target_pairs={{4,0},{5,1},{6,2},{7,3},{8,4},{9,5},{10,6},{11,7},{12,8},{13,9},{1... | collective-permute-start | bytes 1769480 | tf_op jit(solution)/shard_map/ppermute | solution.py:22
  6.4 1.5 %collective-permute-start = (bf16[384,768]{1,0:T(8,128)(2,1)S(1)}, bf16[384,768]{1,0:T(8,128)(2,1)S(1)}, u32[]{:S(2)}, u32[]{:S(2)}) collective-permute-start(bf16[384,768]{1,0:T(8,128)(2,1)S(1)} %unit.1.own), channel_id=1, source_target_pairs={{2,0},{3,1},{0,2},{1,3},{6,4},{7,5},{4,6},{5,7},{10,8},{11,9},{8,1... | collective-permute-start | bytes 1769480 | tf_op jit(solution)/shard_map/ppermute | solution.py:22
  11.4 1.4 %collective-permute-start.4 = (bf16[384,224]{1,0:T(8,128)(2,1)S(1)}, bf16[384,224]{1,0:T(8,128)(2,1)S(1)}, u32[]{:S(2)}, u32[]{:S(2)}) collective-permute-start(bf16[384,224]{1,0:T(8,128)(2,1)S(1)} %get-tuple-element.34), channel_id=1, source_target_pairs={{3,0},{2,1},{1,2},{0,3},{7,4},{6,5},{5,6},{4,7},{11,8},{10,9},{9,1... | collective-permute-start | bytes 516104 | tf_op jit(solution)/shard_map/ppermute | solution.py:22
  12.8 1.5 %collective-permute-start.5 = (bf16[384,768]{1,0:T(8,128)(2,1)S(1)}, bf16[384,768]{1,0:T(8,128)(2,1)}, u32[]{:S(2)}, u32[]{:S(2)}) collective-permute-start(bf16[384,768]{1,0:T(8,128)(2,1)S(1)} %unit.1.own), channel_id=1, source_target_pairs={{16,0},{0,16},{17,1},{1,17},{18,2},{2,18},{19,3},{3,19},{20,4},{4,... | collective-permute-start | bytes 1769480 | tf_op jit(solution)/shard_map/ppermute | solution.py:43
  14.3 4.6 %collective-permute-done.2.up = bf16[384,768]{1,0:T(8,128)(2,1)S(1)} collective-permute-done((bf16[384,768]{1,0:T(8,128)(2,1)S(1)}, bf16[384,768]{1,0:T(8,128)(2,1)S(1)}, u32[]{:S(2)}, u32[]{:S(2)}) %collective-permute-start.2) | collective-permute-done | bytes 589856 | tf_op jit(solution)/shard_map/ppermute | solution.py:22
  19.0 7.9 %collective-permute-done.3.rest_1_ = bf16[384,224]{1,0:T(8,128)(2,1)S(1)} collective-permute-done((bf16[384,224]{1,0:T(8,128)(2,1)S(1)}, bf16[384,224]{1,0:T(8,128)(2,1)S(1)}, u32[]{:S(2)}, u32[]{:S(2)}) %collective-permute-start.3) | collective-permute-done | bytes 172064 | tf_op jit(solution)/shard_map/ppermute | solution.py:22
  26.9 1.8 %collective-permute-done.4.rest_2_ = bf16[384,224]{1,0:T(8,128)(2,1)S(1)} collective-permute-done((bf16[384,224]{1,0:T(8,128)(2,1)S(1)}, bf16[384,224]{1,0:T(8,128)(2,1)S(1)}, u32[]{:S(2)}, u32[]{:S(2)}) %collective-permute-start.4) | collective-permute-done | bytes 172064 | tf_op jit(solution)/shard_map/ppermute | solution.py:22
  30.4 1.5 %collective-permute-start.8 = (bf16[384,768]{1,0:T(8,128)(2,1)}, bf16[384,768]{1,0:T(8,128)(2,1)}, u32[]{:S(2)}, u32[]{:S(2)}) collective-permute-start(bf16[384,768]{1,0:T(8,128)(2,1)} %copy-done.2), channel_id=1, source_target_pairs={{2,0},{3,1},{0,2},{1,3},{6,4},{7,5},{4,6},{5,7},{10,8},{11,9},{8,1... | collective-permute-start | bytes 1769480 | tf_op jit(solution)/shard_map/ppermute | solution.py:22
  32.4 1.6 %cross.1.t0 = bf16[384,384]{1,0:T(8,128)(2,1)S(1)} custom-call(bf16[384,768]{1,0:T(8,128)(2,1)S(1)} %unit.1.own, bf16[384,768]{1,0:T(8,128)(2,1)} %collective-permute-done.5.rest_0_), custom_call_target="tpu_custom_call" | custom-call | tf_op jit(solution)/shard_map/cross/pallas_call | solution.py:58
  34.1 5.1 %near.1 = (bf16[1536,768]{1,0:T(8,128)(2,1)S(1)}, bf16[1536,1536]{1,0:T(8,128)(2,1)S(1)}) custom-call(s32[4]{0:T(128)S(1)} %pad_add_fusion.1.clusters, bf16[384,768]{1,0:T(8,128)(2,1)S(1)} %unit.1.own, bf16[384,768]{1,0:T(8,128)(2,1)S(1)} %collective-permute-done.side, bf16[384,768]{1,0:T(8,128)(2,1)S(1)} %collective-permute-done.6.core, ...), custom_call_target="tpu_custom_call" | custom-call | tf_op jit(solution)/shard_map/near/pallas_call | solution.py:58
  39.2 6.8 %collective-permute-done.8.side = bf16[384,768]{1,0:T(8,128)(2,1)} collective-permute-done((bf16[384,768]{1,0:T(8,128)(2,1)}, bf16[384,768]{1,0:T(8,128)(2,1)}, u32[]{:S(2)}, u32[]{:S(2)}) %collective-permute-start.8) | collective-permute-done | bytes 589856 | tf_op jit(solution)/shard_map/ppermute | solution.py:22
  46.0 1.5 %collective-permute-start.15 = (bf16[384,896]{1,0:T(8,128)(2,1)S(1)}, bf16[384,896]{1,0:T(8,128)(2,1)S(1)}, u32[]{:S(2)}, u32[]{:S(2)}) collective-permute-start(bf16[384,896]{1,0:T(8,128)(2,1)S(1)} %pack.2.own.seed), channel_id=1, source_target_pairs={{16,0},{0,16},{17,1},{1,17},{18,2},{2,18},{19,3},{3,19},{20,4},{4,... | collective-permute-start | bytes 2064392 | tf_op jit(solution)/shard_map/ppermute | solution.py:43
  47.6 1.5 %collective-permute-done.10.up = bf16[384,896]{1,0:T(8,128)(2,1)S(1)} collective-permute-done((bf16[384,896]{1,0:T(8,128)(2,1)S(1)}, bf16[384,896]{1,0:T(8,128)(2,1)S(1)}, u32[]{:S(2)}, u32[]{:S(2)}) %collective-permute-start.10) | collective-permute-done | bytes 688160 | tf_op jit(solution)/shard_map/ppermute | solution.py:22
  49.0 4.8 %far.1 = (bf16[1536,1536]{1,0:T(8,128)(2,1)S(1)}, bf16[384,896]{1,0:T(8,128)(2,1)S(1)}) custom-call(s32[4]{0:T(128)S(1)} %pad_add_fusion.1.clusters, bf16[1536,768]{1,0:T(8,128)(2,1)S(1)} %get-tuple-element.38.units, bf16[384,768]{1,0:T(8,128)(2,1)S(1)} %copy-done.3, bf16[384,768]{1,0:T(8,128)(2,1)} %collective-permute-done.8.side, ...), custom_call_target="tpu_custom_call" | custom-call | tf_op jit(solution)/shard_map/far/pallas_call | solution.py:58
  54.9 7.6 %collective-permute-done.12.t1 = bf16[384,384]{1,0:T(8,128)(2,1)S(1)} collective-permute-done((bf16[384,384]{1,0:T(8,128)(2,1)S(1)}, bf16[384,384]{1,0:T(8,128)(2,1)S(1)}, u32[]{:S(2)}, u32[]{:S(2)}) %collective-permute-start.12) | collective-permute-done | bytes 294944 | tf_op jit(solution)/shard_map/ppermute | solution.py:22
  62.4 1.4 %collective-permute-done.15.rest_0_ = bf16[384,896]{1,0:T(8,128)(2,1)S(1)} collective-permute-done((bf16[384,896]{1,0:T(8,128)(2,1)S(1)}, bf16[384,896]{1,0:T(8,128)(2,1)S(1)}, u32[]{:S(2)}, u32[]{:S(2)}) %collective-permute-start.15) | collective-permute-done | bytes 688160 | tf_op jit(solution)/shard_map/ppermute | solution.py:43
  64.0 3.5 %gather.2.kept = f32[384,896]{1,0:T(8,128)S(1)} custom-call(s32[4]{0:T(128)S(1)} %pad_add_fusion.1.clusters, bf16[1536,1536]{1,0:T(8,128)(2,1)S(1)} %get-tuple-element.37.near, bf16[1536,1536]{1,0:T(8,128)(2,1)S(1)} %get-tuple-element.41.far, bf16[384,384]{1,0:T(8,128)(2,1)S(1)} %cross.1.t0, bf16[384,384]{1,0:T(8,128)(2,1)S(1)} %collective-permute-done.12.t1, ...), custom_call_target="tpu_custom_call" | custom-call | tf_op jit(solution)/shard_map/gather/pallas_call | solution.py:58
  67.5 5.1 %collective-permute-done.16.sent = bf16[384,896]{1,0:T(8,128)(2,1)S(1)} collective-permute-done((bf16[384,896]{1,0:T(8,128)(2,1)S(1)}, bf16[384,896]{1,0:T(8,128)(2,1)S(1)}, u32[]{:S(2)}, u32[]{:S(2)}) %collective-permute-start.16) | collective-permute-done | bytes 688160 | tf_op jit(solution)/shard_map/ppermute | solution.py:22
  72.6 1.8 %combine.1 = (f32[384,896]{1,0:T(8,128)S(1)}, f32[8,384]{1,0:T(8,128)S(1)}) custom-call(s32[2]{0:T(128)S(1)} %pad_add_fusion.scalars, f32[384,896]{1,0:T(8,128)S(1)} %gather.2.kept, bf16[384,896]{1,0:T(8,128)(2,1)S(1)} %collective-permute-done.16.sent), custom_call_target="tpu_custom_call" | custom-call | tf_op jit(solution)/shard_map/combine/pallas_call | solution.py:58
  74.3 1.5 %collective-permute-start.18 = (f32[8,384]{1,0:T(8,128)S(1)}, f32[8,384]{1,0:T(8,128)S(1)}, u32[]{:S(2)}, u32[]{:S(2)}) collective-permute-start(f32[8,384]{1,0:T(8,128)S(1)} %get-tuple-element.45.s0), channel_id=1, source_target_pairs={{2,0},{3,1},{0,2},{1,3},{6,4},{7,5},{4,6},{5,7},{10,8},{11,9},{8,1... | collective-permute-start | bytes 36872 | tf_op jit(solution)/shard_map/ppermute | solution.py:22
  76.2 1.9 %collective-permute-done.18.s2 = f32[8,384]{1,0:T(8,128)S(1)} collective-permute-done((f32[8,384]{1,0:T(8,128)S(1)}, f32[8,384]{1,0:T(8,128)S(1)}, u32[]{:S(2)}, u32[]{:S(2)}) %collective-permute-start.18) | collective-permute-done | bytes 12320 | tf_op jit(solution)/shard_map/ppermute | solution.py:22
  80.4 2.5 %scatter.1 = (bf16[384,896]{1,0:T(8,128)(2,1)S(1)}, bf16[384,224]{1,0:T(8,128)(2,1)S(1)}, bf16[384,224]{1,0:T(8,128)(2,1)S(1)}, bf16[384,224]{1,0:T(8,128)(2,1)S(1)}) custom-call(s32[2]{0:T(128)S(1)} %pad_add_fusion.scalars, bf16[1536,1536]{1,0:T(8,128)(2,1)S(1)} %get-tuple-element.41.far, bf16[384,896]{1,0:T(8,128)(2,1)S(1)} %mix.1.own), custom_call_target="tpu_custom_call" | custom-call | tf_op jit(solution)/shard_map/scatter/pallas_call | solution.py:58
  82.9 1.6 %collective-permute-start.24 = (bf16[384,896]{1,0:T(8,128)(2,1)S(1)}, bf16[384,896]{1,0:T(8,128)(2,1)S(1)}, u32[]{:S(2)}, u32[]{:S(2)}) collective-permute-start(bf16[384,896]{1,0:T(8,128)(2,1)S(1)} %mix.1.own), channel_id=1, source_target_pairs={{16,0},{0,16},{17,1},{1,17},{18,2},{2,18},{19,3},{3,19},{20,4},{4,... | collective-permute-start | bytes 2064392 | tf_op jit(solution)/shard_map/ppermute | solution.py:43
  85.0 1.3 %collective-permute-start.23 = (bf16[384,224]{1,0:T(8,128)(2,1)S(1)}, bf16[384,224]{1,0:T(8,128)(2,1)S(1)}, u32[]{:S(2)}, u32[]{:S(2)}) collective-permute-start(bf16[384,224]{1,0:T(8,128)(2,1)S(1)} %get-tuple-element.49), channel_id=1, source_target_pairs={{3,0},{2,1},{1,2},{0,3},{7,4},{6,5},{5,6},{4,7},{11,8},{10,9},{9,1... | collective-permute-start | bytes 516104 | tf_op jit(solution)/shard_map/ppermute | solution.py:22
  86.4 5.8 %collective-permute-done.22.rest_1_ = bf16[384,224]{1,0:T(8,128)(2,1)S(1)} collective-permute-done((bf16[384,224]{1,0:T(8,128)(2,1)S(1)}, bf16[384,224]{1,0:T(8,128)(2,1)S(1)}, u32[]{:S(2)}, u32[]{:S(2)}) %collective-permute-start.22) | collective-permute-done | bytes 172064 | tf_op jit(solution)/shard_map/ppermute | solution.py:22
  92.2 3.4 %collective-permute-done.23.rest_2_ = bf16[384,224]{1,0:T(8,128)(2,1)S(1)} collective-permute-done((bf16[384,224]{1,0:T(8,128)(2,1)S(1)}, bf16[384,224]{1,0:T(8,128)(2,1)S(1)}, u32[]{:S(2)}, u32[]{:S(2)}) %collective-permute-start.23) | collective-permute-done | bytes 172064 | tf_op jit(solution)/shard_map/ppermute | solution.py:22
  96.6 2.1 %collective-permute-start.28 = (bf16[384,896]{1,0:T(8,128)(2,1)S(1)}, bf16[384,896]{1,0:T(8,128)(2,1)S(1)}, u32[]{:S(2)}, u32[]{:S(2)}) collective-permute-start(bf16[384,896]{1,0:T(8,128)(2,1)S(1)} %pack.3), channel_id=1, source_target_pairs={{12,0},{13,1},{14,2},{15,3},{0,4},{1,5},{2,6},{3,7},{4,8},{5,9},{6... | collective-permute-start | bytes 2064392 | tf_op jit(solution)/shard_map/ppermute | solution.py:22
  98.7 1.7 %collective-permute-done.24.rest_0_ = bf16[384,896]{1,0:T(8,128)(2,1)S(1)} collective-permute-done((bf16[384,896]{1,0:T(8,128)(2,1)S(1)}, bf16[384,896]{1,0:T(8,128)(2,1)S(1)}, u32[]{:S(2)}, u32[]{:S(2)}) %collective-permute-start.24) | collective-permute-done | bytes 688160 | tf_op jit(solution)/shard_map/ppermute | solution.py:43
  100.4 3.9 %gather.3 = (bf16[384,896]{1,0:T(8,128)(2,1)S(1)}, bf16[384,224]{1,0:T(8,128)(2,1)S(1)}, bf16[384,224]{1,0:T(8,128)(2,1)S(1)}, bf16[384,224]{1,0:T(8,128)(2,1)S(1)}) custom-call(s32[4]{0:T(128)S(1)} %pad_add_fusion.1.clusters, bf16[1536,1536]{1,0:T(8,128)(2,1)S(1)} %get-tuple-element.37.near, bf16[1536,1536]{1,0:T(8,128)(2,1)S(1)} %get-tuple-element.41.far, ...), custom_call_target="tpu_custom_call" | custom-call | tf_op jit(solution)/shard_map/gather/pallas_call | solution.py:58
  106.2 5.9 %collective-permute-done.26.k2 = bf16[384,224]{1,0:T(8,128)(2,1)S(1)} collective-permute-done((bf16[384,224]{1,0:T(8,128)(2,1)S(1)}, bf16[384,224]{1,0:T(8,128)(2,1)S(1)}, u32[]{:S(2)}, u32[]{:S(2)}) %collective-permute-start.26) | collective-permute-done | bytes 172064 | tf_op jit(solution)/shard_map/ppermute | solution.py:22
  112.1 3.3 %collective-permute-done.27.k3 = bf16[384,224]{1,0:T(8,128)(2,1)S(1)} collective-permute-done((bf16[384,224]{1,0:T(8,128)(2,1)S(1)}, bf16[384,224]{1,0:T(8,128)(2,1)S(1)}, u32[]{:S(2)}, u32[]{:S(2)}) %collective-permute-start.27) | collective-permute-done | bytes 172064 | tf_op jit(solution)/shard_map/ppermute | solution.py:22
  116.2 2.4 %finish.1 = bf16[384,896]{1,0:T(8,128)(2,1)} custom-call(s32[2]{0:T(128)S(1)} %pad_add_fusion.scalars, bf16[384,896]{1,0:T(8,128)(2,1)S(1)} %get-tuple-element.51.kept, bf16[384,224]{1,0:T(8,128)(2,1)S(1)} %collective-permute-done.25.k1, bf16[384,224]{1,0:T(8,128)(2,1)S(1)} %collective-permute-done.26.k2, bf16[384,224]{1,0:T(8,128)(2,1)S(1)} %collective-permute-done.27.k3, ...), custom_call_target="tpu_custom_call" | custom-call | tf_op jit(solution)/shard_map/finish/pallas_call | solution.py:58
  (49 shorter events, 14.5 us)
Async XLA Ops:
  1.3 17.7 %collective-permute-start.2 = (bf16[384,768]{1,0:T(8,128)(2,1)S(1)}, bf16[384,768]{1,0:T(8,128)(2,1)S(1)}, u32[]{:S(2)}, u32[]{:S(2)}) collective-permute-start(bf16[384,768]{1,0:T(8,128)(2,1)S(1)} %unit.1.own), channel_id=1, source_target_pairs={{4,0},{5,1},{6,2},{7,3},{8,4},{9,5},{10,6},{11,7},{12,8},{13,9},{1... | collective-permute-start | bytes 1769480 | tf_op jit(solution)/shard_map/ppermute | solution.py:22
  6.4 23.2 %collective-permute-start = (bf16[384,768]{1,0:T(8,128)(2,1)S(1)}, bf16[384,768]{1,0:T(8,128)(2,1)S(1)}, u32[]{:S(2)}, u32[]{:S(2)}) collective-permute-start(bf16[384,768]{1,0:T(8,128)(2,1)S(1)} %unit.1.own), channel_id=1, source_target_pairs={{2,0},{3,1},{0,2},{1,3},{6,4},{7,5},{4,6},{5,7},{10,8},{11,9},{8,1... | collective-permute-start | bytes 1769480 | tf_op jit(solution)/shard_map/ppermute | solution.py:22
  8.6 1.1 copy-start
  10.9 1.9 %collective-permute-start.1 = (bf16[384,224]{1,0:T(8,128)(2,1)S(1)}, bf16[384,224]{1,0:T(8,128)(2,1)S(1)}, u32[]{:S(2)}, u32[]{:S(2)}) collective-permute-start(bf16[384,224]{1,0:T(8,128)(2,1)S(1)} %get-tuple-element.31), channel_id=1, source_target_pairs={{1,0},{0,1},{3,2},{2,3},{5,4},{4,5},{7,6},{6,7},{9,8},{8,9},{11,10... | collective-permute-start | bytes 516104 | tf_op jit(solution)/shard_map/ppermute | solution.py:22
  11.0 15.9 %collective-permute-start.3 = (bf16[384,224]{1,0:T(8,128)(2,1)S(1)}, bf16[384,224]{1,0:T(8,128)(2,1)S(1)}, u32[]{:S(2)}, u32[]{:S(2)}) collective-permute-start(bf16[384,224]{1,0:T(8,128)(2,1)S(1)} %get-tuple-element.33), channel_id=1, source_target_pairs={{2,0},{3,1},{0,2},{1,3},{6,4},{7,5},{4,6},{5,7},{10,8},{11,9},{8,1... | collective-permute-start | bytes 516104 | tf_op jit(solution)/shard_map/ppermute | solution.py:22
  11.4 17.2 %collective-permute-start.4 = (bf16[384,224]{1,0:T(8,128)(2,1)S(1)}, bf16[384,224]{1,0:T(8,128)(2,1)S(1)}, u32[]{:S(2)}, u32[]{:S(2)}) collective-permute-start(bf16[384,224]{1,0:T(8,128)(2,1)S(1)} %get-tuple-element.34), channel_id=1, source_target_pairs={{3,0},{2,1},{1,2},{0,3},{7,4},{6,5},{5,6},{4,7},{11,8},{10,9},{9,1... | collective-permute-start | bytes 516104 | tf_op jit(solution)/shard_map/ppermute | solution.py:22
  12.8 19.6 %collective-permute-start.5 = (bf16[384,768]{1,0:T(8,128)(2,1)S(1)}, bf16[384,768]{1,0:T(8,128)(2,1)}, u32[]{:S(2)}, u32[]{:S(2)}) collective-permute-start(bf16[384,768]{1,0:T(8,128)(2,1)S(1)} %unit.1.own), channel_id=1, source_target_pairs={{16,0},{0,16},{17,1},{1,17},{18,2},{2,18},{19,3},{3,19},{20,4},{4,... | collective-permute-start | bytes 1769480 | tf_op jit(solution)/shard_map/ppermute | solution.py:43
  19.0 9.6 %copy-start.2 = (bf16[384,768]{1,0:T(8,128)(2,1)}, bf16[384,768]{1,0:T(8,128)(2,1)S(1)}, u32[]{:S(2)}) copy-start(bf16[384,768]{1,0:T(8,128)(2,1)S(1)} %collective-permute-done.2.up) | copy-start | bytes 1769476
  19.0 15.1 %collective-permute-start.6 = (bf16[384,768]{1,0:T(8,128)(2,1)S(1)}, bf16[384,768]{1,0:T(8,128)(2,1)S(1)}, u32[]{:S(2)}, u32[]{:S(2)}) collective-permute-start(bf16[384,768]{1,0:T(8,128)(2,1)S(1)} %unit.1.own), channel_id=1, source_target_pairs={{1,0},{0,1},{3,2},{2,3},{5,4},{4,5},{7,6},{6,7},{9,8},{8,9},{11,10... | collective-permute-start | bytes 1769480 | tf_op jit(solution)/shard_map/ppermute | solution.py:22
  29.6 4.5 %collective-permute-start.7 = (bf16[384,768]{1,0:T(8,128)(2,1)S(1)}, bf16[384,768]{1,0:T(8,128)(2,1)}, u32[]{:S(2)}, u32[]{:S(2)}) collective-permute-start(bf16[384,768]{1,0:T(8,128)(2,1)S(1)} %collective-permute-done.side), channel_id=1, source_target_pairs={{1,0},{0,1},{3,2},{2,3},{5,4},{4,5},{7,6},{6,7},{9,8},{8,9},{11,10... | collective-permute-start | bytes 1769480 | tf_op jit(solution)/shard_map/ppermute | solution.py:22
  30.4 15.6 %collective-permute-start.8 = (bf16[384,768]{1,0:T(8,128)(2,1)}, bf16[384,768]{1,0:T(8,128)(2,1)}, u32[]{:S(2)}, u32[]{:S(2)}) collective-permute-start(bf16[384,768]{1,0:T(8,128)(2,1)} %copy-done.2), channel_id=1, source_target_pairs={{2,0},{3,1},{0,2},{1,3},{6,4},{7,5},{4,6},{5,7},{10,8},{11,9},{8,1... | collective-permute-start | bytes 1769480 | tf_op jit(solution)/shard_map/ppermute | solution.py:22
  31.9 17.1 %copy-start.3 = (bf16[384,768]{1,0:T(8,128)(2,1)S(1)}, bf16[384,768]{1,0:T(8,128)(2,1)}, u32[]{:S(2)}) copy-start(bf16[384,768]{1,0:T(8,128)(2,1)} %copy-done.2) | copy-start | bytes 1769476
  31.9 17.1 %collective-permute-start.10 = (bf16[384,896]{1,0:T(8,128)(2,1)S(1)}, bf16[384,896]{1,0:T(8,128)(2,1)S(1)}, u32[]{:S(2)}, u32[]{:S(2)}) collective-permute-start(bf16[384,896]{1,0:T(8,128)(2,1)S(1)} %pack.2.own.seed), channel_id=1, source_target_pairs={{4,0},{5,1},{6,2},{7,3},{8,4},{9,5},{10,6},{11,7},{12,8},{13,9},{1... | collective-permute-start | bytes 2064392 | tf_op jit(solution)/shard_map/ppermute | solution.py:22
  34.0 13.6 %collective-permute-start.9 = (bf16[384,768]{1,0:T(8,128)(2,1)}, bf16[384,768]{1,0:T(8,128)(2,1)S(1)}, u32[]{:S(2)}, u32[]{:S(2)}) collective-permute-start(bf16[384,768]{1,0:T(8,128)(2,1)} %copy-done.2), channel_id=1, source_target_pairs={{1,0},{0,1},{3,2},{2,3},{5,4},{4,5},{7,6},{6,7},{9,8},{8,9},{11,10... | collective-permute-start | bytes 1769480 | tf_op jit(solution)/shard_map/ppermute | solution.py:22
  46.0 3.0 %collective-permute-start.11 = (bf16[384,768]{1,0:T(8,128)(2,1)}, bf16[384,768]{1,0:T(8,128)(2,1)S(1)}, u32[]{:S(2)}, u32[]{:S(2)}) collective-permute-start(bf16[384,768]{1,0:T(8,128)(2,1)} %collective-permute-done.8.side), channel_id=1, source_target_pairs={{1,0},{0,1},{3,2},{2,3},{5,4},{4,5},{7,6},{6,7},{9,8},{8,9},{11,10... | collective-permute-start | bytes 1769480 | tf_op jit(solution)/shard_map/ppermute | solution.py:22
  46.0 17.8 %collective-permute-start.15 = (bf16[384,896]{1,0:T(8,128)(2,1)S(1)}, bf16[384,896]{1,0:T(8,128)(2,1)S(1)}, u32[]{:S(2)}, u32[]{:S(2)}) collective-permute-start(bf16[384,896]{1,0:T(8,128)(2,1)S(1)} %pack.2.own.seed), channel_id=1, source_target_pairs={{16,0},{0,16},{17,1},{1,17},{18,2},{2,18},{19,3},{3,19},{20,4},{4,... | collective-permute-start | bytes 2064392 | tf_op jit(solution)/shard_map/ppermute | solution.py:43
  53.9 18.7 %collective-permute-start.16 = (bf16[384,896]{1,0:T(8,128)(2,1)S(1)}, bf16[384,896]{1,0:T(8,128)(2,1)S(1)}, u32[]{:S(2)}, u32[]{:S(2)}) collective-permute-start(bf16[384,896]{1,0:T(8,128)(2,1)S(1)} %get-tuple-element.43), channel_id=1, source_target_pairs={{12,0},{13,1},{14,2},{15,3},{0,4},{1,5},{2,6},{3,7},{4,8},{5,9},{6... | collective-permute-start | bytes 2064392 | tf_op jit(solution)/shard_map/ppermute | solution.py:22
  54.1 8.3 %collective-permute-start.12 = (bf16[384,384]{1,0:T(8,128)(2,1)S(1)}, bf16[384,384]{1,0:T(8,128)(2,1)S(1)}, u32[]{:S(2)}, u32[]{:S(2)}) collective-permute-start(bf16[384,384]{1,0:T(8,128)(2,1)S(1)} %cross.1.t0), channel_id=1, source_target_pairs={{2,0},{3,1},{0,2},{1,3},{6,4},{7,5},{4,6},{5,7},{10,8},{11,9},{8,1... | collective-permute-start | bytes 884744 | tf_op jit(solution)/shard_map/ppermute | solution.py:22
  54.9 9.0 %collective-permute-start.13 = (bf16[384,384]{1,0:T(8,128)(2,1)S(1)}, bf16[384,384]{1,0:T(8,128)(2,1)S(1)}, u32[]{:S(2)}, u32[]{:S(2)}) collective-permute-start(bf16[384,384]{1,0:T(8,128)(2,1)S(1)} %cross.1.t0), channel_id=1, source_target_pairs={{1,0},{0,1},{3,2},{2,3},{5,4},{4,5},{7,6},{6,7},{9,8},{8,9},{11,10... | collective-permute-start | bytes 884744 | tf_op jit(solution)/shard_map/ppermute | solution.py:22
  62.4 1.6 %collective-permute-start.14 = (bf16[384,384]{1,0:T(8,128)(2,1)S(1)}, bf16[384,384]{1,0:T(8,128)(2,1)S(1)}, u32[]{:S(2)}, u32[]{:S(2)}) collective-permute-start(bf16[384,384]{1,0:T(8,128)(2,1)S(1)} %collective-permute-done.12.t1), channel_id=1, source_target_pairs={{1,0},{0,1},{3,2},{2,3},{5,4},{4,5},{7,6},{6,7},{9,8},{8,9},{11,10... | collective-permute-start | bytes 884744 | tf_op jit(solution)/shard_map/ppermute | solution.py:22
  74.3 1.9 %collective-permute-start.17 = (f32[8,384]{1,0:T(8,128)S(1)}, f32[8,384]{1,0:T(8,128)S(1)}, u32[]{:S(2)}, u32[]{:S(2)}) collective-permute-start(f32[8,384]{1,0:T(8,128)S(1)} %get-tuple-element.45.s0), channel_id=1, source_target_pairs={{1,0},{0,1},{3,2},{2,3},{5,4},{4,5},{7,6},{6,7},{9,8},{8,9},{11,10... | collective-permute-start | bytes 36872 | tf_op jit(solution)/shard_map/ppermute | solution.py:22
  74.3 3.7 %collective-permute-start.18 = (f32[8,384]{1,0:T(8,128)S(1)}, f32[8,384]{1,0:T(8,128)S(1)}, u32[]{:S(2)}, u32[]{:S(2)}) collective-permute-start(f32[8,384]{1,0:T(8,128)S(1)} %get-tuple-element.45.s0), channel_id=1, source_target_pairs={{2,0},{3,1},{0,2},{1,3},{6,4},{7,5},{4,6},{5,7},{10,8},{11,9},{8,1... | collective-permute-start | bytes 36872 | tf_op jit(solution)/shard_map/ppermute | solution.py:22
  75.9 3.1 %collective-permute-start.19 = (f32[8,384]{1,0:T(8,128)S(1)}, f32[8,384]{1,0:T(8,128)S(1)}, u32[]{:S(2)}, u32[]{:S(2)}) collective-permute-start(f32[8,384]{1,0:T(8,128)S(1)} %get-tuple-element.45.s0), channel_id=1, source_target_pairs={{3,0},{2,1},{1,2},{0,3},{7,4},{6,5},{5,6},{4,7},{11,8},{10,9},{9,1... | collective-permute-start | bytes 36872 | tf_op jit(solution)/shard_map/ppermute | solution.py:22
  80.3 18.4 %collective-permute-start.20 = (bf16[384,896]{1,0:T(8,128)(2,1)S(1)}, bf16[384,896]{1,0:T(8,128)(2,1)S(1)}, u32[]{:S(2)}, u32[]{:S(2)}) collective-permute-start(bf16[384,896]{1,0:T(8,128)(2,1)S(1)} %mix.1.own), channel_id=1, source_target_pairs={{4,0},{5,1},{6,2},{7,3},{8,4},{9,5},{10,6},{11,7},{12,8},{13,9},{1... | collective-permute-start | bytes 2064392 | tf_op jit(solution)/shard_map/ppermute | solution.py:22
  82.9 17.4 %collective-permute-start.24 = (bf16[384,896]{1,0:T(8,128)(2,1)S(1)}, bf16[384,896]{1,0:T(8,128)(2,1)S(1)}, u32[]{:S(2)}, u32[]{:S(2)}) collective-permute-start(bf16[384,896]{1,0:T(8,128)(2,1)S(1)} %mix.1.own), channel_id=1, source_target_pairs={{16,0},{0,16},{17,1},{1,17},{18,2},{2,18},{19,3},{3,19},{20,4},{4,... | collective-permute-start | bytes 2064392 | tf_op jit(solution)/shard_map/ppermute | solution.py:43
  84.5 1.9 %collective-permute-start.21 = (bf16[384,224]{1,0:T(8,128)(2,1)S(1)}, bf16[384,224]{1,0:T(8,128)(2,1)S(1)}, u32[]{:S(2)}, u32[]{:S(2)}) collective-permute-start(bf16[384,224]{1,0:T(8,128)(2,1)S(1)} %get-tuple-element.47), channel_id=1, source_target_pairs={{1,0},{0,1},{3,2},{2,3},{5,4},{4,5},{7,6},{6,7},{9,8},{8,9},{11,10... | collective-permute-start | bytes 516104 | tf_op jit(solution)/shard_map/ppermute | solution.py:22
  84.5 7.7 %collective-permute-start.22 = (bf16[384,224]{1,0:T(8,128)(2,1)S(1)}, bf16[384,224]{1,0:T(8,128)(2,1)S(1)}, u32[]{:S(2)}, u32[]{:S(2)}) collective-permute-start(bf16[384,224]{1,0:T(8,128)(2,1)S(1)} %get-tuple-element.48), channel_id=1, source_target_pairs={{2,0},{3,1},{0,2},{1,3},{6,4},{7,5},{4,6},{5,7},{10,8},{11,9},{8,1... | collective-permute-start | bytes 516104 | tf_op jit(solution)/shard_map/ppermute | solution.py:22
  85.0 10.6 %collective-permute-start.23 = (bf16[384,224]{1,0:T(8,128)(2,1)S(1)}, bf16[384,224]{1,0:T(8,128)(2,1)S(1)}, u32[]{:S(2)}, u32[]{:S(2)}) collective-permute-start(bf16[384,224]{1,0:T(8,128)(2,1)S(1)} %get-tuple-element.49), channel_id=1, source_target_pairs={{3,0},{2,1},{1,2},{0,3},{7,4},{6,5},{5,6},{4,7},{11,8},{10,9},{9,1... | collective-permute-start | bytes 516104 | tf_op jit(solution)/shard_map/ppermute | solution.py:22
  96.6 19.6 %collective-permute-start.28 = (bf16[384,896]{1,0:T(8,128)(2,1)S(1)}, bf16[384,896]{1,0:T(8,128)(2,1)S(1)}, u32[]{:S(2)}, u32[]{:S(2)}) collective-permute-start(bf16[384,896]{1,0:T(8,128)(2,1)S(1)} %pack.3), channel_id=1, source_target_pairs={{12,0},{13,1},{14,2},{15,3},{0,4},{1,5},{2,6},{3,7},{4,8},{5,9},{6... | collective-permute-start | bytes 2064392 | tf_op jit(solution)/shard_map/ppermute | solution.py:22
  104.3 1.9 %collective-permute-start.25 = (bf16[384,224]{1,0:T(8,128)(2,1)S(1)}, bf16[384,224]{1,0:T(8,128)(2,1)S(1)}, u32[]{:S(2)}, u32[]{:S(2)}) collective-permute-start(bf16[384,224]{1,0:T(8,128)(2,1)S(1)} %get-tuple-element.52), channel_id=1, source_target_pairs={{1,0},{0,1},{3,2},{2,3},{5,4},{4,5},{7,6},{6,7},{9,8},{8,9},{11,10... | collective-permute-start | bytes 516104 | tf_op jit(solution)/shard_map/ppermute | solution.py:22
  104.3 7.8 %collective-permute-start.26 = (bf16[384,224]{1,0:T(8,128)(2,1)S(1)}, bf16[384,224]{1,0:T(8,128)(2,1)S(1)}, u32[]{:S(2)}, u32[]{:S(2)}) collective-permute-start(bf16[384,224]{1,0:T(8,128)(2,1)S(1)} %get-tuple-element.53), channel_id=1, source_target_pairs={{2,0},{3,1},{0,2},{1,3},{6,4},{7,5},{4,6},{5,7},{10,8},{11,9},{8,1... | collective-permute-start | bytes 516104 | tf_op jit(solution)/shard_map/ppermute | solution.py:22
  104.9 10.5 %collective-permute-start.27 = (bf16[384,224]{1,0:T(8,128)(2,1)S(1)}, bf16[384,224]{1,0:T(8,128)(2,1)S(1)}, u32[]{:S(2)}, u32[]{:S(2)}) collective-permute-start(bf16[384,224]{1,0:T(8,128)(2,1)S(1)} %get-tuple-element.54), channel_id=1, source_target_pairs={{3,0},{2,1},{1,2},{0,3},{7,4},{6,5},{5,6},{4,7},{11,8},{10,9},{9,1... | collective-permute-start | bytes 516104 | tf_op jit(solution)/shard_map/ppermute | solution.py:22
  (1 other events, 1.1 us)

commit v2 on v1

v2 whole, which is shorter than its diff:
```python
import functools
import math

import jax
import jax.numpy as jnp
from jax import lax
from jax.experimental import pallas as pl
from jax.experimental.pallas import tpu as pltpu
from jax.sharding import PartitionSpec as P

sharpness = 25.0
keep_share = 0.8
BF16 = jnp.bfloat16
F32 = jnp.float32
QUAD = 4
INVALID = 1e38
MB = 2**20


def along_dev(block, source):
    size = lax.axis_size("dev")
    return lax.ppermute(block, "dev", [(source(i) % size, i) for i in range(size)])


def from_up(block):
    return along_dev(block, lambda i: i + QUAD)


def from_down(block):
    return along_dev(block, lambda i: i - QUAD)


def from_side(block):
    return along_dev(block, lambda i: i ^ 2)


def from_core(block):
    return along_dev(block, lambda i: i ^ 1)


def from_group(block, step):
    size = lax.axis_size("grp")
    return lax.ppermute(block, "grp", [((i + step) % size, i) for i in range(size)])


def after(value, earlier):
    return lax.optimization_barrier((value, earlier))[0]


def exchange(pieces):
    return [along_dev(piece, lambda i, m=m: i ^ m) for m, piece in enumerate(pieces, 1)]


def call(kernel, name, operands, out_shape, scratch=(), limit=12, aliases={}):
    specs = [
        pl.BlockSpec(memory_space=pltpu.SMEM if x.dtype == jnp.int32 else pltpu.VMEM) for x in operands
    ]
    return pl.pallas_call(
        kernel,
        in_specs=specs,
        out_shape=out_shape,
        scratch_shapes=list(scratch),
        input_output_aliases=aliases,
        compiler_params=pltpu.CompilerParams(vmem_limit_bytes=limit * MB),
        name=name,
    )(*operands)


def like(shape, dtype):
    return jax.ShapeDtypeStruct(tuple(shape), dtype)


def dot(left, right):
    return jnp.dot(left, right, preferred_element_type=F32)


def affinity(left, right):
    cosine = lax.dot_general(left, right, (((1,), (1,)), ((), ())), preferred_element_type=F32)
    return jnp.exp2(cosine * (sharpness * math.log2(math.e)))


def cut(block, place, pieces):
    quarter = block.shape[1] // QUAD
    for k in range(QUAD):
        for m, piece in pieces:

            @pl.when(place ^ m == k)
            def _():
                piece[...] = block[:, k * quarter : (k + 1) * quarter]


def join(place, pieces, out):
    quarter = out.shape[1] // QUAD
    for k in range(QUAD):
        for m, piece in pieces:

            @pl.when(place ^ m == k)
            def _():
                out[:, k * quarter : (k + 1) * quarter] = piece[...]


def unit_kernel(embeddings, unit, *parts):
    values = embeddings[...].astype(F32)
    scaled = values * lax.rsqrt(jnp.mean(values * values, axis=-1, keepdims=True) + 1e-06)
    unit[...] = (scaled / math.sqrt(values.shape[-1])).astype(BF16)
    halve(unit, parts)


def halve(block, parts):
    first = 0
    for part in parts:
        part[...] = block[first : first + part.shape[0], :]
        first = first + part.shape[0]


def seed_kernel(scalars, labels, seed, *pieces):
    row = lax.broadcasted_iota(jnp.int32, labels.shape, 0)
    seed[...] = jnp.where(row < scalars[1], labels[...].astype(F32), 0.0).astype(BF16)
    cut(seed, scalars[0], list(enumerate(pieces, 1)))


def pack_kernel(scalars, whole, p1, p2, p3, out, *parts):
    out[...] = whole[...]
    join(scalars[0], [(1, p1), (2, p2), (3, p3)], out)
    halve(out, parts)


def at(cluster, rows):
    return pl.ds(pl.multiple_of(cluster * rows, rows), rows)


def place_rows(cluster, blocks, rows, stack):
    start = cluster * rows
    for block in blocks:
        count = block.shape[0]
        stack[pl.ds(pl.multiple_of(start, count), count), :] = block[...]
        start = start + count


def near_kernel(units, near):
    rows = units.shape[0] // QUAD
    for k in range(QUAD):
        for pair in range(2):
            span = slice(2 * pair * rows, 2 * (pair + 1) * rows)
            tile = affinity(units[k * rows : (k + 1) * rows, :], units[span, :])
            if k // 2 == pair:
                row = lax.broadcasted_iota(jnp.int32, tile.shape, 0)
                lane = lax.broadcasted_iota(jnp.int32, tile.shape, 1)
                tile = jnp.where(row + (k % 2) * rows == lane, 0.0, tile)
            near[k * rows : (k + 1) * rows, span] = tile.astype(BF16)


def stage_kernel(clusters, unit, side_a, core, across_a, up, up_side_a, up_core, up_across_a, own, units, up_units, stack):
    rows = unit.shape[0]
    for i, (mine, upper) in enumerate(
        ((unit, up), (side_a, up_side_a), (core, up_core), (across_a, up_across_a))
    ):
        place_rows(clusters[i], (mine,), rows, units)
        place_rows(clusters[i], (upper,), rows, up_units)
    unpack(own, stack)


def far_kernel(clusters, units_in, up_in, side_b, across_b, stack, units, up_units, far, sums):
    rows = units.shape[0] // QUAD
    half = rows // 2
    for i, block in ((1, side_b), (3, across_b)):
        start = pl.multiple_of(clusters[i] * rows + half, half)
        units[pl.ds(start, half), :] = block[:half, :]
        up_units[pl.ds(start, half), :] = block[half:, :]
    for k in range(QUAD):
        here = slice(k * rows, (k + 1) * rows)
        for first in range(0, k + 1, 2):
            span = slice(first * rows, min(first + 2, k + 1) * rows)
            far[here, span] = affinity(units[here, :], up_units[span, :]).astype(BF16)
    scatter(far, stack, sums)


def unpack(block, stack):
    rows, quarter = stack.shape[0] // QUAD, stack.shape[1]
    for k in range(QUAD):
        stack[k * rows : (k + 1) * rows, :] = block[:, k * quarter : (k + 1) * quarter]


def scatter(far, stack, out):
    rows, quarter = stack.shape[0] // QUAD, stack.shape[1]
    for k in range(QUAD):
        total = lax.dot_general(
            far[k * rows :, k * rows : (k + 1) * rows],
            stack[k * rows :, :],
            (((0,), (0,)), ((), ())),
            preferred_element_type=F32,
        )
        out[:, k * quarter : (k + 1) * quarter] = total.astype(out.dtype)


def mix_kernel(scalars, far, summed, s0, s1, s2, s3, seed, factor, mixed, stack, out, p1, p2, p3):
    total = (s0[...] + s1[...]) + (s2[...] + s3[...])
    factor[...] = jnp.where(total > INVALID / 10, 0.0, lax.rsqrt(total / summed.shape[1] + 1e-06))
    mixed[...] = mix(summed, factor, seed)
    unpack(mixed, stack)
    scatter(far, stack, out)
    cut(out, scalars[0], [(1, p1), (2, p2), (3, p3)])


def cross_kernel(weight, unit, *rest):
    others, out = rest[:-1], rest[-1]
    rows = unit.shape[0]
    for n, other in enumerate(others):
        out[n * rows : (n + 1) * rows, :] = (affinity(unit[...], other[...]) * weight).astype(BF16)


def near_products(near, stack, total):
    rows = stack.shape[0] // QUAD
    for k in range(QUAD):
        here = slice(k * rows, (k + 1) * rows)
        total[here, :] = dot(near[here, :], stack[...])


def cross_products(clusters, tiles, n, stack, total):
    rows = stack.shape[0] // QUAD
    for i, tile in enumerate(tiles):
        here = at(clusters[i], rows)
        total[here, :] += dot(tile[n * rows : (n + 1) * rows, :], stack[here, :])


def far_products(far, stack, total, out):
    rows, quarter = stack.shape[0] // QUAD, stack.shape[1]
    for k in range(QUAD):
        here = slice(k * rows, (k + 1) * rows)
        done = total[here, :] + dot(far[here, : (k + 1) * rows], stack[: (k + 1) * rows, :])
        out[:, k * quarter : (k + 1) * quarter] = done.astype(out.dtype)


def gather_kernel(clusters, near, far, t0, t1, t2, t3, own, up, *rest):
    cross, (out, stack, total) = rest[:-3], rest[-3:]
    unpack(own, stack)
    near_products(near, stack, total)
    for n, block in enumerate(cross):
        unpack(block, stack)
        cross_products(clusters, (t0, t1, t2, t3), n, stack, total)
    unpack(up, stack)
    far_products(far, stack, total, out)


def gather_mixed_kernel(clusters, far, t0, t1, t2, t3, total_in, *rest):
    triples, (total, out, p1, p2, p3, mixed, stack) = rest[:-7], rest[-7:]
    triples = [triples[i : i + 3] for i in range(0, len(triples), 3)]
    for n, (summed, factor, seed) in enumerate(triples[1:]):
        mixed[...] = mix(summed, factor, seed)
        unpack(mixed, stack)
        cross_products(clusters, (t0, t1, t2, t3), n, stack, total)
    mixed[...] = mix(*triples[0])
    unpack(mixed, stack)
    far_products(far, stack, total, out)
    cut(out, clusters[0], [(1, p1), (2, p2), (3, p3)])


def lanes_of(lanes):
    quarter = lanes // QUAD
    row = lax.broadcasted_iota(jnp.int32, (8, lanes), 0)
    lane = lax.broadcasted_iota(jnp.int32, (8, lanes), 1)
    return ((lane >= row * quarter) & (lane < (row + 1) * quarter)).astype(F32)


def mix(summed, factor, seed):
    spread = lax.dot_general(
        factor[...],
        lanes_of(summed.shape[1]),
        (((0,), (0,)), ((), ())),
        precision=lax.Precision.HIGHEST,
        preferred_element_type=F32,
    )
    share = keep_share * summed[...].astype(F32) * spread
    return (share + (1.0 - keep_share) * seed[...].astype(F32)).astype(BF16)


def combine_kernel(scalars, kept, sent, summed, squares):
    total = kept[...] + sent[...].astype(F32)
    summed[...] = total.astype(BF16)
    sums = lax.dot_general(
        lanes_of(total.shape[1]),
        total * total,
        (((1,), (1,)), ((), ())),
        precision=lax.Precision.HIGHEST,
        preferred_element_type=F32,
    )
    row = lax.broadcasted_iota(jnp.int32, sums.shape, 0)
    lane = lax.broadcasted_iota(jnp.int32, sums.shape, 1)
    squares[...] = sums + jnp.where((row == scalars[0]) & (lane >= scalars[1]), INVALID, 0.0)


def finish_kernel(scalars, kept, sent, seed, out):
    summed = kept[...].astype(F32) + sent[...].astype(F32)
    factor = lax.rsqrt(jnp.mean(summed * summed, axis=-1, keepdims=True) + 1e-06)
    result = keep_share * summed * factor + (1.0 - keep_share) * seed[...].astype(F32)
    row = lax.broadcasted_iota(jnp.int32, summed.shape, 0)
    out[...] = jnp.where(row < scalars[1], result, 0.0).astype(BF16)


def body(embeddings, labels, cluster_rows):
    rows, classes = labels.shape
    depth = embeddings.shape[1]
    groups = lax.axis_size("grp")
    steps, weight = ([1], 2.0) if groups == 2 else ([1, -1], 1.0)
    place = (lax.axis_index("dev") % QUAD).astype(jnp.int32)
    clusters = jnp.stack([place, place ^ 2, place ^ 1, place ^ 3])
    scalars = jnp.stack([place, cluster_rows[0]])
    stack = pltpu.VMEM((QUAD * rows, classes // QUAD), BF16)
    total = pltpu.VMEM((QUAD * rows, classes // QUAD), F32)
    packed = like(labels.shape, BF16)
    piece = like((rows, classes // QUAD), BF16)
    matrix = like((QUAD * rows, QUAD * rows), BF16)

    half_rows = rows // 2
    unit_half = like((half_rows, depth), BF16)

    unit, unit_a, unit_b = call(
        unit_kernel, "unit", (embeddings,), (like(embeddings.shape, BF16), unit_half, unit_half)
    )
    side_a = from_side(unit_a)
    unit_up = from_up(unit)
    seed, *pieces = call(seed_kernel, "seed", (scalars, labels), (packed, piece, piece, piece))
    received = exchange(pieces)
    unit_core = from_core(unit)
    cross_unit = [from_group(after(unit, seed), step) for step in steps]
    up_side_a = from_up(side_a)
    side_b = from_side(after(jnp.concatenate([after(unit_b, side_a), unit_up[half_rows:]]), received[1:]))
    received[0] = after(received[0], unit_up)
    packed_seed = call(pack_kernel, "pack", (scalars, seed, *received), packed)
    seed_up = from_up(packed_seed)
    seed_cross = [from_group(packed_seed, step) for step in steps]
    cross0 = call(
        functools.partial(cross_kernel, weight), "cross", (unit, *cross_unit), like((len(steps) * rows, rows), BF16)
    )
    across_a, up_core, up_across_a = from_core(side_a), from_core(unit_up), from_core(after(up_side_a, packed_seed))
    unit_stack = like((QUAD * rows, depth), BF16)
    units, up_units, seed_stack = call(
        stage_kernel,
        "stage",
        (clusters, unit, side_a, unit_core, across_a, unit_up, up_side_a, up_core, up_across_a, packed_seed),
        (unit_stack, unit_stack, like((QUAD * rows, classes // QUAD), BF16)),
    )
    side_b = after(side_b, (cross0, units))
    across_b = from_core(side_b)
    cross0 = after(cross0, (side_b, seed_up, seed_cross))
    cross1, cross2 = from_side(cross0), from_core(cross0)
    units, _, far, sums = call(
        far_kernel,
        "far",
        (clusters, units, up_units, side_b, across_b, seed_stack),
        (unit_stack, unit_stack, matrix, packed),
        aliases={1: 0, 2: 1},
    )
    near = call(near_kernel, "near", (units,), matrix)
    cross3 = from_core(after(cross1, near))

    sent = from_down(sums)
    crosses = (cross0, cross1, cross2, cross3)
    kept = call(
        gather_kernel,
        "gather",
        (clusters, near, far, *crosses, packed_seed, seed_up, *seed_cross),
        like(labels.shape, F32),
        [stack, total],
    )
    summed, squares = call(combine_kernel, "combine", (scalars, kept, sent), (packed, like((8, rows), F32)))

    summed_up = from_up(summed)
    summed_cross = [from_group(summed, step) for step in steps]
    factor, current, current_stack, sums, *pieces = call(
        mix_kernel,
        "mix",
        (scalars, far, summed, squares, *exchange([squares] * 3), packed_seed),
        (
            like((8, rows), F32), packed, like((QUAD * rows, classes // QUAD), BF16),
            packed, piece, piece, piece,
        ),
    )
    received = exchange(pieces)
    near_total = call(near_products, "near_products", (near, after(current_stack, received[0])), like((QUAD * rows, classes // QUAD), F32))
    factor = after(factor, near_total)
    factor_up = from_up(factor)
    factor_cross = [from_group(factor, step) for step in steps]
    received[0] = after(received[0], (summed_up, summed_cross, factor_up, factor_cross, near_total))
    sums = call(pack_kernel, "pack", (scalars, sums, *received), packed)
    sent = from_down(sums)
    summed_up = after(summed_up, sums)
    triples = [summed_up, factor_up, seed_up]
    for s, f, own in zip(summed_cross, factor_cross, seed_cross):
        triples += [s, f, own]
    _, kept, *pieces = call(
        gather_mixed_kernel,
        "gather_mixed",
        (clusters, far, *crosses, near_total, *triples),
        (like((QUAD * rows, classes // QUAD), F32), packed, piece, piece, piece),
        [pltpu.VMEM(labels.shape, BF16), stack],
        aliases={6: 0},
    )
    kept = call(pack_kernel, "pack", (scalars, kept, *exchange(pieces)), packed)
    return call(finish_kernel, "finish", (scalars, kept, sent, seed), packed)


def solution(mesh):
    placed = (P(("grp", "dev"), None), P(("grp", "dev"), None), P(("grp", "dev")))
    return jax.shard_map(
        body, mesh=mesh, in_specs=placed, out_specs=P(("grp", "dev"), None), check_vma=False
    )
```

time: 119 us -> 116 us (0.975)
  waiting for transfers between devices: 60.6 us -> 41.5 us
  starting transfers between devices: 24.7 us -> 34.9 us
  Pallas kernels: 30.1 us -> 33.7 us
  local copies, waits for them, and re-layouts: 2.17 us -> 4.08 us
    ppermute x26 -> x29, waiting for transfers between devices: 57.4 us -> 37.2 us  [along_dev(): lax.ppermute(block, 'dev', [(source(i) % size, i) for i in range(size)])]
    ppermute x26 -> x29, starting transfers between devices: 20.1 us -> 29.8 us  [along_dev(): lax.ppermute(block, 'dev', [(source(i) % size, i) for i in range(size)])]
    pallas_call x13 -> x15, Pallas kernels: 30.1 us -> 33.7 us  [call(): pl.pallas_call(kernel, in_specs=specs, out_shape=out_shape, scratch_shape...]
    unnamed x8, local copies, waits for them, and re-layouts: 2.17 us -> 4.06 us
    ppermute x3 -> x4, waiting for transfers between devices: 3.13 us -> 4.36 us  [from_group(): lax.ppermute(block, 'grp', [((i + step) % size, i) for i in range(size)])]
    ppermute x3 -> x4, starting transfers between devices: 4.63 us -> 5.13 us  [from_group(): lax.ppermute(block, 'grp', [((i + step) % size, i) for i in range(size)])]
  transfers between devices with their start and end apart: 29 -> 33, of which waited for: 17 -> 17; matrix products, arithmetic and copies ran while one was open for 0% -> 1% of each run, Pallas kernels for 21% -> 25%
where the time goes in v2:
time: 116 us
  waiting for transfers between devices  41.5 us (36%)
  starting transfers between devices  34.9 us (30%)
  Pallas kernels  33.7 us (29%)
  local copies, waits for them, and re-layouts  4.08 us (4%)
    ppermute x29, waiting for transfers between devices, along_dev(): lax.ppermute(block, 'dev', [(source(i) % size, i) for i in range(size)])  37.2 us
    pallas_call x15, Pallas kernels, call(): pl.pallas_call(kernel, in_specs=specs, out_shape=out_shape, scratch_shape...  33.7 us
    ppermute x29, starting transfers between devices, along_dev(): lax.ppermute(block, 'dev', [(source(i) % size, i) for i in range(size)])  29.8 us
    ppermute x4, starting transfers between devices, from_group(): lax.ppermute(block, 'grp', [((i + step) % size, i) for i in range(size)])  5.13 us
    ppermute x4, waiting for transfers between devices, from_group(): lax.ppermute(block, 'grp', [((i + step) % size, i) for i in range(size)])  4.36 us
    unnamed x8, local copies, waits for them, and re-layouts  4.06 us
  transfers between devices with their start and end apart: 33, of which 17 were waited for; matrix products, arithmetic and copies ran while one was open for 1% of the time, Pallas kernels for 25%

profile of v2, /device:TPU:0, one launch (start us, length us, event | category | flops | bytes accessed | tf_op | source)
XLA Modules:
  0.0 116.1 jit_solution(3147850707654049738)
XLA Ops:
  1.3 5.1 %collective-permute-start.3 = (bf16[384,768]{1,0:T(8,128)(2,1)S(1)}, bf16[384,768]{1,0:T(8,128)(2,1)S(1)}, u32[]{:S(2)}, u32[]{:S(2)}) collective-permute-start(bf16[384,768]{1,0:T(8,128)(2,1)S(1)} %get-tuple-element.55.unit), channel_id=1, source_target_pairs={{4,0},{5,1},{6,2},{7,3},{8,4},{9,5},{10,6},{11,7},{12,8},{13,9},{1... | collective-permute-start | bytes 1769480 | tf_op jit(solution)/shard_map/ppermute | solution.py:22
  6.4 1.5 %collective-permute-start = (bf16[192,768]{1,0:T(8,128)(2,1)S(1)}, bf16[192,768]{1,0:T(8,128)(2,1)S(1)}, u32[]{:S(2)}, u32[]{:S(2)}) collective-permute-start(bf16[192,768]{1,0:T(8,128)(2,1)S(1)} %get-tuple-element.43), channel_id=1, source_target_pairs={{2,0},{3,1},{0,2},{1,3},{6,4},{7,5},{4,6},{5,7},{10,8},{11,9},{8,1... | collective-permute-start | bytes 884744 | tf_op jit(solution)/shard_map/ppermute | solution.py:22
  10.9 1.6 %collective-permute-start.11 = (bf16[384,768]{1,0:T(8,128)(2,1)S(1)}, bf16[384,768]{1,0:T(8,128)(2,1)S(1)}, u32[]{:S(2)}, u32[]{:S(2)}) collective-permute-start(bf16[384,768]{1,0:T(8,128)(2,1)S(1)} %get-tuple-element.55.unit), channel_id=1, source_target_pairs={{16,0},{0,16},{17,1},{1,17},{18,2},{2,18},{19,3},{3,19},{20,4},{4,... | collective-permute-start | bytes 1769480 | tf_op jit(solution)/shard_map/ppermute | solution.py:43
  12.9 2.9 %collective-permute-done.side_a = bf16[192,768]{1,0:T(8,128)(2,1)S(1)} collective-permute-done((bf16[192,768]{1,0:T(8,128)(2,1)S(1)}, bf16[192,768]{1,0:T(8,128)(2,1)S(1)}, u32[]{:S(2)}, u32[]{:S(2)}) %collective-permute-start) | collective-permute-done | bytes 294944 | tf_op jit(solution)/shard_map/ppermute | solution.py:22
  15.8 3.2 %collective-permute-done.3.up = bf16[384,768]{1,0:T(8,128)(2,1)S(1)} collective-permute-done((bf16[384,768]{1,0:T(8,128)(2,1)S(1)}, bf16[384,768]{1,0:T(8,128)(2,1)S(1)}, u32[]{:S(2)}, u32[]{:S(2)}) %collective-permute-start.3) | collective-permute-done | bytes 589856 | tf_op jit(solution)/shard_map/ppermute | solution.py:22
  19.0 4.3 %collective-permute-start.4 = (bf16[192,768]{1,0:T(8,128)(2,1)S(1)}, bf16[192,768]{1,0:T(8,128)(2,1)}, u32[]{:S(2)}, u32[]{:S(2)}) collective-permute-start(bf16[192,768]{1,0:T(8,128)(2,1)S(1)} %collective-permute-done.side_a), channel_id=1, source_target_pairs={{4,0},{5,1},{6,2},{7,3},{8,4},{9,5},{10,6},{11,7},{12,8},{13,9},{1... | collective-permute-start | bytes 884744 | tf_op jit(solution)/shard_map/ppermute | solution.py:22
  24.7 1.5 %collective-permute-start.10 = (bf16[384,768]{1,0:T(8,128)(2,1)}, bf16[384,768]{1,0:T(8,128)(2,1)}, u32[]{:S(2)}, u32[]{:S(2)}) collective-permute-start(bf16[384,768]{1,0:T(8,128)(2,1)} %pad_maximum_fusion), channel_id=1, source_target_pairs={{2,0},{3,1},{0,2},{1,3},{6,4},{7,5},{4,6},{5,7},{10,8},{11,9},{8,1... | collective-permute-start | bytes 1769480 | tf_op jit(solution)/shard_map/ppermute | solution.py:22
  27.1 1.5 %collective-permute-done.4.up_side_a = bf16[192,768]{1,0:T(8,128)(2,1)} collective-permute-done((bf16[192,768]{1,0:T(8,128)(2,1)S(1)}, bf16[192,768]{1,0:T(8,128)(2,1)}, u32[]{:S(2)}, u32[]{:S(2)}) %collective-permute-start.4) | collective-permute-done | bytes 294944 | tf_op jit(solution)/shard_map/ppermute | solution.py:22
  31.7 4.4 %collective-permute-start.13 = (bf16[384,896]{1,0:T(8,128)(2,1)S(1)}, bf16[384,896]{1,0:T(8,128)(2,1)S(1)}, u32[]{:S(2)}, u32[]{:S(2)}) collective-permute-start(bf16[384,896]{1,0:T(8,128)(2,1)S(1)} %pack.3.own.seed), channel_id=1, source_target_pairs={{4,0},{5,1},{6,2},{7,3},{8,4},{9,5},{10,6},{11,7},{12,8},{13,9},{1... | collective-permute-start | bytes 2064392 | tf_op jit(solution)/shard_map/ppermute | solution.py:22
  36.1 1.5 %collective-permute-start.14 = (bf16[384,896]{1,0:T(8,128)(2,1)S(1)}, bf16[384,896]{1,0:T(8,128)(2,1)S(1)}, u32[]{:S(2)}, u32[]{:S(2)}) collective-permute-start(bf16[384,896]{1,0:T(8,128)(2,1)S(1)} %pack.3.own.seed), channel_id=1, source_target_pairs={{16,0},{0,16},{17,1},{1,17},{18,2},{2,18},{19,3},{3,19},{20,4},{4,... | collective-permute-start | bytes 2064392 | tf_op jit(solution)/shard_map/ppermute | solution.py:43
  37.6 1.8 %stage.1 = (bf16[1536,768]{1,0:T(8,128)(2,1)S(1)}, bf16[1536,768]{1,0:T(8,128)(2,1)S(1)}, bf16[1536,224]{1,0:T(8,128)(2,1)S(1)}) custom-call(s32[4]{0:T(128)S(1)} %pad_add_fusion.1.clusters, bf16[384,768]{1,0:T(8,128)(2,1)S(1)} %get-tuple-element.55.unit, bf16[192,768]{1,0:T(8,128)(2,1)S(1)} %collective-permute-done.side_a, ...), custom_call_target="tpu_custom_call" | custom-call | tf_op jit(solution)/shard_map/stage/pallas_call | solution.py:58
  40.3 2.2 %collective-permute-done.12.across_b = bf16[384,768]{1,0:T(8,128)(2,1)S(1)} collective-permute-done((bf16[384,768]{1,0:T(8,128)(2,1)}, bf16[384,768]{1,0:T(8,128)(2,1)S(1)}, u32[]{:S(2)}, u32[]{:S(2)}) %collective-permute-start.12) | collective-permute-done | bytes 589856 | tf_op jit(solution)/shard_map/ppermute | solution.py:22
  42.5 4.7 %far.1 = (bf16[1536,768]{1,0:T(8,128)(2,1)S(1)}, bf16[1536,768]{1,0:T(8,128)(2,1)S(1)}, bf16[1536,1536]{1,0:T(8,128)(2,1)S(1)}, bf16[384,896]{1,0:T(8,128)(2,1)S(1)}) custom-call(s32[4]{0:T(128)S(1)} %pad_add_fusion.1.clusters, bf16[1536,768]{1,0:T(8,128)(2,1)S(1)} %get-tuple-element.50.units_in, ...), custom_call_target="tpu_custom_call", output_to_operand_aliasing={{0}: (1, {}), {1}: (2, {})} | custom-call | tf_op jit(solution)/shard_map/far/pallas_call | solution.py:58
  47.5 4.5 %collective-permute-done.13.up.rest_2_ = bf16[384,896]{1,0:T(8,128)(2,1)S(1)} collective-permute-done((bf16[384,896]{1,0:T(8,128)(2,1)S(1)}, bf16[384,896]{1,0:T(8,128)(2,1)S(1)}, u32[]{:S(2)}, u32[]{:S(2)}) %collective-permute-start.13) | collective-permute-done | bytes 688160 | tf_op jit(solution)/shard_map/ppermute | solution.py:22
  53.2 1.5 %collective-permute-start.15 = (bf16[384,384]{1,0:T(8,128)(2,1)S(1)}, bf16[384,384]{1,0:T(8,128)(2,1)S(1)}, u32[]{:S(2)}, u32[]{:S(2)}) collective-permute-start(bf16[384,384]{1,0:T(8,128)(2,1)S(1)} %cross.1.t0), channel_id=1, source_target_pairs={{2,0},{3,1},{0,2},{1,3},{6,4},{7,5},{4,6},{5,7},{10,8},{11,9},{8,1... | collective-permute-start | bytes 884744 | tf_op jit(solution)/shard_map/ppermute | solution.py:22
  54.7 3.9 %near.1 = bf16[1536,1536]{1,0:T(8,128)(2,1)S(1)} custom-call(bf16[1536,768]{1,0:T(8,128)(2,1)S(1)} %get-tuple-element.60.units), custom_call_target="tpu_custom_call" | custom-call | tf_op jit(solution)/shard_map/near/pallas_call | solution.py:58
  58.6 2.4 %collective-permute-done.15.t1 = bf16[384,384]{1,0:T(8,128)(2,1)S(1)} collective-permute-done((bf16[384,384]{1,0:T(8,128)(2,1)S(1)}, bf16[384,384]{1,0:T(8,128)(2,1)S(1)}, u32[]{:S(2)}, u32[]{:S(2)}) %collective-permute-start.15) | collective-permute-done | bytes 294944 | tf_op jit(solution)/shard_map/ppermute | solution.py:22
  60.9 1.6 %collective-permute-done.17.t3 = bf16[384,384]{1,0:T(8,128)(2,1)S(1)} collective-permute-done((bf16[384,384]{1,0:T(8,128)(2,1)S(1)}, bf16[384,384]{1,0:T(8,128)(2,1)S(1)}, u32[]{:S(2)}, u32[]{:S(2)}) %collective-permute-start.17) | collective-permute-done | bytes 294944 | tf_op jit(solution)/shard_map/ppermute | solution.py:22
  62.5 3.7 %gather.1.kept = f32[384,896]{1,0:T(8,128)S(1)} custom-call(s32[4]{0:T(128)S(1)} %pad_add_fusion.1.clusters, bf16[1536,1536]{1,0:T(8,128)(2,1)S(1)} %near.1, bf16[1536,1536]{1,0:T(8,128)(2,1)S(1)} %get-tuple-element.58.far, bf16[384,384]{1,0:T(8,128)(2,1)S(1)} %cross.1.t0, bf16[384,384]{1,0:T(8,128)(2,1)S(1)} %collective-permute-done.15.t1, ...), custom_call_target="tpu_custom_call" | custom-call | tf_op jit(solution)/shard_map/gather/pallas_call | solution.py:58
  66.7 1.8 %combine.1 = (bf16[384,896]{1,0:T(8,128)(2,1)S(1)}, f32[8,384]{1,0:T(8,128)S(1)}) custom-call(s32[2]{0:T(128)S(1)} %pad_add_fusion.scalars, f32[384,896]{1,0:T(8,128)S(1)} %gather.1.kept, bf16[384,896]{1,0:T(8,128)(2,1)S(1)} %collective-permute-done.18.sent), custom_call_target="tpu_custom_call" | custom-call | tf_op jit(solution)/shard_map/combine/pallas_call | solution.py:58
  68.5 3.4 %collective-permute-start.23 = (bf16[384,896]{1,0:T(8,128)(2,1)S(1)}, bf16[384,896]{1,0:T(8,128)(2,1)S(1)}, u32[]{:S(2)}, u32[]{:S(2)}) collective-permute-start(bf16[384,896]{1,0:T(8,128)(2,1)S(1)} %get-tuple-element.63.summed), channel_id=1, source_target_pairs={{4,0},{5,1},{6,2},{7,3},{8,4},{9,5},{10,6},{11,7},{12,8},{13,9},{1... | collective-permute-start | bytes 2064392 | tf_op jit(solution)/shard_map/ppermute | solution.py:22
  71.9 1.5 %collective-permute-start.24 = (bf16[384,896]{1,0:T(8,128)(2,1)S(1)}, bf16[384,896]{1,0:T(8,128)(2,1)S(1)}, u32[]{:S(2)}, u32[]{:S(2)}) collective-permute-start(bf16[384,896]{1,0:T(8,128)(2,1)S(1)} %get-tuple-element.63.summed), channel_id=1, source_target_pairs={{16,0},{0,16},{17,1},{1,17},{18,2},{2,18},{19,3},{3,19},{20,4},{4,... | collective-permute-start | bytes 2064392 | tf_op jit(solution)/shard_map/ppermute | solution.py:43
  73.4 1.5 %collective-permute-start.20 = (f32[8,384]{1,0:T(8,128)S(1)}, f32[8,384]{1,0:T(8,128)S(1)}, u32[]{:S(2)}, u32[]{:S(2)}) collective-permute-start(f32[8,384]{1,0:T(8,128)S(1)} %get-tuple-element.64.s0), channel_id=1, source_target_pairs={{2,0},{3,1},{0,2},{1,3},{6,4},{7,5},{4,6},{5,7},{10,8},{11,9},{8,1... | collective-permute-start | bytes 36872 | tf_op jit(solution)/shard_map/ppermute | solution.py:22
  75.3 1.8 %collective-permute-done.20.s2 = f32[8,384]{1,0:T(8,128)S(1)} collective-permute-done((f32[8,384]{1,0:T(8,128)S(1)}, f32[8,384]{1,0:T(8,128)S(1)}, u32[]{:S(2)}, u32[]{:S(2)}) %collective-permute-start.20) | collective-permute-done | bytes 12320 | tf_op jit(solution)/shard_map/ppermute | solution.py:22
  78.0 4.5 %mix.1 = (f32[8,384]{1,0:T(8,128)S(1)}, bf16[384,896]{1,0:T(8,128)(2,1)}, bf16[1536,224]{1,0:T(8,128)(2,1)S(1)}, bf16[384,896]{1,0:T(8,128)(2,1)S(1)}, bf16[384,...) custom-call(s32[2]{0:T(128)S(1)} %pad_add_fusion.scalars, ...), custom_call_target="tpu_custom_call" | custom-call | tf_op jit(solution)/shard_map/mix/pallas_call | solution.py:58
  86.3 3.2 %collective-permute-done.25.rest_1_ = f32[8,384]{1,0:T(8,128)S(1)} collective-permute-done((f32[8,384]{1,0:T(8,128)S(1)}, f32[8,384]{1,0:T(8,128)S(1)}, u32[]{:S(2)}, u32[]{:S(2)}) %collective-permute-start.25) | collective-permute-done | bytes 12320 | tf_op jit(solution)/shard_map/ppermute | solution.py:22
  90.0 3.2 %collective-permute-done.26.rest_4_ = f32[8,384]{1,0:T(8,128)S(1)} collective-permute-done((f32[8,384]{1,0:T(8,128)S(1)}, f32[8,384]{1,0:T(8,128)S(1)}, u32[]{:S(2)}, u32[]{:S(2)}) %collective-permute-start.26) | collective-permute-done | bytes 12320 | tf_op jit(solution)/shard_map/ppermute | solution.py:43
  94.5 5.3 %gather_mixed.1 = (f32[1536,224]{1,0:T(8,128)S(1)}, bf16[384,896]{1,0:T(8,128)(2,1)S(1)}, bf16[384,224]{1,0:T(8,128)(2,1)S(1)}, bf16[384,224]{1,0:T(8,128)(2,1)S(1)}, bf16[384,224]{1,0:T(8,128)(2,1)S(1)}) custom-call(s32[4]{0:T(128)S(1)} %pad_add_fusion.1.clusters, bf16[1536,1536]{1,0:T(8,128)(2,1)S(1)} %get-tuple-element.58.far, ...), custom_call_target="tpu_custom_call", output_to_operand_aliasing={{0}: (6, {})} | custom-call | tf_op jit(solution)/shard_map/gather_mixed/pallas_call | solution.py:58
  101.7 6.3 %collective-permute-done.30.p2 = bf16[384,224]{1,0:T(8,128)(2,1)S(1)} collective-permute-done((bf16[384,224]{1,0:T(8,128)(2,1)S(1)}, bf16[384,224]{1,0:T(8,128)(2,1)S(1)}, u32[]{:S(2)}, u32[]{:S(2)}) %collective-permute-start.30) | collective-permute-done | bytes 172064 | tf_op jit(solution)/shard_map/ppermute | solution.py:22
  108.0 2.6 %collective-permute-done.31.p3 = bf16[384,224]{1,0:T(8,128)(2,1)S(1)} collective-permute-done((bf16[384,224]{1,0:T(8,128)(2,1)S(1)}, bf16[384,224]{1,0:T(8,128)(2,1)S(1)}, u32[]{:S(2)}, u32[]{:S(2)}) %collective-permute-start.31) | collective-permute-done | bytes 172064 | tf_op jit(solution)/shard_map/ppermute | solution.py:22
  111.5 2.6 %collective-permute-done.32.sent = bf16[384,896]{1,0:T(8,128)(2,1)S(1)} collective-permute-done((bf16[384,896]{1,0:T(8,128)(2,1)S(1)}, bf16[384,896]{1,0:T(8,128)(2,1)S(1)}, u32[]{:S(2)}, u32[]{:S(2)}) %collective-permute-start.32) | collective-permute-done | bytes 688160 | tf_op jit(solution)/shard_map/ppermute | solution.py:22
  114.1 1.9 %finish.1 = bf16[384,896]{1,0:T(8,128)(2,1)} custom-call(s32[2]{0:T(128)S(1)} %pad_add_fusion.scalars, bf16[384,896]{1,0:T(8,128)(2,1)S(1)} %pack.5.kept, bf16[384,896]{1,0:T(8,128)(2,1)S(1)} %collective-permute-done.32.sent, bf16[384,896]{1,0:T(8,128)(2,1)S(1)} %get-tuple-element.44.whole.seed), custom_call_target="tpu_custom_call" | custom-call | tf_op jit(solution)/shard_map/finish/pallas_call | solution.py:58
  (61 shorter events, 21.9 us)
Async XLA Ops:
  1.3 17.7 %collective-permute-start.3 = (bf16[384,768]{1,0:T(8,128)(2,1)S(1)}, bf16[384,768]{1,0:T(8,128)(2,1)S(1)}, u32[]{:S(2)}, u32[]{:S(2)}) collective-permute-start(bf16[384,768]{1,0:T(8,128)(2,1)S(1)} %get-tuple-element.55.unit), channel_id=1, source_target_pairs={{4,0},{5,1},{6,2},{7,3},{8,4},{9,5},{10,6},{11,7},{12,8},{13,9},{1... | collective-permute-start | bytes 1769480 | tf_op jit(solution)/shard_map/ppermute | solution.py:22
  6.4 9.4 %collective-permute-start = (bf16[192,768]{1,0:T(8,128)(2,1)S(1)}, bf16[192,768]{1,0:T(8,128)(2,1)S(1)}, u32[]{:S(2)}, u32[]{:S(2)}) collective-permute-start(bf16[192,768]{1,0:T(8,128)(2,1)S(1)} %get-tuple-element.43), channel_id=1, source_target_pairs={{2,0},{3,1},{0,2},{1,3},{6,4},{7,5},{4,6},{5,7},{10,8},{11,9},{8,1... | collective-permute-start | bytes 884744 | tf_op jit(solution)/shard_map/ppermute | solution.py:22
  10.9 17.8 %collective-permute-start.11 = (bf16[384,768]{1,0:T(8,128)(2,1)S(1)}, bf16[384,768]{1,0:T(8,128)(2,1)S(1)}, u32[]{:S(2)}, u32[]{:S(2)}) collective-permute-start(bf16[384,768]{1,0:T(8,128)(2,1)S(1)} %get-tuple-element.55.unit), channel_id=1, source_target_pairs={{16,0},{0,16},{17,1},{1,17},{18,2},{2,18},{19,3},{3,19},{20,4},{4,... | collective-permute-start | bytes 1769480 | tf_op jit(solution)/shard_map/ppermute | solution.py:43
  12.5 11.7 %collective-permute-start.7 = (bf16[384,224]{1,0:T(8,128)(2,1)S(1)}, bf16[384,224]{1,0:T(8,128)(2,1)S(1)}, u32[]{:S(2)}, u32[]{:S(2)}) collective-permute-start(bf16[384,224]{1,0:T(8,128)(2,1)S(1)} %get-tuple-element.47), channel_id=1, source_target_pairs={{2,0},{3,1},{0,2},{1,3},{6,4},{7,5},{4,6},{5,7},{10,8},{11,9},{8,1... | collective-permute-start | bytes 516104 | tf_op jit(solution)/shard_map/ppermute | solution.py:22
  12.9 11.3 %collective-permute-start.8 = (bf16[384,224]{1,0:T(8,128)(2,1)S(1)}, bf16[384,224]{1,0:T(8,128)(2,1)S(1)}, u32[]{:S(2)}, u32[]{:S(2)}) collective-permute-start(bf16[384,224]{1,0:T(8,128)(2,1)S(1)} %get-tuple-element.48), channel_id=1, source_target_pairs={{3,0},{2,1},{1,2},{0,3},{7,4},{6,5},{5,6},{4,7},{11,8},{10,9},{9,1... | collective-permute-start | bytes 516104 | tf_op jit(solution)/shard_map/ppermute | solution.py:22
  15.8 8.9 %collective-permute-start.6 = (bf16[384,224]{1,0:T(8,128)(2,1)S(1)}, bf16[384,224]{1,0:T(8,128)(2,1)S(1)}, u32[]{:S(2)}, u32[]{:S(2)}) collective-permute-start(bf16[384,224]{1,0:T(8,128)(2,1)S(1)} %get-tuple-element.45), channel_id=1, source_target_pairs={{1,0},{0,1},{3,2},{2,3},{5,4},{4,5},{7,6},{6,7},{9,8},{8,9},{11,10... | collective-permute-start | bytes 516104 | tf_op jit(solution)/shard_map/ppermute | solution.py:22
  19.0 9.7 %collective-permute-start.4 = (bf16[192,768]{1,0:T(8,128)(2,1)S(1)}, bf16[192,768]{1,0:T(8,128)(2,1)}, u32[]{:S(2)}, u32[]{:S(2)}) collective-permute-start(bf16[192,768]{1,0:T(8,128)(2,1)S(1)} %collective-permute-done.side_a), channel_id=1, source_target_pairs={{4,0},{5,1},{6,2},{7,3},{8,4},{9,5},{10,6},{11,7},{12,8},{13,9},{1... | collective-permute-start | bytes 884744 | tf_op jit(solution)/shard_map/ppermute | solution.py:22
  24.2 7.5 %collective-permute-start.1 = (bf16[384,768]{1,0:T(8,128)(2,1)S(1)}, bf16[384,768]{1,0:T(8,128)(2,1)S(1)}, u32[]{:S(2)}, u32[]{:S(2)}) collective-permute-start(bf16[384,768]{1,0:T(8,128)(2,1)S(1)} %get-tuple-element.55.unit), channel_id=1, source_target_pairs={{1,0},{0,1},{3,2},{2,3},{5,4},{4,5},{7,6},{6,7},{9,8},{8,9},{11,10... | collective-permute-start | bytes 1769480 | tf_op jit(solution)/shard_map/ppermute | solution.py:22
  24.2 13.5 %collective-permute-start.5 = (bf16[384,768]{1,0:T(8,128)(2,1)S(1)}, bf16[384,768]{1,0:T(8,128)(2,1)}, u32[]{:S(2)}, u32[]{:S(2)}) collective-permute-start(bf16[384,768]{1,0:T(8,128)(2,1)S(1)} %collective-permute-done.3.up), channel_id=1, source_target_pairs={{1,0},{0,1},{3,2},{2,3},{5,4},{4,5},{7,6},{6,7},{9,8},{8,9},{11,10... | collective-permute-start | bytes 1769480 | tf_op jit(solution)/shard_map/ppermute | solution.py:22
  24.7 15.6 %collective-permute-start.10 = (bf16[384,768]{1,0:T(8,128)(2,1)}, bf16[384,768]{1,0:T(8,128)(2,1)}, u32[]{:S(2)}, u32[]{:S(2)}) collective-permute-start(bf16[384,768]{1,0:T(8,128)(2,1)} %pad_maximum_fusion), channel_id=1, source_target_pairs={{2,0},{3,1},{0,2},{1,3},{6,4},{7,5},{4,6},{5,7},{10,8},{11,9},{8,1... | collective-permute-start | bytes 1769480 | tf_op jit(solution)/shard_map/ppermute | solution.py:22
  28.7 7.4 %collective-permute-start.2 = (bf16[192,768]{1,0:T(8,128)(2,1)S(1)}, bf16[192,768]{1,0:T(8,128)(2,1)}, u32[]{:S(2)}, u32[]{:S(2)}) collective-permute-start(bf16[192,768]{1,0:T(8,128)(2,1)S(1)} %collective-permute-done.side_a), channel_id=1, source_target_pairs={{1,0},{0,1},{3,2},{2,3},{5,4},{4,5},{7,6},{6,7},{9,8},{8,9},{11,10... | collective-permute-start | bytes 884744 | tf_op jit(solution)/shard_map/ppermute | solution.py:22
  29.5 8.1 %collective-permute-start.9 = (bf16[192,768]{1,0:T(8,128)(2,1)}, bf16[192,768]{1,0:T(8,128)(2,1)}, u32[]{:S(2)}, u32[]{:S(2)}) collective-permute-start(bf16[192,768]{1,0:T(8,128)(2,1)} %collective-permute-done.4.up_side_a), channel_id=1, source_target_pairs={{1,0},{0,1},{3,2},{2,3},{5,4},{4,5},{7,6},{6,7},{9,8},{8,9},{11,10... | collective-permute-start | bytes 884744 | tf_op jit(solution)/shard_map/ppermute | solution.py:22
  31.7 20.3 %collective-permute-start.13 = (bf16[384,896]{1,0:T(8,128)(2,1)S(1)}, bf16[384,896]{1,0:T(8,128)(2,1)S(1)}, u32[]{:S(2)}, u32[]{:S(2)}) collective-permute-start(bf16[384,896]{1,0:T(8,128)(2,1)S(1)} %pack.3.own.seed), channel_id=1, source_target_pairs={{4,0},{5,1},{6,2},{7,3},{8,4},{9,5},{10,6},{11,7},{12,8},{13,9},{1... | collective-permute-start | bytes 2064392 | tf_op jit(solution)/shard_map/ppermute | solution.py:22
  36.1 17.1 %collective-permute-start.14 = (bf16[384,896]{1,0:T(8,128)(2,1)S(1)}, bf16[384,896]{1,0:T(8,128)(2,1)S(1)}, u32[]{:S(2)}, u32[]{:S(2)}) collective-permute-start(bf16[384,896]{1,0:T(8,128)(2,1)S(1)} %pack.3.own.seed), channel_id=1, source_target_pairs={{16,0},{0,16},{17,1},{1,17},{18,2},{2,18},{19,3},{3,19},{20,4},{4,... | collective-permute-start | bytes 2064392 | tf_op jit(solution)/shard_map/ppermute | solution.py:43
  40.3 2.2 %collective-permute-start.12 = (bf16[384,768]{1,0:T(8,128)(2,1)}, bf16[384,768]{1,0:T(8,128)(2,1)S(1)}, u32[]{:S(2)}, u32[]{:S(2)}) collective-permute-start(bf16[384,768]{1,0:T(8,128)(2,1)} %collective-permute-done.10.side_b), channel_id=1, source_target_pairs={{1,0},{0,1},{3,2},{2,3},{5,4},{4,5},{7,6},{6,7},{9,8},{8,9},{11,10... | collective-permute-start | bytes 1769480 | tf_op jit(solution)/shard_map/ppermute | solution.py:22
  47.2 19.5 %collective-permute-start.18 = (bf16[384,896]{1,0:T(8,128)(2,1)S(1)}, bf16[384,896]{1,0:T(8,128)(2,1)S(1)}, u32[]{:S(2)}, u32[]{:S(2)}) collective-permute-start(bf16[384,896]{1,0:T(8,128)(2,1)S(1)} %get-tuple-element.62), channel_id=1, source_target_pairs={{12,0},{13,1},{14,2},{15,3},{0,4},{1,5},{2,6},{3,7},{4,8},{5,9},{6... | collective-permute-start | bytes 2064392 | tf_op jit(solution)/shard_map/ppermute | solution.py:22
  53.2 7.8 %collective-permute-start.15 = (bf16[384,384]{1,0:T(8,128)(2,1)S(1)}, bf16[384,384]{1,0:T(8,128)(2,1)S(1)}, u32[]{:S(2)}, u32[]{:S(2)}) collective-permute-start(bf16[384,384]{1,0:T(8,128)(2,1)S(1)} %cross.1.t0), channel_id=1, source_target_pairs={{2,0},{3,1},{0,2},{1,3},{6,4},{7,5},{4,6},{5,7},{10,8},{11,9},{8,1... | collective-permute-start | bytes 884744 | tf_op jit(solution)/shard_map/ppermute | solution.py:22
  54.7 6.3 %collective-permute-start.16 = (bf16[384,384]{1,0:T(8,128)(2,1)S(1)}, bf16[384,384]{1,0:T(8,128)(2,1)S(1)}, u32[]{:S(2)}, u32[]{:S(2)}) collective-permute-start(bf16[384,384]{1,0:T(8,128)(2,1)S(1)} %cross.1.t0), channel_id=1, source_target_pairs={{1,0},{0,1},{3,2},{2,3},{5,4},{4,5},{7,6},{6,7},{9,8},{8,9},{11,10... | collective-permute-start | bytes 884744 | tf_op jit(solution)/shard_map/ppermute | solution.py:22
  68.5 24.7 %collective-permute-start.23 = (bf16[384,896]{1,0:T(8,128)(2,1)S(1)}, bf16[384,896]{1,0:T(8,128)(2,1)S(1)}, u32[]{:S(2)}, u32[]{:S(2)}) collective-permute-start(bf16[384,896]{1,0:T(8,128)(2,1)S(1)} %get-tuple-element.63.summed), channel_id=1, source_target_pairs={{4,0},{5,1},{6,2},{7,3},{8,4},{9,5},{10,6},{11,7},{12,8},{13,9},{1... | collective-permute-start | bytes 2064392 | tf_op jit(solution)/shard_map/ppermute | solution.py:22
  71.9 21.3 %collective-permute-start.24 = (bf16[384,896]{1,0:T(8,128)(2,1)S(1)}, bf16[384,896]{1,0:T(8,128)(2,1)S(1)}, u32[]{:S(2)}, u32[]{:S(2)}) collective-permute-start(bf16[384,896]{1,0:T(8,128)(2,1)S(1)} %get-tuple-element.63.summed), channel_id=1, source_target_pairs={{16,0},{0,16},{17,1},{1,17},{18,2},{2,18},{19,3},{3,19},{20,4},{4,... | collective-permute-start | bytes 2064392 | tf_op jit(solution)/shard_map/ppermute | solution.py:43
  73.4 1.9 %collective-permute-start.19 = (f32[8,384]{1,0:T(8,128)S(1)}, f32[8,384]{1,0:T(8,128)S(1)}, u32[]{:S(2)}, u32[]{:S(2)}) collective-permute-start(f32[8,384]{1,0:T(8,128)S(1)} %get-tuple-element.64.s0), channel_id=1, source_target_pairs={{1,0},{0,1},{3,2},{2,3},{5,4},{4,5},{7,6},{6,7},{9,8},{8,9},{11,10... | collective-permute-start | bytes 36872 | tf_op jit(solution)/shard_map/ppermute | solution.py:22
  73.4 3.7 %collective-permute-start.20 = (f32[8,384]{1,0:T(8,128)S(1)}, f32[8,384]{1,0:T(8,128)S(1)}, u32[]{:S(2)}, u32[]{:S(2)}) collective-permute-start(f32[8,384]{1,0:T(8,128)S(1)} %get-tuple-element.64.s0), channel_id=1, source_target_pairs={{2,0},{3,1},{0,2},{1,3},{6,4},{7,5},{4,6},{5,7},{10,8},{11,9},{8,1... | collective-permute-start | bytes 36872 | tf_op jit(solution)/shard_map/ppermute | solution.py:22
  74.9 3.1 %collective-permute-start.21 = (f32[8,384]{1,0:T(8,128)S(1)}, f32[8,384]{1,0:T(8,128)S(1)}, u32[]{:S(2)}, u32[]{:S(2)}) collective-permute-start(f32[8,384]{1,0:T(8,128)S(1)} %get-tuple-element.64.s0), channel_id=1, source_target_pairs={{3,0},{2,1},{1,2},{0,3},{7,4},{6,5},{5,6},{4,7},{11,8},{10,9},{9,1... | collective-permute-start | bytes 36872 | tf_op jit(solution)/shard_map/ppermute | solution.py:22
  82.5 1.9 %collective-permute-start.22 = (bf16[384,224]{1,0:T(8,128)(2,1)S(1)}, bf16[384,224]{1,0:T(8,128)(2,1)S(1)}, u32[]{:S(2)}, u32[]{:S(2)}) collective-permute-start(bf16[384,224]{1,0:T(8,128)(2,1)S(1)} %get-tuple-element.66), channel_id=1, source_target_pairs={{1,0},{0,1},{3,2},{2,3},{5,4},{4,5},{7,6},{6,7},{9,8},{8,9},{11,10... | collective-permute-start | bytes 516104 | tf_op jit(solution)/shard_map/ppermute | solution.py:22
  82.9 10.3 %collective-permute-start.27 = (bf16[384,224]{1,0:T(8,128)(2,1)S(1)}, bf16[384,224]{1,0:T(8,128)(2,1)S(1)}, u32[]{:S(2)}, u32[]{:S(2)}) collective-permute-start(bf16[384,224]{1,0:T(8,128)(2,1)S(1)} %get-tuple-element.72), channel_id=1, source_target_pairs={{2,0},{3,1},{0,2},{1,3},{6,4},{7,5},{4,6},{5,7},{10,8},{11,9},{8,1... | collective-permute-start | bytes 516104 | tf_op jit(solution)/shard_map/ppermute | solution.py:22
  83.5 9.7 %collective-permute-start.28 = (bf16[384,224]{1,0:T(8,128)(2,1)S(1)}, bf16[384,224]{1,0:T(8,128)(2,1)S(1)}, u32[]{:S(2)}, u32[]{:S(2)}) collective-permute-start(bf16[384,224]{1,0:T(8,128)(2,1)S(1)} %get-tuple-element.73), channel_id=1, source_target_pairs={{3,0},{2,1},{1,2},{0,3},{7,4},{6,5},{5,6},{4,7},{11,8},{10,9},{9,1... | collective-permute-start | bytes 516104 | tf_op jit(solution)/shard_map/ppermute | solution.py:22
  85.7 3.7 %collective-permute-start.25 = (f32[8,384]{1,0:T(8,128)S(1)}, f32[8,384]{1,0:T(8,128)S(1)}, u32[]{:S(2)}, u32[]{:S(2)}) collective-permute-start(f32[8,384]{1,0:T(8,128)S(1)} %get-tuple-element.70), channel_id=1, source_target_pairs={{4,0},{5,1},{6,2},{7,3},{8,4},{9,5},{10,6},{11,7},{12,8},{13,9},{1... | collective-permute-start | bytes 36872 | tf_op jit(solution)/shard_map/ppermute | solution.py:22
  89.5 3.7 %collective-permute-start.26 = (f32[8,384]{1,0:T(8,128)S(1)}, f32[8,384]{1,0:T(8,128)S(1)}, u32[]{:S(2)}, u32[]{:S(2)}) collective-permute-start(f32[8,384]{1,0:T(8,128)S(1)} %get-tuple-element.70), channel_id=1, source_target_pairs={{16,0},{0,16},{17,1},{1,17},{18,2},{2,18},{19,3},{3,19},{20,4},{4,... | collective-permute-start | bytes 36872 | tf_op jit(solution)/shard_map/ppermute | solution.py:43
  94.2 20.0 %collective-permute-start.32 = (bf16[384,896]{1,0:T(8,128)(2,1)S(1)}, bf16[384,896]{1,0:T(8,128)(2,1)S(1)}, u32[]{:S(2)}, u32[]{:S(2)}) collective-permute-start(bf16[384,896]{1,0:T(8,128)(2,1)S(1)} %pack.4), channel_id=1, source_target_pairs={{12,0},{13,1},{14,2},{15,3},{0,4},{1,5},{2,6},{3,7},{4,8},{5,9},{6... | collective-permute-start | bytes 2064392 | tf_op jit(solution)/shard_map/ppermute | solution.py:22
  99.8 1.9 %collective-permute-start.29 = (bf16[384,224]{1,0:T(8,128)(2,1)S(1)}, bf16[384,224]{1,0:T(8,128)(2,1)S(1)}, u32[]{:S(2)}, u32[]{:S(2)}) collective-permute-start(bf16[384,224]{1,0:T(8,128)(2,1)S(1)} %get-tuple-element.76), channel_id=1, source_target_pairs={{1,0},{0,1},{3,2},{2,3},{5,4},{4,5},{7,6},{6,7},{9,8},{8,9},{11,10... | collective-permute-start | bytes 516104 | tf_op jit(solution)/shard_map/ppermute | solution.py:22
  100.2 7.8 %collective-permute-start.30 = (bf16[384,224]{1,0:T(8,128)(2,1)S(1)}, bf16[384,224]{1,0:T(8,128)(2,1)S(1)}, u32[]{:S(2)}, u32[]{:S(2)}) collective-permute-start(bf16[384,224]{1,0:T(8,128)(2,1)S(1)} %get-tuple-element.77), channel_id=1, source_target_pairs={{2,0},{3,1},{0,2},{1,3},{6,4},{7,5},{4,6},{5,7},{10,8},{11,9},{8,1... | collective-permute-start | bytes 516104 | tf_op jit(solution)/shard_map/ppermute | solution.py:22
  100.8 9.8 %collective-permute-start.31 = (bf16[384,224]{1,0:T(8,128)(2,1)S(1)}, bf16[384,224]{1,0:T(8,128)(2,1)S(1)}, u32[]{:S(2)}, u32[]{:S(2)}) collective-permute-start(bf16[384,224]{1,0:T(8,128)(2,1)S(1)} %get-tuple-element.78), channel_id=1, source_target_pairs={{3,0},{2,1},{1,2},{0,3},{7,4},{6,5},{5,6},{4,7},{11,8},{10,9},{9,1... | collective-permute-start | bytes 516104 | tf_op jit(solution)/shard_map/ppermute | solution.py:22
  (5 other events, 5.6 us)

commit v3 on v2

--- a/solution.py
+++ b/solution.py
@@ -14,6 +14,7 @@
 F32 = jnp.float32
 QUAD = 4
 INVALID = 1e38
+FACTORS = 16
 MB = 2**20
 
 
@@ -193,10 +194,17 @@
         out[:, k * quarter : (k + 1) * quarter] = total.astype(out.dtype)
 
 
-def mix_kernel(scalars, far, summed, s0, s1, s2, s3, seed, factor, mixed, stack, out, p1, p2, p3):
+def mix_kernel(scalars, far, summed, s0, s1, s2, s3, seed, tail, mixed, stack, out, p1, p2, p3):
     total = (s0[...] + s1[...]) + (s2[...] + s3[...])
-    factor[...] = jnp.where(total > INVALID / 10, 0.0, lax.rsqrt(total / summed.shape[1] + 1e-06))
-    mixed[...] = mix(summed, factor, seed)
+    rows = summed.shape[0]
+    kept = tail.shape[0] - 2 * FACTORS
+    factor = jnp.where(total > INVALID / 10, 0.0, lax.rsqrt(total / summed.shape[1] + 1e-06))
+    high = factor.astype(BF16)
+    tail[:kept, :] = summed[rows - kept :, :]
+    tail[kept:, :] = jnp.zeros((2 * FACTORS, tail.shape[1]), BF16)
+    tail[kept : kept + FACTORS, :rows] = high
+    tail[kept + FACTORS :, :rows] = (factor - high.astype(F32)).astype(BF16)
+    mix(summed.at[: rows - kept], tail, seed, mixed)
     unpack(mixed, stack)
     scatter(far, stack, out)
     cut(out, scalars[0], [(1, p1), (2, p2), (3, p3)])
@@ -245,44 +253,48 @@
 def gather_mixed_kernel(clusters, far, t0, t1, t2, t3, total_in, *rest):
     triples, (total, out, p1, p2, p3, mixed, stack) = rest[:-7], rest[-7:]
     triples = [triples[i : i + 3] for i in range(0, len(triples), 3)]
-    for n, (summed, factor, seed) in enumerate(triples[1:]):
-        mixed[...] = mix(summed, factor, seed)
+    for n, triple in enumerate(triples[1:]):
+        mix(*triple, mixed)
         unpack(mixed, stack)
         cross_products(clusters, (t0, t1, t2, t3), n, stack, total)
-    mixed[...] = mix(*triples[0])
+    mix(*triples[0], mixed)
     unpack(mixed, stack)
     far_products(far, stack, total, out)
     cut(out, clusters[0], [(1, p1), (2, p2), (3, p3)])
 
 
-def lanes_of(lanes):
+def lanes_of(count, lanes):
     quarter = lanes // QUAD
-    row = lax.broadcasted_iota(jnp.int32, (8, lanes), 0)
-    lane = lax.broadcasted_iota(jnp.int32, (8, lanes), 1)
-    return ((lane >= row * quarter) & (lane < (row + 1) * quarter)).astype(F32)
-
-
-def mix(summed, factor, seed):
+    row = lax.broadcasted_iota(jnp.int32, (count, lanes), 0) & (FACTORS - 1)
+    lane = lax.broadcasted_iota(jnp.int32, (count, lanes), 1)
+    return ((lane >= row * quarter) & (lane < (row + 1) * quarter)).astype(F32).astype(BF16)
+
+
+def mix(head, tail, seed, out):
+    rows, lanes = seed.shape
+    first = head.shape[0]
+    kept = rows - first
     spread = lax.dot_general(
-        factor[...],
-        lanes_of(summed.shape[1]),
+        tail[kept:, :rows],
+        lanes_of(2 * FACTORS, lanes),
         (((0,), (0,)), ((), ())),
-        precision=lax.Precision.HIGHEST,
         preferred_element_type=F32,
     )
-    share = keep_share * summed[...].astype(F32) * spread
-    return (share + (1.0 - keep_share) * seed[...].astype(F32)).astype(BF16)
-
-
-def combine_kernel(scalars, kept, sent, summed, squares):
+    for block, start, stop in ((head[...], 0, first), (tail[:kept, :], first, rows)):
+        share = keep_share * block.astype(F32) * spread[start:stop, :]
+        out[start:stop, :] = (share + (1.0 - keep_share) * seed[start:stop, :].astype(F32)).astype(BF16)
+
+
+def combine_kernel(scalars, kept, sent, summed, head, squares):
     total = kept[...] + sent[...].astype(F32)
     summed[...] = total.astype(BF16)
-    sums = lax.dot_general(
-        lanes_of(total.shape[1]),
-        total * total,
-        (((1,), (1,)), ((), ())),
-        precision=lax.Precision.HIGHEST,
-        preferred_element_type=F32,
+    head[...] = summed[: head.shape[0], :]
+    square = total * total
+    high = square.astype(BF16)
+    marks = lanes_of(FACTORS, total.shape[1])
+    sums = sum(
+        lax.dot_general(marks, part, (((1,), (1,)), ((), ())), preferred_element_type=F32)
+        for part in (high, (square - high.astype(F32)).astype(BF16))
     )
     row = lax.broadcasted_iota(jnp.int32, sums.shape, 0)
     lane = lax.broadcasted_iota(jnp.int32, sums.shape, 1)
@@ -332,16 +344,19 @@
     cross0 = call(
         functools.partial(cross_kernel, weight), "cross", (unit, *cross_unit), like((len(steps) * rows, rows), BF16)
     )
-    across_a, up_core, up_across_a = from_core(side_a), from_core(unit_up), from_core(after(up_side_a, packed_seed))
+    side_b = after(side_b, (packed_seed, cross0, up_side_a))
+    across_b = from_core(side_b)
+    across_a, up_core, up_across_a = from_core(side_a), from_core(unit_up), from_core(up_side_a)
     unit_stack = like((QUAD * rows, depth), BF16)
     units, up_units, seed_stack = call(
         stage_kernel,
         "stage",
-        (clusters, unit, side_a, unit_core, across_a, unit_up, up_side_a, up_core, up_across_a, packed_seed),
+        (
+            clusters, after(unit, side_b), side_a, unit_core, across_a, unit_up, up_side_a, up_core, up_across_a,
+            packed_seed,
+        ),
         (unit_stack, unit_stack, like((QUAD * rows, classes // QUAD), BF16)),
     )
-    side_b = after(side_b, (cross0, units))
-    across_b = from_core(side_b)
     cross0 = after(cross0, (side_b, seed_up, seed_cross))
     cross1, cross2 = from_side(cross0), from_core(cross0)
     units, _, far, sums = call(
@@ -363,31 +378,38 @@
         like(labels.shape, F32),
         [stack, total],
     )
-    summed, squares = call(combine_kernel, "combine", (scalars, kept, sent), (packed, like((8, rows), F32)))
-
-    summed_up = from_up(summed)
-    summed_cross = [from_group(summed, step) for step in steps]
-    factor, current, current_stack, sums, *pieces = call(
+    tail_rows = rows // 96 * 16
+    head = like((rows - tail_rows, classes), BF16)
+    tail = like((tail_rows + 2 * FACTORS, classes), BF16)
+    summed, head, squares = call(
+        combine_kernel, "combine", (scalars, kept, sent), (packed, head, like((FACTORS, rows), F32))
+    )
+
+    head_up = from_up(head)
+    head_cross = [from_group(head, step) for step in steps]
+    tail, current, current_stack, sums, *pieces = call(
         mix_kernel,
         "mix",
         (scalars, far, summed, squares, *exchange([squares] * 3), packed_seed),
-        (
-            like((8, rows), F32), packed, like((QUAD * rows, classes // QUAD), BF16),
-            packed, piece, piece, piece,
-        ),
+        (tail, packed, like((QUAD * rows, classes // QUAD), BF16), packed, piece, piece, piece),
     )
     received = exchange(pieces)
-    near_total = call(near_products, "near_products", (near, after(current_stack, received[0])), like((QUAD * rows, classes // QUAD), F32))
-    factor = after(factor, near_total)
-    factor_up = from_up(factor)
-    factor_cross = [from_group(factor, step) for step in steps]
-    received[0] = after(received[0], (summed_up, summed_cross, factor_up, factor_cross, near_total))
+    near_total = call(
+        near_products,
+        "near_products",
+        (near, after(current_stack, received[0])),
+        like((QUAD * rows, classes // QUAD), F32),
+    )
+    tail = after(tail, near_total)
+    tail_up = from_up(tail)
+    tail_cross = [from_group(tail, step) for step in steps]
     sums = call(pack_kernel, "pack", (scalars, sums, *received), packed)
+    sums = after(sums, (head_up, head_cross, tail_up, tail_cross))
     sent = from_down(sums)
-    summed_up = after(summed_up, sums)
-    triples = [summed_up, factor_up, seed_up]
-    for s, f, own in zip(summed_cross, factor_cross, seed_cross):
-        triples += [s, f, own]
+    head_up = after(head_up, sums)
+    triples = [head_up, tail_up, seed_up]
+    for top, rest, own in zip(head_cross, tail_cross, seed_cross):
+        triples += [top, rest, own]
     _, kept, *pieces = call(
         gather_mixed_kernel,
         "gather_mixed",

time: 116 us -> 116 us (level)
  starting transfers between devices: 34.9 us -> 26.8 us
  waiting for transfers between devices: 41.5 us -> 48.6 us
  local copies, waits for them, and re-layouts: 4.08 us -> 6.69 us
    ppermute x29, waiting for transfers between devices: 37.2 us -> 46.8 us  [along_dev(): lax.ppermute(block, 'dev', [(source(i) % size, i) for i in range(size)])]
    ppermute x29, starting transfers between devices: 29.8 us -> 21.7 us  [along_dev(): lax.ppermute(block, 'dev', [(source(i) % size, i) for i in range(size)])]
    ppermute x4, waiting for transfers between devices: 4.36 us -> 1.8 us  [from_group(): lax.ppermute(block, 'grp', [((i + step) % size, i) for i in range(size)])]
    unnamed x8 -> x12, local copies, waits for them, and re-layouts: 4.06 us -> 5.71 us
  transfers between devices with their start and end apart: 33 -> 33, of which waited for: 17 -> 19; matrix products, arithmetic and copies ran while one was open for 1% -> 1% of each run, Pallas kernels for 25% -> 25%
where the time goes in v3:
time: 116 us
  waiting for transfers between devices  48.6 us (42%)
  Pallas kernels  33 us (28%)
  starting transfers between devices  26.8 us (23%)
  local copies, waits for them, and re-layouts  6.69 us (6%)
    ppermute x29, waiting for transfers between devices, along_dev(): lax.ppermute(block, 'dev', [(source(i) % size, i) for i in range(size)])  46.8 us
    pallas_call x15, Pallas kernels, call(): pl.pallas_call(kernel, in_specs=specs, out_shape=out_shape, scratch_shape...  33 us
    ppermute x29, starting transfers between devices, along_dev(): lax.ppermute(block, 'dev', [(source(i) % size, i) for i in range(size)])  21.7 us
    unnamed x12, local copies, waits for them, and re-layouts  5.71 us
    ppermute x4, starting transfers between devices, from_group(): lax.ppermute(block, 'grp', [((i + step) % size, i) for i in range(size)])  5.13 us
  transfers between devices with their start and end apart: 33, of which 19 were waited for; matrix products, arithmetic and copies ran while one was open for 1% of the time, Pallas kernels for 25%

profile of v3, /device:TPU:0, one launch (start us, length us, event | category | flops | bytes accessed | tf_op | source)
XLA Modules:
  0.0 116.1 jit_solution(14026488535907543888)
XLA Ops:
  2.1 5.0 %collective-permute-start.1 = (bf16[384,768]{1,0:T(8,128)(2,1)}, bf16[384,768]{1,0:T(8,128)(2,1)}, u32[]{:S(2)}, u32[]{:S(2)}) collective-permute-start(bf16[384,768]{1,0:T(8,128)(2,1)} %get-tuple-element.55.unit), channel_id=1, source_target_pairs={{4,0},{5,1},{6,2},{7,3},{8,4},{9,5},{10,6},{11,7},{12,8},{13,9},{1... | collective-permute-start | bytes 1769480 | tf_op jit(solution)/shard_map/ppermute | solution.py:23
  7.2 1.5 %collective-permute-start = (bf16[192,768]{1,0:T(8,128)(2,1)S(1)}, bf16[192,768]{1,0:T(8,128)(2,1)S(1)}, u32[]{:S(2)}, u32[]{:S(2)}) collective-permute-start(bf16[192,768]{1,0:T(8,128)(2,1)S(1)} %get-tuple-element.45), channel_id=1, source_target_pairs={{2,0},{3,1},{0,2},{1,3},{6,4},{7,5},{4,6},{5,7},{10,8},{11,9},{8,1... | collective-permute-start | bytes 884744 | tf_op jit(solution)/shard_map/ppermute | solution.py:23
  12.2 1.5 %collective-permute-start.6 = (bf16[384,768]{1,0:T(8,128)(2,1)}, bf16[384,768]{1,0:T(8,128)(2,1)S(1)}, u32[]{:S(2)}, u32[]{:S(2)}) collective-permute-start(bf16[384,768]{1,0:T(8,128)(2,1)} %get-tuple-element.55.unit), channel_id=1, source_target_pairs={{16,0},{0,16},{17,1},{1,17},{18,2},{2,18},{19,3},{3,19},{20,4},{4,... | collective-permute-start | bytes 1769480 | tf_op jit(solution)/shard_map/ppermute | solution.py:44
  13.7 3.4 %collective-permute-done.side_a = bf16[192,768]{1,0:T(8,128)(2,1)S(1)} collective-permute-done((bf16[192,768]{1,0:T(8,128)(2,1)S(1)}, bf16[192,768]{1,0:T(8,128)(2,1)S(1)}, u32[]{:S(2)}, u32[]{:S(2)}) %collective-permute-start) | collective-permute-done | bytes 294944 | tf_op jit(solution)/shard_map/ppermute | solution.py:23
  17.1 3.0 %collective-permute-done.1.up = bf16[384,768]{1,0:T(8,128)(2,1)} collective-permute-done((bf16[384,768]{1,0:T(8,128)(2,1)}, bf16[384,768]{1,0:T(8,128)(2,1)}, u32[]{:S(2)}, u32[]{:S(2)}) %collective-permute-start.1) | collective-permute-done | bytes 589856 | tf_op jit(solution)/shard_map/ppermute | solution.py:23
  21.3 1.8 %collective-permute-done.3.p3 = bf16[384,224]{1,0:T(8,128)(2,1)S(1)} collective-permute-done((bf16[384,224]{1,0:T(8,128)(2,1)S(1)}, bf16[384,224]{1,0:T(8,128)(2,1)S(1)}, u32[]{:S(2)}, u32[]{:S(2)}) %collective-permute-start.3) | collective-permute-done | bytes 172064 | tf_op jit(solution)/shard_map/ppermute | solution.py:23
  24.1 1.3 %collective-permute-start.8 = (bf16[384,768]{1,0:T(8,128)(2,1)}, bf16[384,768]{1,0:T(8,128)(2,1)S(1)}, u32[]{:S(2)}, u32[]{:S(2)}) collective-permute-start(bf16[384,768]{1,0:T(8,128)(2,1)} %get-tuple-element.55.unit), channel_id=1, source_target_pairs={{1,0},{0,1},{3,2},{2,3},{5,4},{4,5},{7,6},{6,7},{9,8},{8,9},{11,10... | collective-permute-start | bytes 1769480 | tf_op jit(solution)/shard_map/ppermute | solution.py:23
  25.4 1.6 %collective-permute-start.7 = (bf16[192,768]{1,0:T(8,128)(2,1)S(1)}, bf16[192,768]{1,0:T(8,128)(2,1)}, u32[]{:S(2)}, u32[]{:S(2)}) collective-permute-start(bf16[192,768]{1,0:T(8,128)(2,1)S(1)} %collective-permute-done.side_a), channel_id=1, source_target_pairs={{4,0},{5,1},{6,2},{7,3},{8,4},{9,5},{10,6},{11,7},{12,8},{13,9},{1... | collective-permute-start | bytes 884744 | tf_op jit(solution)/shard_map/ppermute | solution.py:23
  30.3 1.6 %cross.1.t0 = bf16[384,384]{1,0:T(8,128)(2,1)S(1)} custom-call(bf16[384,768]{1,0:T(8,128)(2,1)} %get-tuple-element.55.unit, bf16[384,768]{1,0:T(8,128)(2,1)S(1)} %collective-permute-done.6.rest_0_), custom_call_target="tpu_custom_call" | custom-call | tf_op jit(solution)/shard_map/cross/pallas_call | solution.py:59
  31.9 3.5 %collective-permute-done.7.up_side_a = bf16[192,768]{1,0:T(8,128)(2,1)} collective-permute-done((bf16[192,768]{1,0:T(8,128)(2,1)S(1)}, bf16[192,768]{1,0:T(8,128)(2,1)}, u32[]{:S(2)}, u32[]{:S(2)}) %collective-permute-start.7) | collective-permute-done | bytes 294944 | tf_op jit(solution)/shard_map/ppermute | solution.py:23
  35.4 1.5 %collective-permute-start.14 = (bf16[384,896]{1,0:T(8,128)(2,1)S(1)}, bf16[384,896]{1,0:T(8,128)(2,1)S(1)}, u32[]{:S(2)}, u32[]{:S(2)}) collective-permute-start(bf16[384,896]{1,0:T(8,128)(2,1)S(1)} %pack.3.own.seed), channel_id=1, source_target_pairs={{16,0},{0,16},{17,1},{1,17},{18,2},{2,18},{19,3},{3,19},{20,4},{4,... | collective-permute-start | bytes 2064392 | tf_op jit(solution)/shard_map/ppermute | solution.py:44
  36.9 2.4 %collective-permute-done.4.side_b = bf16[384,768]{1,0:T(8,128)(2,1)} collective-permute-done((bf16[384,768]{1,0:T(8,128)(2,1)S(1)}, bf16[384,768]{1,0:T(8,128)(2,1)}, u32[]{:S(2)}, u32[]{:S(2)}) %collective-permute-start.4) | collective-permute-done | bytes 589856 | tf_op jit(solution)/shard_map/ppermute | solution.py:23
  41.5 1.7 %collective-permute-done.11.up_across_a = bf16[192,768]{1,0:T(8,128)(2,1)} collective-permute-done((bf16[192,768]{1,0:T(8,128)(2,1)}, bf16[192,768]{1,0:T(8,128)(2,1)}, u32[]{:S(2)}, u32[]{:S(2)}) %collective-permute-start.11) | collective-permute-done | bytes 294944 | tf_op jit(solution)/shard_map/ppermute | solution.py:23
  45.2 2.1 %stage.1 = (bf16[1536,768]{1,0:T(8,128)(2,1)S(1)}, bf16[1536,768]{1,0:T(8,128)(2,1)S(1)}, bf16[1536,224]{1,0:T(8,128)(2,1)S(1)}) custom-call(s32[4]{0:T(128)S(1)} %pad_add_fusion.1.clusters, bf16[384,768]{1,0:T(8,128)(2,1)} %get-tuple-element.55.unit, bf16[192,768]{1,0:T(8,128)(2,1)S(1)} %collective-permute-done.side_a, bf16[384,768]{1,0:T(8,128)(2,1)S(1)} %copy-done.2, ...), custom_call_target="tpu_custom_call" | custom-call | tf_op jit(solution)/shard_map/stage/pallas_call | solution.py:59
  47.3 4.9 %far.1 = (bf16[1536,768]{1,0:T(8,128)(2,1)S(1)}, bf16[1536,768]{1,0:T(8,128)(2,1)S(1)}, bf16[1536,1536]{1,0:T(8,128)(2,1)S(1)}, bf16[384,896]{1,0:T(8,128)(2,1)S(1)}) custom-call(s32[4]{0:T(128)S(1)} %pad_add_fusion.1.clusters, bf16[1536,768]{1,0:T(8,128)(2,1)S(1)} %get-tuple-element.56.units_in, ...), custom_call_target="tpu_custom_call", output_to_operand_aliasing={{0}: (1, {}), {1}: (2, {})} | custom-call | tf_op jit(solution)/shard_map/far/pallas_call | solution.py:59
  53.5 3.9 %near.1 = bf16[1536,1536]{1,0:T(8,128)(2,1)S(1)} custom-call(bf16[1536,768]{1,0:T(8,128)(2,1)S(1)} %get-tuple-element.61.units), custom_call_target="tpu_custom_call" | custom-call | tf_op jit(solution)/shard_map/near/pallas_call | solution.py:59
  57.4 4.3 %collective-permute-done.15.t1 = bf16[384,384]{1,0:T(8,128)(2,1)S(1)} collective-permute-done((bf16[384,384]{1,0:T(8,128)(2,1)S(1)}, bf16[384,384]{1,0:T(8,128)(2,1)S(1)}, u32[]{:S(2)}, u32[]{:S(2)}) %collective-permute-start.15) | collective-permute-done | bytes 294944 | tf_op jit(solution)/shard_map/ppermute | solution.py:23
  61.7 1.6 %collective-permute-done.17.t3 = bf16[384,384]{1,0:T(8,128)(2,1)S(1)} collective-permute-done((bf16[384,384]{1,0:T(8,128)(2,1)S(1)}, bf16[384,384]{1,0:T(8,128)(2,1)S(1)}, u32[]{:S(2)}, u32[]{:S(2)}) %collective-permute-start.17) | collective-permute-done | bytes 294944 | tf_op jit(solution)/shard_map/ppermute | solution.py:23
  63.2 3.6 %gather.1.kept = f32[384,896]{1,0:T(8,128)S(1)} custom-call(s32[4]{0:T(128)S(1)} %pad_add_fusion.1.clusters, bf16[1536,1536]{1,0:T(8,128)(2,1)S(1)} %near.1, bf16[1536,1536]{1,0:T(8,128)(2,1)S(1)} %get-tuple-element.59.far, bf16[384,384]{1,0:T(8,128)(2,1)S(1)} %cross.1.t0, bf16[384,384]{1,0:T(8,128)(2,1)S(1)} %collective-permute-done.15.t1, ...), custom_call_target="tpu_custom_call" | custom-call | tf_op jit(solution)/shard_map/gather/pallas_call | solution.py:59
  66.9 4.9 %collective-permute-done.18.sent = bf16[384,896]{1,0:T(8,128)(2,1)S(1)} collective-permute-done((bf16[384,896]{1,0:T(8,128)(2,1)S(1)}, bf16[384,896]{1,0:T(8,128)(2,1)S(1)}, u32[]{:S(2)}, u32[]{:S(2)}) %collective-permute-start.18) | collective-permute-done | bytes 688160 | tf_op jit(solution)/shard_map/ppermute | solution.py:23
  73.0 1.6 %collective-permute-start.26 = (bf16[320,896]{1,0:T(8,128)(2,1)S(1)}, bf16[320,896]{1,0:T(8,128)(2,1)S(1)}, u32[]{:S(2)}, u32[]{:S(2)}) collective-permute-start(bf16[320,896]{1,0:T(8,128)(2,1)S(1)} %get-tuple-element.69), channel_id=1, source_target_pairs={{16,0},{0,16},{17,1},{1,17},{18,2},{2,18},{19,3},{3,19},{20,4},{4,... | collective-permute-start | bytes 1720328 | tf_op jit(solution)/shard_map/ppermute | solution.py:44
  76.4 2.0 %collective-permute-done.20.s2 = f32[16,384]{1,0:T(8,128)S(1)} collective-permute-done((f32[16,384]{1,0:T(8,128)S(1)}, f32[16,384]{1,0:T(8,128)S(1)}, u32[]{:S(2)}, u32[]{:S(2)}) %collective-permute-start.20) | collective-permute-done | bytes 24608 | tf_op jit(solution)/shard_map/ppermute | solution.py:23
  78.8 3.6 %mix.1 = (bf16[96,896]{1,0:T(8,128)(2,1)S(1)}, bf16[384,896]{1,0:T(8,128)(2,1)}, bf16[1536,224]{1,0:T(8,128)(2,1)S(1)}, bf16[384,896]{1,0:T(8,128)(2,1)S(1)}, bf...) custom-call(s32[2]{0:T(128)S(1)} %pad_add_fusion.scalars, ...), custom_call_target="tpu_custom_call" | custom-call | tf_op jit(solution)/shard_map/mix/pallas_call | solution.py:59
  84.3 1.4 %near_products.1.total_in = f32[1536,224]{1,0:T(8,128)S(1)} custom-call(bf16[1536,1536]{1,0:T(8,128)(2,1)S(1)} %near.1, bf16[1536,224]{1,0:T(8,128)(2,1)S(1)} %get-tuple-element.68.stack), custom_call_target="tpu_custom_call" | custom-call | tf_op jit(solution)/shard_map/near_products/pallas_call | solution.py:59
  85.8 4.8 %collective-permute-done.24.p2 = bf16[384,224]{1,0:T(8,128)(2,1)S(1)} collective-permute-done((bf16[384,224]{1,0:T(8,128)(2,1)S(1)}, bf16[384,224]{1,0:T(8,128)(2,1)S(1)}, u32[]{:S(2)}, u32[]{:S(2)}) %collective-permute-start.24) | collective-permute-done | bytes 172064 | tf_op jit(solution)/shard_map/ppermute | solution.py:23
  91.1 2.1 %collective-permute-done.25.p3 = bf16[384,224]{1,0:T(8,128)(2,1)S(1)} collective-permute-done((bf16[384,224]{1,0:T(8,128)(2,1)S(1)}, bf16[384,224]{1,0:T(8,128)(2,1)S(1)}, u32[]{:S(2)}, u32[]{:S(2)}) %collective-permute-start.25) | collective-permute-done | bytes 172064 | tf_op jit(solution)/shard_map/ppermute | solution.py:23
  94.2 1.8 %collective-permute-done.28.rest_4_ = bf16[96,896]{1,0:T(8,128)(2,1)S(1)} collective-permute-done((bf16[96,896]{1,0:T(8,128)(2,1)S(1)}, bf16[96,896]{1,0:T(8,128)(2,1)S(1)}, u32[]{:S(2)}, u32[]{:S(2)}) %collective-permute-start.28) | collective-permute-done | bytes 172064 | tf_op jit(solution)/shard_map/ppermute | solution.py:44
  96.0 2.0 %collective-permute-start.32 = (bf16[384,896]{1,0:T(8,128)(2,1)S(1)}, bf16[384,896]{1,0:T(8,128)(2,1)S(1)}, u32[]{:S(2)}, u32[]{:S(2)}) collective-permute-start(bf16[384,896]{1,0:T(8,128)(2,1)S(1)} %pack.4), channel_id=1, source_target_pairs={{12,0},{13,1},{14,2},{15,3},{0,4},{1,5},{2,6},{3,7},{4,8},{5,9},{6... | collective-permute-start | bytes 2064392 | tf_op jit(solution)/shard_map/ppermute | solution.py:23
  97.9 3.7 %gather_mixed.1 = (f32[1536,224]{1,0:T(8,128)S(1)}, bf16[384,896]{1,0:T(8,128)(2,1)S(1)}, bf16[384,224]{1,0:T(8,128)(2,1)S(1)}, bf16[384,224]{1,0:T(8,128)(2,1)S(1)}, bf16[384,224]{1,0:T(8,128)(2,1)S(1)}) custom-call(s32[4]{0:T(128)S(1)} %pad_add_fusion.1.clusters, bf16[1536,1536]{1,0:T(8,128)(2,1)S(1)} %get-tuple-element.59.far, ...), custom_call_target="tpu_custom_call", output_to_operand_aliasing={{0}: (6, {})} | custom-call | tf_op jit(solution)/shard_map/gather_mixed/pallas_call | solution.py:59
  103.6 5.9 %collective-permute-done.30.p2 = bf16[384,224]{1,0:T(8,128)(2,1)S(1)} collective-permute-done((bf16[384,224]{1,0:T(8,128)(2,1)S(1)}, bf16[384,224]{1,0:T(8,128)(2,1)S(1)}, u32[]{:S(2)}, u32[]{:S(2)}) %collective-permute-start.30) | collective-permute-done | bytes 172064 | tf_op jit(solution)/shard_map/ppermute | solution.py:23
  109.5 3.3 %collective-permute-done.31.p3 = bf16[384,224]{1,0:T(8,128)(2,1)S(1)} collective-permute-done((bf16[384,224]{1,0:T(8,128)(2,1)S(1)}, bf16[384,224]{1,0:T(8,128)(2,1)S(1)}, u32[]{:S(2)}, u32[]{:S(2)}) %collective-permute-start.31) | collective-permute-done | bytes 172064 | tf_op jit(solution)/shard_map/ppermute | solution.py:23
  114.1 1.9 %finish.1 = bf16[384,896]{1,0:T(8,128)(2,1)} custom-call(s32[2]{0:T(128)S(1)} %pad_add_fusion.scalars, bf16[384,896]{1,0:T(8,128)(2,1)S(1)} %pack.5.kept, bf16[384,896]{1,0:T(8,128)(2,1)S(1)} %collective-permute-done.32.sent, bf16[384,896]{1,0:T(8,128)(2,1)S(1)} %get-tuple-element.50.whole.seed), custom_call_target="tpu_custom_call" | custom-call | tf_op jit(solution)/shard_map/finish/pallas_call | solution.py:59
  (65 shorter events, 26.2 us)
Async XLA Ops:
  2.1 18.0 %collective-permute-start.1 = (bf16[384,768]{1,0:T(8,128)(2,1)}, bf16[384,768]{1,0:T(8,128)(2,1)}, u32[]{:S(2)}, u32[]{:S(2)}) collective-permute-start(bf16[384,768]{1,0:T(8,128)(2,1)} %get-tuple-element.55.unit), channel_id=1, source_target_pairs={{4,0},{5,1},{6,2},{7,3},{8,4},{9,5},{10,6},{11,7},{12,8},{13,9},{1... | collective-permute-start | bytes 1769480 | tf_op jit(solution)/shard_map/ppermute | solution.py:23
  7.2 9.9 %collective-permute-start = (bf16[192,768]{1,0:T(8,128)(2,1)S(1)}, bf16[192,768]{1,0:T(8,128)(2,1)S(1)}, u32[]{:S(2)}, u32[]{:S(2)}) collective-permute-start(bf16[192,768]{1,0:T(8,128)(2,1)S(1)} %get-tuple-element.45), channel_id=1, source_target_pairs={{2,0},{3,1},{0,2},{1,3},{6,4},{7,5},{4,6},{5,7},{10,8},{11,9},{8,1... | collective-permute-start | bytes 884744 | tf_op jit(solution)/shard_map/ppermute | solution.py:23
  11.6 9.7 %collective-permute-start.2 = (bf16[384,224]{1,0:T(8,128)(2,1)S(1)}, bf16[384,224]{1,0:T(8,128)(2,1)S(1)}, u32[]{:S(2)}, u32[]{:S(2)}) collective-permute-start(bf16[384,224]{1,0:T(8,128)(2,1)S(1)} %get-tuple-element.47), channel_id=1, source_target_pairs={{2,0},{3,1},{0,2},{1,3},{6,4},{7,5},{4,6},{5,7},{10,8},{11,9},{8,1... | collective-permute-start | bytes 516104 | tf_op jit(solution)/shard_map/ppermute | solution.py:23
  12.1 11.0 %collective-permute-start.3 = (bf16[384,224]{1,0:T(8,128)(2,1)S(1)}, bf16[384,224]{1,0:T(8,128)(2,1)S(1)}, u32[]{:S(2)}, u32[]{:S(2)}) collective-permute-start(bf16[384,224]{1,0:T(8,128)(2,1)S(1)} %get-tuple-element.48), channel_id=1, source_target_pairs={{3,0},{2,1},{1,2},{0,3},{7,4},{6,5},{5,6},{4,7},{11,8},{10,9},{9,1... | collective-permute-start | bytes 516104 | tf_op jit(solution)/shard_map/ppermute | solution.py:23
  12.2 17.4 %collective-permute-start.6 = (bf16[384,768]{1,0:T(8,128)(2,1)}, bf16[384,768]{1,0:T(8,128)(2,1)S(1)}, u32[]{:S(2)}, u32[]{:S(2)}) collective-permute-start(bf16[384,768]{1,0:T(8,128)(2,1)} %get-tuple-element.55.unit), channel_id=1, source_target_pairs={{16,0},{0,16},{17,1},{1,17},{18,2},{2,18},{19,3},{3,19},{20,4},{4,... | collective-permute-start | bytes 1769480 | tf_op jit(solution)/shard_map/ppermute | solution.py:44
  23.1 16.2 %collective-permute-start.4 = (bf16[384,768]{1,0:T(8,128)(2,1)S(1)}, bf16[384,768]{1,0:T(8,128)(2,1)}, u32[]{:S(2)}, u32[]{:S(2)}) collective-permute-start(bf16[384,768]{1,0:T(8,128)(2,1)S(1)} %pad_maximum_fusion), channel_id=1, source_target_pairs={{2,0},{3,1},{0,2},{1,3},{6,4},{7,5},{4,6},{5,7},{10,8},{11,9},{8,1... | collective-permute-start | bytes 1769480 | tf_op jit(solution)/shard_map/ppermute | solution.py:23
  24.1 15.3 %collective-permute-start.8 = (bf16[384,768]{1,0:T(8,128)(2,1)}, bf16[384,768]{1,0:T(8,128)(2,1)S(1)}, u32[]{:S(2)}, u32[]{:S(2)}) collective-permute-start(bf16[384,768]{1,0:T(8,128)(2,1)} %get-tuple-element.55.unit), channel_id=1, source_target_pairs={{1,0},{0,1},{3,2},{2,3},{5,4},{4,5},{7,6},{6,7},{9,8},{8,9},{11,10... | collective-permute-start | bytes 1769480 | tf_op jit(solution)/shard_map/ppermute | solution.py:23
  25.4 10.0 %collective-permute-start.7 = (bf16[192,768]{1,0:T(8,128)(2,1)S(1)}, bf16[192,768]{1,0:T(8,128)(2,1)}, u32[]{:S(2)}, u32[]{:S(2)}) collective-permute-start(bf16[192,768]{1,0:T(8,128)(2,1)S(1)} %collective-permute-done.side_a), channel_id=1, source_target_pairs={{4,0},{5,1},{6,2},{7,3},{8,4},{9,5},{10,6},{11,7},{12,8},{13,9},{1... | collective-permute-start | bytes 884744 | tf_op jit(solution)/shard_map/ppermute | solution.py:23
  28.4 12.2 %collective-permute-start.9 = (bf16[192,768]{1,0:T(8,128)(2,1)S(1)}, bf16[192,768]{1,0:T(8,128)(2,1)S(1)}, u32[]{:S(2)}, u32[]{:S(2)}) collective-permute-start(bf16[192,768]{1,0:T(8,128)(2,1)S(1)} %collective-permute-done.side_a), channel_id=1, source_target_pairs={{1,0},{0,1},{3,2},{2,3},{5,4},{4,5},{7,6},{6,7},{9,8},{8,9},{11,10... | collective-permute-start | bytes 884744 | tf_op jit(solution)/shard_map/ppermute | solution.py:23
  29.6 22.9 %collective-permute-start.13 = (bf16[384,896]{1,0:T(8,128)(2,1)S(1)}, bf16[384,896]{1,0:T(8,128)(2,1)S(1)}, u32[]{:S(2)}, u32[]{:S(2)}) collective-permute-start(bf16[384,896]{1,0:T(8,128)(2,1)S(1)} %pack.3.own.seed), channel_id=1, source_target_pairs={{4,0},{5,1},{6,2},{7,3},{8,4},{9,5},{10,6},{11,7},{12,8},{13,9},{1... | collective-permute-start | bytes 2064392 | tf_op jit(solution)/shard_map/ppermute | solution.py:23
  35.4 17.1 %collective-permute-start.14 = (bf16[384,896]{1,0:T(8,128)(2,1)S(1)}, bf16[384,896]{1,0:T(8,128)(2,1)S(1)}, u32[]{:S(2)}, u32[]{:S(2)}) collective-permute-start(bf16[384,896]{1,0:T(8,128)(2,1)S(1)} %pack.3.own.seed), channel_id=1, source_target_pairs={{16,0},{0,16},{17,1},{1,17},{18,2},{2,18},{19,3},{3,19},{20,4},{4,... | collective-permute-start | bytes 2064392 | tf_op jit(solution)/shard_map/ppermute | solution.py:44
  39.2 4.0 %collective-permute-start.10 = (bf16[384,768]{1,0:T(8,128)(2,1)}, bf16[384,768]{1,0:T(8,128)(2,1)}, u32[]{:S(2)}, u32[]{:S(2)}) collective-permute-start(bf16[384,768]{1,0:T(8,128)(2,1)} %collective-permute-done.1.up), channel_id=1, source_target_pairs={{1,0},{0,1},{3,2},{2,3},{5,4},{4,5},{7,6},{6,7},{9,8},{8,9},{11,10... | collective-permute-start | bytes 1769480 | tf_op jit(solution)/shard_map/ppermute | solution.py:23
  40.2 7.1 %collective-permute-start.12 = (bf16[384,768]{1,0:T(8,128)(2,1)}, bf16[384,768]{1,0:T(8,128)(2,1)}, u32[]{:S(2)}, u32[]{:S(2)}) collective-permute-start(bf16[384,768]{1,0:T(8,128)(2,1)} %collective-permute-done.4.side_b), channel_id=1, source_target_pairs={{1,0},{0,1},{3,2},{2,3},{5,4},{4,5},{7,6},{6,7},{9,8},{8,9},{11,10... | collective-permute-start | bytes 1769480 | tf_op jit(solution)/shard_map/ppermute | solution.py:23
  41.3 1.9 %collective-permute-start.11 = (bf16[192,768]{1,0:T(8,128)(2,1)}, bf16[192,768]{1,0:T(8,128)(2,1)}, u32[]{:S(2)}, u32[]{:S(2)}) collective-permute-start(bf16[192,768]{1,0:T(8,128)(2,1)} %collective-permute-done.7.up_side_a), channel_id=1, source_target_pairs={{1,0},{0,1},{3,2},{2,3},{5,4},{4,5},{7,6},{6,7},{9,8},{8,9},{11,10... | collective-permute-start | bytes 884744 | tf_op jit(solution)/shard_map/ppermute | solution.py:23
  52.3 19.5 %collective-permute-start.18 = (bf16[384,896]{1,0:T(8,128)(2,1)S(1)}, bf16[384,896]{1,0:T(8,128)(2,1)S(1)}, u32[]{:S(2)}, u32[]{:S(2)}) collective-permute-start(bf16[384,896]{1,0:T(8,128)(2,1)S(1)} %get-tuple-element.63), channel_id=1, source_target_pairs={{12,0},{13,1},{14,2},{15,3},{0,4},{1,5},{2,6},{3,7},{4,8},{5,9},{6... | collective-permute-start | bytes 2064392 | tf_op jit(solution)/shard_map/ppermute | solution.py:23
  52.5 9.1 %collective-permute-start.15 = (bf16[384,384]{1,0:T(8,128)(2,1)S(1)}, bf16[384,384]{1,0:T(8,128)(2,1)S(1)}, u32[]{:S(2)}, u32[]{:S(2)}) collective-permute-start(bf16[384,384]{1,0:T(8,128)(2,1)S(1)} %cross.1.t0), channel_id=1, source_target_pairs={{2,0},{3,1},{0,2},{1,3},{6,4},{7,5},{4,6},{5,7},{10,8},{11,9},{8,1... | collective-permute-start | bytes 884744 | tf_op jit(solution)/shard_map/ppermute | solution.py:23
  53.4 8.3 %collective-permute-start.16 = (bf16[384,384]{1,0:T(8,128)(2,1)S(1)}, bf16[384,384]{1,0:T(8,128)(2,1)S(1)}, u32[]{:S(2)}, u32[]{:S(2)}) collective-permute-start(bf16[384,384]{1,0:T(8,128)(2,1)S(1)} %cross.1.t0), channel_id=1, source_target_pairs={{1,0},{0,1},{3,2},{2,3},{5,4},{4,5},{7,6},{6,7},{9,8},{8,9},{11,10... | collective-permute-start | bytes 884744 | tf_op jit(solution)/shard_map/ppermute | solution.py:23
  61.6 1.6 %collective-permute-start.17 = (bf16[384,384]{1,0:T(8,128)(2,1)S(1)}, bf16[384,384]{1,0:T(8,128)(2,1)S(1)}, u32[]{:S(2)}, u32[]{:S(2)}) collective-permute-start(bf16[384,384]{1,0:T(8,128)(2,1)S(1)} %collective-permute-done.15.t1), channel_id=1, source_target_pairs={{1,0},{0,1},{3,2},{2,3},{5,4},{4,5},{7,6},{6,7},{9,8},{8,9},{11,10... | collective-permute-start | bytes 884744 | tf_op jit(solution)/shard_map/ppermute | solution.py:23
  72.9 23.1 %collective-permute-start.23 = (bf16[320,896]{1,0:T(8,128)(2,1)S(1)}, bf16[320,896]{1,0:T(8,128)(2,1)S(1)}, u32[]{:S(2)}, u32[]{:S(2)}) collective-permute-start(bf16[320,896]{1,0:T(8,128)(2,1)S(1)} %get-tuple-element.69), channel_id=1, source_target_pairs={{4,0},{5,1},{6,2},{7,3},{8,4},{9,5},{10,6},{11,7},{12,8},{13,9},{1... | collective-permute-start | bytes 1720328 | tf_op jit(solution)/shard_map/ppermute | solution.py:23
  73.0 23.0 %collective-permute-start.26 = (bf16[320,896]{1,0:T(8,128)(2,1)S(1)}, bf16[320,896]{1,0:T(8,128)(2,1)S(1)}, u32[]{:S(2)}, u32[]{:S(2)}) collective-permute-start(bf16[320,896]{1,0:T(8,128)(2,1)S(1)} %get-tuple-element.69), channel_id=1, source_target_pairs={{16,0},{0,16},{17,1},{1,17},{18,2},{2,18},{19,3},{3,19},{20,4},{4,... | collective-permute-start | bytes 1720328 | tf_op jit(solution)/shard_map/ppermute | solution.py:44
  74.6 1.9 %collective-permute-start.19 = (f32[16,384]{1,0:T(8,128)S(1)}, f32[16,384]{1,0:T(8,128)S(1)}, u32[]{:S(2)}, u32[]{:S(2)}) collective-permute-start(f32[16,384]{1,0:T(8,128)S(1)} %get-tuple-element.65.s0), channel_id=1, source_target_pairs={{1,0},{0,1},{3,2},{2,3},{5,4},{4,5},{7,6},{6,7},{9,8},{8,9},{11,10... | collective-permute-start | bytes 73736 | tf_op jit(solution)/shard_map/ppermute | solution.py:23
  74.6 3.8 %collective-permute-start.20 = (f32[16,384]{1,0:T(8,128)S(1)}, f32[16,384]{1,0:T(8,128)S(1)}, u32[]{:S(2)}, u32[]{:S(2)}) collective-permute-start(f32[16,384]{1,0:T(8,128)S(1)} %get-tuple-element.65.s0), channel_id=1, source_target_pairs={{2,0},{3,1},{0,2},{1,3},{6,4},{7,5},{4,6},{5,7},{10,8},{11,9},{8,1... | collective-permute-start | bytes 73736 | tf_op jit(solution)/shard_map/ppermute | solution.py:23
  75.6 3.3 %collective-permute-start.21 = (f32[16,384]{1,0:T(8,128)S(1)}, f32[16,384]{1,0:T(8,128)S(1)}, u32[]{:S(2)}, u32[]{:S(2)}) collective-permute-start(f32[16,384]{1,0:T(8,128)S(1)} %get-tuple-element.65.s0), channel_id=1, source_target_pairs={{3,0},{2,1},{1,2},{0,3},{7,4},{6,5},{5,6},{4,7},{11,8},{10,9},{9,1... | collective-permute-start | bytes 73736 | tf_op jit(solution)/shard_map/ppermute | solution.py:23
  82.5 1.9 %collective-permute-start.22 = (bf16[384,224]{1,0:T(8,128)(2,1)S(1)}, bf16[384,224]{1,0:T(8,128)(2,1)S(1)}, u32[]{:S(2)}, u32[]{:S(2)}) collective-permute-start(bf16[384,224]{1,0:T(8,128)(2,1)S(1)} %get-tuple-element.67), channel_id=1, source_target_pairs={{1,0},{0,1},{3,2},{2,3},{5,4},{4,5},{7,6},{6,7},{9,8},{8,9},{11,10... | collective-permute-start | bytes 516104 | tf_op jit(solution)/shard_map/ppermute | solution.py:23
  82.8 7.7 %collective-permute-start.24 = (bf16[384,224]{1,0:T(8,128)(2,1)S(1)}, bf16[384,224]{1,0:T(8,128)(2,1)S(1)}, u32[]{:S(2)}, u32[]{:S(2)}) collective-permute-start(bf16[384,224]{1,0:T(8,128)(2,1)S(1)} %get-tuple-element.71), channel_id=1, source_target_pairs={{2,0},{3,1},{0,2},{1,3},{6,4},{7,5},{4,6},{5,7},{10,8},{11,9},{8,1... | collective-permute-start | bytes 516104 | tf_op jit(solution)/shard_map/ppermute | solution.py:23
  83.9 9.3 %collective-permute-start.25 = (bf16[384,224]{1,0:T(8,128)(2,1)S(1)}, bf16[384,224]{1,0:T(8,128)(2,1)S(1)}, u32[]{:S(2)}, u32[]{:S(2)}) collective-permute-start(bf16[384,224]{1,0:T(8,128)(2,1)S(1)} %get-tuple-element.72), channel_id=1, source_target_pairs={{3,0},{2,1},{1,2},{0,3},{7,4},{6,5},{5,6},{4,7},{11,8},{10,9},{9,1... | collective-permute-start | bytes 516104 | tf_op jit(solution)/shard_map/ppermute | solution.py:23
  85.7 8.5 %collective-permute-start.27 = (bf16[96,896]{1,0:T(8,128)(2,1)S(1)}, bf16[96,896]{1,0:T(8,128)(2,1)S(1)}, u32[]{:S(2)}, u32[]{:S(2)}) collective-permute-start(bf16[96,896]{1,0:T(8,128)(2,1)S(1)} %get-tuple-element.74), channel_id=1, source_target_pairs={{4,0},{5,1},{6,2},{7,3},{8,4},{9,5},{10,6},{11,7},{12,8},{13,9},{1... | collective-permute-start | bytes 516104 | tf_op jit(solution)/shard_map/ppermute | solution.py:23
  90.6 5.4 %collective-permute-start.28 = (bf16[96,896]{1,0:T(8,128)(2,1)S(1)}, bf16[96,896]{1,0:T(8,128)(2,1)S(1)}, u32[]{:S(2)}, u32[]{:S(2)}) collective-permute-start(bf16[96,896]{1,0:T(8,128)(2,1)S(1)} %get-tuple-element.74), channel_id=1, source_target_pairs={{16,0},{0,16},{17,1},{1,17},{18,2},{2,18},{19,3},{3,19},{20,4},{4,... | collective-permute-start | bytes 516104 | tf_op jit(solution)/shard_map/ppermute | solution.py:44
  96.0 18.2 %collective-permute-start.32 = (bf16[384,896]{1,0:T(8,128)(2,1)S(1)}, bf16[384,896]{1,0:T(8,128)(2,1)S(1)}, u32[]{:S(2)}, u32[]{:S(2)}) collective-permute-start(bf16[384,896]{1,0:T(8,128)(2,1)S(1)} %pack.4), channel_id=1, source_target_pairs={{12,0},{13,1},{14,2},{15,3},{0,4},{1,5},{2,6},{3,7},{4,8},{5,9},{6... | collective-permute-start | bytes 2064392 | tf_op jit(solution)/shard_map/ppermute | solution.py:23
  101.6 1.9 %collective-permute-start.29 = (bf16[384,224]{1,0:T(8,128)(2,1)S(1)}, bf16[384,224]{1,0:T(8,128)(2,1)S(1)}, u32[]{:S(2)}, u32[]{:S(2)}) collective-permute-start(bf16[384,224]{1,0:T(8,128)(2,1)S(1)} %get-tuple-element.78), channel_id=1, source_target_pairs={{1,0},{0,1},{3,2},{2,3},{5,4},{4,5},{7,6},{6,7},{9,8},{8,9},{11,10... | collective-permute-start | bytes 516104 | tf_op jit(solution)/shard_map/ppermute | solution.py:23
  101.7 7.8 %collective-permute-start.30 = (bf16[384,224]{1,0:T(8,128)(2,1)S(1)}, bf16[384,224]{1,0:T(8,128)(2,1)S(1)}, u32[]{:S(2)}, u32[]{:S(2)}) collective-permute-start(bf16[384,224]{1,0:T(8,128)(2,1)S(1)} %get-tuple-element.79), channel_id=1, source_target_pairs={{2,0},{3,1},{0,2},{1,3},{6,4},{7,5},{4,6},{5,7},{10,8},{11,9},{8,1... | collective-permute-start | bytes 516104 | tf_op jit(solution)/shard_map/ppermute | solution.py:23
  102.7 10.1 %collective-permute-start.31 = (bf16[384,224]{1,0:T(8,128)(2,1)S(1)}, bf16[384,224]{1,0:T(8,128)(2,1)S(1)}, u32[]{:S(2)}, u32[]{:S(2)}) collective-permute-start(bf16[384,224]{1,0:T(8,128)(2,1)S(1)} %get-tuple-element.80), channel_id=1, source_target_pairs={{3,0},{2,1},{1,2},{0,3},{7,4},{6,5},{5,6},{4,7},{11,8},{10,9},{9,1... | collective-permute-start | bytes 516104 | tf_op jit(solution)/shard_map/ppermute | solution.py:23
  (7 other events, 7.2 us)

commit v4 on v3

--- a/solution.py
+++ b/solution.py
@@ -100,18 +100,10 @@
                 out[:, k * quarter : (k + 1) * quarter] = piece[...]
 
 
-def unit_kernel(embeddings, unit, *parts):
-    values = embeddings[...].astype(F32)
+def unit_rows(embeddings):
+    values = embeddings.astype(F32)
     scaled = values * lax.rsqrt(jnp.mean(values * values, axis=-1, keepdims=True) + 1e-06)
-    unit[...] = (scaled / math.sqrt(values.shape[-1])).astype(BF16)
-    halve(unit, parts)
-
-
-def halve(block, parts):
-    first = 0
-    for part in parts:
-        part[...] = block[first : first + part.shape[0], :]
-        first = first + part.shape[0]
+    return (scaled / math.sqrt(values.shape[-1])).astype(BF16)
 
 
 def seed_kernel(scalars, labels, seed, *pieces):
@@ -120,22 +112,18 @@
     cut(seed, scalars[0], list(enumerate(pieces, 1)))
 
 
-def pack_kernel(scalars, whole, p1, p2, p3, out, *parts):
+def pack_kernel(scalars, whole, p1, p2, p3, out):
     out[...] = whole[...]
     join(scalars[0], [(1, p1), (2, p2), (3, p3)], out)
-    halve(out, parts)
 
 
 def at(cluster, rows):
     return pl.ds(pl.multiple_of(cluster * rows, rows), rows)
 
 
-def place_rows(cluster, blocks, rows, stack):
-    start = cluster * rows
-    for block in blocks:
-        count = block.shape[0]
-        stack[pl.ds(pl.multiple_of(start, count), count), :] = block[...]
-        start = start + count
+def place_units(start, block, stack):
+    count = block.shape[0]
+    stack[pl.ds(pl.multiple_of(start, count), count), :] = unit_rows(block[...])
 
 
 def near_kernel(units, near):
@@ -151,23 +139,24 @@
             near[k * rows : (k + 1) * rows, span] = tile.astype(BF16)
 
 
-def stage_kernel(clusters, unit, side_a, core, across_a, up, up_side_a, up_core, up_across_a, own, units, up_units, stack):
-    rows = unit.shape[0]
-    for i, (mine, upper) in enumerate(
-        ((unit, up), (side_a, up_side_a), (core, up_core), (across_a, up_across_a))
-    ):
-        place_rows(clusters[i], (mine,), rows, units)
-        place_rows(clusters[i], (upper,), rows, up_units)
-    unpack(own, stack)
+def stage_kernel(clusters, own, side_a, core, across_a, units):
+    rows = own.shape[0]
+    for i, block in enumerate((own, side_a, core, across_a)):
+        place_units(clusters[i] * rows, block, units)
+
+
+def stage_seed_kernel(clusters, own, side_a, core, across_a, seed, units, stack):
+    stage_kernel(clusters, own, side_a, core, across_a, units)
+    unpack(seed, stack)
 
 
 def far_kernel(clusters, units_in, up_in, side_b, across_b, stack, units, up_units, far, sums):
     rows = units.shape[0] // QUAD
     half = rows // 2
     for i, block in ((1, side_b), (3, across_b)):
-        start = pl.multiple_of(clusters[i] * rows + half, half)
-        units[pl.ds(start, half), :] = block[:half, :]
-        up_units[pl.ds(start, half), :] = block[half:, :]
+        start = clusters[i] * rows + half
+        place_units(start, block.at[:half], units)
+        place_units(start, block.at[half:], up_units)
     for k in range(QUAD):
         here = slice(k * rows, (k + 1) * rows)
         for first in range(0, k + 1, 2):
@@ -210,11 +199,12 @@
     cut(out, scalars[0], [(1, p1), (2, p2), (3, p3)])
 
 
-def cross_kernel(weight, unit, *rest):
+def cross_kernel(weight, own, *rest):
     others, out = rest[:-1], rest[-1]
-    rows = unit.shape[0]
+    rows = own.shape[0]
+    unit = unit_rows(own[...])
     for n, other in enumerate(others):
-        out[n * rows : (n + 1) * rows, :] = (affinity(unit[...], other[...]) * weight).astype(BF16)
+        out[n * rows : (n + 1) * rows, :] = (affinity(unit, unit_rows(other[...])) * weight).astype(BF16)
 
 
 def near_products(near, stack, total):
@@ -324,38 +314,36 @@
     matrix = like((QUAD * rows, QUAD * rows), BF16)
 
     half_rows = rows // 2
-    unit_half = like((half_rows, depth), BF16)
-
-    unit, unit_a, unit_b = call(
-        unit_kernel, "unit", (embeddings,), (like(embeddings.shape, BF16), unit_half, unit_half)
-    )
-    side_a = from_side(unit_a)
-    unit_up = from_up(unit)
+
+    own_up = from_up(embeddings)
+    side_a = from_side(embeddings[:half_rows])
     seed, *pieces = call(seed_kernel, "seed", (scalars, labels), (packed, piece, piece, piece))
     received = exchange(pieces)
-    unit_core = from_core(unit)
-    cross_unit = [from_group(after(unit, seed), step) for step in steps]
+    own_core = from_core(embeddings)
+    cross_own = [from_group(after(embeddings, seed), step) for step in steps]
     up_side_a = from_up(side_a)
-    side_b = from_side(after(jnp.concatenate([after(unit_b, side_a), unit_up[half_rows:]]), received[1:]))
-    received[0] = after(received[0], unit_up)
+    late = jnp.concatenate([after(embeddings, side_a)[half_rows:], own_up[half_rows:]])
+    side_b = from_side(after(late, received[1:]))
+    received[0] = after(received[0], own_up)
     packed_seed = call(pack_kernel, "pack", (scalars, seed, *received), packed)
     seed_up = from_up(packed_seed)
     seed_cross = [from_group(packed_seed, step) for step in steps]
     cross0 = call(
-        functools.partial(cross_kernel, weight), "cross", (unit, *cross_unit), like((len(steps) * rows, rows), BF16)
-    )
-    side_b = after(side_b, (packed_seed, cross0, up_side_a))
+        functools.partial(cross_kernel, weight), "cross", (embeddings, *cross_own), like((len(steps) * rows, rows), BF16)
+    )
+    across_a = from_core(side_a)
+    unit_stack = like((QUAD * rows, depth), BF16)
+    units, seed_stack = call(
+        stage_seed_kernel,
+        "stage_own",
+        (clusters, embeddings, side_a, own_core, across_a, packed_seed),
+        (unit_stack, like((QUAD * rows, classes // QUAD), BF16)),
+    )
+    side_b = after(side_b, (cross0, units, up_side_a))
     across_b = from_core(side_b)
-    across_a, up_core, up_across_a = from_core(side_a), from_core(unit_up), from_core(up_side_a)
-    unit_stack = like((QUAD * rows, depth), BF16)
-    units, up_units, seed_stack = call(
-        stage_kernel,
-        "stage",
-        (
-            clusters, after(unit, side_b), side_a, unit_core, across_a, unit_up, up_side_a, up_core, up_across_a,
-            packed_seed,
-        ),
-        (unit_stack, unit_stack, like((QUAD * rows, classes // QUAD), BF16)),
+    up_core, up_across_a = from_core(own_up), from_core(up_side_a)
+    up_units = call(
+        stage_kernel, "stage_up", (clusters, after(own_up, side_b), up_side_a, up_core, up_across_a), unit_stack
     )
     cross0 = after(cross0, (side_b, seed_up, seed_cross))
     cross1, cross2 = from_side(cross0), from_core(cross0)

time: 116 us -> 113 us (0.974)
  waiting for transfers between devices: 48.6 us -> 44.1 us
    ppermute x29, waiting for transfers between devices: 46.8 us -> 42.6 us  [along_dev(): lax.ppermute(block, 'dev', [(source(i) % size, i) for i in range(size)])]
    unnamed x12, local copies, waits for them, and re-layouts: 5.71 us -> 4.33 us
  transfers between devices with their start and end apart: 33 -> 33, of which waited for: 19 -> 18; matrix products, arithmetic and copies ran while one was open for 1% -> 3% of each run, Pallas kernels for 25% -> 27%
where the time goes in v4:
time: 113 us
  waiting for transfers between devices  44.1 us (39%)
  Pallas kernels  33.1 us (29%)
  starting transfers between devices  27.2 us (24%)
  local copies, waits for them, and re-layouts  6.38 us (6%)
    ppermute x29, waiting for transfers between devices, along_dev(): lax.ppermute(block, 'dev', [(source(i) % size, i) for i in range(size)])  42.6 us
    pallas_call x15, Pallas kernels, call(): pl.pallas_call(kernel, in_specs=specs, out_shape=out_shape, scratch_shape...  33.1 us
    ppermute x29, starting transfers between devices, along_dev(): lax.ppermute(block, 'dev', [(source(i) % size, i) for i in range(size)])  22.1 us
    ppermute x4, starting transfers between devices, from_group(): lax.ppermute(block, 'grp', [((i + step) % size, i) for i in range(size)])  5.13 us
    unnamed x12, local copies, waits for them, and re-layouts  4.33 us
  transfers between devices with their start and end apart: 33, of which 18 were waited for; matrix products, arithmetic and copies ran while one was open for 3% of the time, Pallas kernels for 27%

profile of v4, /device:TPU:0, one launch (start us, length us, event | category | flops | bytes accessed | tf_op | source)
XLA Modules:
  0.0 112.6 jit_solution(17759000970802364465)
XLA Ops:
  0.0 5.0 %collective-permute-start.4 = (bf16[384,768]{1,0:T(8,128)(2,1)}, bf16[384,768]{1,0:T(8,128)(2,1)S(1)}, u32[]{:S(2)}, u32[]{:S(2)}) collective-permute-start(bf16[384,768]{1,0:T(8,128)(2,1)} %own.3), channel_id=1, source_target_pairs={{4,0},{5,1},{6,2},{7,3},{8,4},{9,5},{10,6},{11,7},{12,8},{13,9},{1... | collective-permute-start | bytes 1769480 | tf_op jit(solution)/shard_map/ppermute | solution.py:23
  6.1 1.6 %collective-permute-start = (bf16[192,768]{1,0:T(8,128)(2,1)S(1)}, bf16[192,768]{1,0:T(8,128)(2,1)}, u32[]{:S(2)}, u32[]{:S(2)}) collective-permute-start(bf16[192,768]{1,0:T(8,128)(2,1)S(1)} %slice.9), channel_id=1, source_target_pairs={{2,0},{3,1},{0,2},{1,3},{6,4},{7,5},{4,6},{5,7},{10,8},{11,9},{8,1... | collective-permute-start | bytes 884744 | tf_op jit(solution)/shard_map/ppermute | solution.py:23
  11.2 1.7 %collective-permute-start.1 = (bf16[384,768]{1,0:T(8,128)(2,1)}, bf16[384,768]{1,0:T(8,128)(2,1)S(1)}, u32[]{:S(2)}, u32[]{:S(2)}) collective-permute-start(bf16[384,768]{1,0:T(8,128)(2,1)} %own.3), channel_id=1, source_target_pairs={{1,0},{0,1},{3,2},{2,3},{5,4},{4,5},{7,6},{6,7},{9,8},{8,9},{11,10... | collective-permute-start | bytes 1769480 | tf_op jit(solution)/shard_map/ppermute | solution.py:23
  12.8 3.3 %collective-permute-done.side_a = bf16[192,768]{1,0:T(8,128)(2,1)} collective-permute-done((bf16[192,768]{1,0:T(8,128)(2,1)S(1)}, bf16[192,768]{1,0:T(8,128)(2,1)}, u32[]{:S(2)}, u32[]{:S(2)}) %collective-permute-start) | collective-permute-done | bytes 294944 | tf_op jit(solution)/shard_map/ppermute | solution.py:23
  16.2 1.5 %collective-permute-start.8 = (bf16[384,768]{1,0:T(8,128)(2,1)}, bf16[384,768]{1,0:T(8,128)(2,1)}, u32[]{:S(2)}, u32[]{:S(2)}) collective-permute-start(bf16[384,768]{1,0:T(8,128)(2,1)} %own.3), channel_id=1, source_target_pairs={{16,0},{0,16},{17,1},{1,17},{18,2},{2,18},{19,3},{3,19},{20,4},{4,... | collective-permute-start | bytes 1769480 | tf_op jit(solution)/shard_map/ppermute | solution.py:44
  20.3 1.8 %collective-permute-done.6.p3 = bf16[384,224]{1,0:T(8,128)(2,1)S(1)} collective-permute-done((bf16[384,224]{1,0:T(8,128)(2,1)S(1)}, bf16[384,224]{1,0:T(8,128)(2,1)S(1)}, u32[]{:S(2)}, u32[]{:S(2)}) %collective-permute-start.6) | collective-permute-done | bytes 172064 | tf_op jit(solution)/shard_map/ppermute | solution.py:23
  23.7 1.4 %collective-permute-start.3 = (bf16[384,224]{1,0:T(8,128)(2,1)S(1)}, bf16[384,224]{1,0:T(8,128)(2,1)S(1)}, u32[]{:S(2)}, u32[]{:S(2)}) collective-permute-start(bf16[384,224]{1,0:T(8,128)(2,1)S(1)} %get-tuple-element.40), channel_id=1, source_target_pairs={{1,0},{0,1},{3,2},{2,3},{5,4},{4,5},{7,6},{6,7},{9,8},{8,9},{11,10... | collective-permute-start | bytes 516104 | tf_op jit(solution)/shard_map/ppermute | solution.py:23
  31.0 1.8 %cross.1.t0 = bf16[384,384]{1,0:T(8,128)(2,1)S(1)} custom-call(bf16[384,768]{1,0:T(8,128)(2,1)S(1)} %copy-done, bf16[384,768]{1,0:T(8,128)(2,1)} %collective-permute-done.8.rest_0_), custom_call_target="tpu_custom_call" | custom-call | tf_op jit(solution)/shard_map/cross/pallas_call | solution.py:59
  32.9 1.6 %collective-permute-start.14 = (bf16[384,896]{1,0:T(8,128)(2,1)S(1)}, bf16[384,896]{1,0:T(8,128)(2,1)S(1)}, u32[]{:S(2)}, u32[]{:S(2)}) collective-permute-start(bf16[384,896]{1,0:T(8,128)(2,1)S(1)} %pack.3.seed.own), channel_id=1, source_target_pairs={{16,0},{0,16},{17,1},{1,17},{18,2},{2,18},{19,3},{3,19},{20,4},{4,... | collective-permute-start | bytes 2064392 | tf_op jit(solution)/shard_map/ppermute | solution.py:44
  34.4 1.9 %stage_own.1 = (bf16[1536,768]{1,0:T(8,128)(2,1)S(1)}, bf16[1536,224]{1,0:T(8,128)(2,1)S(1)}) custom-call(s32[4]{0:T(128)S(1)} %pad_add_fusion.1.clusters, bf16[384,768]{1,0:T(8,128)(2,1)S(1)} %copy-done, bf16[192,768]{1,0:T(8,128)(2,1)} %collective-permute-done.side_a, bf16[384,768]{1,0:T(8,128)(2,1)S(1)} %collective-permute-done.1.core, ...), custom_call_target="tpu_custom_call" | custom-call | tf_op jit(solution)/shard_map/stage_own/pallas_call | solution.py:59
  37.2 1.7 %collective-permute-done.7.side_b = bf16[384,768]{1,0:T(8,128)(2,1)S(1)} collective-permute-done((bf16[384,768]{1,0:T(8,128)(2,1)}, bf16[384,768]{1,0:T(8,128)(2,1)S(1)}, u32[]{:S(2)}, u32[]{:S(2)}) %collective-permute-start.7) | collective-permute-done | bytes 589856 | tf_op jit(solution)/shard_map/ppermute | solution.py:23
  39.4 1.9 %collective-permute-done.11.across_a = bf16[192,768]{1,0:T(8,128)(2,1)S(1)} collective-permute-done((bf16[192,768]{1,0:T(8,128)(2,1)S(1)}, bf16[192,768]{1,0:T(8,128)(2,1)S(1)}, u32[]{:S(2)}, u32[]{:S(2)}) %collective-permute-start.11) | collective-permute-done | bytes 294944 | tf_op jit(solution)/shard_map/ppermute | solution.py:23
  42.6 4.7 %far.1 = (bf16[1536,768]{1,0:T(8,128)(2,1)S(1)}, bf16[1536,768]{1,0:T(8,128)(2,1)S(1)}, bf16[1536,1536]{1,0:T(8,128)(2,1)S(1)}, bf16[384,896]{1,0:T(8,128)(2,1)S(1)}) custom-call(s32[4]{0:T(128)S(1)} %pad_add_fusion.1.clusters, bf16[1536,768]{1,0:T(8,128)(2,1)S(1)} %get-tuple-element.44.units_in, ...), custom_call_target="tpu_custom_call", output_to_operand_aliasing={{0}: (1, {}), {1}: (2, {})} | custom-call | tf_op jit(solution)/shard_map/far/pallas_call | solution.py:59
  47.5 3.9 %collective-permute-done.13.up.rest_2_ = bf16[384,896]{1,0:T(8,128)(2,1)S(1)} collective-permute-done((bf16[384,896]{1,0:T(8,128)(2,1)S(1)}, bf16[384,896]{1,0:T(8,128)(2,1)S(1)}, u32[]{:S(2)}, u32[]{:S(2)}) %collective-permute-start.13) | collective-permute-done | bytes 688160 | tf_op jit(solution)/shard_map/ppermute | solution.py:23
  51.9 3.9 %near.1 = bf16[1536,1536]{1,0:T(8,128)(2,1)S(1)} custom-call(bf16[1536,768]{1,0:T(8,128)(2,1)S(1)} %get-tuple-element.53.units), custom_call_target="tpu_custom_call" | custom-call | tf_op jit(solution)/shard_map/near/pallas_call | solution.py:59
  55.8 4.0 %collective-permute-done.15.t1 = bf16[384,384]{1,0:T(8,128)(2,1)S(1)} collective-permute-done((bf16[384,384]{1,0:T(8,128)(2,1)S(1)}, bf16[384,384]{1,0:T(8,128)(2,1)S(1)}, u32[]{:S(2)}, u32[]{:S(2)}) %collective-permute-start.15) | collective-permute-done | bytes 294944 | tf_op jit(solution)/shard_map/ppermute | solution.py:23
  59.9 1.6 %collective-permute-done.17.t3 = bf16[384,384]{1,0:T(8,128)(2,1)S(1)} collective-permute-done((bf16[384,384]{1,0:T(8,128)(2,1)S(1)}, bf16[384,384]{1,0:T(8,128)(2,1)S(1)}, u32[]{:S(2)}, u32[]{:S(2)}) %collective-permute-start.17) | collective-permute-done | bytes 294944 | tf_op jit(solution)/shard_map/ppermute | solution.py:23
  61.5 3.7 %gather.1.kept = f32[384,896]{1,0:T(8,128)S(1)} custom-call(s32[4]{0:T(128)S(1)} %pad_add_fusion.1.clusters, bf16[1536,1536]{1,0:T(8,128)(2,1)S(1)} %near.1, bf16[1536,1536]{1,0:T(8,128)(2,1)S(1)} %get-tuple-element.51.far, bf16[384,384]{1,0:T(8,128)(2,1)S(1)} %cross.1.t0, bf16[384,384]{1,0:T(8,128)(2,1)S(1)} %collective-permute-done.15.t1, ...), custom_call_target="tpu_custom_call" | custom-call | tf_op jit(solution)/shard_map/gather/pallas_call | solution.py:59
  65.1 1.9 %collective-permute-done.18.sent = bf16[384,896]{1,0:T(8,128)(2,1)S(1)} collective-permute-done((bf16[384,896]{1,0:T(8,128)(2,1)S(1)}, bf16[384,896]{1,0:T(8,128)(2,1)S(1)}, u32[]{:S(2)}, u32[]{:S(2)}) %collective-permute-start.18) | collective-permute-done | bytes 688160 | tf_op jit(solution)/shard_map/ppermute | solution.py:23
  69.4 1.6 %collective-permute-start.26 = (bf16[320,896]{1,0:T(8,128)(2,1)S(1)}, bf16[320,896]{1,0:T(8,128)(2,1)S(1)}, u32[]{:S(2)}, u32[]{:S(2)}) collective-permute-start(bf16[320,896]{1,0:T(8,128)(2,1)S(1)} %get-tuple-element.61), channel_id=1, source_target_pairs={{16,0},{0,16},{17,1},{1,17},{18,2},{2,18},{19,3},{3,19},{20,4},{4,... | collective-permute-start | bytes 1720328 | tf_op jit(solution)/shard_map/ppermute | solution.py:44
  72.8 2.2 %collective-permute-done.20.s2 = f32[16,384]{1,0:T(8,128)S(1)} collective-permute-done((f32[16,384]{1,0:T(8,128)S(1)}, f32[16,384]{1,0:T(8,128)S(1)}, u32[]{:S(2)}, u32[]{:S(2)}) %collective-permute-start.20) | collective-permute-done | bytes 24608 | tf_op jit(solution)/shard_map/ppermute | solution.py:23
  75.1 3.6 %mix.1 = (bf16[96,896]{1,0:T(8,128)(2,1)S(1)}, bf16[384,896]{1,0:T(8,128)(2,1)}, bf16[1536,224]{1,0:T(8,128)(2,1)S(1)}, bf16[384,896]{1,0:T(8,128)(2,1)S(1)}, bf...) custom-call(s32[2]{0:T(128)S(1)} %pad_add_fusion.scalars, ...), custom_call_target="tpu_custom_call" | custom-call | tf_op jit(solution)/shard_map/mix/pallas_call | solution.py:59
  78.9 1.4 %collective-permute-start.24 = (bf16[384,224]{1,0:T(8,128)(2,1)S(1)}, bf16[384,224]{1,0:T(8,128)(2,1)S(1)}, u32[]{:S(2)}, u32[]{:S(2)}) collective-permute-start(bf16[384,224]{1,0:T(8,128)(2,1)S(1)} %get-tuple-element.63), channel_id=1, source_target_pairs={{2,0},{3,1},{0,2},{1,3},{6,4},{7,5},{4,6},{5,7},{10,8},{11,9},{8,1... | collective-permute-start | bytes 516104 | tf_op jit(solution)/shard_map/ppermute | solution.py:23
  80.6 1.4 %near_products.1.total_in = f32[1536,224]{1,0:T(8,128)S(1)} custom-call(bf16[1536,1536]{1,0:T(8,128)(2,1)S(1)} %near.1, bf16[1536,224]{1,0:T(8,128)(2,1)S(1)} %get-tuple-element.60.stack), custom_call_target="tpu_custom_call" | custom-call | tf_op jit(solution)/shard_map/near_products/pallas_call | solution.py:59
  82.5 4.1 %collective-permute-done.24.p2 = bf16[384,224]{1,0:T(8,128)(2,1)S(1)} collective-permute-done((bf16[384,224]{1,0:T(8,128)(2,1)S(1)}, bf16[384,224]{1,0:T(8,128)(2,1)S(1)}, u32[]{:S(2)}, u32[]{:S(2)}) %collective-permute-start.24) | collective-permute-done | bytes 172064 | tf_op jit(solution)/shard_map/ppermute | solution.py:23
  87.1 2.5 %collective-permute-done.25.p3 = bf16[384,224]{1,0:T(8,128)(2,1)S(1)} collective-permute-done((bf16[384,224]{1,0:T(8,128)(2,1)S(1)}, bf16[384,224]{1,0:T(8,128)(2,1)S(1)}, u32[]{:S(2)}, u32[]{:S(2)}) %collective-permute-start.25) | collective-permute-done | bytes 172064 | tf_op jit(solution)/shard_map/ppermute | solution.py:23
  90.6 1.5 %collective-permute-done.28.rest_4_ = bf16[96,896]{1,0:T(8,128)(2,1)S(1)} collective-permute-done((bf16[96,896]{1,0:T(8,128)(2,1)S(1)}, bf16[96,896]{1,0:T(8,128)(2,1)S(1)}, u32[]{:S(2)}, u32[]{:S(2)}) %collective-permute-start.28) | collective-permute-done | bytes 172064 | tf_op jit(solution)/shard_map/ppermute | solution.py:44
  93.2 3.7 %gather_mixed.1 = (f32[1536,224]{1,0:T(8,128)S(1)}, bf16[384,896]{1,0:T(8,128)(2,1)S(1)}, bf16[384,224]{1,0:T(8,128)(2,1)S(1)}, bf16[384,224]{1,0:T(8,128)(2,1)S(1)}, bf16[384,224]{1,0:T(8,128)(2,1)S(1)}) custom-call(s32[4]{0:T(128)S(1)} %pad_add_fusion.1.clusters, bf16[1536,1536]{1,0:T(8,128)(2,1)S(1)} %get-tuple-element.51.far, ...), custom_call_target="tpu_custom_call", output_to_operand_aliasing={{0}: (6, {})} | custom-call | tf_op jit(solution)/shard_map/gather_mixed/pallas_call | solution.py:59
  98.9 5.9 %collective-permute-done.30.p2 = bf16[384,224]{1,0:T(8,128)(2,1)S(1)} collective-permute-done((bf16[384,224]{1,0:T(8,128)(2,1)S(1)}, bf16[384,224]{1,0:T(8,128)(2,1)S(1)}, u32[]{:S(2)}, u32[]{:S(2)}) %collective-permute-start.30) | collective-permute-done | bytes 172064 | tf_op jit(solution)/shard_map/ppermute | solution.py:23
  104.8 3.3 %collective-permute-done.31.p3 = bf16[384,224]{1,0:T(8,128)(2,1)S(1)} collective-permute-done((bf16[384,224]{1,0:T(8,128)(2,1)S(1)}, bf16[384,224]{1,0:T(8,128)(2,1)S(1)}, u32[]{:S(2)}, u32[]{:S(2)}) %collective-permute-start.31) | collective-permute-done | bytes 172064 | tf_op jit(solution)/shard_map/ppermute | solution.py:23
  109.0 1.7 %collective-permute-done.32.sent = bf16[384,896]{1,0:T(8,128)(2,1)S(1)} collective-permute-done((bf16[384,896]{1,0:T(8,128)(2,1)S(1)}, bf16[384,896]{1,0:T(8,128)(2,1)S(1)}, u32[]{:S(2)}, u32[]{:S(2)}) %collective-permute-start.32) | collective-permute-done | bytes 688160 | tf_op jit(solution)/shard_map/ppermute | solution.py:23
  110.7 1.9 %finish.1 = bf16[384,896]{1,0:T(8,128)(2,1)} custom-call(s32[2]{0:T(128)S(1)} %pad_add_fusion.scalars, bf16[384,896]{1,0:T(8,128)(2,1)S(1)} %pack.5.kept, bf16[384,896]{1,0:T(8,128)(2,1)S(1)} %collective-permute-done.32.sent, bf16[384,896]{1,0:T(8,128)(2,1)S(1)} %get-tuple-element.39.whole.seed), custom_call_target="tpu_custom_call" | custom-call | tf_op jit(solution)/shard_map/finish/pallas_call | solution.py:59
  (67 shorter events, 28.2 us)
Async XLA Ops:
  0.0 18.7 %collective-permute-start.4 = (bf16[384,768]{1,0:T(8,128)(2,1)}, bf16[384,768]{1,0:T(8,128)(2,1)S(1)}, u32[]{:S(2)}, u32[]{:S(2)}) collective-permute-start(bf16[384,768]{1,0:T(8,128)(2,1)} %own.3), channel_id=1, source_target_pairs={{4,0},{5,1},{6,2},{7,3},{8,4},{9,5},{10,6},{11,7},{12,8},{13,9},{1... | collective-permute-start | bytes 1769480 | tf_op jit(solution)/shard_map/ppermute | solution.py:23
  6.1 10.1 %collective-permute-start = (bf16[192,768]{1,0:T(8,128)(2,1)S(1)}, bf16[192,768]{1,0:T(8,128)(2,1)}, u32[]{:S(2)}, u32[]{:S(2)}) collective-permute-start(bf16[192,768]{1,0:T(8,128)(2,1)S(1)} %slice.9), channel_id=1, source_target_pairs={{2,0},{3,1},{0,2},{1,3},{6,4},{7,5},{4,6},{5,7},{10,8},{11,9},{8,1... | collective-permute-start | bytes 884744 | tf_op jit(solution)/shard_map/ppermute | solution.py:23
  10.6 9.7 %collective-permute-start.5 = (bf16[384,224]{1,0:T(8,128)(2,1)S(1)}, bf16[384,224]{1,0:T(8,128)(2,1)S(1)}, u32[]{:S(2)}, u32[]{:S(2)}) collective-permute-start(bf16[384,224]{1,0:T(8,128)(2,1)S(1)} %get-tuple-element.42), channel_id=1, source_target_pairs={{2,0},{3,1},{0,2},{1,3},{6,4},{7,5},{4,6},{5,7},{10,8},{11,9},{8,1... | collective-permute-start | bytes 516104 | tf_op jit(solution)/shard_map/ppermute | solution.py:23
  11.1 11.0 %collective-permute-start.6 = (bf16[384,224]{1,0:T(8,128)(2,1)S(1)}, bf16[384,224]{1,0:T(8,128)(2,1)S(1)}, u32[]{:S(2)}, u32[]{:S(2)}) collective-permute-start(bf16[384,224]{1,0:T(8,128)(2,1)S(1)} %get-tuple-element.43), channel_id=1, source_target_pairs={{3,0},{2,1},{1,2},{0,3},{7,4},{6,5},{5,6},{4,7},{11,8},{10,9},{9,1... | collective-permute-start | bytes 516104 | tf_op jit(solution)/shard_map/ppermute | solution.py:23
  11.2 23.3 %collective-permute-start.1 = (bf16[384,768]{1,0:T(8,128)(2,1)}, bf16[384,768]{1,0:T(8,128)(2,1)S(1)}, u32[]{:S(2)}, u32[]{:S(2)}) collective-permute-start(bf16[384,768]{1,0:T(8,128)(2,1)} %own.3), channel_id=1, source_target_pairs={{1,0},{0,1},{3,2},{2,3},{5,4},{4,5},{7,6},{6,7},{9,8},{8,9},{11,10... | collective-permute-start | bytes 1769480 | tf_op jit(solution)/shard_map/ppermute | solution.py:23
  16.2 14.1 %collective-permute-start.8 = (bf16[384,768]{1,0:T(8,128)(2,1)}, bf16[384,768]{1,0:T(8,128)(2,1)}, u32[]{:S(2)}, u32[]{:S(2)}) collective-permute-start(bf16[384,768]{1,0:T(8,128)(2,1)} %own.3), channel_id=1, source_target_pairs={{16,0},{0,16},{17,1},{1,17},{18,2},{2,18},{19,3},{3,19},{20,4},{4,... | collective-permute-start | bytes 1769480 | tf_op jit(solution)/shard_map/ppermute | solution.py:44
  22.7 16.2 %collective-permute-start.7 = (bf16[384,768]{1,0:T(8,128)(2,1)}, bf16[384,768]{1,0:T(8,128)(2,1)S(1)}, u32[]{:S(2)}, u32[]{:S(2)}) collective-permute-start(bf16[384,768]{1,0:T(8,128)(2,1)} %pad_maximum_fusion), channel_id=1, source_target_pairs={{2,0},{3,1},{0,2},{1,3},{6,4},{7,5},{4,6},{5,7},{10,8},{11,9},{8,1... | collective-permute-start | bytes 1769480 | tf_op jit(solution)/shard_map/ppermute | solution.py:23
  23.7 2.7 %collective-permute-start.3 = (bf16[384,224]{1,0:T(8,128)(2,1)S(1)}, bf16[384,224]{1,0:T(8,128)(2,1)S(1)}, u32[]{:S(2)}, u32[]{:S(2)}) collective-permute-start(bf16[384,224]{1,0:T(8,128)(2,1)S(1)} %get-tuple-element.40), channel_id=1, source_target_pairs={{1,0},{0,1},{3,2},{2,3},{5,4},{4,5},{7,6},{6,7},{9,8},{8,9},{11,10... | collective-permute-start | bytes 516104 | tf_op jit(solution)/shard_map/ppermute | solution.py:23
  25.1 7.7 %collective-permute-start.2 = (bf16[192,768]{1,0:T(8,128)(2,1)}, bf16[192,768]{1,0:T(8,128)(2,1)}, u32[]{:S(2)}, u32[]{:S(2)}) collective-permute-start(bf16[192,768]{1,0:T(8,128)(2,1)} %collective-permute-done.side_a), channel_id=1, source_target_pairs={{1,0},{0,1},{3,2},{2,3},{5,4},{4,5},{7,6},{6,7},{9,8},{8,9},{11,10... | collective-permute-start | bytes 884744 | tf_op jit(solution)/shard_map/ppermute | solution.py:23
  27.2 10.1 %collective-permute-start.9 = (bf16[192,768]{1,0:T(8,128)(2,1)}, bf16[192,768]{1,0:T(8,128)(2,1)S(1)}, u32[]{:S(2)}, u32[]{:S(2)}) collective-permute-start(bf16[192,768]{1,0:T(8,128)(2,1)} %collective-permute-done.side_a), channel_id=1, source_target_pairs={{4,0},{5,1},{6,2},{7,3},{8,4},{9,5},{10,6},{11,7},{12,8},{13,9},{1... | collective-permute-start | bytes 884744 | tf_op jit(solution)/shard_map/ppermute | solution.py:23
  30.3 21.1 %collective-permute-start.13 = (bf16[384,896]{1,0:T(8,128)(2,1)S(1)}, bf16[384,896]{1,0:T(8,128)(2,1)S(1)}, u32[]{:S(2)}, u32[]{:S(2)}) collective-permute-start(bf16[384,896]{1,0:T(8,128)(2,1)S(1)} %pack.3.seed.own), channel_id=1, source_target_pairs={{4,0},{5,1},{6,2},{7,3},{8,4},{9,5},{10,6},{11,7},{12,8},{13,9},{1... | collective-permute-start | bytes 2064392 | tf_op jit(solution)/shard_map/ppermute | solution.py:23
  32.9 18.6 %collective-permute-start.14 = (bf16[384,896]{1,0:T(8,128)(2,1)S(1)}, bf16[384,896]{1,0:T(8,128)(2,1)S(1)}, u32[]{:S(2)}, u32[]{:S(2)}) collective-permute-start(bf16[384,896]{1,0:T(8,128)(2,1)S(1)} %pack.3.seed.own), channel_id=1, source_target_pairs={{16,0},{0,16},{17,1},{1,17},{18,2},{2,18},{19,3},{3,19},{20,4},{4,... | collective-permute-start | bytes 2064392 | tf_op jit(solution)/shard_map/ppermute | solution.py:44
  34.4 6.9 %collective-permute-start.10 = (bf16[384,768]{1,0:T(8,128)(2,1)S(1)}, bf16[384,768]{1,0:T(8,128)(2,1)S(1)}, u32[]{:S(2)}, u32[]{:S(2)}) collective-permute-start(bf16[384,768]{1,0:T(8,128)(2,1)S(1)} %collective-permute-done.4.own), channel_id=1, source_target_pairs={{1,0},{0,1},{3,2},{2,3},{5,4},{4,5},{7,6},{6,7},{9,8},{8,9},{11,10... | collective-permute-start | bytes 1769480 | tf_op jit(solution)/shard_map/ppermute | solution.py:23
  38.9 3.7 %collective-permute-start.12 = (bf16[384,768]{1,0:T(8,128)(2,1)S(1)}, bf16[384,768]{1,0:T(8,128)(2,1)S(1)}, u32[]{:S(2)}, u32[]{:S(2)}) collective-permute-start(bf16[384,768]{1,0:T(8,128)(2,1)S(1)} %collective-permute-done.7.side_b), channel_id=1, source_target_pairs={{1,0},{0,1},{3,2},{2,3},{5,4},{4,5},{7,6},{6,7},{9,8},{8,9},{11,10... | collective-permute-start | bytes 1769480 | tf_op jit(solution)/shard_map/ppermute | solution.py:23
  39.2 2.1 %collective-permute-start.11 = (bf16[192,768]{1,0:T(8,128)(2,1)S(1)}, bf16[192,768]{1,0:T(8,128)(2,1)S(1)}, u32[]{:S(2)}, u32[]{:S(2)}) collective-permute-start(bf16[192,768]{1,0:T(8,128)(2,1)S(1)} %collective-permute-done.9.side_a), channel_id=1, source_target_pairs={{1,0},{0,1},{3,2},{2,3},{5,4},{4,5},{7,6},{6,7},{9,8},{8,9},{11,10... | collective-permute-start | bytes 884744 | tf_op jit(solution)/shard_map/ppermute | solution.py:23
  47.3 19.7 %collective-permute-start.18 = (bf16[384,896]{1,0:T(8,128)(2,1)S(1)}, bf16[384,896]{1,0:T(8,128)(2,1)S(1)}, u32[]{:S(2)}, u32[]{:S(2)}) collective-permute-start(bf16[384,896]{1,0:T(8,128)(2,1)S(1)} %get-tuple-element.55), channel_id=1, source_target_pairs={{12,0},{13,1},{14,2},{15,3},{0,4},{1,5},{2,6},{3,7},{4,8},{5,9},{6... | collective-permute-start | bytes 2064392 | tf_op jit(solution)/shard_map/ppermute | solution.py:23
  51.4 8.5 %collective-permute-start.15 = (bf16[384,384]{1,0:T(8,128)(2,1)S(1)}, bf16[384,384]{1,0:T(8,128)(2,1)S(1)}, u32[]{:S(2)}, u32[]{:S(2)}) collective-permute-start(bf16[384,384]{1,0:T(8,128)(2,1)S(1)} %cross.1.t0), channel_id=1, source_target_pairs={{2,0},{3,1},{0,2},{1,3},{6,4},{7,5},{4,6},{5,7},{10,8},{11,9},{8,1... | collective-permute-start | bytes 884744 | tf_op jit(solution)/shard_map/ppermute | solution.py:23
  51.9 7.9 %collective-permute-start.16 = (bf16[384,384]{1,0:T(8,128)(2,1)S(1)}, bf16[384,384]{1,0:T(8,128)(2,1)S(1)}, u32[]{:S(2)}, u32[]{:S(2)}) collective-permute-start(bf16[384,384]{1,0:T(8,128)(2,1)S(1)} %cross.1.t0), channel_id=1, source_target_pairs={{1,0},{0,1},{3,2},{2,3},{5,4},{4,5},{7,6},{6,7},{9,8},{8,9},{11,10... | collective-permute-start | bytes 884744 | tf_op jit(solution)/shard_map/ppermute | solution.py:23
  68.1 23.9 %collective-permute-start.23 = (bf16[320,896]{1,0:T(8,128)(2,1)S(1)}, bf16[320,896]{1,0:T(8,128)(2,1)S(1)}, u32[]{:S(2)}, u32[]{:S(2)}) collective-permute-start(bf16[320,896]{1,0:T(8,128)(2,1)S(1)} %get-tuple-element.61), channel_id=1, source_target_pairs={{4,0},{5,1},{6,2},{7,3},{8,4},{9,5},{10,6},{11,7},{12,8},{13,9},{1... | collective-permute-start | bytes 1720328 | tf_op jit(solution)/shard_map/ppermute | solution.py:23
  69.4 22.6 %collective-permute-start.26 = (bf16[320,896]{1,0:T(8,128)(2,1)S(1)}, bf16[320,896]{1,0:T(8,128)(2,1)S(1)}, u32[]{:S(2)}, u32[]{:S(2)}) collective-permute-start(bf16[320,896]{1,0:T(8,128)(2,1)S(1)} %get-tuple-element.61), channel_id=1, source_target_pairs={{16,0},{0,16},{17,1},{1,17},{18,2},{2,18},{19,3},{3,19},{20,4},{4,... | collective-permute-start | bytes 1720328 | tf_op jit(solution)/shard_map/ppermute | solution.py:44
  71.0 1.9 %collective-permute-start.19 = (f32[16,384]{1,0:T(8,128)S(1)}, f32[16,384]{1,0:T(8,128)S(1)}, u32[]{:S(2)}, u32[]{:S(2)}) collective-permute-start(f32[16,384]{1,0:T(8,128)S(1)} %get-tuple-element.57.s0), channel_id=1, source_target_pairs={{1,0},{0,1},{3,2},{2,3},{5,4},{4,5},{7,6},{6,7},{9,8},{8,9},{11,10... | collective-permute-start | bytes 73736 | tf_op jit(solution)/shard_map/ppermute | solution.py:23
  71.0 4.1 %collective-permute-start.20 = (f32[16,384]{1,0:T(8,128)S(1)}, f32[16,384]{1,0:T(8,128)S(1)}, u32[]{:S(2)}, u32[]{:S(2)}) collective-permute-start(f32[16,384]{1,0:T(8,128)S(1)} %get-tuple-element.57.s0), channel_id=1, source_target_pairs={{2,0},{3,1},{0,2},{1,3},{6,4},{7,5},{4,6},{5,7},{10,8},{11,9},{8,1... | collective-permute-start | bytes 73736 | tf_op jit(solution)/shard_map/ppermute | solution.py:23
  71.6 3.5 %collective-permute-start.21 = (f32[16,384]{1,0:T(8,128)S(1)}, f32[16,384]{1,0:T(8,128)S(1)}, u32[]{:S(2)}, u32[]{:S(2)}) collective-permute-start(f32[16,384]{1,0:T(8,128)S(1)} %get-tuple-element.57.s0), channel_id=1, source_target_pairs={{3,0},{2,1},{1,2},{0,3},{7,4},{6,5},{5,6},{4,7},{11,8},{10,9},{9,1... | collective-permute-start | bytes 73736 | tf_op jit(solution)/shard_map/ppermute | solution.py:23
  78.7 1.9 %collective-permute-start.22 = (bf16[384,224]{1,0:T(8,128)(2,1)S(1)}, bf16[384,224]{1,0:T(8,128)(2,1)S(1)}, u32[]{:S(2)}, u32[]{:S(2)}) collective-permute-start(bf16[384,224]{1,0:T(8,128)(2,1)S(1)} %get-tuple-element.59), channel_id=1, source_target_pairs={{1,0},{0,1},{3,2},{2,3},{5,4},{4,5},{7,6},{6,7},{9,8},{8,9},{11,10... | collective-permute-start | bytes 516104 | tf_op jit(solution)/shard_map/ppermute | solution.py:23
  78.9 7.7 %collective-permute-start.24 = (bf16[384,224]{1,0:T(8,128)(2,1)S(1)}, bf16[384,224]{1,0:T(8,128)(2,1)S(1)}, u32[]{:S(2)}, u32[]{:S(2)}) collective-permute-start(bf16[384,224]{1,0:T(8,128)(2,1)S(1)} %get-tuple-element.63), channel_id=1, source_target_pairs={{2,0},{3,1},{0,2},{1,3},{6,4},{7,5},{4,6},{5,7},{10,8},{11,9},{8,1... | collective-permute-start | bytes 516104 | tf_op jit(solution)/shard_map/ppermute | solution.py:23
  80.3 9.3 %collective-permute-start.25 = (bf16[384,224]{1,0:T(8,128)(2,1)S(1)}, bf16[384,224]{1,0:T(8,128)(2,1)S(1)}, u32[]{:S(2)}, u32[]{:S(2)}) collective-permute-start(bf16[384,224]{1,0:T(8,128)(2,1)S(1)} %get-tuple-element.64), channel_id=1, source_target_pairs={{3,0},{2,1},{1,2},{0,3},{7,4},{6,5},{5,6},{4,7},{11,8},{10,9},{9,1... | collective-permute-start | bytes 516104 | tf_op jit(solution)/shard_map/ppermute | solution.py:23
  82.0 8.6 %collective-permute-start.27 = (bf16[96,896]{1,0:T(8,128)(2,1)S(1)}, bf16[96,896]{1,0:T(8,128)(2,1)S(1)}, u32[]{:S(2)}, u32[]{:S(2)}) collective-permute-start(bf16[96,896]{1,0:T(8,128)(2,1)S(1)} %get-tuple-element.66), channel_id=1, source_target_pairs={{4,0},{5,1},{6,2},{7,3},{8,4},{9,5},{10,6},{11,7},{12,8},{13,9},{1... | collective-permute-start | bytes 516104 | tf_op jit(solution)/shard_map/ppermute | solution.py:23
  86.7 5.4 %collective-permute-start.28 = (bf16[96,896]{1,0:T(8,128)(2,1)S(1)}, bf16[96,896]{1,0:T(8,128)(2,1)S(1)}, u32[]{:S(2)}, u32[]{:S(2)}) collective-permute-start(bf16[96,896]{1,0:T(8,128)(2,1)S(1)} %get-tuple-element.66), channel_id=1, source_target_pairs={{16,0},{0,16},{17,1},{1,17},{18,2},{2,18},{19,3},{3,19},{20,4},{4,... | collective-permute-start | bytes 516104 | tf_op jit(solution)/shard_map/ppermute | solution.py:44
  92.1 18.6 %collective-permute-start.32 = (bf16[384,896]{1,0:T(8,128)(2,1)S(1)}, bf16[384,896]{1,0:T(8,128)(2,1)S(1)}, u32[]{:S(2)}, u32[]{:S(2)}) collective-permute-start(bf16[384,896]{1,0:T(8,128)(2,1)S(1)} %pack.4), channel_id=1, source_target_pairs={{12,0},{13,1},{14,2},{15,3},{0,4},{1,5},{2,6},{3,7},{4,8},{5,9},{6... | collective-permute-start | bytes 2064392 | tf_op jit(solution)/shard_map/ppermute | solution.py:23
  96.9 1.9 %collective-permute-start.29 = (bf16[384,224]{1,0:T(8,128)(2,1)S(1)}, bf16[384,224]{1,0:T(8,128)(2,1)S(1)}, u32[]{:S(2)}, u32[]{:S(2)}) collective-permute-start(bf16[384,224]{1,0:T(8,128)(2,1)S(1)} %get-tuple-element.70), channel_id=1, source_target_pairs={{1,0},{0,1},{3,2},{2,3},{5,4},{4,5},{7,6},{6,7},{9,8},{8,9},{11,10... | collective-permute-start | bytes 516104 | tf_op jit(solution)/shard_map/ppermute | solution.py:23
  97.0 7.8 %collective-permute-start.30 = (bf16[384,224]{1,0:T(8,128)(2,1)S(1)}, bf16[384,224]{1,0:T(8,128)(2,1)S(1)}, u32[]{:S(2)}, u32[]{:S(2)}) collective-permute-start(bf16[384,224]{1,0:T(8,128)(2,1)S(1)} %get-tuple-element.71), channel_id=1, source_target_pairs={{2,0},{3,1},{0,2},{1,3},{6,4},{7,5},{4,6},{5,7},{10,8},{11,9},{8,1... | collective-permute-start | bytes 516104 | tf_op jit(solution)/shard_map/ppermute | solution.py:23
  98.0 10.1 %collective-permute-start.31 = (bf16[384,224]{1,0:T(8,128)(2,1)S(1)}, bf16[384,224]{1,0:T(8,128)(2,1)S(1)}, u32[]{:S(2)}, u32[]{:S(2)}) collective-permute-start(bf16[384,224]{1,0:T(8,128)(2,1)S(1)} %get-tuple-element.72), channel_id=1, source_target_pairs={{3,0},{2,1},{1,2},{0,3},{7,4},{6,5},{5,6},{4,7},{11,8},{10,9},{9,1... | collective-permute-start | bytes 516104 | tf_op jit(solution)/shard_map/ppermute | solution.py:23
  (7 other events, 27.5 us)

commit v5 on v4

--- a/solution.py
+++ b/solution.py
@@ -162,7 +162,7 @@
         for first in range(0, k + 1, 2):
             span = slice(first * rows, min(first + 2, k + 1) * rows)
             far[here, span] = affinity(units[here, :], up_units[span, :]).astype(BF16)
-    scatter(far, stack, sums)
+    scatter(far, stack, (sums,))
 
 
 def unpack(block, stack):
@@ -171,7 +171,7 @@
         stack[k * rows : (k + 1) * rows, :] = block[:, k * quarter : (k + 1) * quarter]
 
 
-def scatter(far, stack, out):
+def scatter(far, stack, outs):
     rows, quarter = stack.shape[0] // QUAD, stack.shape[1]
     for k in range(QUAD):
         total = lax.dot_general(
@@ -180,10 +180,13 @@
             (((0,), (0,)), ((), ())),
             preferred_element_type=F32,
         )
-        out[:, k * quarter : (k + 1) * quarter] = total.astype(out.dtype)
-
-
-def mix_kernel(scalars, far, summed, s0, s1, s2, s3, seed, tail, mixed, stack, out, p1, p2, p3):
+        first = 0
+        for out in outs:
+            out[:, k * quarter : (k + 1) * quarter] = total[first : first + out.shape[0], :].astype(out.dtype)
+            first = first + out.shape[0]
+
+
+def mix_kernel(scalars, far, summed, s0, s1, s2, s3, seed, tail, mixed, stack, out_b, out_a, p1, p2, p3):
     total = (s0[...] + s1[...]) + (s2[...] + s3[...])
     rows = summed.shape[0]
     kept = tail.shape[0] - 2 * FACTORS
@@ -195,8 +198,8 @@
     tail[kept + FACTORS :, :rows] = (factor - high.astype(F32)).astype(BF16)
     mix(summed.at[: rows - kept], tail, seed, mixed)
     unpack(mixed, stack)
-    scatter(far, stack, out)
-    cut(out, scalars[0], [(1, p1), (2, p2), (3, p3)])
+    scatter(far, stack, (out_a, out_b))
+    cut(out_a, scalars[0], [(1, p1), (2, p2), (3, p3)])
 
 
 def cross_kernel(weight, own, *rest):
@@ -221,12 +224,15 @@
         total[here, :] += dot(tile[n * rows : (n + 1) * rows, :], stack[here, :])
 
 
-def far_products(far, stack, total, out):
+def far_products(far, stack, total, outs):
     rows, quarter = stack.shape[0] // QUAD, stack.shape[1]
     for k in range(QUAD):
         here = slice(k * rows, (k + 1) * rows)
         done = total[here, :] + dot(far[here, : (k + 1) * rows], stack[: (k + 1) * rows, :])
-        out[:, k * quarter : (k + 1) * quarter] = done.astype(out.dtype)
+        first = 0
+        for out in outs:
+            out[:, k * quarter : (k + 1) * quarter] = done[first : first + out.shape[0], :].astype(out.dtype)
+            first = first + out.shape[0]
 
 
 def gather_kernel(clusters, near, far, t0, t1, t2, t3, own, up, *rest):
@@ -237,11 +243,11 @@
         unpack(block, stack)
         cross_products(clusters, (t0, t1, t2, t3), n, stack, total)
     unpack(up, stack)
-    far_products(far, stack, total, out)
+    far_products(far, stack, total, (out,))
 
 
 def gather_mixed_kernel(clusters, far, t0, t1, t2, t3, total_in, *rest):
-    triples, (total, out, p1, p2, p3, mixed, stack) = rest[:-7], rest[-7:]
+    triples, (total, out_b, out_a, p1, p2, p3, mixed, stack) = rest[:-8], rest[-8:]
     triples = [triples[i : i + 3] for i in range(0, len(triples), 3)]
     for n, triple in enumerate(triples[1:]):
         mix(*triple, mixed)
@@ -249,8 +255,8 @@
         cross_products(clusters, (t0, t1, t2, t3), n, stack, total)
     mix(*triples[0], mixed)
     unpack(mixed, stack)
-    far_products(far, stack, total, out)
-    cut(out, clusters[0], [(1, p1), (2, p2), (3, p3)])
+    far_products(far, stack, total, (out_a, out_b))
+    cut(out_a, clusters[0], [(1, p1), (2, p2), (3, p3)])
 
 
 def lanes_of(count, lanes):
@@ -291,12 +297,24 @@
     squares[...] = sums + jnp.where((row == scalars[0]) & (lane >= scalars[1]), INVALID, 0.0)
 
 
-def finish_kernel(scalars, kept, sent, seed, out):
-    summed = kept[...].astype(F32) + sent[...].astype(F32)
-    factor = lax.rsqrt(jnp.mean(summed * summed, axis=-1, keepdims=True) + 1e-06)
-    result = keep_share * summed * factor + (1.0 - keep_share) * seed[...].astype(F32)
-    row = lax.broadcasted_iota(jnp.int32, summed.shape, 0)
-    out[...] = jnp.where(row < scalars[1], result, 0.0).astype(BF16)
+def add_kernel(scalars, kept, sent, out, p1, p2, p3):
+    out[...] = (kept[...] + sent[...].astype(F32)).astype(BF16)
+    cut(out, scalars[0], [(1, p1), (2, p2), (3, p3)])
+
+
+def finish_kernel(scalars, kept_a, sent_a, sums_b, p1, p2, p3, seed, out, whole_b):
+    whole_b[...] = sums_b[...]
+    join(scalars[0], [(1, p1), (2, p2), (3, p3)], whole_b)
+    half = kept_a.shape[0]
+    for first, summed in (
+        (0, kept_a[...].astype(F32) + sent_a[...].astype(F32)),
+        (half, whole_b[...].astype(F32)),
+    ):
+        here = slice(first, first + summed.shape[0])
+        factor = lax.rsqrt(jnp.mean(summed * summed, axis=-1, keepdims=True) + 1e-06)
+        result = keep_share * summed * factor + (1.0 - keep_share) * seed[here, :].astype(F32)
+        row = lax.broadcasted_iota(jnp.int32, summed.shape, 0) + first
+        out[here, :] = jnp.where(row < scalars[1], result, 0.0).astype(BF16)
 
 
 def body(embeddings, labels, cluster_rows):
@@ -375,11 +393,15 @@
 
     head_up = from_up(head)
     head_cross = [from_group(head, step) for step in steps]
-    tail, current, current_stack, sums, *pieces = call(
+    half, half_piece = like((half_rows, classes), BF16), like((half_rows, classes // QUAD), BF16)
+    tail, _, current_stack, sums_b, sums_a, *pieces = call(
         mix_kernel,
         "mix",
         (scalars, far, summed, squares, *exchange([squares] * 3), packed_seed),
-        (tail, packed, like((QUAD * rows, classes // QUAD), BF16), packed, piece, piece, piece),
+        (
+            tail, packed, like((QUAD * rows, classes // QUAD), BF16),
+            half, half, half_piece, half_piece, half_piece,
+        ),
     )
     received = exchange(pieces)
     near_total = call(
@@ -388,26 +410,37 @@
         (near, after(current_stack, received[0])),
         like((QUAD * rows, classes // QUAD), F32),
     )
-    tail = after(tail, near_total)
     tail_up = from_up(tail)
-    tail_cross = [from_group(tail, step) for step in steps]
-    sums = call(pack_kernel, "pack", (scalars, sums, *received), packed)
-    sums = after(sums, (head_up, head_cross, tail_up, tail_cross))
-    sent = from_down(sums)
-    head_up = after(head_up, sums)
+    tail_cross = [from_group(after(tail, near_total), step) for step in steps]
+    sent_b = from_down(sums_b)
+    sums_a = call(pack_kernel, "pack", (scalars, sums_a, *received), half)
+    sums_a = after(sums_a, (head_up, head_cross, tail_up, tail_cross))
+    sent_a = from_down(sums_a)
+    head_up = after(head_up, sums_a)
     triples = [head_up, tail_up, seed_up]
     for top, rest, own in zip(head_cross, tail_cross, seed_cross):
         triples += [top, rest, own]
-    _, kept, *pieces = call(
+    _, kept_b, kept_a, *pieces = call(
         gather_mixed_kernel,
         "gather_mixed",
         (clusters, far, *crosses, near_total, *triples),
-        (like((QUAD * rows, classes // QUAD), F32), packed, piece, piece, piece),
+        (
+            like((QUAD * rows, classes // QUAD), F32),
+            like(half.shape, F32), half, half_piece, half_piece, half_piece,
+        ),
         [pltpu.VMEM(labels.shape, BF16), stack],
         aliases={6: 0},
     )
-    kept = call(pack_kernel, "pack", (scalars, kept, *exchange(pieces)), packed)
-    return call(finish_kernel, "finish", (scalars, kept, sent, seed), packed)
+    received = exchange(pieces)
+    sums_b, *pieces = call(add_kernel, "add", (scalars, after(kept_b, received[0]), sent_b), (half, half_piece, half_piece, half_piece))
+    kept_a = call(pack_kernel, "pack", (scalars, kept_a, *received), half)
+    return call(
+        finish_kernel,
+        "finish",
+        (scalars, kept_a, sent_a, sums_b, *exchange(pieces), seed),
+        packed,
+        [pltpu.VMEM(half.shape, BF16)],
+    )
 
 
 def solution(mesh):

time: 113 us -> 108 us (0.956)
  waiting for transfers between devices: 44.1 us -> 36.3 us
  starting transfers between devices: 27.2 us -> 29.7 us
    ppermute x29 -> x33, waiting for transfers between devices: 42.6 us -> 33.8 us  [along_dev(): lax.ppermute(block, 'dev', [(source(i) % size, i) for i in range(size)])]
    ppermute x29 -> x33, starting transfers between devices: 22.1 us -> 24.6 us  [along_dev(): lax.ppermute(block, 'dev', [(source(i) % size, i) for i in range(size)])]
    pallas_call x15 -> x16, Pallas kernels: 33.1 us -> 33.9 us  [call(): pl.pallas_call(kernel, in_specs=specs, out_shape=out_shape, scratch_shape...]
  transfers between devices with their start and end apart: 33 -> 37, of which waited for: 18 -> 21; matrix products, arithmetic and copies ran while one was open for 3% -> 3% of each run, Pallas kernels for 27% -> 28%
where the time goes in v5:
time: 108 us
  waiting for transfers between devices  36.3 us (34%)
  Pallas kernels  33.9 us (31%)
  starting transfers between devices  29.7 us (28%)
  local copies, waits for them, and re-layouts  6.37 us (6%)
    pallas_call x16, Pallas kernels, call(): pl.pallas_call(kernel, in_specs=specs, out_shape=out_shape, scratch_shape...  33.9 us
    ppermute x33, waiting for transfers between devices, along_dev(): lax.ppermute(block, 'dev', [(source(i) % size, i) for i in range(size)])  33.8 us
    ppermute x33, starting transfers between devices, along_dev(): lax.ppermute(block, 'dev', [(source(i) % size, i) for i in range(size)])  24.6 us
    ppermute x4, starting transfers between devices, from_group(): lax.ppermute(block, 'grp', [((i + step) % size, i) for i in range(size)])  5.15 us
    unnamed x12, local copies, waits for them, and re-layouts  4.32 us
    ppermute x4, waiting for transfers between devices, from_group(): lax.ppermute(block, 'grp', [((i + step) % size, i) for i in range(size)])  2.56 us
  transfers between devices with their start and end apart: 37, of which 21 were waited for; matrix products, arithmetic and copies ran while one was open for 3% of the time, Pallas kernels for 28%

profile of v5, /device:TPU:0, one launch (start us, length us, event | category | flops | bytes accessed | tf_op | source)
XLA Modules:
  0.0 108.2 jit_solution(6776777184150264755)
XLA Ops:
  0.0 5.0 %collective-permute-start.4 = (bf16[384,768]{1,0:T(8,128)(2,1)}, bf16[384,768]{1,0:T(8,128)(2,1)S(1)}, u32[]{:S(2)}, u32[]{:S(2)}) collective-permute-start(bf16[384,768]{1,0:T(8,128)(2,1)} %own.3), channel_id=1, source_target_pairs={{4,0},{5,1},{6,2},{7,3},{8,4},{9,5},{10,6},{11,7},{12,8},{13,9},{1... | collective-permute-start | bytes 1769480 | tf_op jit(solution)/shard_map/ppermute | solution.py:23
  6.1 1.6 %collective-permute-start = (bf16[192,768]{1,0:T(8,128)(2,1)S(1)}, bf16[192,768]{1,0:T(8,128)(2,1)}, u32[]{:S(2)}, u32[]{:S(2)}) collective-permute-start(bf16[192,768]{1,0:T(8,128)(2,1)S(1)} %slice.9), channel_id=1, source_target_pairs={{2,0},{3,1},{0,2},{1,3},{6,4},{7,5},{4,6},{5,7},{10,8},{11,9},{8,1... | collective-permute-start | bytes 884744 | tf_op jit(solution)/shard_map/ppermute | solution.py:23
  11.2 1.7 %collective-permute-start.1 = (bf16[384,768]{1,0:T(8,128)(2,1)}, bf16[384,768]{1,0:T(8,128)(2,1)S(1)}, u32[]{:S(2)}, u32[]{:S(2)}) collective-permute-start(bf16[384,768]{1,0:T(8,128)(2,1)} %own.3), channel_id=1, source_target_pairs={{1,0},{0,1},{3,2},{2,3},{5,4},{4,5},{7,6},{6,7},{9,8},{8,9},{11,10... | collective-permute-start | bytes 1769480 | tf_op jit(solution)/shard_map/ppermute | solution.py:23
  12.8 3.3 %collective-permute-done.side_a = bf16[192,768]{1,0:T(8,128)(2,1)} collective-permute-done((bf16[192,768]{1,0:T(8,128)(2,1)S(1)}, bf16[192,768]{1,0:T(8,128)(2,1)}, u32[]{:S(2)}, u32[]{:S(2)}) %collective-permute-start) | collective-permute-done | bytes 294944 | tf_op jit(solution)/shard_map/ppermute | solution.py:23
  16.2 1.5 %collective-permute-start.8 = (bf16[384,768]{1,0:T(8,128)(2,1)}, bf16[384,768]{1,0:T(8,128)(2,1)}, u32[]{:S(2)}, u32[]{:S(2)}) collective-permute-start(bf16[384,768]{1,0:T(8,128)(2,1)} %own.3), channel_id=1, source_target_pairs={{16,0},{0,16},{17,1},{1,17},{18,2},{2,18},{19,3},{3,19},{20,4},{4,... | collective-permute-start | bytes 1769480 | tf_op jit(solution)/shard_map/ppermute | solution.py:44
  20.3 1.8 %collective-permute-done.6.p3 = bf16[384,224]{1,0:T(8,128)(2,1)S(1)} collective-permute-done((bf16[384,224]{1,0:T(8,128)(2,1)S(1)}, bf16[384,224]{1,0:T(8,128)(2,1)S(1)}, u32[]{:S(2)}, u32[]{:S(2)}) %collective-permute-start.6) | collective-permute-done | bytes 172064 | tf_op jit(solution)/shard_map/ppermute | solution.py:23
  23.7 1.4 %collective-permute-start.3 = (bf16[384,224]{1,0:T(8,128)(2,1)S(1)}, bf16[384,224]{1,0:T(8,128)(2,1)S(1)}, u32[]{:S(2)}, u32[]{:S(2)}) collective-permute-start(bf16[384,224]{1,0:T(8,128)(2,1)S(1)} %get-tuple-element.47), channel_id=1, source_target_pairs={{1,0},{0,1},{3,2},{2,3},{5,4},{4,5},{7,6},{6,7},{9,8},{8,9},{11,10... | collective-permute-start | bytes 516104 | tf_op jit(solution)/shard_map/ppermute | solution.py:23
  25.1 1.3 %collective-permute-done.3.p1 = bf16[384,224]{1,0:T(8,128)(2,1)S(1)} collective-permute-done((bf16[384,224]{1,0:T(8,128)(2,1)S(1)}, bf16[384,224]{1,0:T(8,128)(2,1)S(1)}, u32[]{:S(2)}, u32[]{:S(2)}) %collective-permute-start.3) | collective-permute-done | bytes 172064 | tf_op jit(solution)/shard_map/ppermute | solution.py:23
  31.0 1.8 %cross.1.t0 = bf16[384,384]{1,0:T(8,128)(2,1)S(1)} custom-call(bf16[384,768]{1,0:T(8,128)(2,1)S(1)} %copy-done, bf16[384,768]{1,0:T(8,128)(2,1)} %collective-permute-done.8.rest_0_), custom_call_target="tpu_custom_call" | custom-call | tf_op jit(solution)/shard_map/cross/pallas_call | solution.py:59
  32.8 1.6 %collective-permute-start.14 = (bf16[384,896]{1,0:T(8,128)(2,1)S(1)}, bf16[384,896]{1,0:T(8,128)(2,1)S(1)}, u32[]{:S(2)}, u32[]{:S(2)}) collective-permute-start(bf16[384,896]{1,0:T(8,128)(2,1)S(1)} %pack.3.seed.own), channel_id=1, source_target_pairs={{16,0},{0,16},{17,1},{1,17},{18,2},{2,18},{19,3},{3,19},{20,4},{4,... | collective-permute-start | bytes 2064392 | tf_op jit(solution)/shard_map/ppermute | solution.py:44
  34.4 1.9 %stage_own.1 = (bf16[1536,768]{1,0:T(8,128)(2,1)S(1)}, bf16[1536,224]{1,0:T(8,128)(2,1)S(1)}) custom-call(s32[4]{0:T(128)S(1)} %pad_add_fusion.1.clusters, bf16[384,768]{1,0:T(8,128)(2,1)S(1)} %copy-done, bf16[192,768]{1,0:T(8,128)(2,1)} %collective-permute-done.side_a, bf16[384,768]{1,0:T(8,128)(2,1)S(1)} %collective-permute-done.1.core, ...), custom_call_target="tpu_custom_call" | custom-call | tf_op jit(solution)/shard_map/stage_own/pallas_call | solution.py:59
  37.2 1.7 %collective-permute-done.7.side_b = bf16[384,768]{1,0:T(8,128)(2,1)S(1)} collective-permute-done((bf16[384,768]{1,0:T(8,128)(2,1)}, bf16[384,768]{1,0:T(8,128)(2,1)S(1)}, u32[]{:S(2)}, u32[]{:S(2)}) %collective-permute-start.7) | collective-permute-done | bytes 589856 | tf_op jit(solution)/shard_map/ppermute | solution.py:23
  39.4 1.9 %collective-permute-done.11.across_a = bf16[192,768]{1,0:T(8,128)(2,1)S(1)} collective-permute-done((bf16[192,768]{1,0:T(8,128)(2,1)S(1)}, bf16[192,768]{1,0:T(8,128)(2,1)S(1)}, u32[]{:S(2)}, u32[]{:S(2)}) %collective-permute-start.11) | collective-permute-done | bytes 294944 | tf_op jit(solution)/shard_map/ppermute | solution.py:23
  42.6 4.7 %far.1 = (bf16[1536,768]{1,0:T(8,128)(2,1)S(1)}, bf16[1536,768]{1,0:T(8,128)(2,1)S(1)}, bf16[1536,1536]{1,0:T(8,128)(2,1)S(1)}, bf16[384,896]{1,0:T(8,128)(2,1)S(1)}) custom-call(s32[4]{0:T(128)S(1)} %pad_add_fusion.1.clusters, bf16[1536,768]{1,0:T(8,128)(2,1)S(1)} %get-tuple-element.51.units_in, ...), custom_call_target="tpu_custom_call", output_to_operand_aliasing={{0}: (1, {}), {1}: (2, {})} | custom-call | tf_op jit(solution)/shard_map/far/pallas_call | solution.py:59
  47.5 3.9 %collective-permute-done.13.up.rest_2_ = bf16[384,896]{1,0:T(8,128)(2,1)S(1)} collective-permute-done((bf16[384,896]{1,0:T(8,128)(2,1)S(1)}, bf16[384,896]{1,0:T(8,128)(2,1)S(1)}, u32[]{:S(2)}, u32[]{:S(2)}) %collective-permute-start.13) | collective-permute-done | bytes 688160 | tf_op jit(solution)/shard_map/ppermute | solution.py:23
  51.9 3.9 %near.1 = bf16[1536,1536]{1,0:T(8,128)(2,1)S(1)} custom-call(bf16[1536,768]{1,0:T(8,128)(2,1)S(1)} %get-tuple-element.60.units), custom_call_target="tpu_custom_call" | custom-call | tf_op jit(solution)/shard_map/near/pallas_call | solution.py:59
  55.8 4.0 %collective-permute-done.15.t1 = bf16[384,384]{1,0:T(8,128)(2,1)S(1)} collective-permute-done((bf16[384,384]{1,0:T(8,128)(2,1)S(1)}, bf16[384,384]{1,0:T(8,128)(2,1)S(1)}, u32[]{:S(2)}, u32[]{:S(2)}) %collective-permute-start.15) | collective-permute-done | bytes 294944 | tf_op jit(solution)/shard_map/ppermute | solution.py:23
  59.9 1.6 %collective-permute-done.17.t3 = bf16[384,384]{1,0:T(8,128)(2,1)S(1)} collective-permute-done((bf16[384,384]{1,0:T(8,128)(2,1)S(1)}, bf16[384,384]{1,0:T(8,128)(2,1)S(1)}, u32[]{:S(2)}, u32[]{:S(2)}) %collective-permute-start.17) | collective-permute-done | bytes 294944 | tf_op jit(solution)/shard_map/ppermute | solution.py:23
  61.4 3.7 %gather.1.kept = f32[384,896]{1,0:T(8,128)S(1)} custom-call(s32[4]{0:T(128)S(1)} %pad_add_fusion.1.clusters, bf16[1536,1536]{1,0:T(8,128)(2,1)S(1)} %near.1, bf16[1536,1536]{1,0:T(8,128)(2,1)S(1)} %get-tuple-element.58.far, bf16[384,384]{1,0:T(8,128)(2,1)S(1)} %cross.1.t0, bf16[384,384]{1,0:T(8,128)(2,1)S(1)} %collective-permute-done.15.t1, ...), custom_call_target="tpu_custom_call" | custom-call | tf_op jit(solution)/shard_map/gather/pallas_call | solution.py:59
  65.1 1.9 %collective-permute-done.18.sent = bf16[384,896]{1,0:T(8,128)(2,1)S(1)} collective-permute-done((bf16[384,896]{1,0:T(8,128)(2,1)S(1)}, bf16[384,896]{1,0:T(8,128)(2,1)S(1)}, u32[]{:S(2)}, u32[]{:S(2)}) %collective-permute-start.18) | collective-permute-done | bytes 688160 | tf_op jit(solution)/shard_map/ppermute | solution.py:23
  68.1 1.3 %collective-permute-start.23 = (bf16[320,896]{1,0:T(8,128)(2,1)S(1)}, bf16[320,896]{1,0:T(8,128)(2,1)S(1)}, u32[]{:S(2)}, u32[]{:S(2)}) collective-permute-start(bf16[320,896]{1,0:T(8,128)(2,1)S(1)} %get-tuple-element.68), channel_id=1, source_target_pairs={{4,0},{5,1},{6,2},{7,3},{8,4},{9,5},{10,6},{11,7},{12,8},{13,9},{1... | collective-permute-start | bytes 1720328 | tf_op jit(solution)/shard_map/ppermute | solution.py:23
  69.4 1.6 %collective-permute-start.26 = (bf16[320,896]{1,0:T(8,128)(2,1)S(1)}, bf16[320,896]{1,0:T(8,128)(2,1)S(1)}, u32[]{:S(2)}, u32[]{:S(2)}) collective-permute-start(bf16[320,896]{1,0:T(8,128)(2,1)S(1)} %get-tuple-element.68), channel_id=1, source_target_pairs={{16,0},{0,16},{17,1},{1,17},{18,2},{2,18},{19,3},{3,19},{20,4},{4,... | collective-permute-start | bytes 1720328 | tf_op jit(solution)/shard_map/ppermute | solution.py:44
  72.8 2.2 %collective-permute-done.20.s2 = f32[16,384]{1,0:T(8,128)S(1)} collective-permute-done((f32[16,384]{1,0:T(8,128)S(1)}, f32[16,384]{1,0:T(8,128)S(1)}, u32[]{:S(2)}, u32[]{:S(2)}) %collective-permute-start.20) | collective-permute-done | bytes 24608 | tf_op jit(solution)/shard_map/ppermute | solution.py:23
  75.1 3.5 %mix.1 = (bf16[96,896]{1,0:T(8,128)(2,1)S(1)}, bf16[384,896]{1,0:T(8,128)(2,1)}, bf16[1536,224]{1,0:T(8,128)(2,1)S(1)}, bf16[192,896]{1,0:T(8,128)(2,1)S(1)}, bf...) custom-call(s32[2]{0:T(128)S(1)} %pad_add_fusion.scalars, ...), custom_call_target="tpu_custom_call" | custom-call | tf_op jit(solution)/shard_map/mix/pallas_call | solution.py:59
  78.8 1.4 %collective-permute-start.24 = (bf16[192,224]{1,0:T(8,128)(2,1)S(1)}, bf16[192,224]{1,0:T(8,128)(2,1)S(1)}, u32[]{:S(2)}, u32[]{:S(2)}) collective-permute-start(bf16[192,224]{1,0:T(8,128)(2,1)S(1)} %get-tuple-element.70), channel_id=1, source_target_pairs={{2,0},{3,1},{0,2},{1,3},{6,4},{7,5},{4,6},{5,7},{10,8},{11,9},{8,1... | collective-permute-start | bytes 258056 | tf_op jit(solution)/shard_map/ppermute | solution.py:23
  80.9 1.4 %near_products.1.total_in = f32[1536,224]{1,0:T(8,128)S(1)} custom-call(bf16[1536,1536]{1,0:T(8,128)(2,1)S(1)} %near.1, bf16[1536,224]{1,0:T(8,128)(2,1)S(1)} %get-tuple-element.67.stack), custom_call_target="tpu_custom_call" | custom-call | tf_op jit(solution)/shard_map/near_products/pallas_call | solution.py:59
  82.3 2.1 %collective-permute-done.24.p2 = bf16[192,224]{1,0:T(8,128)(2,1)S(1)} collective-permute-done((bf16[192,224]{1,0:T(8,128)(2,1)S(1)}, bf16[192,224]{1,0:T(8,128)(2,1)S(1)}, u32[]{:S(2)}, u32[]{:S(2)}) %collective-permute-start.24) | collective-permute-done | bytes 86048 | tf_op jit(solution)/shard_map/ppermute | solution.py:23
  87.3 2.6 %collective-permute-done.28.rest_4_ = bf16[96,896]{1,0:T(8,128)(2,1)S(1)} collective-permute-done((bf16[96,896]{1,0:T(8,128)(2,1)S(1)}, bf16[96,896]{1,0:T(8,128)(2,1)S(1)}, u32[]{:S(2)}, u32[]{:S(2)}) %collective-permute-start.28) | collective-permute-done | bytes 172064 | tf_op jit(solution)/shard_map/ppermute | solution.py:44
  90.9 3.6 %gather_mixed.1 = (f32[1536,224]{1,0:T(8,128)S(1)}, f32[192,896]{1,0:T(8,128)S(1)}, bf16[192,896]{1,0:T(8,128)(2,1)S(1)}, bf16[192,224]{1,0:T(8,128)(2,1)S(1)}, ...) custom-call(s32[4]{0:T(128)S(1)} %pad_add_fusion.1.clusters, ...), custom_call_target="tpu_custom_call", output_to_operand_aliasing={{0}: (6, {})} | custom-call | tf_op jit(solution)/shard_map/gather_mixed/pallas_call | solution.py:59
  96.4 1.5 %collective-permute-done.33.sent = bf16[192,896]{1,0:T(8,128)(2,1)S(1)} collective-permute-done((bf16[192,896]{1,0:T(8,128)(2,1)S(1)}, bf16[192,896]{1,0:T(8,128)(2,1)S(1)}, u32[]{:S(2)}, u32[]{:S(2)}) %collective-permute-start.33) | collective-permute-done | bytes 344096 | tf_op jit(solution)/shard_map/ppermute | solution.py:23
  102.3 2.4 %collective-permute-done.35.p2 = bf16[192,224]{1,0:T(8,128)(2,1)S(1)} collective-permute-done((bf16[192,224]{1,0:T(8,128)(2,1)S(1)}, bf16[192,224]{1,0:T(8,128)(2,1)S(1)}, u32[]{:S(2)}, u32[]{:S(2)}) %collective-permute-start.35) | collective-permute-done | bytes 86048 | tf_op jit(solution)/shard_map/ppermute | solution.py:23
  105.9 2.2 %finish.1 = bf16[384,896]{1,0:T(8,128)(2,1)} custom-call(s32[2]{0:T(128)S(1)} %pad_add_fusion.scalars, bf16[192,896]{1,0:T(8,128)(2,1)S(1)} %pack.5.kept_a, bf16[192,896]{1,0:T(8,128)(2,1)S(1)} %collective-permute-done.32.sent_a, bf16[192,896]{1,0:T(8,128)(2,1)S(1)} %get-tuple-element.83.sums_b, bf16[192,224]{1,0:T(8,128)(2,1)S(1)} %collective-permute-done.34.p1, ...), custom_call_target="tpu_custom_call" | custom-call | tf_op jit(solution)/shard_map/finish/pallas_call | solution.py:59
  (76 shorter events, 31.4 us)
Async XLA Ops:
  0.0 18.7 %collective-permute-start.4 = (bf16[384,768]{1,0:T(8,128)(2,1)}, bf16[384,768]{1,0:T(8,128)(2,1)S(1)}, u32[]{:S(2)}, u32[]{:S(2)}) collective-permute-start(bf16[384,768]{1,0:T(8,128)(2,1)} %own.3), channel_id=1, source_target_pairs={{4,0},{5,1},{6,2},{7,3},{8,4},{9,5},{10,6},{11,7},{12,8},{13,9},{1... | collective-permute-start | bytes 1769480 | tf_op jit(solution)/shard_map/ppermute | solution.py:23
  6.1 10.1 %collective-permute-start = (bf16[192,768]{1,0:T(8,128)(2,1)S(1)}, bf16[192,768]{1,0:T(8,128)(2,1)}, u32[]{:S(2)}, u32[]{:S(2)}) collective-permute-start(bf16[192,768]{1,0:T(8,128)(2,1)S(1)} %slice.9), channel_id=1, source_target_pairs={{2,0},{3,1},{0,2},{1,3},{6,4},{7,5},{4,6},{5,7},{10,8},{11,9},{8,1... | collective-permute-start | bytes 884744 | tf_op jit(solution)/shard_map/ppermute | solution.py:23
  10.6 9.7 %collective-permute-start.5 = (bf16[384,224]{1,0:T(8,128)(2,1)S(1)}, bf16[384,224]{1,0:T(8,128)(2,1)S(1)}, u32[]{:S(2)}, u32[]{:S(2)}) collective-permute-start(bf16[384,224]{1,0:T(8,128)(2,1)S(1)} %get-tuple-element.49), channel_id=1, source_target_pairs={{2,0},{3,1},{0,2},{1,3},{6,4},{7,5},{4,6},{5,7},{10,8},{11,9},{8,1... | collective-permute-start | bytes 516104 | tf_op jit(solution)/shard_map/ppermute | solution.py:23
  11.1 11.0 %collective-permute-start.6 = (bf16[384,224]{1,0:T(8,128)(2,1)S(1)}, bf16[384,224]{1,0:T(8,128)(2,1)S(1)}, u32[]{:S(2)}, u32[]{:S(2)}) collective-permute-start(bf16[384,224]{1,0:T(8,128)(2,1)S(1)} %get-tuple-element.50), channel_id=1, source_target_pairs={{3,0},{2,1},{1,2},{0,3},{7,4},{6,5},{5,6},{4,7},{11,8},{10,9},{9,1... | collective-permute-start | bytes 516104 | tf_op jit(solution)/shard_map/ppermute | solution.py:23
  11.2 23.3 %collective-permute-start.1 = (bf16[384,768]{1,0:T(8,128)(2,1)}, bf16[384,768]{1,0:T(8,128)(2,1)S(1)}, u32[]{:S(2)}, u32[]{:S(2)}) collective-permute-start(bf16[384,768]{1,0:T(8,128)(2,1)} %own.3), channel_id=1, source_target_pairs={{1,0},{0,1},{3,2},{2,3},{5,4},{4,5},{7,6},{6,7},{9,8},{8,9},{11,10... | collective-permute-start | bytes 1769480 | tf_op jit(solution)/shard_map/ppermute | solution.py:23
  16.2 14.1 %collective-permute-start.8 = (bf16[384,768]{1,0:T(8,128)(2,1)}, bf16[384,768]{1,0:T(8,128)(2,1)}, u32[]{:S(2)}, u32[]{:S(2)}) collective-permute-start(bf16[384,768]{1,0:T(8,128)(2,1)} %own.3), channel_id=1, source_target_pairs={{16,0},{0,16},{17,1},{1,17},{18,2},{2,18},{19,3},{3,19},{20,4},{4,... | collective-permute-start | bytes 1769480 | tf_op jit(solution)/shard_map/ppermute | solution.py:44
  22.7 16.2 %collective-permute-start.7 = (bf16[384,768]{1,0:T(8,128)(2,1)}, bf16[384,768]{1,0:T(8,128)(2,1)S(1)}, u32[]{:S(2)}, u32[]{:S(2)}) collective-permute-start(bf16[384,768]{1,0:T(8,128)(2,1)} %pad_maximum_fusion), channel_id=1, source_target_pairs={{2,0},{3,1},{0,2},{1,3},{6,4},{7,5},{4,6},{5,7},{10,8},{11,9},{8,1... | collective-permute-start | bytes 1769480 | tf_op jit(solution)/shard_map/ppermute | solution.py:23
  23.7 2.7 %collective-permute-start.3 = (bf16[384,224]{1,0:T(8,128)(2,1)S(1)}, bf16[384,224]{1,0:T(8,128)(2,1)S(1)}, u32[]{:S(2)}, u32[]{:S(2)}) collective-permute-start(bf16[384,224]{1,0:T(8,128)(2,1)S(1)} %get-tuple-element.47), channel_id=1, source_target_pairs={{1,0},{0,1},{3,2},{2,3},{5,4},{4,5},{7,6},{6,7},{9,8},{8,9},{11,10... | collective-permute-start | bytes 516104 | tf_op jit(solution)/shard_map/ppermute | solution.py:23
  25.1 7.7 %collective-permute-start.2 = (bf16[192,768]{1,0:T(8,128)(2,1)}, bf16[192,768]{1,0:T(8,128)(2,1)}, u32[]{:S(2)}, u32[]{:S(2)}) collective-permute-start(bf16[192,768]{1,0:T(8,128)(2,1)} %collective-permute-done.side_a), channel_id=1, source_target_pairs={{1,0},{0,1},{3,2},{2,3},{5,4},{4,5},{7,6},{6,7},{9,8},{8,9},{11,10... | collective-permute-start | bytes 884744 | tf_op jit(solution)/shard_map/ppermute | solution.py:23
  27.1 10.1 %collective-permute-start.9 = (bf16[192,768]{1,0:T(8,128)(2,1)}, bf16[192,768]{1,0:T(8,128)(2,1)S(1)}, u32[]{:S(2)}, u32[]{:S(2)}) collective-permute-start(bf16[192,768]{1,0:T(8,128)(2,1)} %collective-permute-done.side_a), channel_id=1, source_target_pairs={{4,0},{5,1},{6,2},{7,3},{8,4},{9,5},{10,6},{11,7},{12,8},{13,9},{1... | collective-permute-start | bytes 884744 | tf_op jit(solution)/shard_map/ppermute | solution.py:23
  30.3 21.1 %collective-permute-start.13 = (bf16[384,896]{1,0:T(8,128)(2,1)S(1)}, bf16[384,896]{1,0:T(8,128)(2,1)S(1)}, u32[]{:S(2)}, u32[]{:S(2)}) collective-permute-start(bf16[384,896]{1,0:T(8,128)(2,1)S(1)} %pack.3.seed.own), channel_id=1, source_target_pairs={{4,0},{5,1},{6,2},{7,3},{8,4},{9,5},{10,6},{11,7},{12,8},{13,9},{1... | collective-permute-start | bytes 2064392 | tf_op jit(solution)/shard_map/ppermute | solution.py:23
  32.8 18.6 %collective-permute-start.14 = (bf16[384,896]{1,0:T(8,128)(2,1)S(1)}, bf16[384,896]{1,0:T(8,128)(2,1)S(1)}, u32[]{:S(2)}, u32[]{:S(2)}) collective-permute-start(bf16[384,896]{1,0:T(8,128)(2,1)S(1)} %pack.3.seed.own), channel_id=1, source_target_pairs={{16,0},{0,16},{17,1},{1,17},{18,2},{2,18},{19,3},{3,19},{20,4},{4,... | collective-permute-start | bytes 2064392 | tf_op jit(solution)/shard_map/ppermute | solution.py:44
  34.4 6.9 %collective-permute-start.10 = (bf16[384,768]{1,0:T(8,128)(2,1)S(1)}, bf16[384,768]{1,0:T(8,128)(2,1)S(1)}, u32[]{:S(2)}, u32[]{:S(2)}) collective-permute-start(bf16[384,768]{1,0:T(8,128)(2,1)S(1)} %collective-permute-done.4.own), channel_id=1, source_target_pairs={{1,0},{0,1},{3,2},{2,3},{5,4},{4,5},{7,6},{6,7},{9,8},{8,9},{11,10... | collective-permute-start | bytes 1769480 | tf_op jit(solution)/shard_map/ppermute | solution.py:23
  38.9 3.7 %collective-permute-start.12 = (bf16[384,768]{1,0:T(8,128)(2,1)S(1)}, bf16[384,768]{1,0:T(8,128)(2,1)S(1)}, u32[]{:S(2)}, u32[]{:S(2)}) collective-permute-start(bf16[384,768]{1,0:T(8,128)(2,1)S(1)} %collective-permute-done.7.side_b), channel_id=1, source_target_pairs={{1,0},{0,1},{3,2},{2,3},{5,4},{4,5},{7,6},{6,7},{9,8},{8,9},{11,10... | collective-permute-start | bytes 1769480 | tf_op jit(solution)/shard_map/ppermute | solution.py:23
  47.2 19.7 %collective-permute-start.18 = (bf16[384,896]{1,0:T(8,128)(2,1)S(1)}, bf16[384,896]{1,0:T(8,128)(2,1)S(1)}, u32[]{:S(2)}, u32[]{:S(2)}) collective-permute-start(bf16[384,896]{1,0:T(8,128)(2,1)S(1)} %get-tuple-element.62), channel_id=1, source_target_pairs={{12,0},{13,1},{14,2},{15,3},{0,4},{1,5},{2,6},{3,7},{4,8},{5,9},{6... | collective-permute-start | bytes 2064392 | tf_op jit(solution)/shard_map/ppermute | solution.py:23
  51.4 8.5 %collective-permute-start.15 = (bf16[384,384]{1,0:T(8,128)(2,1)S(1)}, bf16[384,384]{1,0:T(8,128)(2,1)S(1)}, u32[]{:S(2)}, u32[]{:S(2)}) collective-permute-start(bf16[384,384]{1,0:T(8,128)(2,1)S(1)} %cross.1.t0), channel_id=1, source_target_pairs={{2,0},{3,1},{0,2},{1,3},{6,4},{7,5},{4,6},{5,7},{10,8},{11,9},{8,1... | collective-permute-start | bytes 884744 | tf_op jit(solution)/shard_map/ppermute | solution.py:23
  51.9 7.9 %collective-permute-start.16 = (bf16[384,384]{1,0:T(8,128)(2,1)S(1)}, bf16[384,384]{1,0:T(8,128)(2,1)S(1)}, u32[]{:S(2)}, u32[]{:S(2)}) collective-permute-start(bf16[384,384]{1,0:T(8,128)(2,1)S(1)} %cross.1.t0), channel_id=1, source_target_pairs={{1,0},{0,1},{3,2},{2,3},{5,4},{4,5},{7,6},{6,7},{9,8},{8,9},{11,10... | collective-permute-start | bytes 884744 | tf_op jit(solution)/shard_map/ppermute | solution.py:23
  68.1 21.7 %collective-permute-start.23 = (bf16[320,896]{1,0:T(8,128)(2,1)S(1)}, bf16[320,896]{1,0:T(8,128)(2,1)S(1)}, u32[]{:S(2)}, u32[]{:S(2)}) collective-permute-start(bf16[320,896]{1,0:T(8,128)(2,1)S(1)} %get-tuple-element.68), channel_id=1, source_target_pairs={{4,0},{5,1},{6,2},{7,3},{8,4},{9,5},{10,6},{11,7},{12,8},{13,9},{1... | collective-permute-start | bytes 1720328 | tf_op jit(solution)/shard_map/ppermute | solution.py:23
  69.4 20.4 %collective-permute-start.26 = (bf16[320,896]{1,0:T(8,128)(2,1)S(1)}, bf16[320,896]{1,0:T(8,128)(2,1)S(1)}, u32[]{:S(2)}, u32[]{:S(2)}) collective-permute-start(bf16[320,896]{1,0:T(8,128)(2,1)S(1)} %get-tuple-element.68), channel_id=1, source_target_pairs={{16,0},{0,16},{17,1},{1,17},{18,2},{2,18},{19,3},{3,19},{20,4},{4,... | collective-permute-start | bytes 1720328 | tf_op jit(solution)/shard_map/ppermute | solution.py:44
  71.0 4.1 %collective-permute-start.20 = (f32[16,384]{1,0:T(8,128)S(1)}, f32[16,384]{1,0:T(8,128)S(1)}, u32[]{:S(2)}, u32[]{:S(2)}) collective-permute-start(f32[16,384]{1,0:T(8,128)S(1)} %get-tuple-element.64.s0), channel_id=1, source_target_pairs={{2,0},{3,1},{0,2},{1,3},{6,4},{7,5},{4,6},{5,7},{10,8},{11,9},{8,1... | collective-permute-start | bytes 73736 | tf_op jit(solution)/shard_map/ppermute | solution.py:23
  71.6 3.5 %collective-permute-start.21 = (f32[16,384]{1,0:T(8,128)S(1)}, f32[16,384]{1,0:T(8,128)S(1)}, u32[]{:S(2)}, u32[]{:S(2)}) collective-permute-start(f32[16,384]{1,0:T(8,128)S(1)} %get-tuple-element.64.s0), channel_id=1, source_target_pairs={{3,0},{2,1},{1,2},{0,3},{7,4},{6,5},{5,6},{4,7},{11,8},{10,9},{9,1... | collective-permute-start | bytes 73736 | tf_op jit(solution)/shard_map/ppermute | solution.py:23
  78.8 5.6 %collective-permute-start.24 = (bf16[192,224]{1,0:T(8,128)(2,1)S(1)}, bf16[192,224]{1,0:T(8,128)(2,1)S(1)}, u32[]{:S(2)}, u32[]{:S(2)}) collective-permute-start(bf16[192,224]{1,0:T(8,128)(2,1)S(1)} %get-tuple-element.70), channel_id=1, source_target_pairs={{2,0},{3,1},{0,2},{1,3},{6,4},{7,5},{4,6},{5,7},{10,8},{11,9},{8,1... | collective-permute-start | bytes 258056 | tf_op jit(solution)/shard_map/ppermute | solution.py:23
  80.2 5.1 %collective-permute-start.25 = (bf16[192,224]{1,0:T(8,128)(2,1)S(1)}, bf16[192,224]{1,0:T(8,128)(2,1)S(1)}, u32[]{:S(2)}, u32[]{:S(2)}) collective-permute-start(bf16[192,224]{1,0:T(8,128)(2,1)S(1)} %get-tuple-element.71), channel_id=1, source_target_pairs={{3,0},{2,1},{1,2},{0,3},{7,4},{6,5},{5,6},{4,7},{11,8},{10,9},{9,1... | collective-permute-start | bytes 258056 | tf_op jit(solution)/shard_map/ppermute | solution.py:23
  80.4 6.8 %collective-permute-start.27 = (bf16[96,896]{1,0:T(8,128)(2,1)S(1)}, bf16[96,896]{1,0:T(8,128)(2,1)S(1)}, u32[]{:S(2)}, u32[]{:S(2)}) collective-permute-start(bf16[96,896]{1,0:T(8,128)(2,1)S(1)} %get-tuple-element.73), channel_id=1, source_target_pairs={{4,0},{5,1},{6,2},{7,3},{8,4},{9,5},{10,6},{11,7},{12,8},{13,9},{1... | collective-permute-start | bytes 516104 | tf_op jit(solution)/shard_map/ppermute | solution.py:23
  84.4 5.4 %collective-permute-start.28 = (bf16[96,896]{1,0:T(8,128)(2,1)S(1)}, bf16[96,896]{1,0:T(8,128)(2,1)S(1)}, u32[]{:S(2)}, u32[]{:S(2)}) collective-permute-start(bf16[96,896]{1,0:T(8,128)(2,1)S(1)} %get-tuple-element.73), channel_id=1, source_target_pairs={{16,0},{0,16},{17,1},{1,17},{18,2},{2,18},{19,3},{3,19},{20,4},{4,... | collective-permute-start | bytes 516104 | tf_op jit(solution)/shard_map/ppermute | solution.py:44
  85.3 12.7 %collective-permute-start.33 = (bf16[192,896]{1,0:T(8,128)(2,1)S(1)}, bf16[192,896]{1,0:T(8,128)(2,1)S(1)}, u32[]{:S(2)}, u32[]{:S(2)}) collective-permute-start(bf16[192,896]{1,0:T(8,128)(2,1)S(1)} %get-tuple-element.82), channel_id=1, source_target_pairs={{12,0},{13,1},{14,2},{15,3},{0,4},{1,5},{2,6},{3,7},{4,8},{5,9},{6... | collective-permute-start | bytes 1032200 | tf_op jit(solution)/shard_map/ppermute | solution.py:23
  89.8 16.1 %collective-permute-start.32 = (bf16[192,896]{1,0:T(8,128)(2,1)S(1)}, bf16[192,896]{1,0:T(8,128)(2,1)S(1)}, u32[]{:S(2)}, u32[]{:S(2)}) collective-permute-start(bf16[192,896]{1,0:T(8,128)(2,1)S(1)} %pack.4), channel_id=1, source_target_pairs={{12,0},{13,1},{14,2},{15,3},{0,4},{1,5},{2,6},{3,7},{4,8},{5,9},{6... | collective-permute-start | bytes 1032200 | tf_op jit(solution)/shard_map/ppermute | solution.py:23
  94.6 5.7 %collective-permute-start.30 = (bf16[192,224]{1,0:T(8,128)(2,1)S(1)}, bf16[192,224]{1,0:T(8,128)(2,1)S(1)}, u32[]{:S(2)}, u32[]{:S(2)}) collective-permute-start(bf16[192,224]{1,0:T(8,128)(2,1)S(1)} %get-tuple-element.78), channel_id=1, source_target_pairs={{2,0},{3,1},{0,2},{1,3},{6,4},{7,5},{4,6},{5,7},{10,8},{11,9},{8,1... | collective-permute-start | bytes 258056 | tf_op jit(solution)/shard_map/ppermute | solution.py:23
  95.5 6.0 %collective-permute-start.31 = (bf16[192,224]{1,0:T(8,128)(2,1)S(1)}, bf16[192,224]{1,0:T(8,128)(2,1)S(1)}, u32[]{:S(2)}, u32[]{:S(2)}) collective-permute-start(bf16[192,224]{1,0:T(8,128)(2,1)S(1)} %get-tuple-element.79), channel_id=1, source_target_pairs={{3,0},{2,1},{1,2},{0,3},{7,4},{6,5},{5,6},{4,7},{11,8},{10,9},{9,1... | collective-permute-start | bytes 258056 | tf_op jit(solution)/shard_map/ppermute | solution.py:23
  99.0 3.3 %collective-permute-start.34 = (bf16[192,224]{1,0:T(8,128)(2,1)S(1)}, bf16[192,224]{1,0:T(8,128)(2,1)S(1)}, u32[]{:S(2)}, u32[]{:S(2)}) collective-permute-start(bf16[192,224]{1,0:T(8,128)(2,1)S(1)} %get-tuple-element.84), channel_id=1, source_target_pairs={{1,0},{0,1},{3,2},{2,3},{5,4},{4,5},{7,6},{6,7},{9,8},{8,9},{11,10... | collective-permute-start | bytes 258056 | tf_op jit(solution)/shard_map/ppermute | solution.py:23
  99.1 5.7 %collective-permute-start.35 = (bf16[192,224]{1,0:T(8,128)(2,1)S(1)}, bf16[192,224]{1,0:T(8,128)(2,1)S(1)}, u32[]{:S(2)}, u32[]{:S(2)}) collective-permute-start(bf16[192,224]{1,0:T(8,128)(2,1)S(1)} %get-tuple-element.85), channel_id=1, source_target_pairs={{2,0},{3,1},{0,2},{1,3},{6,4},{7,5},{4,6},{5,7},{10,8},{11,9},{8,1... | collective-permute-start | bytes 258056 | tf_op jit(solution)/shard_map/ppermute | solution.py:23
  100.2 5.7 %collective-permute-start.36 = (bf16[192,224]{1,0:T(8,128)(2,1)S(1)}, bf16[192,224]{1,0:T(8,128)(2,1)S(1)}, u32[]{:S(2)}, u32[]{:S(2)}) collective-permute-start(bf16[192,224]{1,0:T(8,128)(2,1)S(1)} %get-tuple-element.86), channel_id=1, source_target_pairs={{3,0},{2,1},{1,2},{0,3},{7,4},{6,5},{5,6},{4,7},{11,8},{10,9},{9,1... | collective-permute-start | bytes 258056 | tf_op jit(solution)/shard_map/ppermute | solution.py:23
  (11 other events, 35.2 us)

commit v6 on v5

--- a/solution.py
+++ b/solution.py
@@ -14,7 +14,7 @@
 F32 = jnp.float32
 QUAD = 4
 INVALID = 1e38
-FACTORS = 16
+FACTORS = 8
 MB = 2**20
 
 
@@ -139,24 +139,21 @@
             near[k * rows : (k + 1) * rows, span] = tile.astype(BF16)
 
 
-def stage_kernel(clusters, own, side_a, core, across_a, units):
+def stage_kernel(clusters, own, side, core, across, units):
     rows = own.shape[0]
-    for i, block in enumerate((own, side_a, core, across_a)):
+    for i, block in enumerate((own, side, core, across)):
         place_units(clusters[i] * rows, block, units)
 
 
-def stage_seed_kernel(clusters, own, side_a, core, across_a, seed, units, stack):
-    stage_kernel(clusters, own, side_a, core, across_a, units)
+def stage_seed_kernel(clusters, own, side, core, across, seed, units, stack):
+    stage_kernel(clusters, own, side, core, across, units)
     unpack(seed, stack)
 
 
-def far_kernel(clusters, units_in, up_in, side_b, across_b, stack, units, up_units, far, sums):
+def far_kernel(clusters, units, up_in, side_b, across_b, stack, up_units, far, sums):
     rows = units.shape[0] // QUAD
-    half = rows // 2
     for i, block in ((1, side_b), (3, across_b)):
-        start = clusters[i] * rows + half
-        place_units(start, block.at[:half], units)
-        place_units(start, block.at[half:], up_units)
+        place_units((clusters[i] + 1) * rows - block.shape[0], block, up_units)
     for k in range(QUAD):
         here = slice(k * rows, (k + 1) * rows)
         for first in range(0, k + 1, 2):
@@ -191,11 +188,10 @@
     rows = summed.shape[0]
     kept = tail.shape[0] - 2 * FACTORS
     factor = jnp.where(total > INVALID / 10, 0.0, lax.rsqrt(total / summed.shape[1] + 1e-06))
-    high = factor.astype(BF16)
+    high = factor.astype(BF16).astype(F32)
     tail[:kept, :] = summed[rows - kept :, :]
     tail[kept:, :] = jnp.zeros((2 * FACTORS, tail.shape[1]), BF16)
-    tail[kept : kept + FACTORS, :rows] = high
-    tail[kept + FACTORS :, :rows] = (factor - high.astype(F32)).astype(BF16)
+    tail[kept:, :rows] = jnp.concatenate([high, factor - high]).astype(BF16)
     mix(summed.at[: rows - kept], tail, seed, mixed)
     unpack(mixed, stack)
     scatter(far, stack, (out_a, out_b))
@@ -287,14 +283,15 @@
     head[...] = summed[: head.shape[0], :]
     square = total * total
     high = square.astype(BF16)
-    marks = lanes_of(FACTORS, total.shape[1])
+    marks = lanes_of(2 * FACTORS, total.shape[1])
     sums = sum(
         lax.dot_general(marks, part, (((1,), (1,)), ((), ())), preferred_element_type=F32)
         for part in (high, (square - high.astype(F32)).astype(BF16))
     )
     row = lax.broadcasted_iota(jnp.int32, sums.shape, 0)
     lane = lax.broadcasted_iota(jnp.int32, sums.shape, 1)
-    squares[...] = sums + jnp.where((row == scalars[0]) & (lane >= scalars[1]), INVALID, 0.0)
+    sums = sums + jnp.where((row == scalars[0]) & (lane >= scalars[1]), INVALID, 0.0)
+    squares[...] = sums[:FACTORS, :]
 
 
 def add_kernel(scalars, kept, sent, out, p1, p2, p3):
@@ -302,19 +299,45 @@
     cut(out, scalars[0], [(1, p1), (2, p2), (3, p3)])
 
 
-def finish_kernel(scalars, kept_a, sent_a, sums_b, p1, p2, p3, seed, out, whole_b):
-    whole_b[...] = sums_b[...]
-    join(scalars[0], [(1, p1), (2, p2), (3, p3)], whole_b)
-    half = kept_a.shape[0]
-    for first, summed in (
-        (0, kept_a[...].astype(F32) + sent_a[...].astype(F32)),
-        (half, whole_b[...].astype(F32)),
-    ):
-        here = slice(first, first + summed.shape[0])
-        factor = lax.rsqrt(jnp.mean(summed * summed, axis=-1, keepdims=True) + 1e-06)
-        result = keep_share * summed * factor + (1.0 - keep_share) * seed[here, :].astype(F32)
-        row = lax.broadcasted_iota(jnp.int32, summed.shape, 0) + first
-        out[here, :] = jnp.where(row < scalars[1], result, 0.0).astype(BF16)
+def finished(scalars, summed, seed, first):
+    factor = lax.rsqrt(jnp.mean(summed * summed, axis=-1, keepdims=True) + 1e-06)
+    result = keep_share * summed * factor + (1.0 - keep_share) * seed[...].astype(F32)
+    row = lax.broadcasted_iota(jnp.int32, summed.shape, 0) + first
+    return jnp.where(row < scalars[1], result, 0.0).astype(BF16)
+
+
+def finish_b_kernel(scalars, sums, p1, p2, p3, seed, out, whole):
+    whole[...] = sums[...]
+    join(scalars[0], [(1, p1), (2, p2), (3, p3)], whole)
+    out[...] = finished(scalars, whole[...].astype(F32), seed, sums.shape[0])
+
+
+def finish_a_kernel(scalars, out_b, kept, sent, seed, out):
+    out[...] = finished(scalars, kept[...].astype(F32) + sent[...].astype(F32), seed, 0)
+
+
+def finish(kernel, name, half, operands, whole, scratch=(), aliases={}):
+    rows, classes = whole.shape
+    block = (rows // 2, classes)
+
+    def spec(i, x):
+        if x.dtype == jnp.int32:
+            return pl.BlockSpec(memory_space=pltpu.SMEM)
+        if i in aliases:
+            return pl.BlockSpec(memory_space=pl.ANY)
+        return pl.BlockSpec(block, lambda _: (half, 0)) if x.shape == whole.shape else pl.BlockSpec(x.shape, lambda _: (0, 0))
+
+    return pl.pallas_call(
+        kernel,
+        grid=(1,),
+        in_specs=[spec(i, x) for i, x in enumerate(operands)],
+        out_specs=pl.BlockSpec(block, lambda _: (half, 0)),
+        out_shape=whole,
+        scratch_shapes=list(scratch),
+        input_output_aliases=aliases,
+        compiler_params=pltpu.CompilerParams(vmem_limit_bytes=12 * MB),
+        name=name,
+    )(*operands)
 
 
 def body(embeddings, labels, cluster_rows):
@@ -333,28 +356,27 @@
 
     half_rows = rows // 2
 
+    side = from_side(embeddings)
     own_up = from_up(embeddings)
-    side_a = from_side(embeddings[:half_rows])
     seed, *pieces = call(seed_kernel, "seed", (scalars, labels), (packed, piece, piece, piece))
     received = exchange(pieces)
     own_core = from_core(embeddings)
     cross_own = [from_group(after(embeddings, seed), step) for step in steps]
-    up_side_a = from_up(side_a)
-    late = jnp.concatenate([after(embeddings, side_a)[half_rows:], own_up[half_rows:]])
-    side_b = from_side(after(late, received[1:]))
+    up_side_a = from_up(side[:half_rows])
+    side_b = from_side(after(own_up[half_rows:], received[1:]))
     received[0] = after(received[0], own_up)
     packed_seed = call(pack_kernel, "pack", (scalars, seed, *received), packed)
     seed_up = from_up(packed_seed)
-    seed_cross = [from_group(packed_seed, step) for step in steps]
+    seed_cross = [from_group(after(packed_seed, up_side_a), step) for step in steps]
     cross0 = call(
         functools.partial(cross_kernel, weight), "cross", (embeddings, *cross_own), like((len(steps) * rows, rows), BF16)
     )
-    across_a = from_core(side_a)
+    across = from_core(side)
     unit_stack = like((QUAD * rows, depth), BF16)
     units, seed_stack = call(
         stage_seed_kernel,
         "stage_own",
-        (clusters, embeddings, side_a, own_core, across_a, packed_seed),
+        (clusters, embeddings, side, own_core, across, packed_seed),
         (unit_stack, like((QUAD * rows, classes // QUAD), BF16)),
     )
     side_b = after(side_b, (cross0, units, up_side_a))
@@ -365,14 +387,14 @@
     )
     cross0 = after(cross0, (side_b, seed_up, seed_cross))
     cross1, cross2 = from_side(cross0), from_core(cross0)
-    units, _, far, sums = call(
+    _, far, sums = call(
         far_kernel,
         "far",
         (clusters, units, up_units, side_b, across_b, seed_stack),
-        (unit_stack, unit_stack, matrix, packed),
-        aliases={1: 0, 2: 1},
-    )
-    near = call(near_kernel, "near", (units,), matrix)
+        (unit_stack, matrix, packed),
+        aliases={2: 0},
+    )
+    near = call(near_kernel, "near", (after(units, sums),), matrix)
     cross3 = from_core(after(cross1, near))
 
     sent = from_down(sums)
@@ -434,13 +456,15 @@
     received = exchange(pieces)
     sums_b, *pieces = call(add_kernel, "add", (scalars, after(kept_b, received[0]), sent_b), (half, half_piece, half_piece, half_piece))
     kept_a = call(pack_kernel, "pack", (scalars, kept_a, *received), half)
-    return call(
-        finish_kernel,
-        "finish",
-        (scalars, kept_a, sent_a, sums_b, *exchange(pieces), seed),
+    result = finish(
+        finish_b_kernel,
+        "finish_b",
+        1,
+        (scalars, sums_b, *exchange(pieces), seed),
         packed,
         [pltpu.VMEM(half.shape, BF16)],
     )
+    return finish(finish_a_kernel, "finish_a", 0, (scalars, result, kept_a, sent_a, seed), packed, aliases={1: 0})
 
 
 def solution(mesh):

time: 108 us -> 113 us (1.046)
  starting transfers between devices: 29.7 us -> 36.4 us
  local copies, waits for them, and re-layouts: 6.37 us -> 4.75 us
    ppermute x33, starting transfers between devices: 24.6 us -> 31.1 us  [along_dev(): lax.ppermute(block, 'dev', [(source(i) % size, i) for i in range(size)])]
    pallas_call x0 -> x2, Pallas kernels: none -> 3.4 us  [finish(): pl.pallas_call(kernel, grid=(1,), in_specs=[spec(i, x) for i, x in enumer...]
    pallas_call x16 -> x15, Pallas kernels: 33.9 us -> 31.5 us  [call(): pl.pallas_call(kernel, in_specs=specs, out_shape=out_shape, scratch_shape...]
    ppermute x4, waiting for transfers between devices: 2.56 us -> 0.75 us  [from_group(): lax.ppermute(block, 'grp', [((i + step) % size, i) for i in range(size)])]
    unnamed x12 -> x16, local copies, waits for them, and re-layouts: 4.32 us -> 3.04 us
  transfers between devices with their start and end apart: 37 -> 37, of which waited for: 21 -> 15; matrix products, arithmetic and copies ran while one was open for 3% -> 2% of each run, Pallas kernels for 28% -> 29%
where the time goes in v6:
time: 113 us
  starting transfers between devices  36.4 us (32%)
  waiting for transfers between devices  35.4 us (31%)
  Pallas kernels  34.9 us (31%)
  local copies, waits for them, and re-layouts  4.75 us (4%)
    ppermute x33, waiting for transfers between devices, along_dev(): lax.ppermute(block, 'dev', [(source(i) % size, i) for i in range(size)])  34.7 us
    pallas_call x15, Pallas kernels, call(): pl.pallas_call(kernel, in_specs=specs, out_shape=out_shape, scratch_shape...  31.5 us
    ppermute x33, starting transfers between devices, along_dev(): lax.ppermute(block, 'dev', [(source(i) % size, i) for i in range(size)])  31.1 us
    ppermute x4, starting transfers between devices, from_group(): lax.ppermute(block, 'grp', [((i + step) % size, i) for i in range(size)])  5.27 us
    pallas_call x2, Pallas kernels, finish(): pl.pallas_call(kernel, grid=(1,), in_specs=[spec(i, x) for i, x in enumer...  3.4 us
    unnamed x16, local copies, waits for them, and re-layouts  3.04 us
  transfers between devices with their start and end apart: 37, of which 15 were waited for; matrix products, arithmetic and copies ran while one was open for 2% of the time, Pallas kernels for 29%

profile of v6, /device:TPU:0, one launch (start us, length us, event | category | flops | bytes accessed | tf_op | source)
XLA Modules:
  0.0 112.5 jit_solution(850373496690823165)
XLA Ops:
  0.0 2.9 %collective-permute-start = (bf16[384,768]{1,0:T(8,128)(2,1)}, bf16[384,768]{1,0:T(8,128)(2,1)}, u32[]{:S(2)}, u32[]{:S(2)}) collective-permute-start(bf16[384,768]{1,0:T(8,128)(2,1)} %own.3), channel_id=1, source_target_pairs={{2,0},{3,1},{0,2},{1,3},{6,4},{7,5},{4,6},{5,7},{10,8},{11,9},{8,1... | collective-permute-start | bytes 1769480 | tf_op jit(solution)/shard_map/ppermute | solution.py:23
  2.9 3.6 %collective-permute-start.4 = (bf16[384,768]{1,0:T(8,128)(2,1)}, bf16[384,768]{1,0:T(8,128)(2,1)S(1)}, u32[]{:S(2)}, u32[]{:S(2)}) collective-permute-start(bf16[384,768]{1,0:T(8,128)(2,1)} %own.3), channel_id=1, source_target_pairs={{4,0},{5,1},{6,2},{7,3},{8,4},{9,5},{10,6},{11,7},{12,8},{13,9},{1... | collective-permute-start | bytes 1769480 | tf_op jit(solution)/shard_map/ppermute | solution.py:23
  9.5 1.6 %collective-permute-start.8 = (bf16[384,768]{1,0:T(8,128)(2,1)}, bf16[384,768]{1,0:T(8,128)(2,1)S(1)}, u32[]{:S(2)}, u32[]{:S(2)}) collective-permute-start(bf16[384,768]{1,0:T(8,128)(2,1)} %own.3), channel_id=1, source_target_pairs={{16,0},{0,16},{17,1},{1,17},{18,2},{2,18},{19,3},{3,19},{20,4},{4,... | collective-permute-start | bytes 1769480 | tf_op jit(solution)/shard_map/ppermute | solution.py:44
  11.2 5.4 %collective-permute-done.side = bf16[384,768]{1,0:T(8,128)(2,1)} collective-permute-done((bf16[384,768]{1,0:T(8,128)(2,1)}, bf16[384,768]{1,0:T(8,128)(2,1)}, u32[]{:S(2)}, u32[]{:S(2)}) %collective-permute-start) | collective-permute-done | bytes 589856 | tf_op jit(solution)/shard_map/ppermute | solution.py:23
  16.7 1.7 %collective-permute-start.5 = (bf16[384,224]{1,0:T(8,128)(2,1)S(1)}, bf16[384,224]{1,0:T(8,128)(2,1)S(1)}, u32[]{:S(2)}, u32[]{:S(2)}) collective-permute-start(bf16[384,224]{1,0:T(8,128)(2,1)S(1)} %get-tuple-element.49), channel_id=1, source_target_pairs={{2,0},{3,1},{0,2},{1,3},{6,4},{7,5},{4,6},{5,7},{10,8},{11,9},{8,1... | collective-permute-start | bytes 516104 | tf_op jit(solution)/shard_map/ppermute | solution.py:23
  19.3 3.7 %collective-permute-start.9 = (bf16[192,768]{1,0:T(8,128)(2,1)S(1)}, bf16[192,768]{1,0:T(8,128)(2,1)S(1)}, u32[]{:S(2)}, u32[]{:S(2)}) collective-permute-start(bf16[192,768]{1,0:T(8,128)(2,1)S(1)} %slice.9), channel_id=1, source_target_pairs={{4,0},{5,1},{6,2},{7,3},{8,4},{9,5},{10,6},{11,7},{12,8},{13,9},{1... | collective-permute-start | bytes 884744 | tf_op jit(solution)/shard_map/ppermute | solution.py:23
  24.9 4.8 %collective-permute-done.6.p3 = bf16[384,224]{1,0:T(8,128)(2,1)S(1)} collective-permute-done((bf16[384,224]{1,0:T(8,128)(2,1)S(1)}, bf16[384,224]{1,0:T(8,128)(2,1)S(1)}, u32[]{:S(2)}, u32[]{:S(2)}) %collective-permute-start.6) | collective-permute-done | bytes 172064 | tf_op jit(solution)/shard_map/ppermute | solution.py:23
  30.7 3.3 %collective-permute-start.13 = (bf16[384,896]{1,0:T(8,128)(2,1)S(1)}, bf16[384,896]{1,0:T(8,128)(2,1)S(1)}, u32[]{:S(2)}, u32[]{:S(2)}) collective-permute-start(bf16[384,896]{1,0:T(8,128)(2,1)S(1)} %pack.3.seed.own), channel_id=1, source_target_pairs={{4,0},{5,1},{6,2},{7,3},{8,4},{9,5},{10,6},{11,7},{12,8},{13,9},{1... | collective-permute-start | bytes 2064392 | tf_op jit(solution)/shard_map/ppermute | solution.py:23
  34.0 1.6 %collective-permute-start.14 = (bf16[384,896]{1,0:T(8,128)(2,1)S(1)}, bf16[384,896]{1,0:T(8,128)(2,1)S(1)}, u32[]{:S(2)}, u32[]{:S(2)}) collective-permute-start(bf16[384,896]{1,0:T(8,128)(2,1)S(1)} %pack.3.seed.own), channel_id=1, source_target_pairs={{16,0},{0,16},{17,1},{1,17},{18,2},{2,18},{19,3},{3,19},{20,4},{4,... | collective-permute-start | bytes 2064392 | tf_op jit(solution)/shard_map/ppermute | solution.py:44
  40.3 2.5 %stage_own.1 = (bf16[1536,768]{1,0:T(8,128)(2,1)S(1)}, bf16[1536,224]{1,0:T(8,128)(2,1)S(1)}) custom-call(s32[4]{0:T(128)S(1)} %pad_add_fusion.1.clusters, bf16[384,768]{1,0:T(8,128)(2,1)S(1)} %copy-done, bf16[384,768]{1,0:T(8,128)(2,1)} %collective-permute-done.side, bf16[384,768]{1,0:T(8,128)(2,1)} %collective-permute-done.1.core, ...), custom_call_target="tpu_custom_call" | custom-call | tf_op jit(solution)/shard_map/stage_own/pallas_call | solution.py:59
  42.8 1.7 %collective-permute-done.7.side_b = bf16[192,768]{1,0:T(8,128)(2,1)} collective-permute-done((bf16[192,768]{1,0:T(8,128)(2,1)}, bf16[192,768]{1,0:T(8,128)(2,1)}, u32[]{:S(2)}, u32[]{:S(2)}) %collective-permute-start.7) | collective-permute-done | bytes 294944 | tf_op jit(solution)/shard_map/ppermute | solution.py:23
  44.5 1.8 %stage_up.1.up_in = bf16[1536,768]{1,0:T(8,128)(2,1)S(1)} custom-call(s32[4]{0:T(128)S(1)} %pad_add_fusion.1.clusters, bf16[384,768]{1,0:T(8,128)(2,1)S(1)} %copy-done.2, bf16[192,768]{1,0:T(8,128)(2,1)S(1)} %copy-done.7, bf16[384,768]{1,0:T(8,128)(2,1)} %collective-permute-done.10.core, bf16[192,768]{1,0:T(8,128)(2,1)S(1)} %collective-permute-done.11.across), custom_call_target="tpu_custom_call" | custom-call | tf_op jit(solution)/shard_map/stage_up/pallas_call | solution.py:59
  46.3 4.8 %far.1 = (bf16[1536,768]{1,0:T(8,128)(2,1)S(1)}, bf16[1536,1536]{1,0:T(8,128)(2,1)S(1)}, bf16[384,896]{1,0:T(8,128)(2,1)S(1)}) custom-call(s32[4]{0:T(128)S(1)} %pad_add_fusion.1.clusters, bf16[1536,768]{1,0:T(8,128)(2,1)S(1)} %get-tuple-element.61.units, bf16[1536,768]{1,0:T(8,128)(2,1)S(1)} %stage_up.1.up_in, ...), custom_call_target="tpu_custom_call", output_to_operand_aliasing={{0}: (2, {})} | custom-call | tf_op jit(solution)/shard_map/far/pallas_call | solution.py:59
  51.4 1.5 %collective-permute-start.15 = (bf16[384,384]{1,0:T(8,128)(2,1)S(1)}, bf16[384,384]{1,0:T(8,128)(2,1)S(1)}, u32[]{:S(2)}, u32[]{:S(2)}) collective-permute-start(bf16[384,384]{1,0:T(8,128)(2,1)S(1)} %cross.1.t0), channel_id=1, source_target_pairs={{2,0},{3,1},{0,2},{1,3},{6,4},{7,5},{4,6},{5,7},{10,8},{11,9},{8,1... | collective-permute-start | bytes 884744 | tf_op jit(solution)/shard_map/ppermute | solution.py:23
  52.9 3.9 %near.1 = bf16[1536,1536]{1,0:T(8,128)(2,1)S(1)} custom-call(bf16[1536,768]{1,0:T(8,128)(2,1)S(1)} %get-tuple-element.61.units), custom_call_target="tpu_custom_call" | custom-call | tf_op jit(solution)/shard_map/near/pallas_call | solution.py:59
  57.1 3.7 %collective-permute-done.15.t1 = bf16[384,384]{1,0:T(8,128)(2,1)S(1)} collective-permute-done((bf16[384,384]{1,0:T(8,128)(2,1)S(1)}, bf16[384,384]{1,0:T(8,128)(2,1)S(1)}, u32[]{:S(2)}, u32[]{:S(2)}) %collective-permute-start.15) | collective-permute-done | bytes 294944 | tf_op jit(solution)/shard_map/ppermute | solution.py:23
  60.9 1.6 %collective-permute-done.17.t3 = bf16[384,384]{1,0:T(8,128)(2,1)S(1)} collective-permute-done((bf16[384,384]{1,0:T(8,128)(2,1)S(1)}, bf16[384,384]{1,0:T(8,128)(2,1)S(1)}, u32[]{:S(2)}, u32[]{:S(2)}) %collective-permute-start.17) | collective-permute-done | bytes 294944 | tf_op jit(solution)/shard_map/ppermute | solution.py:23
  62.4 3.5 %gather.1.kept = f32[384,896]{1,0:T(8,128)S(1)} custom-call(s32[4]{0:T(128)S(1)} %pad_add_fusion.1.clusters, bf16[1536,1536]{1,0:T(8,128)(2,1)S(1)} %near.1, bf16[1536,1536]{1,0:T(8,128)(2,1)S(1)} %get-tuple-element.57.far, bf16[384,384]{1,0:T(8,128)(2,1)S(1)} %cross.1.t0, bf16[384,384]{1,0:T(8,128)(2,1)S(1)} %collective-permute-done.15.t1, ...), custom_call_target="tpu_custom_call" | custom-call | tf_op jit(solution)/shard_map/gather/pallas_call | solution.py:59
  65.9 5.1 %collective-permute-done.18.sent = bf16[384,896]{1,0:T(8,128)(2,1)S(1)} collective-permute-done((bf16[384,896]{1,0:T(8,128)(2,1)S(1)}, bf16[384,896]{1,0:T(8,128)(2,1)S(1)}, u32[]{:S(2)}, u32[]{:S(2)}) %collective-permute-start.18) | collective-permute-done | bytes 688160 | tf_op jit(solution)/shard_map/ppermute | solution.py:23
  72.7 1.5 %collective-permute-start.20 = (f32[8,384]{1,0:T(8,128)S(1)}, f32[8,384]{1,0:T(8,128)S(1)}, u32[]{:S(2)}, u32[]{:S(2)}) collective-permute-start(f32[8,384]{1,0:T(8,128)S(1)} %get-tuple-element.64.s0), channel_id=1, source_target_pairs={{2,0},{3,1},{0,2},{1,3},{6,4},{7,5},{4,6},{5,7},{10,8},{11,9},{8,1... | collective-permute-start | bytes 36872 | tf_op jit(solution)/shard_map/ppermute | solution.py:23
  74.6 1.8 %collective-permute-done.20.s2 = f32[8,384]{1,0:T(8,128)S(1)} collective-permute-done((f32[8,384]{1,0:T(8,128)S(1)}, f32[8,384]{1,0:T(8,128)S(1)}, u32[]{:S(2)}, u32[]{:S(2)}) %collective-permute-start.20) | collective-permute-done | bytes 12320 | tf_op jit(solution)/shard_map/ppermute | solution.py:23
  77.4 3.5 %mix.1 = (bf16[80,896]{1,0:T(8,128)(2,1)S(1)}, bf16[384,896]{1,0:T(8,128)(2,1)}, bf16[1536,224]{1,0:T(8,128)(2,1)S(1)}, bf16[192,896]{1,0:T(8,128)(2,1)S(1)}, bf...) custom-call(s32[2]{0:T(128)S(1)} %pad_add_fusion.scalars, ...), custom_call_target="tpu_custom_call" | custom-call | tf_op jit(solution)/shard_map/mix/pallas_call | solution.py:59
  84.1 2.8 %collective-permute-done.24.p2 = bf16[192,224]{1,0:T(8,128)(2,1)S(1)} collective-permute-done((bf16[192,224]{1,0:T(8,128)(2,1)S(1)}, bf16[192,224]{1,0:T(8,128)(2,1)S(1)}, u32[]{:S(2)}, u32[]{:S(2)}) %collective-permute-start.24) | collective-permute-done | bytes 86048 | tf_op jit(solution)/shard_map/ppermute | solution.py:23
  86.9 1.5 %collective-permute-start.28 = (bf16[80,896]{1,0:T(8,128)(2,1)S(1)}, bf16[80,896]{1,0:T(8,128)(2,1)S(1)}, u32[]{:S(2)}, u32[]{:S(2)}) collective-permute-start(bf16[80,896]{1,0:T(8,128)(2,1)S(1)} %get-tuple-element.73), channel_id=1, source_target_pairs={{16,0},{0,16},{17,1},{1,17},{18,2},{2,18},{19,3},{3,19},{20,4},{4,... | collective-permute-start | bytes 430088 | tf_op jit(solution)/shard_map/ppermute | solution.py:44
  88.4 2.0 %collective-permute-start.30 = (bf16[192,896]{1,0:T(8,128)(2,1)S(1)}, bf16[192,896]{1,0:T(8,128)(2,1)S(1)}, u32[]{:S(2)}, u32[]{:S(2)}) collective-permute-start(bf16[192,896]{1,0:T(8,128)(2,1)S(1)} %get-tuple-element.79), channel_id=1, source_target_pairs={{12,0},{13,1},{14,2},{15,3},{0,4},{1,5},{2,6},{3,7},{4,8},{5,9},{6... | collective-permute-start | bytes 1032200 | tf_op jit(solution)/shard_map/ppermute | solution.py:23
  92.0 2.0 %collective-permute-start.36 = (bf16[192,896]{1,0:T(8,128)(2,1)S(1)}, bf16[192,896]{1,0:T(8,128)(2,1)S(1)}, u32[]{:S(2)}, u32[]{:S(2)}) collective-permute-start(bf16[192,896]{1,0:T(8,128)(2,1)S(1)} %pack.4), channel_id=1, source_target_pairs={{12,0},{13,1},{14,2},{15,3},{0,4},{1,5},{2,6},{3,7},{4,8},{5,9},{6... | collective-permute-start | bytes 1032200 | tf_op jit(solution)/shard_map/ppermute | solution.py:23
  94.0 3.5 %gather_mixed.1 = (f32[1536,224]{1,0:T(8,128)S(1)}, f32[192,896]{1,0:T(8,128)S(1)}, bf16[192,896]{1,0:T(8,128)(2,1)S(1)}, bf16[192,224]{1,0:T(8,128)(2,1)S(1)}, ...) custom-call(s32[4]{0:T(128)S(1)} %pad_add_fusion.1.clusters, ...), custom_call_target="tpu_custom_call", output_to_operand_aliasing={{0}: (6, {})} | custom-call | tf_op jit(solution)/shard_map/gather_mixed/pallas_call | solution.py:59
  97.7 1.8 %collective-permute-start.35 = (bf16[192,224]{1,0:T(8,128)(2,1)S(1)}, bf16[192,224]{1,0:T(8,128)(2,1)S(1)}, u32[]{:S(2)}, u32[]{:S(2)}) collective-permute-start(bf16[192,224]{1,0:T(8,128)(2,1)S(1)} %get-tuple-element.86), channel_id=1, source_target_pairs={{3,0},{2,1},{1,2},{0,3},{7,4},{6,5},{5,6},{4,7},{11,8},{10,9},{9,1... | collective-permute-start | bytes 258056 | tf_op jit(solution)/shard_map/ppermute | solution.py:23
  99.5 1.7 %collective-permute-done.30.sent = bf16[192,896]{1,0:T(8,128)(2,1)S(1)} collective-permute-done((bf16[192,896]{1,0:T(8,128)(2,1)S(1)}, bf16[192,896]{1,0:T(8,128)(2,1)S(1)}, u32[]{:S(2)}, u32[]{:S(2)}) %collective-permute-start.30) | collective-permute-done | bytes 344096 | tf_op jit(solution)/shard_map/ppermute | solution.py:23
  105.3 2.6 %collective-permute-done.32.p2 = bf16[192,224]{1,0:T(8,128)(2,1)S(1)} collective-permute-done((bf16[192,224]{1,0:T(8,128)(2,1)S(1)}, bf16[192,224]{1,0:T(8,128)(2,1)S(1)}, u32[]{:S(2)}, u32[]{:S(2)}) %collective-permute-start.32) | collective-permute-done | bytes 86048 | tf_op jit(solution)/shard_map/ppermute | solution.py:23
  109.1 1.9 %finish_b.1.out_b = bf16[384,896]{1,0:T(8,128)(2,1)} custom-call(s32[2]{0:T(128)S(1)} %pad_add_fusion.scalars, bf16[192,896]{1,0:T(8,128)(2,1)S(1)} %get-tuple-element.80.sums, bf16[192,224]{1,0:T(8,128)(2,1)S(1)} %collective-permute-done.31.p1, bf16[192,224]{1,0:T(8,128)(2,1)S(1)} %collective-permute-done.32.p2, ...), custom_call_target="tpu_custom_call" | custom-call | tf_op jit(solution)/shard_map/finish_b/pallas_call | solution.py:330
  111.0 1.5 %finish_a.1 = bf16[384,896]{1,0:T(8,128)(2,1)} custom-call(s32[2]{0:T(128)S(1)} %pad_add_fusion.scalars, bf16[384,896]{1,0:T(8,128)(2,1)} %finish_b.1.out_b, bf16[192,896]{1,0:T(8,128)(2,1)S(1)} %pack.5.kept, bf16[192,896]{1,0:T(8,128)(2,1)S(1)} %collective-permute-done.36.sent, ...), custom_call_target="tpu_custom_call", output_to_operand_aliasing={{}: (1, {})} | custom-call | tf_op jit(solution)/shard_map/finish_a/pallas_call | solution.py:330
  (79 shorter events, 25.0 us)
Async XLA Ops:
  0.0 16.6 %collective-permute-start = (bf16[384,768]{1,0:T(8,128)(2,1)}, bf16[384,768]{1,0:T(8,128)(2,1)}, u32[]{:S(2)}, u32[]{:S(2)}) collective-permute-start(bf16[384,768]{1,0:T(8,128)(2,1)} %own.3), channel_id=1, source_target_pairs={{2,0},{3,1},{0,2},{1,3},{6,4},{7,5},{4,6},{5,7},{10,8},{11,9},{8,1... | collective-permute-start | bytes 1769480 | tf_op jit(solution)/shard_map/ppermute | solution.py:23
  2.9 20.0 %collective-permute-start.4 = (bf16[384,768]{1,0:T(8,128)(2,1)}, bf16[384,768]{1,0:T(8,128)(2,1)S(1)}, u32[]{:S(2)}, u32[]{:S(2)}) collective-permute-start(bf16[384,768]{1,0:T(8,128)(2,1)} %own.3), channel_id=1, source_target_pairs={{4,0},{5,1},{6,2},{7,3},{8,4},{9,5},{10,6},{11,7},{12,8},{13,9},{1... | collective-permute-start | bytes 1769480 | tf_op jit(solution)/shard_map/ppermute | solution.py:23
  6.5 29.0 %collective-permute-start.1 = (bf16[384,768]{1,0:T(8,128)(2,1)}, bf16[384,768]{1,0:T(8,128)(2,1)}, u32[]{:S(2)}, u32[]{:S(2)}) collective-permute-start(bf16[384,768]{1,0:T(8,128)(2,1)} %own.3), channel_id=1, source_target_pairs={{1,0},{0,1},{3,2},{2,3},{5,4},{4,5},{7,6},{6,7},{9,8},{8,9},{11,10... | collective-permute-start | bytes 1769480 | tf_op jit(solution)/shard_map/ppermute | solution.py:23
  9.5 27.4 %collective-permute-start.8 = (bf16[384,768]{1,0:T(8,128)(2,1)}, bf16[384,768]{1,0:T(8,128)(2,1)S(1)}, u32[]{:S(2)}, u32[]{:S(2)}) collective-permute-start(bf16[384,768]{1,0:T(8,128)(2,1)} %own.3), channel_id=1, source_target_pairs={{16,0},{0,16},{17,1},{1,17},{18,2},{2,18},{19,3},{3,19},{20,4},{4,... | collective-permute-start | bytes 1769480 | tf_op jit(solution)/shard_map/ppermute | solution.py:44
  11.1 8.2 %collective-permute-start.3 = (bf16[384,224]{1,0:T(8,128)(2,1)S(1)}, bf16[384,224]{1,0:T(8,128)(2,1)S(1)}, u32[]{:S(2)}, u32[]{:S(2)}) collective-permute-start(bf16[384,224]{1,0:T(8,128)(2,1)S(1)} %get-tuple-element.47), channel_id=1, source_target_pairs={{1,0},{0,1},{3,2},{2,3},{5,4},{4,5},{7,6},{6,7},{9,8},{8,9},{11,10... | collective-permute-start | bytes 516104 | tf_op jit(solution)/shard_map/ppermute | solution.py:23
  16.7 6.3 %collective-permute-start.5 = (bf16[384,224]{1,0:T(8,128)(2,1)S(1)}, bf16[384,224]{1,0:T(8,128)(2,1)S(1)}, u32[]{:S(2)}, u32[]{:S(2)}) collective-permute-start(bf16[384,224]{1,0:T(8,128)(2,1)S(1)} %get-tuple-element.49), channel_id=1, source_target_pairs={{2,0},{3,1},{0,2},{1,3},{6,4},{7,5},{4,6},{5,7},{10,8},{11,9},{8,1... | collective-permute-start | bytes 516104 | tf_op jit(solution)/shard_map/ppermute | solution.py:23
  19.3 14.6 %collective-permute-start.9 = (bf16[192,768]{1,0:T(8,128)(2,1)S(1)}, bf16[192,768]{1,0:T(8,128)(2,1)S(1)}, u32[]{:S(2)}, u32[]{:S(2)}) collective-permute-start(bf16[192,768]{1,0:T(8,128)(2,1)S(1)} %slice.9), channel_id=1, source_target_pairs={{4,0},{5,1},{6,2},{7,3},{8,4},{9,5},{10,6},{11,7},{12,8},{13,9},{1... | collective-permute-start | bytes 884744 | tf_op jit(solution)/shard_map/ppermute | solution.py:23
  23.0 16.7 %collective-permute-start.2 = (bf16[384,768]{1,0:T(8,128)(2,1)}, bf16[384,768]{1,0:T(8,128)(2,1)}, u32[]{:S(2)}, u32[]{:S(2)}) collective-permute-start(bf16[384,768]{1,0:T(8,128)(2,1)} %collective-permute-done.side), channel_id=1, source_target_pairs={{1,0},{0,1},{3,2},{2,3},{5,4},{4,5},{7,6},{6,7},{9,8},{8,9},{11,10... | collective-permute-start | bytes 1769480 | tf_op jit(solution)/shard_map/ppermute | solution.py:23
  23.0 6.7 %collective-permute-start.6 = (bf16[384,224]{1,0:T(8,128)(2,1)S(1)}, bf16[384,224]{1,0:T(8,128)(2,1)S(1)}, u32[]{:S(2)}, u32[]{:S(2)}) collective-permute-start(bf16[384,224]{1,0:T(8,128)(2,1)S(1)} %get-tuple-element.50), channel_id=1, source_target_pairs={{3,0},{2,1},{1,2},{0,3},{7,4},{6,5},{5,6},{4,7},{11,8},{10,9},{9,1... | collective-permute-start | bytes 516104 | tf_op jit(solution)/shard_map/ppermute | solution.py:23
  30.7 20.7 %collective-permute-start.13 = (bf16[384,896]{1,0:T(8,128)(2,1)S(1)}, bf16[384,896]{1,0:T(8,128)(2,1)S(1)}, u32[]{:S(2)}, u32[]{:S(2)}) collective-permute-start(bf16[384,896]{1,0:T(8,128)(2,1)S(1)} %pack.3.seed.own), channel_id=1, source_target_pairs={{4,0},{5,1},{6,2},{7,3},{8,4},{9,5},{10,6},{11,7},{12,8},{13,9},{1... | collective-permute-start | bytes 2064392 | tf_op jit(solution)/shard_map/ppermute | solution.py:23
  34.0 17.4 %collective-permute-start.14 = (bf16[384,896]{1,0:T(8,128)(2,1)S(1)}, bf16[384,896]{1,0:T(8,128)(2,1)S(1)}, u32[]{:S(2)}, u32[]{:S(2)}) collective-permute-start(bf16[384,896]{1,0:T(8,128)(2,1)S(1)} %pack.3.seed.own), channel_id=1, source_target_pairs={{16,0},{0,16},{17,1},{1,17},{18,2},{2,18},{19,3},{3,19},{20,4},{4,... | collective-permute-start | bytes 2064392 | tf_op jit(solution)/shard_map/ppermute | solution.py:44
  35.5 9.0 %collective-permute-start.7 = (bf16[192,768]{1,0:T(8,128)(2,1)}, bf16[192,768]{1,0:T(8,128)(2,1)}, u32[]{:S(2)}, u32[]{:S(2)}) collective-permute-start(bf16[192,768]{1,0:T(8,128)(2,1)} %slice.8), channel_id=1, source_target_pairs={{2,0},{3,1},{0,2},{1,3},{6,4},{7,5},{4,6},{5,7},{10,8},{11,9},{8,1... | collective-permute-start | bytes 884744 | tf_op jit(solution)/shard_map/ppermute | solution.py:23
  37.8 6.7 %collective-permute-start.10 = (bf16[384,768]{1,0:T(8,128)(2,1)}, bf16[384,768]{1,0:T(8,128)(2,1)}, u32[]{:S(2)}, u32[]{:S(2)}) collective-permute-start(bf16[384,768]{1,0:T(8,128)(2,1)} %copy-done.1), channel_id=1, source_target_pairs={{1,0},{0,1},{3,2},{2,3},{5,4},{4,5},{7,6},{6,7},{9,8},{8,9},{11,10... | collective-permute-start | bytes 1769480 | tf_op jit(solution)/shard_map/ppermute | solution.py:23
  39.7 4.8 %collective-permute-start.11 = (bf16[192,768]{1,0:T(8,128)(2,1)}, bf16[192,768]{1,0:T(8,128)(2,1)S(1)}, u32[]{:S(2)}, u32[]{:S(2)}) collective-permute-start(bf16[192,768]{1,0:T(8,128)(2,1)} %copy-done.6), channel_id=1, source_target_pairs={{1,0},{0,1},{3,2},{2,3},{5,4},{4,5},{7,6},{6,7},{9,8},{8,9},{11,10... | collective-permute-start | bytes 884744 | tf_op jit(solution)/shard_map/ppermute | solution.py:23
  51.1 19.9 %collective-permute-start.18 = (bf16[384,896]{1,0:T(8,128)(2,1)S(1)}, bf16[384,896]{1,0:T(8,128)(2,1)S(1)}, u32[]{:S(2)}, u32[]{:S(2)}) collective-permute-start(bf16[384,896]{1,0:T(8,128)(2,1)S(1)} %get-tuple-element.60), channel_id=1, source_target_pairs={{12,0},{13,1},{14,2},{15,3},{0,4},{1,5},{2,6},{3,7},{4,8},{5,9},{6... | collective-permute-start | bytes 2064392 | tf_op jit(solution)/shard_map/ppermute | solution.py:23
  51.4 9.5 %collective-permute-start.15 = (bf16[384,384]{1,0:T(8,128)(2,1)S(1)}, bf16[384,384]{1,0:T(8,128)(2,1)S(1)}, u32[]{:S(2)}, u32[]{:S(2)}) collective-permute-start(bf16[384,384]{1,0:T(8,128)(2,1)S(1)} %cross.1.t0), channel_id=1, source_target_pairs={{2,0},{3,1},{0,2},{1,3},{6,4},{7,5},{4,6},{5,7},{10,8},{11,9},{8,1... | collective-permute-start | bytes 884744 | tf_op jit(solution)/shard_map/ppermute | solution.py:23
  56.8 4.1 %collective-permute-start.16 = (bf16[384,384]{1,0:T(8,128)(2,1)S(1)}, bf16[384,384]{1,0:T(8,128)(2,1)S(1)}, u32[]{:S(2)}, u32[]{:S(2)}) collective-permute-start(bf16[384,384]{1,0:T(8,128)(2,1)S(1)} %cross.1.t0), channel_id=1, source_target_pairs={{1,0},{0,1},{3,2},{2,3},{5,4},{4,5},{7,6},{6,7},{9,8},{8,9},{11,10... | collective-permute-start | bytes 884744 | tf_op jit(solution)/shard_map/ppermute | solution.py:23
  72.1 19.9 %collective-permute-start.23 = (bf16[320,896]{1,0:T(8,128)(2,1)S(1)}, bf16[320,896]{1,0:T(8,128)(2,1)S(1)}, u32[]{:S(2)}, u32[]{:S(2)}) collective-permute-start(bf16[320,896]{1,0:T(8,128)(2,1)S(1)} %get-tuple-element.68), channel_id=1, source_target_pairs={{4,0},{5,1},{6,2},{7,3},{8,4},{9,5},{10,6},{11,7},{12,8},{13,9},{1... | collective-permute-start | bytes 1720328 | tf_op jit(solution)/shard_map/ppermute | solution.py:23
  72.2 19.9 %collective-permute-start.26 = (bf16[320,896]{1,0:T(8,128)(2,1)S(1)}, bf16[320,896]{1,0:T(8,128)(2,1)S(1)}, u32[]{:S(2)}, u32[]{:S(2)}) collective-permute-start(bf16[320,896]{1,0:T(8,128)(2,1)S(1)} %get-tuple-element.68), channel_id=1, source_target_pairs={{16,0},{0,16},{17,1},{1,17},{18,2},{2,18},{19,3},{3,19},{20,4},{4,... | collective-permute-start | bytes 1720328 | tf_op jit(solution)/shard_map/ppermute | solution.py:44
  72.7 3.7 %collective-permute-start.20 = (f32[8,384]{1,0:T(8,128)S(1)}, f32[8,384]{1,0:T(8,128)S(1)}, u32[]{:S(2)}, u32[]{:S(2)}) collective-permute-start(f32[8,384]{1,0:T(8,128)S(1)} %get-tuple-element.64.s0), channel_id=1, source_target_pairs={{2,0},{3,1},{0,2},{1,3},{6,4},{7,5},{4,6},{5,7},{10,8},{11,9},{8,1... | collective-permute-start | bytes 36872 | tf_op jit(solution)/shard_map/ppermute | solution.py:23
  74.2 3.1 %collective-permute-start.21 = (f32[8,384]{1,0:T(8,128)S(1)}, f32[8,384]{1,0:T(8,128)S(1)}, u32[]{:S(2)}, u32[]{:S(2)}) collective-permute-start(f32[8,384]{1,0:T(8,128)S(1)} %get-tuple-element.64.s0), channel_id=1, source_target_pairs={{3,0},{2,1},{1,2},{0,3},{7,4},{6,5},{5,6},{4,7},{11,8},{10,9},{9,1... | collective-permute-start | bytes 36872 | tf_op jit(solution)/shard_map/ppermute | solution.py:23
  81.2 5.7 %collective-permute-start.24 = (bf16[192,224]{1,0:T(8,128)(2,1)S(1)}, bf16[192,224]{1,0:T(8,128)(2,1)S(1)}, u32[]{:S(2)}, u32[]{:S(2)}) collective-permute-start(bf16[192,224]{1,0:T(8,128)(2,1)S(1)} %get-tuple-element.70), channel_id=1, source_target_pairs={{2,0},{3,1},{0,2},{1,3},{6,4},{7,5},{4,6},{5,7},{10,8},{11,9},{8,1... | collective-permute-start | bytes 258056 | tf_op jit(solution)/shard_map/ppermute | solution.py:23
  81.8 6.6 %collective-permute-start.25 = (bf16[192,224]{1,0:T(8,128)(2,1)S(1)}, bf16[192,224]{1,0:T(8,128)(2,1)S(1)}, u32[]{:S(2)}, u32[]{:S(2)}) collective-permute-start(bf16[192,224]{1,0:T(8,128)(2,1)S(1)} %get-tuple-element.71), channel_id=1, source_target_pairs={{3,0},{2,1},{1,2},{0,3},{7,4},{6,5},{5,6},{4,7},{11,8},{10,9},{9,1... | collective-permute-start | bytes 258056 | tf_op jit(solution)/shard_map/ppermute | solution.py:23
  82.7 8.6 %collective-permute-start.27 = (bf16[80,896]{1,0:T(8,128)(2,1)S(1)}, bf16[80,896]{1,0:T(8,128)(2,1)S(1)}, u32[]{:S(2)}, u32[]{:S(2)}) collective-permute-start(bf16[80,896]{1,0:T(8,128)(2,1)S(1)} %get-tuple-element.73), channel_id=1, source_target_pairs={{4,0},{5,1},{6,2},{7,3},{8,4},{9,5},{10,6},{11,7},{12,8},{13,9},{1... | collective-permute-start | bytes 430088 | tf_op jit(solution)/shard_map/ppermute | solution.py:23
  86.9 5.1 %collective-permute-start.28 = (bf16[80,896]{1,0:T(8,128)(2,1)S(1)}, bf16[80,896]{1,0:T(8,128)(2,1)S(1)}, u32[]{:S(2)}, u32[]{:S(2)}) collective-permute-start(bf16[80,896]{1,0:T(8,128)(2,1)S(1)} %get-tuple-element.73), channel_id=1, source_target_pairs={{16,0},{0,16},{17,1},{1,17},{18,2},{2,18},{19,3},{3,19},{20,4},{4,... | collective-permute-start | bytes 430088 | tf_op jit(solution)/shard_map/ppermute | solution.py:44
  88.4 12.8 %collective-permute-start.30 = (bf16[192,896]{1,0:T(8,128)(2,1)S(1)}, bf16[192,896]{1,0:T(8,128)(2,1)S(1)}, u32[]{:S(2)}, u32[]{:S(2)}) collective-permute-start(bf16[192,896]{1,0:T(8,128)(2,1)S(1)} %get-tuple-element.79), channel_id=1, source_target_pairs={{12,0},{13,1},{14,2},{15,3},{0,4},{1,5},{2,6},{3,7},{4,8},{5,9},{6... | collective-permute-start | bytes 1032200 | tf_op jit(solution)/shard_map/ppermute | solution.py:23
  92.0 18.9 %collective-permute-start.36 = (bf16[192,896]{1,0:T(8,128)(2,1)S(1)}, bf16[192,896]{1,0:T(8,128)(2,1)S(1)}, u32[]{:S(2)}, u32[]{:S(2)}) collective-permute-start(bf16[192,896]{1,0:T(8,128)(2,1)S(1)} %pack.4), channel_id=1, source_target_pairs={{12,0},{13,1},{14,2},{15,3},{0,4},{1,5},{2,6},{3,7},{4,8},{5,9},{6... | collective-permute-start | bytes 1032200 | tf_op jit(solution)/shard_map/ppermute | solution.py:23
  97.6 5.7 %collective-permute-start.34 = (bf16[192,224]{1,0:T(8,128)(2,1)S(1)}, bf16[192,224]{1,0:T(8,128)(2,1)S(1)}, u32[]{:S(2)}, u32[]{:S(2)}) collective-permute-start(bf16[192,224]{1,0:T(8,128)(2,1)S(1)} %get-tuple-element.85), channel_id=1, source_target_pairs={{2,0},{3,1},{0,2},{1,3},{6,4},{7,5},{4,6},{5,7},{10,8},{11,9},{8,1... | collective-permute-start | bytes 258056 | tf_op jit(solution)/shard_map/ppermute | solution.py:23
  97.7 6.8 %collective-permute-start.35 = (bf16[192,224]{1,0:T(8,128)(2,1)S(1)}, bf16[192,224]{1,0:T(8,128)(2,1)S(1)}, u32[]{:S(2)}, u32[]{:S(2)}) collective-permute-start(bf16[192,224]{1,0:T(8,128)(2,1)S(1)} %get-tuple-element.86), channel_id=1, source_target_pairs={{3,0},{2,1},{1,2},{0,3},{7,4},{6,5},{5,6},{4,7},{11,8},{10,9},{9,1... | collective-permute-start | bytes 258056 | tf_op jit(solution)/shard_map/ppermute | solution.py:23
  102.2 3.2 %collective-permute-start.31 = (bf16[192,224]{1,0:T(8,128)(2,1)S(1)}, bf16[192,224]{1,0:T(8,128)(2,1)S(1)}, u32[]{:S(2)}, u32[]{:S(2)}) collective-permute-start(bf16[192,224]{1,0:T(8,128)(2,1)S(1)} %get-tuple-element.81), channel_id=1, source_target_pairs={{1,0},{0,1},{3,2},{2,3},{5,4},{4,5},{7,6},{6,7},{9,8},{8,9},{11,10... | collective-permute-start | bytes 258056 | tf_op jit(solution)/shard_map/ppermute | solution.py:23
  102.2 5.7 %collective-permute-start.32 = (bf16[192,224]{1,0:T(8,128)(2,1)S(1)}, bf16[192,224]{1,0:T(8,128)(2,1)S(1)}, u32[]{:S(2)}, u32[]{:S(2)}) collective-permute-start(bf16[192,224]{1,0:T(8,128)(2,1)S(1)} %get-tuple-element.82), channel_id=1, source_target_pairs={{2,0},{3,1},{0,2},{1,3},{6,4},{7,5},{4,6},{5,7},{10,8},{11,9},{8,1... | collective-permute-start | bytes 258056 | tf_op jit(solution)/shard_map/ppermute | solution.py:23
  103.3 5.8 %collective-permute-start.33 = (bf16[192,224]{1,0:T(8,128)(2,1)S(1)}, bf16[192,224]{1,0:T(8,128)(2,1)S(1)}, u32[]{:S(2)}, u32[]{:S(2)}) collective-permute-start(bf16[192,224]{1,0:T(8,128)(2,1)S(1)} %get-tuple-element.83), channel_id=1, source_target_pairs={{3,0},{2,1},{1,2},{0,3},{7,4},{6,5},{5,6},{4,7},{11,8},{10,9},{9,1... | collective-permute-start | bytes 258056 | tf_op jit(solution)/shard_map/ppermute | solution.py:23
  (13 other events, 76.2 us)

commit v7 on v6

--- a/solution.py
+++ b/solution.py
@@ -139,21 +139,24 @@
             near[k * rows : (k + 1) * rows, span] = tile.astype(BF16)
 
 
-def stage_kernel(clusters, own, side, core, across, units):
+def stage_kernel(clusters, own, side_a, core, across_a, units):
     rows = own.shape[0]
-    for i, block in enumerate((own, side, core, across)):
+    for i, block in enumerate((own, side_a, core, across_a)):
         place_units(clusters[i] * rows, block, units)
 
 
-def stage_seed_kernel(clusters, own, side, core, across, seed, units, stack):
-    stage_kernel(clusters, own, side, core, across, units)
+def stage_seed_kernel(clusters, own, side_a, core, across_a, seed, units, stack):
+    stage_kernel(clusters, own, side_a, core, across_a, units)
     unpack(seed, stack)
 
 
-def far_kernel(clusters, units, up_in, side_b, across_b, stack, up_units, far, sums):
+def far_kernel(clusters, units_in, up_in, side_b, across_b, stack, units, up_units, far, sums):
     rows = units.shape[0] // QUAD
+    half = rows // 2
     for i, block in ((1, side_b), (3, across_b)):
-        place_units((clusters[i] + 1) * rows - block.shape[0], block, up_units)
+        start = clusters[i] * rows + half
+        place_units(start, block.at[:half], units)
+        place_units(start, block.at[half:], up_units)
     for k in range(QUAD):
         here = slice(k * rows, (k + 1) * rows)
         for first in range(0, k + 1, 2):
@@ -356,45 +359,46 @@
 
     half_rows = rows // 2
 
-    side = from_side(embeddings)
     own_up = from_up(embeddings)
+    side_a = from_side(embeddings[:half_rows])
     seed, *pieces = call(seed_kernel, "seed", (scalars, labels), (packed, piece, piece, piece))
     received = exchange(pieces)
     own_core = from_core(embeddings)
     cross_own = [from_group(after(embeddings, seed), step) for step in steps]
-    up_side_a = from_up(side[:half_rows])
-    side_b = from_side(after(own_up[half_rows:], received[1:]))
+    up_side_a = from_up(side_a)
+    late = jnp.concatenate([after(embeddings, side_a)[half_rows:], own_up[half_rows:]])
+    side_b = from_side(after(late, received))
     received[0] = after(received[0], own_up)
     packed_seed = call(pack_kernel, "pack", (scalars, seed, *received), packed)
     seed_up = from_up(packed_seed)
-    seed_cross = [from_group(after(packed_seed, up_side_a), step) for step in steps]
-    cross0 = call(
-        functools.partial(cross_kernel, weight), "cross", (embeddings, *cross_own), like((len(steps) * rows, rows), BF16)
-    )
-    across = from_core(side)
+    across_a = from_core(side_a)
     unit_stack = like((QUAD * rows, depth), BF16)
     units, seed_stack = call(
         stage_seed_kernel,
         "stage_own",
-        (clusters, embeddings, side, own_core, across, packed_seed),
+        (clusters, embeddings, side_a, own_core, across_a, packed_seed),
         (unit_stack, like((QUAD * rows, classes // QUAD), BF16)),
     )
-    side_b = after(side_b, (cross0, units, up_side_a))
+    seed_cross = [from_group(after(packed_seed, (cross_own, units)), step) for step in steps]
+    side_b = after(side_b, (units, up_side_a))
     across_b = from_core(side_b)
     up_core, up_across_a = from_core(own_up), from_core(up_side_a)
     up_units = call(
         stage_kernel, "stage_up", (clusters, after(own_up, side_b), up_side_a, up_core, up_across_a), unit_stack
     )
-    cross0 = after(cross0, (side_b, seed_up, seed_cross))
-    cross1, cross2 = from_side(cross0), from_core(cross0)
-    _, far, sums = call(
+    units, _, far, sums = call(
         far_kernel,
         "far",
         (clusters, units, up_units, side_b, across_b, seed_stack),
-        (unit_stack, matrix, packed),
-        aliases={2: 0},
-    )
-    near = call(near_kernel, "near", (after(units, sums),), matrix)
+        (unit_stack, unit_stack, matrix, packed),
+        aliases={1: 0, 2: 1},
+    )
+    cross0 = call(
+        functools.partial(cross_kernel, weight), "cross", (after(embeddings, (sums, seed_up)), *cross_own), like((len(steps) * rows, rows), BF16)
+    )
+    cross0 = after(cross0, seed_cross)
+    cross1, cross2 = from_side(cross0), from_core(cross0)
+    near = call(near_kernel, "near", (units,), matrix)
     cross3 = from_core(after(cross1, near))
 
     sent = from_down(sums)

time: 113 us -> 109 us (0.965)
  starting transfers between devices: 36.4 us -> 32 us
  local copies, waits for them, and re-layouts: 4.75 us -> 6.33 us
    ppermute x33, starting transfers between devices: 31.1 us -> 27.2 us  [along_dev(): lax.ppermute(block, 'dev', [(source(i) % size, i) for i in range(size)])]
    ppermute x33, waiting for transfers between devices: 34.7 us -> 32.9 us  [along_dev(): lax.ppermute(block, 'dev', [(source(i) % size, i) for i in range(size)])]
    unnamed x16 -> x12, local copies, waits for them, and re-layouts: 3.04 us -> 4.32 us
  transfers between devices with their start and end apart: 37 -> 37, of which waited for: 15 -> 18; matrix products, arithmetic and copies ran while one was open for 2% -> 3% of each run, Pallas kernels for 29% -> 29%
where the time goes in v7:
time: 109 us
  waiting for transfers between devices  34.3 us (31%)
  Pallas kernels  34.2 us (31%)
  starting transfers between devices  32 us (29%)
  local copies, waits for them, and re-layouts  6.33 us (6%)
    ppermute x33, waiting for transfers between devices, along_dev(): lax.ppermute(block, 'dev', [(source(i) % size, i) for i in range(size)])  32.9 us
    pallas_call x15, Pallas kernels, call(): pl.pallas_call(kernel, in_specs=specs, out_shape=out_shape, scratch_shape...  30.8 us
    ppermute x33, starting transfers between devices, along_dev(): lax.ppermute(block, 'dev', [(source(i) % size, i) for i in range(size)])  27.2 us
    ppermute x4, starting transfers between devices, from_group(): lax.ppermute(block, 'grp', [((i + step) % size, i) for i in range(size)])  4.78 us
    unnamed x12, local copies, waits for them, and re-layouts  4.32 us
    pallas_call x2, Pallas kernels, finish(): pl.pallas_call(kernel, grid=(1,), in_specs=[spec(i, x) for i, x in enumer...  3.4 us
  transfers between devices with their start and end apart: 37, of which 18 were waited for; matrix products, arithmetic and copies ran while one was open for 3% of the time, Pallas kernels for 29%

profile of v7, /device:TPU:0, one launch (start us, length us, event | category | flops | bytes accessed | tf_op | source)
XLA Modules:
  0.0 108.7 jit_solution(432834153299416601)
XLA Ops:
  0.0 5.0 %collective-permute-start.4 = (bf16[384,768]{1,0:T(8,128)(2,1)}, bf16[384,768]{1,0:T(8,128)(2,1)S(1)}, u32[]{:S(2)}, u32[]{:S(2)}) collective-permute-start(bf16[384,768]{1,0:T(8,128)(2,1)} %own.2), channel_id=1, source_target_pairs={{4,0},{5,1},{6,2},{7,3},{8,4},{9,5},{10,6},{11,7},{12,8},{13,9},{1... | collective-permute-start | bytes 1769480 | tf_op jit(solution)/shard_map/ppermute | solution.py:23
  6.1 1.6 %collective-permute-start = (bf16[192,768]{1,0:T(8,128)(2,1)S(1)}, bf16[192,768]{1,0:T(8,128)(2,1)}, u32[]{:S(2)}, u32[]{:S(2)}) collective-permute-start(bf16[192,768]{1,0:T(8,128)(2,1)S(1)} %slice.9), channel_id=1, source_target_pairs={{2,0},{3,1},{0,2},{1,3},{6,4},{7,5},{4,6},{5,7},{10,8},{11,9},{8,1... | collective-permute-start | bytes 884744 | tf_op jit(solution)/shard_map/ppermute | solution.py:23
  11.1 1.4 %collective-permute-start.6 = (bf16[384,224]{1,0:T(8,128)(2,1)S(1)}, bf16[384,224]{1,0:T(8,128)(2,1)S(1)}, u32[]{:S(2)}, u32[]{:S(2)}) collective-permute-start(bf16[384,224]{1,0:T(8,128)(2,1)S(1)} %get-tuple-element.52), channel_id=1, source_target_pairs={{3,0},{2,1},{1,2},{0,3},{7,4},{6,5},{5,6},{4,7},{11,8},{10,9},{9,1... | collective-permute-start | bytes 516104 | tf_op jit(solution)/shard_map/ppermute | solution.py:23
  12.6 2.9 %collective-permute-done.side_a = bf16[192,768]{1,0:T(8,128)(2,1)} collective-permute-done((bf16[192,768]{1,0:T(8,128)(2,1)S(1)}, bf16[192,768]{1,0:T(8,128)(2,1)}, u32[]{:S(2)}, u32[]{:S(2)}) %collective-permute-start) | collective-permute-done | bytes 294944 | tf_op jit(solution)/shard_map/ppermute | solution.py:23
  16.4 1.5 %collective-permute-done.4.own = bf16[384,768]{1,0:T(8,128)(2,1)S(1)} collective-permute-done((bf16[384,768]{1,0:T(8,128)(2,1)}, bf16[384,768]{1,0:T(8,128)(2,1)S(1)}, u32[]{:S(2)}, u32[]{:S(2)}) %collective-permute-start.4) | collective-permute-done | bytes 589856 | tf_op jit(solution)/shard_map/ppermute | solution.py:23
  18.0 1.5 %collective-permute-start.13 = (bf16[384,768]{1,0:T(8,128)(2,1)}, bf16[384,768]{1,0:T(8,128)(2,1)S(1)}, u32[]{:S(2)}, u32[]{:S(2)}) collective-permute-start(bf16[384,768]{1,0:T(8,128)(2,1)} %own.2), channel_id=1, source_target_pairs={{16,0},{0,16},{17,1},{1,17},{18,2},{2,18},{19,3},{3,19},{20,4},{4,... | collective-permute-start | bytes 1769480 | tf_op jit(solution)/shard_map/ppermute | solution.py:44
  25.0 2.3 %collective-permute-start.8 = (bf16[192,768]{1,0:T(8,128)(2,1)}, bf16[192,768]{1,0:T(8,128)(2,1)S(1)}, u32[]{:S(2)}, u32[]{:S(2)}) collective-permute-start(bf16[192,768]{1,0:T(8,128)(2,1)} %collective-permute-done.side_a), channel_id=1, source_target_pairs={{4,0},{5,1},{6,2},{7,3},{8,4},{9,5},{10,6},{11,7},{12,8},{13,9},{1... | collective-permute-start | bytes 884744 | tf_op jit(solution)/shard_map/ppermute | solution.py:23
  30.4 2.1 %stage_own.1 = (bf16[1536,768]{1,0:T(8,128)(2,1)S(1)}, bf16[1536,224]{1,0:T(8,128)(2,1)S(1)}) custom-call(s32[4]{0:T(128)S(1)} %pad_add_fusion.1.clusters, bf16[384,768]{1,0:T(8,128)(2,1)S(1)} %copy-done, bf16[192,768]{1,0:T(8,128)(2,1)} %collective-permute-done.side_a, bf16[384,768]{1,0:T(8,128)(2,1)} %collective-permute-done.1.core, ...), custom_call_target="tpu_custom_call" | custom-call | tf_op jit(solution)/shard_map/stage_own/pallas_call | solution.py:59
  32.5 1.5 %collective-permute-start.14 = (bf16[384,896]{1,0:T(8,128)(2,1)S(1)}, bf16[384,896]{1,0:T(8,128)(2,1)S(1)}, u32[]{:S(2)}, u32[]{:S(2)}) collective-permute-start(bf16[384,896]{1,0:T(8,128)(2,1)S(1)} %pack.3.seed.own), channel_id=1, source_target_pairs={{16,0},{0,16},{17,1},{1,17},{18,2},{2,18},{19,3},{3,19},{20,4},{4,... | collective-permute-start | bytes 2064392 | tf_op jit(solution)/shard_map/ppermute | solution.py:44
  35.1 4.1 %collective-permute-done.7.side_b = bf16[384,768]{1,0:T(8,128)(2,1)S(1)} collective-permute-done((bf16[384,768]{1,0:T(8,128)(2,1)}, bf16[384,768]{1,0:T(8,128)(2,1)S(1)}, u32[]{:S(2)}, u32[]{:S(2)}) %collective-permute-start.7) | collective-permute-done | bytes 589856 | tf_op jit(solution)/shard_map/ppermute | solution.py:23
  39.8 1.9 %collective-permute-done.10.across_a = bf16[192,768]{1,0:T(8,128)(2,1)S(1)} collective-permute-done((bf16[192,768]{1,0:T(8,128)(2,1)S(1)}, bf16[192,768]{1,0:T(8,128)(2,1)S(1)}, u32[]{:S(2)}, u32[]{:S(2)}) %collective-permute-start.10) | collective-permute-done | bytes 294944 | tf_op jit(solution)/shard_map/ppermute | solution.py:23
  42.9 4.7 %far.1 = (bf16[1536,768]{1,0:T(8,128)(2,1)S(1)}, bf16[1536,768]{1,0:T(8,128)(2,1)S(1)}, bf16[1536,1536]{1,0:T(8,128)(2,1)S(1)}, bf16[384,896]{1,0:T(8,128)(2,1)S(1)}) custom-call(s32[4]{0:T(128)S(1)} %pad_add_fusion.1.clusters, bf16[1536,768]{1,0:T(8,128)(2,1)S(1)} %get-tuple-element.53.units_in, ...), custom_call_target="tpu_custom_call", output_to_operand_aliasing={{0}: (1, {}), {1}: (2, {})} | custom-call | tf_op jit(solution)/shard_map/far/pallas_call | solution.py:59
  47.9 1.8 %collective-permute-done.12.up.rest_2_ = bf16[384,896]{1,0:T(8,128)(2,1)S(1)} collective-permute-done((bf16[384,896]{1,0:T(8,128)(2,1)S(1)}, bf16[384,896]{1,0:T(8,128)(2,1)S(1)}, u32[]{:S(2)}, u32[]{:S(2)}) %collective-permute-start.12) | collective-permute-done | bytes 688160 | tf_op jit(solution)/shard_map/ppermute | solution.py:23
  51.0 3.9 %near.1 = bf16[1536,1536]{1,0:T(8,128)(2,1)S(1)} custom-call(bf16[1536,768]{1,0:T(8,128)(2,1)S(1)} %get-tuple-element.65.units), custom_call_target="tpu_custom_call" | custom-call | tf_op jit(solution)/shard_map/near/pallas_call | solution.py:59
  54.9 3.9 %collective-permute-done.15.t1 = bf16[384,384]{1,0:T(8,128)(2,1)S(1)} collective-permute-done((bf16[384,384]{1,0:T(8,128)(2,1)S(1)}, bf16[384,384]{1,0:T(8,128)(2,1)S(1)}, u32[]{:S(2)}, u32[]{:S(2)}) %collective-permute-start.15) | collective-permute-done | bytes 294944 | tf_op jit(solution)/shard_map/ppermute | solution.py:23
  58.8 1.6 %collective-permute-done.17.t3 = bf16[384,384]{1,0:T(8,128)(2,1)S(1)} collective-permute-done((bf16[384,384]{1,0:T(8,128)(2,1)S(1)}, bf16[384,384]{1,0:T(8,128)(2,1)S(1)}, u32[]{:S(2)}, u32[]{:S(2)}) %collective-permute-start.17) | collective-permute-done | bytes 294944 | tf_op jit(solution)/shard_map/ppermute | solution.py:23
  60.4 3.7 %gather.1.kept = f32[384,896]{1,0:T(8,128)S(1)} custom-call(s32[4]{0:T(128)S(1)} %pad_add_fusion.1.clusters, bf16[1536,1536]{1,0:T(8,128)(2,1)S(1)} %near.1, bf16[1536,1536]{1,0:T(8,128)(2,1)S(1)} %get-tuple-element.59.far, bf16[384,384]{1,0:T(8,128)(2,1)S(1)} %cross.1.t0, bf16[384,384]{1,0:T(8,128)(2,1)S(1)} %collective-permute-done.15.t1, ...), custom_call_target="tpu_custom_call" | custom-call | tf_op jit(solution)/shard_map/gather/pallas_call | solution.py:59
  64.0 3.1 %collective-permute-done.18.sent = bf16[384,896]{1,0:T(8,128)(2,1)S(1)} collective-permute-done((bf16[384,896]{1,0:T(8,128)(2,1)S(1)}, bf16[384,896]{1,0:T(8,128)(2,1)S(1)}, u32[]{:S(2)}, u32[]{:S(2)}) %collective-permute-start.18) | collective-permute-done | bytes 688160 | tf_op jit(solution)/shard_map/ppermute | solution.py:23
  71.9 1.8 %collective-permute-done.20.s2 = f32[8,384]{1,0:T(8,128)S(1)} collective-permute-done((f32[8,384]{1,0:T(8,128)S(1)}, f32[8,384]{1,0:T(8,128)S(1)}, u32[]{:S(2)}, u32[]{:S(2)}) %collective-permute-start.20) | collective-permute-done | bytes 12320 | tf_op jit(solution)/shard_map/ppermute | solution.py:23
  73.9 3.5 %mix.1 = (bf16[80,896]{1,0:T(8,128)(2,1)S(1)}, bf16[384,896]{1,0:T(8,128)(2,1)}, bf16[1536,224]{1,0:T(8,128)(2,1)S(1)}, bf16[192,896]{1,0:T(8,128)(2,1)S(1)}, bf...) custom-call(s32[2]{0:T(128)S(1)} %pad_add_fusion.scalars, ...), custom_call_target="tpu_custom_call" | custom-call | tf_op jit(solution)/shard_map/mix/pallas_call | solution.py:59
  79.7 1.4 %near_products.1.total_in = f32[1536,224]{1,0:T(8,128)S(1)} custom-call(bf16[1536,1536]{1,0:T(8,128)(2,1)S(1)} %near.1, bf16[1536,224]{1,0:T(8,128)(2,1)S(1)} %get-tuple-element.71.stack), custom_call_target="tpu_custom_call" | custom-call | tf_op jit(solution)/shard_map/near_products/pallas_call | solution.py:59
  81.1 2.1 %collective-permute-done.24.p2 = bf16[192,224]{1,0:T(8,128)(2,1)S(1)} collective-permute-done((bf16[192,224]{1,0:T(8,128)(2,1)S(1)}, bf16[192,224]{1,0:T(8,128)(2,1)S(1)}, u32[]{:S(2)}, u32[]{:S(2)}) %collective-permute-start.24) | collective-permute-done | bytes 86048 | tf_op jit(solution)/shard_map/ppermute | solution.py:23
  83.2 1.4 %collective-permute-start.28 = (bf16[80,896]{1,0:T(8,128)(2,1)S(1)}, bf16[80,896]{1,0:T(8,128)(2,1)S(1)}, u32[]{:S(2)}, u32[]{:S(2)}) collective-permute-start(bf16[80,896]{1,0:T(8,128)(2,1)S(1)} %get-tuple-element.77), channel_id=1, source_target_pairs={{16,0},{0,16},{17,1},{1,17},{18,2},{2,18},{19,3},{3,19},{20,4},{4,... | collective-permute-start | bytes 430088 | tf_op jit(solution)/shard_map/ppermute | solution.py:44
  84.5 1.5 %collective-permute-start.30 = (bf16[192,896]{1,0:T(8,128)(2,1)S(1)}, bf16[192,896]{1,0:T(8,128)(2,1)S(1)}, u32[]{:S(2)}, u32[]{:S(2)}) collective-permute-start(bf16[192,896]{1,0:T(8,128)(2,1)S(1)} %get-tuple-element.83), channel_id=1, source_target_pairs={{12,0},{13,1},{14,2},{15,3},{0,4},{1,5},{2,6},{3,7},{4,8},{5,9},{6... | collective-permute-start | bytes 1032200 | tf_op jit(solution)/shard_map/ppermute | solution.py:23
  86.9 1.4 %collective-permute-done.28.rest_4_ = bf16[80,896]{1,0:T(8,128)(2,1)S(1)} collective-permute-done((bf16[80,896]{1,0:T(8,128)(2,1)S(1)}, bf16[80,896]{1,0:T(8,128)(2,1)S(1)}, u32[]{:S(2)}, u32[]{:S(2)}) %collective-permute-start.28) | collective-permute-done | bytes 143392 | tf_op jit(solution)/shard_map/ppermute | solution.py:44
  88.3 2.0 %collective-permute-start.36 = (bf16[192,896]{1,0:T(8,128)(2,1)S(1)}, bf16[192,896]{1,0:T(8,128)(2,1)S(1)}, u32[]{:S(2)}, u32[]{:S(2)}) collective-permute-start(bf16[192,896]{1,0:T(8,128)(2,1)S(1)} %pack.4), channel_id=1, source_target_pairs={{12,0},{13,1},{14,2},{15,3},{0,4},{1,5},{2,6},{3,7},{4,8},{5,9},{6... | collective-permute-start | bytes 1032200 | tf_op jit(solution)/shard_map/ppermute | solution.py:23
  90.3 3.6 %gather_mixed.1 = (f32[1536,224]{1,0:T(8,128)S(1)}, f32[192,896]{1,0:T(8,128)S(1)}, bf16[192,896]{1,0:T(8,128)(2,1)S(1)}, bf16[192,224]{1,0:T(8,128)(2,1)S(1)}, ...) custom-call(s32[4]{0:T(128)S(1)} %pad_add_fusion.1.clusters, ...), custom_call_target="tpu_custom_call", output_to_operand_aliasing={{0}: (6, {})} | custom-call | tf_op jit(solution)/shard_map/gather_mixed/pallas_call | solution.py:59
  98.3 1.9 %collective-permute-start.32 = (bf16[192,224]{1,0:T(8,128)(2,1)S(1)}, bf16[192,224]{1,0:T(8,128)(2,1)S(1)}, u32[]{:S(2)}, u32[]{:S(2)}) collective-permute-start(bf16[192,224]{1,0:T(8,128)(2,1)S(1)} %get-tuple-element.86), channel_id=1, source_target_pairs={{2,0},{3,1},{0,2},{1,3},{6,4},{7,5},{4,6},{5,7},{10,8},{11,9},{8,1... | collective-permute-start | bytes 258056 | tf_op jit(solution)/shard_map/ppermute | solution.py:23
  101.8 2.1 %collective-permute-done.32.p2 = bf16[192,224]{1,0:T(8,128)(2,1)S(1)} collective-permute-done((bf16[192,224]{1,0:T(8,128)(2,1)S(1)}, bf16[192,224]{1,0:T(8,128)(2,1)S(1)}, u32[]{:S(2)}, u32[]{:S(2)}) %collective-permute-start.32) | collective-permute-done | bytes 86048 | tf_op jit(solution)/shard_map/ppermute | solution.py:23
  103.9 1.4 %collective-permute-done.33.p3 = bf16[192,224]{1,0:T(8,128)(2,1)S(1)} collective-permute-done((bf16[192,224]{1,0:T(8,128)(2,1)S(1)}, bf16[192,224]{1,0:T(8,128)(2,1)S(1)}, u32[]{:S(2)}, u32[]{:S(2)}) %collective-permute-start.33) | collective-permute-done | bytes 86048 | tf_op jit(solution)/shard_map/ppermute | solution.py:23
  105.3 1.9 %finish_b.1.out_b = bf16[384,896]{1,0:T(8,128)(2,1)} custom-call(s32[2]{0:T(128)S(1)} %pad_add_fusion.scalars, bf16[192,896]{1,0:T(8,128)(2,1)S(1)} %get-tuple-element.84.sums, bf16[192,224]{1,0:T(8,128)(2,1)S(1)} %collective-permute-done.31.p1, bf16[192,224]{1,0:T(8,128)(2,1)S(1)} %collective-permute-done.32.p2, ...), custom_call_target="tpu_custom_call" | custom-call | tf_op jit(solution)/shard_map/finish_b/pallas_call | solution.py:333
  107.1 1.5 %finish_a.1 = bf16[384,896]{1,0:T(8,128)(2,1)} custom-call(s32[2]{0:T(128)S(1)} %pad_add_fusion.scalars, bf16[384,896]{1,0:T(8,128)(2,1)} %finish_b.1.out_b, bf16[192,896]{1,0:T(8,128)(2,1)S(1)} %pack.5.kept, bf16[192,896]{1,0:T(8,128)(2,1)S(1)} %collective-permute-done.36.sent, ...), custom_call_target="tpu_custom_call", output_to_operand_aliasing={{}: (1, {})} | custom-call | tf_op jit(solution)/shard_map/finish_a/pallas_call | solution.py:333
  (77 shorter events, 31.9 us)
Async XLA Ops:
  0.0 18.0 %collective-permute-start.4 = (bf16[384,768]{1,0:T(8,128)(2,1)}, bf16[384,768]{1,0:T(8,128)(2,1)S(1)}, u32[]{:S(2)}, u32[]{:S(2)}) collective-permute-start(bf16[384,768]{1,0:T(8,128)(2,1)} %own.2), channel_id=1, source_target_pairs={{4,0},{5,1},{6,2},{7,3},{8,4},{9,5},{10,6},{11,7},{12,8},{13,9},{1... | collective-permute-start | bytes 1769480 | tf_op jit(solution)/shard_map/ppermute | solution.py:23
  6.1 9.4 %collective-permute-start = (bf16[192,768]{1,0:T(8,128)(2,1)S(1)}, bf16[192,768]{1,0:T(8,128)(2,1)}, u32[]{:S(2)}, u32[]{:S(2)}) collective-permute-start(bf16[192,768]{1,0:T(8,128)(2,1)S(1)} %slice.9), channel_id=1, source_target_pairs={{2,0},{3,1},{0,2},{1,3},{6,4},{7,5},{4,6},{5,7},{10,8},{11,9},{8,1... | collective-permute-start | bytes 884744 | tf_op jit(solution)/shard_map/ppermute | solution.py:23
  10.6 9.7 %collective-permute-start.3 = (bf16[384,224]{1,0:T(8,128)(2,1)S(1)}, bf16[384,224]{1,0:T(8,128)(2,1)S(1)}, u32[]{:S(2)}, u32[]{:S(2)}) collective-permute-start(bf16[384,224]{1,0:T(8,128)(2,1)S(1)} %get-tuple-element.49), channel_id=1, source_target_pairs={{1,0},{0,1},{3,2},{2,3},{5,4},{4,5},{7,6},{6,7},{9,8},{8,9},{11,10... | collective-permute-start | bytes 516104 | tf_op jit(solution)/shard_map/ppermute | solution.py:23
  10.7 9.7 %collective-permute-start.5 = (bf16[384,224]{1,0:T(8,128)(2,1)S(1)}, bf16[384,224]{1,0:T(8,128)(2,1)S(1)}, u32[]{:S(2)}, u32[]{:S(2)}) collective-permute-start(bf16[384,224]{1,0:T(8,128)(2,1)S(1)} %get-tuple-element.51), channel_id=1, source_target_pairs={{2,0},{3,1},{0,2},{1,3},{6,4},{7,5},{4,6},{5,7},{10,8},{11,9},{8,1... | collective-permute-start | bytes 516104 | tf_op jit(solution)/shard_map/ppermute | solution.py:23
  11.1 11.1 %collective-permute-start.6 = (bf16[384,224]{1,0:T(8,128)(2,1)S(1)}, bf16[384,224]{1,0:T(8,128)(2,1)S(1)}, u32[]{:S(2)}, u32[]{:S(2)}) collective-permute-start(bf16[384,224]{1,0:T(8,128)(2,1)S(1)} %get-tuple-element.52), channel_id=1, source_target_pairs={{3,0},{2,1},{1,2},{0,3},{7,4},{6,5},{5,6},{4,7},{11,8},{10,9},{9,1... | collective-permute-start | bytes 516104 | tf_op jit(solution)/shard_map/ppermute | solution.py:23
  15.4 14.9 %collective-permute-start.1 = (bf16[384,768]{1,0:T(8,128)(2,1)}, bf16[384,768]{1,0:T(8,128)(2,1)}, u32[]{:S(2)}, u32[]{:S(2)}) collective-permute-start(bf16[384,768]{1,0:T(8,128)(2,1)} %own.2), channel_id=1, source_target_pairs={{1,0},{0,1},{3,2},{2,3},{5,4},{4,5},{7,6},{6,7},{9,8},{8,9},{11,10... | collective-permute-start | bytes 1769480 | tf_op jit(solution)/shard_map/ppermute | solution.py:23
  18.0 14.6 %collective-permute-start.13 = (bf16[384,768]{1,0:T(8,128)(2,1)}, bf16[384,768]{1,0:T(8,128)(2,1)S(1)}, u32[]{:S(2)}, u32[]{:S(2)}) collective-permute-start(bf16[384,768]{1,0:T(8,128)(2,1)} %own.2), channel_id=1, source_target_pairs={{16,0},{0,16},{17,1},{1,17},{18,2},{2,18},{19,3},{3,19},{20,4},{4,... | collective-permute-start | bytes 1769480 | tf_op jit(solution)/shard_map/ppermute | solution.py:44
  23.0 16.3 %collective-permute-start.7 = (bf16[384,768]{1,0:T(8,128)(2,1)}, bf16[384,768]{1,0:T(8,128)(2,1)S(1)}, u32[]{:S(2)}, u32[]{:S(2)}) collective-permute-start(bf16[384,768]{1,0:T(8,128)(2,1)} %pad_maximum_fusion), channel_id=1, source_target_pairs={{2,0},{3,1},{0,2},{1,3},{6,4},{7,5},{4,6},{5,7},{10,8},{11,9},{8,1... | collective-permute-start | bytes 1769480 | tf_op jit(solution)/shard_map/ppermute | solution.py:23
  23.7 6.6 %collective-permute-start.2 = (bf16[192,768]{1,0:T(8,128)(2,1)}, bf16[192,768]{1,0:T(8,128)(2,1)}, u32[]{:S(2)}, u32[]{:S(2)}) collective-permute-start(bf16[192,768]{1,0:T(8,128)(2,1)} %collective-permute-done.side_a), channel_id=1, source_target_pairs={{1,0},{0,1},{3,2},{2,3},{5,4},{4,5},{7,6},{6,7},{9,8},{8,9},{11,10... | collective-permute-start | bytes 884744 | tf_op jit(solution)/shard_map/ppermute | solution.py:23
  25.0 10.1 %collective-permute-start.8 = (bf16[192,768]{1,0:T(8,128)(2,1)}, bf16[192,768]{1,0:T(8,128)(2,1)S(1)}, u32[]{:S(2)}, u32[]{:S(2)}) collective-permute-start(bf16[192,768]{1,0:T(8,128)(2,1)} %collective-permute-done.side_a), channel_id=1, source_target_pairs={{4,0},{5,1},{6,2},{7,3},{8,4},{9,5},{10,6},{11,7},{12,8},{13,9},{1... | collective-permute-start | bytes 884744 | tf_op jit(solution)/shard_map/ppermute | solution.py:23
  30.3 19.4 %collective-permute-start.12 = (bf16[384,896]{1,0:T(8,128)(2,1)S(1)}, bf16[384,896]{1,0:T(8,128)(2,1)S(1)}, u32[]{:S(2)}, u32[]{:S(2)}) collective-permute-start(bf16[384,896]{1,0:T(8,128)(2,1)S(1)} %pack.3.seed.own), channel_id=1, source_target_pairs={{4,0},{5,1},{6,2},{7,3},{8,4},{9,5},{10,6},{11,7},{12,8},{13,9},{1... | collective-permute-start | bytes 2064392 | tf_op jit(solution)/shard_map/ppermute | solution.py:23
  32.5 17.9 %collective-permute-start.14 = (bf16[384,896]{1,0:T(8,128)(2,1)S(1)}, bf16[384,896]{1,0:T(8,128)(2,1)S(1)}, u32[]{:S(2)}, u32[]{:S(2)}) collective-permute-start(bf16[384,896]{1,0:T(8,128)(2,1)S(1)} %pack.3.seed.own), channel_id=1, source_target_pairs={{16,0},{0,16},{17,1},{1,17},{18,2},{2,18},{19,3},{3,19},{20,4},{4,... | collective-permute-start | bytes 2064392 | tf_op jit(solution)/shard_map/ppermute | solution.py:44
  34.0 7.7 %collective-permute-start.9 = (bf16[384,768]{1,0:T(8,128)(2,1)S(1)}, bf16[384,768]{1,0:T(8,128)(2,1)S(1)}, u32[]{:S(2)}, u32[]{:S(2)}) collective-permute-start(bf16[384,768]{1,0:T(8,128)(2,1)S(1)} %collective-permute-done.4.own), channel_id=1, source_target_pairs={{1,0},{0,1},{3,2},{2,3},{5,4},{4,5},{7,6},{6,7},{9,8},{8,9},{11,10... | collective-permute-start | bytes 1769480 | tf_op jit(solution)/shard_map/ppermute | solution.py:23
  39.3 3.7 %collective-permute-start.11 = (bf16[384,768]{1,0:T(8,128)(2,1)S(1)}, bf16[384,768]{1,0:T(8,128)(2,1)S(1)}, u32[]{:S(2)}, u32[]{:S(2)}) collective-permute-start(bf16[384,768]{1,0:T(8,128)(2,1)S(1)} %collective-permute-done.7.side_b), channel_id=1, source_target_pairs={{1,0},{0,1},{3,2},{2,3},{5,4},{4,5},{7,6},{6,7},{9,8},{8,9},{11,10... | collective-permute-start | bytes 1769480 | tf_op jit(solution)/shard_map/ppermute | solution.py:23
  47.6 19.5 %collective-permute-start.18 = (bf16[384,896]{1,0:T(8,128)(2,1)S(1)}, bf16[384,896]{1,0:T(8,128)(2,1)S(1)}, u32[]{:S(2)}, u32[]{:S(2)}) collective-permute-start(bf16[384,896]{1,0:T(8,128)(2,1)S(1)} %get-tuple-element.60), channel_id=1, source_target_pairs={{12,0},{13,1},{14,2},{15,3},{0,4},{1,5},{2,6},{3,7},{4,8},{5,9},{6... | collective-permute-start | bytes 2064392 | tf_op jit(solution)/shard_map/ppermute | solution.py:23
  50.5 8.3 %collective-permute-start.15 = (bf16[384,384]{1,0:T(8,128)(2,1)S(1)}, bf16[384,384]{1,0:T(8,128)(2,1)S(1)}, u32[]{:S(2)}, u32[]{:S(2)}) collective-permute-start(bf16[384,384]{1,0:T(8,128)(2,1)S(1)} %cross.1.t0), channel_id=1, source_target_pairs={{2,0},{3,1},{0,2},{1,3},{6,4},{7,5},{4,6},{5,7},{10,8},{11,9},{8,1... | collective-permute-start | bytes 884744 | tf_op jit(solution)/shard_map/ppermute | solution.py:23
  51.0 7.8 %collective-permute-start.16 = (bf16[384,384]{1,0:T(8,128)(2,1)S(1)}, bf16[384,384]{1,0:T(8,128)(2,1)S(1)}, u32[]{:S(2)}, u32[]{:S(2)}) collective-permute-start(bf16[384,384]{1,0:T(8,128)(2,1)S(1)} %cross.1.t0), channel_id=1, source_target_pairs={{1,0},{0,1},{3,2},{2,3},{5,4},{4,5},{7,6},{6,7},{9,8},{8,9},{11,10... | collective-permute-start | bytes 884744 | tf_op jit(solution)/shard_map/ppermute | solution.py:23
  68.3 20.0 %collective-permute-start.23 = (bf16[320,896]{1,0:T(8,128)(2,1)S(1)}, bf16[320,896]{1,0:T(8,128)(2,1)S(1)}, u32[]{:S(2)}, u32[]{:S(2)}) collective-permute-start(bf16[320,896]{1,0:T(8,128)(2,1)S(1)} %get-tuple-element.72), channel_id=1, source_target_pairs={{4,0},{5,1},{6,2},{7,3},{8,4},{9,5},{10,6},{11,7},{12,8},{13,9},{1... | collective-permute-start | bytes 1720328 | tf_op jit(solution)/shard_map/ppermute | solution.py:23
  69.6 18.7 %collective-permute-start.26 = (bf16[320,896]{1,0:T(8,128)(2,1)S(1)}, bf16[320,896]{1,0:T(8,128)(2,1)S(1)}, u32[]{:S(2)}, u32[]{:S(2)}) collective-permute-start(bf16[320,896]{1,0:T(8,128)(2,1)S(1)} %get-tuple-element.72), channel_id=1, source_target_pairs={{16,0},{0,16},{17,1},{1,17},{18,2},{2,18},{19,3},{3,19},{20,4},{4,... | collective-permute-start | bytes 1720328 | tf_op jit(solution)/shard_map/ppermute | solution.py:44
  70.0 3.7 %collective-permute-start.20 = (f32[8,384]{1,0:T(8,128)S(1)}, f32[8,384]{1,0:T(8,128)S(1)}, u32[]{:S(2)}, u32[]{:S(2)}) collective-permute-start(f32[8,384]{1,0:T(8,128)S(1)} %get-tuple-element.68.s0), channel_id=1, source_target_pairs={{2,0},{3,1},{0,2},{1,3},{6,4},{7,5},{4,6},{5,7},{10,8},{11,9},{8,1... | collective-permute-start | bytes 36872 | tf_op jit(solution)/shard_map/ppermute | solution.py:23
  70.8 3.1 %collective-permute-start.21 = (f32[8,384]{1,0:T(8,128)S(1)}, f32[8,384]{1,0:T(8,128)S(1)}, u32[]{:S(2)}, u32[]{:S(2)}) collective-permute-start(f32[8,384]{1,0:T(8,128)S(1)} %get-tuple-element.68.s0), channel_id=1, source_target_pairs={{3,0},{2,1},{1,2},{0,3},{7,4},{6,5},{5,6},{4,7},{11,8},{10,9},{9,1... | collective-permute-start | bytes 36872 | tf_op jit(solution)/shard_map/ppermute | solution.py:23
  77.8 5.4 %collective-permute-start.24 = (bf16[192,224]{1,0:T(8,128)(2,1)S(1)}, bf16[192,224]{1,0:T(8,128)(2,1)S(1)}, u32[]{:S(2)}, u32[]{:S(2)}) collective-permute-start(bf16[192,224]{1,0:T(8,128)(2,1)S(1)} %get-tuple-element.74), channel_id=1, source_target_pairs={{2,0},{3,1},{0,2},{1,3},{6,4},{7,5},{4,6},{5,7},{10,8},{11,9},{8,1... | collective-permute-start | bytes 258056 | tf_op jit(solution)/shard_map/ppermute | solution.py:23
  79.1 5.4 %collective-permute-start.25 = (bf16[192,224]{1,0:T(8,128)(2,1)S(1)}, bf16[192,224]{1,0:T(8,128)(2,1)S(1)}, u32[]{:S(2)}, u32[]{:S(2)}) collective-permute-start(bf16[192,224]{1,0:T(8,128)(2,1)S(1)} %get-tuple-element.75), channel_id=1, source_target_pairs={{3,0},{2,1},{1,2},{0,3},{7,4},{6,5},{5,6},{4,7},{11,8},{10,9},{9,1... | collective-permute-start | bytes 258056 | tf_op jit(solution)/shard_map/ppermute | solution.py:23
  79.3 7.6 %collective-permute-start.27 = (bf16[80,896]{1,0:T(8,128)(2,1)S(1)}, bf16[80,896]{1,0:T(8,128)(2,1)S(1)}, u32[]{:S(2)}, u32[]{:S(2)}) collective-permute-start(bf16[80,896]{1,0:T(8,128)(2,1)S(1)} %get-tuple-element.77), channel_id=1, source_target_pairs={{4,0},{5,1},{6,2},{7,3},{8,4},{9,5},{10,6},{11,7},{12,8},{13,9},{1... | collective-permute-start | bytes 430088 | tf_op jit(solution)/shard_map/ppermute | solution.py:23
  83.2 5.1 %collective-permute-start.28 = (bf16[80,896]{1,0:T(8,128)(2,1)S(1)}, bf16[80,896]{1,0:T(8,128)(2,1)S(1)}, u32[]{:S(2)}, u32[]{:S(2)}) collective-permute-start(bf16[80,896]{1,0:T(8,128)(2,1)S(1)} %get-tuple-element.77), channel_id=1, source_target_pairs={{16,0},{0,16},{17,1},{1,17},{18,2},{2,18},{19,3},{3,19},{20,4},{4,... | collective-permute-start | bytes 430088 | tf_op jit(solution)/shard_map/ppermute | solution.py:44
  84.5 12.7 %collective-permute-start.30 = (bf16[192,896]{1,0:T(8,128)(2,1)S(1)}, bf16[192,896]{1,0:T(8,128)(2,1)S(1)}, u32[]{:S(2)}, u32[]{:S(2)}) collective-permute-start(bf16[192,896]{1,0:T(8,128)(2,1)S(1)} %get-tuple-element.83), channel_id=1, source_target_pairs={{12,0},{13,1},{14,2},{15,3},{0,4},{1,5},{2,6},{3,7},{4,8},{5,9},{6... | collective-permute-start | bytes 1032200 | tf_op jit(solution)/shard_map/ppermute | solution.py:23
  88.3 18.8 %collective-permute-start.36 = (bf16[192,896]{1,0:T(8,128)(2,1)S(1)}, bf16[192,896]{1,0:T(8,128)(2,1)S(1)}, u32[]{:S(2)}, u32[]{:S(2)}) collective-permute-start(bf16[192,896]{1,0:T(8,128)(2,1)S(1)} %pack.4), channel_id=1, source_target_pairs={{12,0},{13,1},{14,2},{15,3},{0,4},{1,5},{2,6},{3,7},{4,8},{5,9},{6... | collective-permute-start | bytes 1032200 | tf_op jit(solution)/shard_map/ppermute | solution.py:23
  94.0 6.1 %collective-permute-start.34 = (bf16[192,224]{1,0:T(8,128)(2,1)S(1)}, bf16[192,224]{1,0:T(8,128)(2,1)S(1)}, u32[]{:S(2)}, u32[]{:S(2)}) collective-permute-start(bf16[192,224]{1,0:T(8,128)(2,1)S(1)} %get-tuple-element.89), channel_id=1, source_target_pairs={{2,0},{3,1},{0,2},{1,3},{6,4},{7,5},{4,6},{5,7},{10,8},{11,9},{8,1... | collective-permute-start | bytes 258056 | tf_op jit(solution)/shard_map/ppermute | solution.py:23
  95.3 5.5 %collective-permute-start.35 = (bf16[192,224]{1,0:T(8,128)(2,1)S(1)}, bf16[192,224]{1,0:T(8,128)(2,1)S(1)}, u32[]{:S(2)}, u32[]{:S(2)}) collective-permute-start(bf16[192,224]{1,0:T(8,128)(2,1)S(1)} %get-tuple-element.90), channel_id=1, source_target_pairs={{3,0},{2,1},{1,2},{0,3},{7,4},{6,5},{5,6},{4,7},{11,8},{10,9},{9,1... | collective-permute-start | bytes 258056 | tf_op jit(solution)/shard_map/ppermute | solution.py:23
  98.2 3.6 %collective-permute-start.31 = (bf16[192,224]{1,0:T(8,128)(2,1)S(1)}, bf16[192,224]{1,0:T(8,128)(2,1)S(1)}, u32[]{:S(2)}, u32[]{:S(2)}) collective-permute-start(bf16[192,224]{1,0:T(8,128)(2,1)S(1)} %get-tuple-element.85), channel_id=1, source_target_pairs={{1,0},{0,1},{3,2},{2,3},{5,4},{4,5},{7,6},{6,7},{9,8},{8,9},{11,10... | collective-permute-start | bytes 258056 | tf_op jit(solution)/shard_map/ppermute | solution.py:23
  98.3 5.6 %collective-permute-start.32 = (bf16[192,224]{1,0:T(8,128)(2,1)S(1)}, bf16[192,224]{1,0:T(8,128)(2,1)S(1)}, u32[]{:S(2)}, u32[]{:S(2)}) collective-permute-start(bf16[192,224]{1,0:T(8,128)(2,1)S(1)} %get-tuple-element.86), channel_id=1, source_target_pairs={{2,0},{3,1},{0,2},{1,3},{6,4},{7,5},{4,6},{5,7},{10,8},{11,9},{8,1... | collective-permute-start | bytes 258056 | tf_op jit(solution)/shard_map/ppermute | solution.py:23
  100.2 5.1 %collective-permute-start.33 = (bf16[192,224]{1,0:T(8,128)(2,1)S(1)}, bf16[192,224]{1,0:T(8,128)(2,1)S(1)}, u32[]{:S(2)}, u32[]{:S(2)}) collective-permute-start(bf16[192,224]{1,0:T(8,128)(2,1)S(1)} %get-tuple-element.87), channel_id=1, source_target_pairs={{3,0},{2,1},{1,2},{0,3},{7,4},{6,5},{5,6},{4,7},{11,8},{10,9},{9,1... | collective-permute-start | bytes 258056 | tf_op jit(solution)/shard_map/ppermute | solution.py:23
  (11 other events, 34.9 us)

commit v8 on v5

--- a/solution.py
+++ b/solution.py
@@ -14,7 +14,7 @@
 F32 = jnp.float32
 QUAD = 4
 INVALID = 1e38
-FACTORS = 16
+FACTORS = 8
 MB = 2**20
 
 
@@ -139,6 +139,12 @@
             near[k * rows : (k + 1) * rows, span] = tile.astype(BF16)
 
 
+def late_kernel(own, up, p1, p2, p3, late):
+    half = late.shape[0] // 2
+    late[:half, :] = own[half:, :]
+    late[half:, :] = up[half:, :]
+
+
 def stage_kernel(clusters, own, side_a, core, across_a, units):
     rows = own.shape[0]
     for i, block in enumerate((own, side_a, core, across_a)):
@@ -191,11 +197,10 @@
     rows = summed.shape[0]
     kept = tail.shape[0] - 2 * FACTORS
     factor = jnp.where(total > INVALID / 10, 0.0, lax.rsqrt(total / summed.shape[1] + 1e-06))
-    high = factor.astype(BF16)
+    high = factor.astype(BF16).astype(F32)
     tail[:kept, :] = summed[rows - kept :, :]
     tail[kept:, :] = jnp.zeros((2 * FACTORS, tail.shape[1]), BF16)
-    tail[kept : kept + FACTORS, :rows] = high
-    tail[kept + FACTORS :, :rows] = (factor - high.astype(F32)).astype(BF16)
+    tail[kept:, :rows] = jnp.concatenate([high, factor - high]).astype(BF16)
     mix(summed.at[: rows - kept], tail, seed, mixed)
     unpack(mixed, stack)
     scatter(far, stack, (out_a, out_b))
@@ -287,14 +292,15 @@
     head[...] = summed[: head.shape[0], :]
     square = total * total
     high = square.astype(BF16)
-    marks = lanes_of(FACTORS, total.shape[1])
+    marks = lanes_of(2 * FACTORS, total.shape[1])
     sums = sum(
         lax.dot_general(marks, part, (((1,), (1,)), ((), ())), preferred_element_type=F32)
         for part in (high, (square - high.astype(F32)).astype(BF16))
     )
     row = lax.broadcasted_iota(jnp.int32, sums.shape, 0)
     lane = lax.broadcasted_iota(jnp.int32, sums.shape, 1)
-    squares[...] = sums + jnp.where((row == scalars[0]) & (lane >= scalars[1]), INVALID, 0.0)
+    sums = sums + jnp.where((row == scalars[0]) & (lane >= scalars[1]), INVALID, 0.0)
+    squares[...] = sums[:FACTORS, :]
 
 
 def add_kernel(scalars, kept, sent, out, p1, p2, p3):
@@ -340,8 +346,10 @@
     own_core = from_core(embeddings)
     cross_own = [from_group(after(embeddings, seed), step) for step in steps]
     up_side_a = from_up(side_a)
-    late = jnp.concatenate([after(embeddings, side_a)[half_rows:], own_up[half_rows:]])
-    side_b = from_side(after(late, received[1:]))
+    late = call(
+        late_kernel, "late", (after(embeddings, side_a), own_up, *received), like(embeddings.shape, BF16)
+    )
+    side_b = from_side(late)
     received[0] = after(received[0], own_up)
     packed_seed = call(pack_kernel, "pack", (scalars, seed, *received), packed)
     seed_up = from_up(packed_seed)

time: 108 us -> 109 us (level)
  waiting for transfers between devices: 36.3 us -> 40.4 us
  local copies, waits for them, and re-layouts: 6.37 us -> 3.18 us
    ppermute x33, waiting for transfers between devices: 33.8 us -> 38.2 us  [along_dev(): lax.ppermute(block, 'dev', [(source(i) % size, i) for i in range(size)])]
    unnamed x12 -> x6, local copies, waits for them, and re-layouts: 4.32 us -> 2.17 us
    pallas_call x16 -> x17, Pallas kernels: 33.9 us -> 34.9 us  [call(): pl.pallas_call(kernel, in_specs=specs, out_shape=out_shape, scratch_shape...]
  transfers between devices with their start and end apart: 37 -> 37, of which waited for: 21 -> 21; matrix products, arithmetic and copies ran while one was open for 3% -> 1% of each run, Pallas kernels for 28% -> 29%
where the time goes in v8:
time: 109 us
  waiting for transfers between devices  40.4 us (37%)
  Pallas kernels  34.9 us (32%)
  starting transfers between devices  29.1 us (27%)
  local copies, waits for them, and re-layouts  3.18 us (3%)
    ppermute x33, waiting for transfers between devices, along_dev(): lax.ppermute(block, 'dev', [(source(i) % size, i) for i in range(size)])  38.2 us
    pallas_call x17, Pallas kernels, call(): pl.pallas_call(kernel, in_specs=specs, out_shape=out_shape, scratch_shape...  34.9 us
    ppermute x33, starting transfers between devices, along_dev(): lax.ppermute(block, 'dev', [(source(i) % size, i) for i in range(size)])  24 us
    ppermute x4, starting transfers between devices, from_group(): lax.ppermute(block, 'grp', [((i + step) % size, i) for i in range(size)])  5.18 us
    ppermute x4, waiting for transfers between devices, from_group(): lax.ppermute(block, 'grp', [((i + step) % size, i) for i in range(size)])  2.27 us
  transfers between devices with their start and end apart: 37, of which 21 were waited for; matrix products, arithmetic and copies ran while one was open for 1% of the time, Pallas kernels for 29%

profile of v8, /device:TPU:0, one launch (start us, length us, event | category | flops | bytes accessed | tf_op | source)
XLA Modules:
  0.0 108.7 jit_solution(16606314424912758205)
XLA Ops:
  0.0 5.0 %collective-permute-start.4 = (bf16[384,768]{1,0:T(8,128)(2,1)}, bf16[384,768]{1,0:T(8,128)(2,1)S(1)}, u32[]{:S(2)}, u32[]{:S(2)}) collective-permute-start(bf16[384,768]{1,0:T(8,128)(2,1)} %own.4), channel_id=1, source_target_pairs={{4,0},{5,1},{6,2},{7,3},{8,4},{9,5},{10,6},{11,7},{12,8},{13,9},{1... | collective-permute-start | bytes 1769480 | tf_op jit(solution)/shard_map/ppermute | solution.py:23
  6.1 1.6 %collective-permute-start = (bf16[192,768]{1,0:T(8,128)(2,1)S(1)}, bf16[192,768]{1,0:T(8,128)(2,1)}, u32[]{:S(2)}, u32[]{:S(2)}) collective-permute-start(bf16[192,768]{1,0:T(8,128)(2,1)S(1)} %slice.3), channel_id=1, source_target_pairs={{2,0},{3,1},{0,2},{1,3},{6,4},{7,5},{4,6},{5,7},{10,8},{11,9},{8,1... | collective-permute-start | bytes 884744 | tf_op jit(solution)/shard_map/ppermute | solution.py:23
  11.1 1.4 %collective-permute-start.6 = (bf16[384,224]{1,0:T(8,128)(2,1)S(1)}, bf16[384,224]{1,0:T(8,128)(2,1)S(1)}, u32[]{:S(2)}, u32[]{:S(2)}) collective-permute-start(bf16[384,224]{1,0:T(8,128)(2,1)S(1)} %get-tuple-element.49), channel_id=1, source_target_pairs={{3,0},{2,1},{1,2},{0,3},{7,4},{6,5},{5,6},{4,7},{11,8},{10,9},{9,1... | collective-permute-start | bytes 516104 | tf_op jit(solution)/shard_map/ppermute | solution.py:23
  12.6 2.9 %collective-permute-done.side_a = bf16[192,768]{1,0:T(8,128)(2,1)} collective-permute-done((bf16[192,768]{1,0:T(8,128)(2,1)S(1)}, bf16[192,768]{1,0:T(8,128)(2,1)}, u32[]{:S(2)}, u32[]{:S(2)}) %collective-permute-start) | collective-permute-done | bytes 294944 | tf_op jit(solution)/shard_map/ppermute | solution.py:23
  15.4 1.5 %collective-permute-start.8 = (bf16[384,768]{1,0:T(8,128)(2,1)}, bf16[384,768]{1,0:T(8,128)(2,1)}, u32[]{:S(2)}, u32[]{:S(2)}) collective-permute-start(bf16[384,768]{1,0:T(8,128)(2,1)} %own.4), channel_id=1, source_target_pairs={{16,0},{0,16},{17,1},{1,17},{18,2},{2,18},{19,3},{3,19},{20,4},{4,... | collective-permute-start | bytes 1769480 | tf_op jit(solution)/shard_map/ppermute | solution.py:44
  17.0 2.6 %collective-permute-done.5.p2 = bf16[384,224]{1,0:T(8,128)(2,1)S(1)} collective-permute-done((bf16[384,224]{1,0:T(8,128)(2,1)S(1)}, bf16[384,224]{1,0:T(8,128)(2,1)S(1)}, u32[]{:S(2)}, u32[]{:S(2)}) %collective-permute-start.5) | collective-permute-done | bytes 172064 | tf_op jit(solution)/shard_map/ppermute | solution.py:23
  19.5 2.7 %collective-permute-done.6.p3 = bf16[384,224]{1,0:T(8,128)(2,1)S(1)} collective-permute-done((bf16[384,224]{1,0:T(8,128)(2,1)S(1)}, bf16[384,224]{1,0:T(8,128)(2,1)S(1)}, u32[]{:S(2)}, u32[]{:S(2)}) %collective-permute-start.6) | collective-permute-done | bytes 172064 | tf_op jit(solution)/shard_map/ppermute | solution.py:23
  25.0 1.4 %collective-permute-start.2 = (bf16[192,768]{1,0:T(8,128)(2,1)}, bf16[192,768]{1,0:T(8,128)(2,1)}, u32[]{:S(2)}, u32[]{:S(2)}) collective-permute-start(bf16[192,768]{1,0:T(8,128)(2,1)} %collective-permute-done.side_a), channel_id=1, source_target_pairs={{1,0},{0,1},{3,2},{2,3},{5,4},{4,5},{7,6},{6,7},{9,8},{8,9},{11,10... | collective-permute-start | bytes 884744 | tf_op jit(solution)/shard_map/ppermute | solution.py:23
  29.4 1.8 %cross.1.t0 = bf16[384,384]{1,0:T(8,128)(2,1)S(1)} custom-call(bf16[384,768]{1,0:T(8,128)(2,1)S(1)} %copy-done.1, bf16[384,768]{1,0:T(8,128)(2,1)} %collective-permute-done.8.rest_0_), custom_call_target="tpu_custom_call" | custom-call | tf_op jit(solution)/shard_map/cross/pallas_call | solution.py:59
  31.2 1.6 %collective-permute-start.14 = (bf16[384,896]{1,0:T(8,128)(2,1)S(1)}, bf16[384,896]{1,0:T(8,128)(2,1)S(1)}, u32[]{:S(2)}, u32[]{:S(2)}) collective-permute-start(bf16[384,896]{1,0:T(8,128)(2,1)S(1)} %pack.3.seed.own), channel_id=1, source_target_pairs={{16,0},{0,16},{17,1},{1,17},{18,2},{2,18},{19,3},{3,19},{20,4},{4,... | collective-permute-start | bytes 2064392 | tf_op jit(solution)/shard_map/ppermute | solution.py:44
  32.7 2.1 %stage_own.1 = (bf16[1536,768]{1,0:T(8,128)(2,1)S(1)}, bf16[1536,224]{1,0:T(8,128)(2,1)S(1)}) custom-call(s32[4]{0:T(128)S(1)} %pad_add_fusion.1.clusters, bf16[384,768]{1,0:T(8,128)(2,1)S(1)} %copy-done.1, bf16[192,768]{1,0:T(8,128)(2,1)} %collective-permute-done.side_a, bf16[384,768]{1,0:T(8,128)(2,1)} %collective-permute-done.1.core, ...), custom_call_target="tpu_custom_call" | custom-call | tf_op jit(solution)/shard_map/stage_own/pallas_call | solution.py:59
  34.9 1.6 %collective-permute-done.9.side_a = bf16[192,768]{1,0:T(8,128)(2,1)S(1)} collective-permute-done((bf16[192,768]{1,0:T(8,128)(2,1)}, bf16[192,768]{1,0:T(8,128)(2,1)S(1)}, u32[]{:S(2)}, u32[]{:S(2)}) %collective-permute-start.9) | collective-permute-done | bytes 294944 | tf_op jit(solution)/shard_map/ppermute | solution.py:23
  36.5 4.1 %collective-permute-done.7.side_b = bf16[384,768]{1,0:T(8,128)(2,1)S(1)} collective-permute-done((bf16[384,768]{1,0:T(8,128)(2,1)}, bf16[384,768]{1,0:T(8,128)(2,1)S(1)}, u32[]{:S(2)}, u32[]{:S(2)}) %collective-permute-start.7) | collective-permute-done | bytes 589856 | tf_op jit(solution)/shard_map/ppermute | solution.py:23
  41.1 1.9 %collective-permute-done.11.across_a = bf16[192,768]{1,0:T(8,128)(2,1)S(1)} collective-permute-done((bf16[192,768]{1,0:T(8,128)(2,1)S(1)}, bf16[192,768]{1,0:T(8,128)(2,1)S(1)}, u32[]{:S(2)}, u32[]{:S(2)}) %collective-permute-start.11) | collective-permute-done | bytes 294944 | tf_op jit(solution)/shard_map/ppermute | solution.py:23
  44.3 4.7 %far.1 = (bf16[1536,768]{1,0:T(8,128)(2,1)S(1)}, bf16[1536,768]{1,0:T(8,128)(2,1)S(1)}, bf16[1536,1536]{1,0:T(8,128)(2,1)S(1)}, bf16[384,896]{1,0:T(8,128)(2,1)S(1)}) custom-call(s32[4]{0:T(128)S(1)} %pad_add_fusion.1.clusters, bf16[1536,768]{1,0:T(8,128)(2,1)S(1)} %get-tuple-element.50.units_in, ...), custom_call_target="tpu_custom_call", output_to_operand_aliasing={{0}: (1, {}), {1}: (2, {})} | custom-call | tf_op jit(solution)/shard_map/far/pallas_call | solution.py:59
  50.8 3.9 %near.1 = bf16[1536,1536]{1,0:T(8,128)(2,1)S(1)} custom-call(bf16[1536,768]{1,0:T(8,128)(2,1)S(1)} %get-tuple-element.58.units), custom_call_target="tpu_custom_call" | custom-call | tf_op jit(solution)/shard_map/near/pallas_call | solution.py:59
  54.7 3.7 %collective-permute-done.15.t1 = bf16[384,384]{1,0:T(8,128)(2,1)S(1)} collective-permute-done((bf16[384,384]{1,0:T(8,128)(2,1)S(1)}, bf16[384,384]{1,0:T(8,128)(2,1)S(1)}, u32[]{:S(2)}, u32[]{:S(2)}) %collective-permute-start.15) | collective-permute-done | bytes 294944 | tf_op jit(solution)/shard_map/ppermute | solution.py:23
  58.4 1.6 %collective-permute-done.17.t3 = bf16[384,384]{1,0:T(8,128)(2,1)S(1)} collective-permute-done((bf16[384,384]{1,0:T(8,128)(2,1)S(1)}, bf16[384,384]{1,0:T(8,128)(2,1)S(1)}, u32[]{:S(2)}, u32[]{:S(2)}) %collective-permute-start.17) | collective-permute-done | bytes 294944 | tf_op jit(solution)/shard_map/ppermute | solution.py:23
  60.0 3.7 %gather.1.kept = f32[384,896]{1,0:T(8,128)S(1)} custom-call(s32[4]{0:T(128)S(1)} %pad_add_fusion.1.clusters, bf16[1536,1536]{1,0:T(8,128)(2,1)S(1)} %near.1, bf16[1536,1536]{1,0:T(8,128)(2,1)S(1)} %get-tuple-element.56.far, bf16[384,384]{1,0:T(8,128)(2,1)S(1)} %cross.1.t0, bf16[384,384]{1,0:T(8,128)(2,1)S(1)} %collective-permute-done.15.t1, ...), custom_call_target="tpu_custom_call" | custom-call | tf_op jit(solution)/shard_map/gather/pallas_call | solution.py:59
  63.6 4.9 %collective-permute-done.18.sent = bf16[384,896]{1,0:T(8,128)(2,1)S(1)} collective-permute-done((bf16[384,896]{1,0:T(8,128)(2,1)S(1)}, bf16[384,896]{1,0:T(8,128)(2,1)S(1)}, u32[]{:S(2)}, u32[]{:S(2)}) %collective-permute-start.18) | collective-permute-done | bytes 688160 | tf_op jit(solution)/shard_map/ppermute | solution.py:23
  69.7 1.6 %collective-permute-start.26 = (bf16[320,896]{1,0:T(8,128)(2,1)S(1)}, bf16[320,896]{1,0:T(8,128)(2,1)S(1)}, u32[]{:S(2)}, u32[]{:S(2)}) collective-permute-start(bf16[320,896]{1,0:T(8,128)(2,1)S(1)} %get-tuple-element.66), channel_id=1, source_target_pairs={{16,0},{0,16},{17,1},{1,17},{18,2},{2,18},{19,3},{3,19},{20,4},{4,... | collective-permute-start | bytes 1720328 | tf_op jit(solution)/shard_map/ppermute | solution.py:44
  73.1 1.8 %collective-permute-done.20.s2 = f32[8,384]{1,0:T(8,128)S(1)} collective-permute-done((f32[8,384]{1,0:T(8,128)S(1)}, f32[8,384]{1,0:T(8,128)S(1)}, u32[]{:S(2)}, u32[]{:S(2)}) %collective-permute-start.20) | collective-permute-done | bytes 12320 | tf_op jit(solution)/shard_map/ppermute | solution.py:23
  75.2 3.5 %mix.1 = (bf16[80,896]{1,0:T(8,128)(2,1)S(1)}, bf16[384,896]{1,0:T(8,128)(2,1)}, bf16[1536,224]{1,0:T(8,128)(2,1)S(1)}, bf16[192,896]{1,0:T(8,128)(2,1)S(1)}, bf...) custom-call(s32[2]{0:T(128)S(1)} %pad_add_fusion.scalars, ...), custom_call_target="tpu_custom_call" | custom-call | tf_op jit(solution)/shard_map/mix/pallas_call | solution.py:59
  80.5 1.4 %near_products.1.total_in = f32[1536,224]{1,0:T(8,128)S(1)} custom-call(bf16[1536,1536]{1,0:T(8,128)(2,1)S(1)} %near.1, bf16[1536,224]{1,0:T(8,128)(2,1)S(1)} %get-tuple-element.65.stack), custom_call_target="tpu_custom_call" | custom-call | tf_op jit(solution)/shard_map/near_products/pallas_call | solution.py:59
  81.9 2.5 %collective-permute-done.24.p2 = bf16[192,224]{1,0:T(8,128)(2,1)S(1)} collective-permute-done((bf16[192,224]{1,0:T(8,128)(2,1)S(1)}, bf16[192,224]{1,0:T(8,128)(2,1)S(1)}, u32[]{:S(2)}, u32[]{:S(2)}) %collective-permute-start.24) | collective-permute-done | bytes 86048 | tf_op jit(solution)/shard_map/ppermute | solution.py:23
  85.4 2.0 %collective-permute-start.33 = (bf16[192,896]{1,0:T(8,128)(2,1)S(1)}, bf16[192,896]{1,0:T(8,128)(2,1)S(1)}, u32[]{:S(2)}, u32[]{:S(2)}) collective-permute-start(bf16[192,896]{1,0:T(8,128)(2,1)S(1)} %get-tuple-element.80), channel_id=1, source_target_pairs={{12,0},{13,1},{14,2},{15,3},{0,4},{1,5},{2,6},{3,7},{4,8},{5,9},{6... | collective-permute-start | bytes 1032200 | tf_op jit(solution)/shard_map/ppermute | solution.py:23
  89.5 2.0 %collective-permute-start.32 = (bf16[192,896]{1,0:T(8,128)(2,1)S(1)}, bf16[192,896]{1,0:T(8,128)(2,1)S(1)}, u32[]{:S(2)}, u32[]{:S(2)}) collective-permute-start(bf16[192,896]{1,0:T(8,128)(2,1)S(1)} %pack.4), channel_id=1, source_target_pairs={{12,0},{13,1},{14,2},{15,3},{0,4},{1,5},{2,6},{3,7},{4,8},{5,9},{6... | collective-permute-start | bytes 1032200 | tf_op jit(solution)/shard_map/ppermute | solution.py:23
  91.5 3.6 %gather_mixed.1 = (f32[1536,224]{1,0:T(8,128)S(1)}, f32[192,896]{1,0:T(8,128)S(1)}, bf16[192,896]{1,0:T(8,128)(2,1)S(1)}, bf16[192,224]{1,0:T(8,128)(2,1)S(1)}, ...) custom-call(s32[4]{0:T(128)S(1)} %pad_add_fusion.1.clusters, ...), custom_call_target="tpu_custom_call", output_to_operand_aliasing={{0}: (6, {})} | custom-call | tf_op jit(solution)/shard_map/gather_mixed/pallas_call | solution.py:59
  95.2 1.6 %collective-permute-start.30 = (bf16[192,224]{1,0:T(8,128)(2,1)S(1)}, bf16[192,224]{1,0:T(8,128)(2,1)S(1)}, u32[]{:S(2)}, u32[]{:S(2)}) collective-permute-start(bf16[192,224]{1,0:T(8,128)(2,1)S(1)} %get-tuple-element.76), channel_id=1, source_target_pairs={{2,0},{3,1},{0,2},{1,3},{6,4},{7,5},{4,6},{5,7},{10,8},{11,9},{8,1... | collective-permute-start | bytes 258056 | tf_op jit(solution)/shard_map/ppermute | solution.py:23
  102.9 1.9 %collective-permute-done.35.p2 = bf16[192,224]{1,0:T(8,128)(2,1)S(1)} collective-permute-done((bf16[192,224]{1,0:T(8,128)(2,1)S(1)}, bf16[192,224]{1,0:T(8,128)(2,1)S(1)}, u32[]{:S(2)}, u32[]{:S(2)}) %collective-permute-start.35) | collective-permute-done | bytes 86048 | tf_op jit(solution)/shard_map/ppermute | solution.py:23
  104.9 1.6 %collective-permute-done.36.p3 = bf16[192,224]{1,0:T(8,128)(2,1)S(1)} collective-permute-done((bf16[192,224]{1,0:T(8,128)(2,1)S(1)}, bf16[192,224]{1,0:T(8,128)(2,1)S(1)}, u32[]{:S(2)}, u32[]{:S(2)}) %collective-permute-start.36) | collective-permute-done | bytes 86048 | tf_op jit(solution)/shard_map/ppermute | solution.py:23
  106.4 2.2 %finish.1 = bf16[384,896]{1,0:T(8,128)(2,1)} custom-call(s32[2]{0:T(128)S(1)} %pad_add_fusion.scalars, bf16[192,896]{1,0:T(8,128)(2,1)S(1)} %pack.5.kept_a, bf16[192,896]{1,0:T(8,128)(2,1)S(1)} %collective-permute-done.32.sent_a, bf16[192,896]{1,0:T(8,128)(2,1)S(1)} %get-tuple-element.81.sums_b, bf16[192,224]{1,0:T(8,128)(2,1)S(1)} %collective-permute-done.34.p1, ...), custom_call_target="tpu_custom_call" | custom-call | tf_op jit(solution)/shard_map/finish/pallas_call | solution.py:59
  (68 shorter events, 27.5 us)
Async XLA Ops:
  0.0 22.3 %collective-permute-start.4 = (bf16[384,768]{1,0:T(8,128)(2,1)}, bf16[384,768]{1,0:T(8,128)(2,1)S(1)}, u32[]{:S(2)}, u32[]{:S(2)}) collective-permute-start(bf16[384,768]{1,0:T(8,128)(2,1)} %own.4), channel_id=1, source_target_pairs={{4,0},{5,1},{6,2},{7,3},{8,4},{9,5},{10,6},{11,7},{12,8},{13,9},{1... | collective-permute-start | bytes 1769480 | tf_op jit(solution)/shard_map/ppermute | solution.py:23
  6.1 9.4 %collective-permute-start = (bf16[192,768]{1,0:T(8,128)(2,1)S(1)}, bf16[192,768]{1,0:T(8,128)(2,1)}, u32[]{:S(2)}, u32[]{:S(2)}) collective-permute-start(bf16[192,768]{1,0:T(8,128)(2,1)S(1)} %slice.3), channel_id=1, source_target_pairs={{2,0},{3,1},{0,2},{1,3},{6,4},{7,5},{4,6},{5,7},{10,8},{11,9},{8,1... | collective-permute-start | bytes 884744 | tf_op jit(solution)/shard_map/ppermute | solution.py:23
  10.6 6.3 %collective-permute-start.3 = (bf16[384,224]{1,0:T(8,128)(2,1)S(1)}, bf16[384,224]{1,0:T(8,128)(2,1)S(1)}, u32[]{:S(2)}, u32[]{:S(2)}) collective-permute-start(bf16[384,224]{1,0:T(8,128)(2,1)S(1)} %get-tuple-element.46), channel_id=1, source_target_pairs={{1,0},{0,1},{3,2},{2,3},{5,4},{4,5},{7,6},{6,7},{9,8},{8,9},{11,10... | collective-permute-start | bytes 516104 | tf_op jit(solution)/shard_map/ppermute | solution.py:23
  10.7 8.9 %collective-permute-start.5 = (bf16[384,224]{1,0:T(8,128)(2,1)S(1)}, bf16[384,224]{1,0:T(8,128)(2,1)S(1)}, u32[]{:S(2)}, u32[]{:S(2)}) collective-permute-start(bf16[384,224]{1,0:T(8,128)(2,1)S(1)} %get-tuple-element.48), channel_id=1, source_target_pairs={{2,0},{3,1},{0,2},{1,3},{6,4},{7,5},{4,6},{5,7},{10,8},{11,9},{8,1... | collective-permute-start | bytes 516104 | tf_op jit(solution)/shard_map/ppermute | solution.py:23
  11.1 11.1 %collective-permute-start.6 = (bf16[384,224]{1,0:T(8,128)(2,1)S(1)}, bf16[384,224]{1,0:T(8,128)(2,1)S(1)}, u32[]{:S(2)}, u32[]{:S(2)}) collective-permute-start(bf16[384,224]{1,0:T(8,128)(2,1)S(1)} %get-tuple-element.49), channel_id=1, source_target_pairs={{3,0},{2,1},{1,2},{0,3},{7,4},{6,5},{5,6},{4,7},{11,8},{10,9},{9,1... | collective-permute-start | bytes 516104 | tf_op jit(solution)/shard_map/ppermute | solution.py:23
  15.4 13.5 %collective-permute-start.8 = (bf16[384,768]{1,0:T(8,128)(2,1)}, bf16[384,768]{1,0:T(8,128)(2,1)}, u32[]{:S(2)}, u32[]{:S(2)}) collective-permute-start(bf16[384,768]{1,0:T(8,128)(2,1)} %own.4), channel_id=1, source_target_pairs={{16,0},{0,16},{17,1},{1,17},{18,2},{2,18},{19,3},{3,19},{20,4},{4,... | collective-permute-start | bytes 1769480 | tf_op jit(solution)/shard_map/ppermute | solution.py:44
  17.0 15.8 %collective-permute-start.1 = (bf16[384,768]{1,0:T(8,128)(2,1)}, bf16[384,768]{1,0:T(8,128)(2,1)}, u32[]{:S(2)}, u32[]{:S(2)}) collective-permute-start(bf16[384,768]{1,0:T(8,128)(2,1)} %own.4), channel_id=1, source_target_pairs={{1,0},{0,1},{3,2},{2,3},{5,4},{4,5},{7,6},{6,7},{9,8},{8,9},{11,10... | collective-permute-start | bytes 1769480 | tf_op jit(solution)/shard_map/ppermute | solution.py:23
  24.2 16.4 %collective-permute-start.7 = (bf16[384,768]{1,0:T(8,128)(2,1)}, bf16[384,768]{1,0:T(8,128)(2,1)S(1)}, u32[]{:S(2)}, u32[]{:S(2)}) collective-permute-start(bf16[384,768]{1,0:T(8,128)(2,1)} %late.1), channel_id=1, source_target_pairs={{2,0},{3,1},{0,2},{1,3},{6,4},{7,5},{4,6},{5,7},{10,8},{11,9},{8,1... | collective-permute-start | bytes 1769480 | tf_op jit(solution)/shard_map/ppermute | solution.py:23
  25.0 6.2 %collective-permute-start.2 = (bf16[192,768]{1,0:T(8,128)(2,1)}, bf16[192,768]{1,0:T(8,128)(2,1)}, u32[]{:S(2)}, u32[]{:S(2)}) collective-permute-start(bf16[192,768]{1,0:T(8,128)(2,1)} %collective-permute-done.side_a), channel_id=1, source_target_pairs={{1,0},{0,1},{3,2},{2,3},{5,4},{4,5},{7,6},{6,7},{9,8},{8,9},{11,10... | collective-permute-start | bytes 884744 | tf_op jit(solution)/shard_map/ppermute | solution.py:23
  26.4 10.1 %collective-permute-start.9 = (bf16[192,768]{1,0:T(8,128)(2,1)}, bf16[192,768]{1,0:T(8,128)(2,1)S(1)}, u32[]{:S(2)}, u32[]{:S(2)}) collective-permute-start(bf16[192,768]{1,0:T(8,128)(2,1)} %collective-permute-done.side_a), channel_id=1, source_target_pairs={{4,0},{5,1},{6,2},{7,3},{8,4},{9,5},{10,6},{11,7},{12,8},{13,9},{1... | collective-permute-start | bytes 884744 | tf_op jit(solution)/shard_map/ppermute | solution.py:23
  28.9 21.4 %collective-permute-start.13 = (bf16[384,896]{1,0:T(8,128)(2,1)S(1)}, bf16[384,896]{1,0:T(8,128)(2,1)S(1)}, u32[]{:S(2)}, u32[]{:S(2)}) collective-permute-start(bf16[384,896]{1,0:T(8,128)(2,1)S(1)} %pack.3.seed.own), channel_id=1, source_target_pairs={{4,0},{5,1},{6,2},{7,3},{8,4},{9,5},{10,6},{11,7},{12,8},{13,9},{1... | collective-permute-start | bytes 2064392 | tf_op jit(solution)/shard_map/ppermute | solution.py:23
  31.2 19.1 %collective-permute-start.14 = (bf16[384,896]{1,0:T(8,128)(2,1)S(1)}, bf16[384,896]{1,0:T(8,128)(2,1)S(1)}, u32[]{:S(2)}, u32[]{:S(2)}) collective-permute-start(bf16[384,896]{1,0:T(8,128)(2,1)S(1)} %pack.3.seed.own), channel_id=1, source_target_pairs={{16,0},{0,16},{17,1},{1,17},{18,2},{2,18},{19,3},{3,19},{20,4},{4,... | collective-permute-start | bytes 2064392 | tf_op jit(solution)/shard_map/ppermute | solution.py:44
  32.7 10.3 %collective-permute-start.10 = (bf16[384,768]{1,0:T(8,128)(2,1)S(1)}, bf16[384,768]{1,0:T(8,128)(2,1)S(1)}, u32[]{:S(2)}, u32[]{:S(2)}) collective-permute-start(bf16[384,768]{1,0:T(8,128)(2,1)S(1)} %collective-permute-done.4.up.own), channel_id=1, source_target_pairs={{1,0},{0,1},{3,2},{2,3},{5,4},{4,5},{7,6},{6,7},{9,8},{8,9},{11,10... | collective-permute-start | bytes 1769480 | tf_op jit(solution)/shard_map/ppermute | solution.py:23
  40.6 3.7 %collective-permute-start.12 = (bf16[384,768]{1,0:T(8,128)(2,1)S(1)}, bf16[384,768]{1,0:T(8,128)(2,1)S(1)}, u32[]{:S(2)}, u32[]{:S(2)}) collective-permute-start(bf16[384,768]{1,0:T(8,128)(2,1)S(1)} %collective-permute-done.7.side_b), channel_id=1, source_target_pairs={{1,0},{0,1},{3,2},{2,3},{5,4},{4,5},{7,6},{6,7},{9,8},{8,9},{11,10... | collective-permute-start | bytes 1769480 | tf_op jit(solution)/shard_map/ppermute | solution.py:23
  49.0 19.5 %collective-permute-start.18 = (bf16[384,896]{1,0:T(8,128)(2,1)S(1)}, bf16[384,896]{1,0:T(8,128)(2,1)S(1)}, u32[]{:S(2)}, u32[]{:S(2)}) collective-permute-start(bf16[384,896]{1,0:T(8,128)(2,1)S(1)} %get-tuple-element.60), channel_id=1, source_target_pairs={{12,0},{13,1},{14,2},{15,3},{0,4},{1,5},{2,6},{3,7},{4,8},{5,9},{6... | collective-permute-start | bytes 2064392 | tf_op jit(solution)/shard_map/ppermute | solution.py:23
  50.3 8.1 %collective-permute-start.15 = (bf16[384,384]{1,0:T(8,128)(2,1)S(1)}, bf16[384,384]{1,0:T(8,128)(2,1)S(1)}, u32[]{:S(2)}, u32[]{:S(2)}) collective-permute-start(bf16[384,384]{1,0:T(8,128)(2,1)S(1)} %cross.1.t0), channel_id=1, source_target_pairs={{2,0},{3,1},{0,2},{1,3},{6,4},{7,5},{4,6},{5,7},{10,8},{11,9},{8,1... | collective-permute-start | bytes 884744 | tf_op jit(solution)/shard_map/ppermute | solution.py:23
  50.8 7.6 %collective-permute-start.16 = (bf16[384,384]{1,0:T(8,128)(2,1)S(1)}, bf16[384,384]{1,0:T(8,128)(2,1)S(1)}, u32[]{:S(2)}, u32[]{:S(2)}) collective-permute-start(bf16[384,384]{1,0:T(8,128)(2,1)S(1)} %cross.1.t0), channel_id=1, source_target_pairs={{1,0},{0,1},{3,2},{2,3},{5,4},{4,5},{7,6},{6,7},{9,8},{8,9},{11,10... | collective-permute-start | bytes 884744 | tf_op jit(solution)/shard_map/ppermute | solution.py:23
  69.7 19.9 %collective-permute-start.23 = (bf16[320,896]{1,0:T(8,128)(2,1)S(1)}, bf16[320,896]{1,0:T(8,128)(2,1)S(1)}, u32[]{:S(2)}, u32[]{:S(2)}) collective-permute-start(bf16[320,896]{1,0:T(8,128)(2,1)S(1)} %get-tuple-element.66), channel_id=1, source_target_pairs={{4,0},{5,1},{6,2},{7,3},{8,4},{9,5},{10,6},{11,7},{12,8},{13,9},{1... | collective-permute-start | bytes 1720328 | tf_op jit(solution)/shard_map/ppermute | solution.py:23
  69.7 19.8 %collective-permute-start.26 = (bf16[320,896]{1,0:T(8,128)(2,1)S(1)}, bf16[320,896]{1,0:T(8,128)(2,1)S(1)}, u32[]{:S(2)}, u32[]{:S(2)}) collective-permute-start(bf16[320,896]{1,0:T(8,128)(2,1)S(1)} %get-tuple-element.66), channel_id=1, source_target_pairs={{16,0},{0,16},{17,1},{1,17},{18,2},{2,18},{19,3},{3,19},{20,4},{4,... | collective-permute-start | bytes 1720328 | tf_op jit(solution)/shard_map/ppermute | solution.py:44
  71.3 3.7 %collective-permute-start.20 = (f32[8,384]{1,0:T(8,128)S(1)}, f32[8,384]{1,0:T(8,128)S(1)}, u32[]{:S(2)}, u32[]{:S(2)}) collective-permute-start(f32[8,384]{1,0:T(8,128)S(1)} %get-tuple-element.62.s0), channel_id=1, source_target_pairs={{2,0},{3,1},{0,2},{1,3},{6,4},{7,5},{4,6},{5,7},{10,8},{11,9},{8,1... | collective-permute-start | bytes 36872 | tf_op jit(solution)/shard_map/ppermute | solution.py:23
  72.0 3.1 %collective-permute-start.21 = (f32[8,384]{1,0:T(8,128)S(1)}, f32[8,384]{1,0:T(8,128)S(1)}, u32[]{:S(2)}, u32[]{:S(2)}) collective-permute-start(f32[8,384]{1,0:T(8,128)S(1)} %get-tuple-element.62.s0), channel_id=1, source_target_pairs={{3,0},{2,1},{1,2},{0,3},{7,4},{6,5},{5,6},{4,7},{11,8},{10,9},{9,1... | collective-permute-start | bytes 36872 | tf_op jit(solution)/shard_map/ppermute | solution.py:23
  79.1 5.3 %collective-permute-start.24 = (bf16[192,224]{1,0:T(8,128)(2,1)S(1)}, bf16[192,224]{1,0:T(8,128)(2,1)S(1)}, u32[]{:S(2)}, u32[]{:S(2)}) collective-permute-start(bf16[192,224]{1,0:T(8,128)(2,1)S(1)} %get-tuple-element.68), channel_id=1, source_target_pairs={{2,0},{3,1},{0,2},{1,3},{6,4},{7,5},{4,6},{5,7},{10,8},{11,9},{8,1... | collective-permute-start | bytes 258056 | tf_op jit(solution)/shard_map/ppermute | solution.py:23
  80.4 5.1 %collective-permute-start.25 = (bf16[192,224]{1,0:T(8,128)(2,1)S(1)}, bf16[192,224]{1,0:T(8,128)(2,1)S(1)}, u32[]{:S(2)}, u32[]{:S(2)}) collective-permute-start(bf16[192,224]{1,0:T(8,128)(2,1)S(1)} %get-tuple-element.69), channel_id=1, source_target_pairs={{3,0},{2,1},{1,2},{0,3},{7,4},{6,5},{5,6},{4,7},{11,8},{10,9},{9,1... | collective-permute-start | bytes 258056 | tf_op jit(solution)/shard_map/ppermute | solution.py:23
  80.5 7.7 %collective-permute-start.27 = (bf16[80,896]{1,0:T(8,128)(2,1)S(1)}, bf16[80,896]{1,0:T(8,128)(2,1)S(1)}, u32[]{:S(2)}, u32[]{:S(2)}) collective-permute-start(bf16[80,896]{1,0:T(8,128)(2,1)S(1)} %get-tuple-element.71), channel_id=1, source_target_pairs={{4,0},{5,1},{6,2},{7,3},{8,4},{9,5},{10,6},{11,7},{12,8},{13,9},{1... | collective-permute-start | bytes 430088 | tf_op jit(solution)/shard_map/ppermute | solution.py:23
  84.4 5.1 %collective-permute-start.28 = (bf16[80,896]{1,0:T(8,128)(2,1)S(1)}, bf16[80,896]{1,0:T(8,128)(2,1)S(1)}, u32[]{:S(2)}, u32[]{:S(2)}) collective-permute-start(bf16[80,896]{1,0:T(8,128)(2,1)S(1)} %get-tuple-element.71), channel_id=1, source_target_pairs={{16,0},{0,16},{17,1},{1,17},{18,2},{2,18},{19,3},{3,19},{20,4},{4,... | collective-permute-start | bytes 430088 | tf_op jit(solution)/shard_map/ppermute | solution.py:44
  85.4 12.7 %collective-permute-start.33 = (bf16[192,896]{1,0:T(8,128)(2,1)S(1)}, bf16[192,896]{1,0:T(8,128)(2,1)S(1)}, u32[]{:S(2)}, u32[]{:S(2)}) collective-permute-start(bf16[192,896]{1,0:T(8,128)(2,1)S(1)} %get-tuple-element.80), channel_id=1, source_target_pairs={{12,0},{13,1},{14,2},{15,3},{0,4},{1,5},{2,6},{3,7},{4,8},{5,9},{6... | collective-permute-start | bytes 1032200 | tf_op jit(solution)/shard_map/ppermute | solution.py:23
  89.5 16.9 %collective-permute-start.32 = (bf16[192,896]{1,0:T(8,128)(2,1)S(1)}, bf16[192,896]{1,0:T(8,128)(2,1)S(1)}, u32[]{:S(2)}, u32[]{:S(2)}) collective-permute-start(bf16[192,896]{1,0:T(8,128)(2,1)S(1)} %pack.4), channel_id=1, source_target_pairs={{12,0},{13,1},{14,2},{15,3},{0,4},{1,5},{2,6},{3,7},{4,8},{5,9},{6... | collective-permute-start | bytes 1032200 | tf_op jit(solution)/shard_map/ppermute | solution.py:23
  95.2 5.7 %collective-permute-start.30 = (bf16[192,224]{1,0:T(8,128)(2,1)S(1)}, bf16[192,224]{1,0:T(8,128)(2,1)S(1)}, u32[]{:S(2)}, u32[]{:S(2)}) collective-permute-start(bf16[192,224]{1,0:T(8,128)(2,1)S(1)} %get-tuple-element.76), channel_id=1, source_target_pairs={{2,0},{3,1},{0,2},{1,3},{6,4},{7,5},{4,6},{5,7},{10,8},{11,9},{8,1... | collective-permute-start | bytes 258056 | tf_op jit(solution)/shard_map/ppermute | solution.py:23
  96.8 5.3 %collective-permute-start.31 = (bf16[192,224]{1,0:T(8,128)(2,1)S(1)}, bf16[192,224]{1,0:T(8,128)(2,1)S(1)}, u32[]{:S(2)}, u32[]{:S(2)}) collective-permute-start(bf16[192,224]{1,0:T(8,128)(2,1)S(1)} %get-tuple-element.77), channel_id=1, source_target_pairs={{3,0},{2,1},{1,2},{0,3},{7,4},{6,5},{5,6},{4,7},{11,8},{10,9},{9,1... | collective-permute-start | bytes 258056 | tf_op jit(solution)/shard_map/ppermute | solution.py:23
  99.1 3.8 %collective-permute-start.34 = (bf16[192,224]{1,0:T(8,128)(2,1)S(1)}, bf16[192,224]{1,0:T(8,128)(2,1)S(1)}, u32[]{:S(2)}, u32[]{:S(2)}) collective-permute-start(bf16[192,224]{1,0:T(8,128)(2,1)S(1)} %get-tuple-element.82), channel_id=1, source_target_pairs={{1,0},{0,1},{3,2},{2,3},{5,4},{4,5},{7,6},{6,7},{9,8},{8,9},{11,10... | collective-permute-start | bytes 258056 | tf_op jit(solution)/shard_map/ppermute | solution.py:23
  99.2 5.7 %collective-permute-start.35 = (bf16[192,224]{1,0:T(8,128)(2,1)S(1)}, bf16[192,224]{1,0:T(8,128)(2,1)S(1)}, u32[]{:S(2)}, u32[]{:S(2)}) collective-permute-start(bf16[192,224]{1,0:T(8,128)(2,1)S(1)} %get-tuple-element.83), channel_id=1, source_target_pairs={{2,0},{3,1},{0,2},{1,3},{6,4},{7,5},{4,6},{5,7},{10,8},{11,9},{8,1... | collective-permute-start | bytes 258056 | tf_op jit(solution)/shard_map/ppermute | solution.py:23
  100.8 5.6 %collective-permute-start.36 = (bf16[192,224]{1,0:T(8,128)(2,1)S(1)}, bf16[192,224]{1,0:T(8,128)(2,1)S(1)}, u32[]{:S(2)}, u32[]{:S(2)}) collective-permute-start(bf16[192,224]{1,0:T(8,128)(2,1)S(1)} %get-tuple-element.84), channel_id=1, source_target_pairs={{3,0},{2,1},{1,2},{0,3},{7,4},{6,5},{5,6},{4,7},{11,8},{10,9},{9,1... | collective-permute-start | bytes 258056 | tf_op jit(solution)/shard_map/ppermute | solution.py:23
  (8 other events, 31.6 us)

commit v9 on v8

--- a/solution.py
+++ b/solution.py
@@ -139,9 +139,9 @@
             near[k * rows : (k + 1) * rows, span] = tile.astype(BF16)
 
 
-def late_kernel(own, up, p1, p2, p3, late):
+def late_kernel(own, up, side, p1, p2, p3, late):
     half = late.shape[0] // 2
-    late[:half, :] = own[half:, :]
+    late[:half, :] = own[...]
     late[half:, :] = up[half:, :]
 
 
@@ -347,7 +347,7 @@
     cross_own = [from_group(after(embeddings, seed), step) for step in steps]
     up_side_a = from_up(side_a)
     late = call(
-        late_kernel, "late", (after(embeddings, side_a), own_up, *received), like(embeddings.shape, BF16)
+        late_kernel, "late", (after(embeddings, side_a)[half_rows:], own_up, side_a, *received), like(embeddings.shape, BF16)
     )
     side_b = from_side(late)
     received[0] = after(received[0], own_up)
@@ -365,9 +365,9 @@
         (clusters, embeddings, side_a, own_core, across_a, packed_seed),
         (unit_stack, like((QUAD * rows, classes // QUAD), BF16)),
     )
-    side_b = after(side_b, (cross0, units, up_side_a))
+    up_core, up_across_a = from_core(own_up), from_core(up_side_a)
+    side_b = after(side_b, (cross0, units, up_across_a))
     across_b = from_core(side_b)
-    up_core, up_across_a = from_core(own_up), from_core(up_side_a)
     up_units = call(
         stage_kernel, "stage_up", (clusters, after(own_up, side_b), up_side_a, up_core, up_across_a), unit_stack
     )

time: 109 us -> 107 us (0.982)
  waiting for transfers between devices: 40.4 us -> 35.2 us
  starting transfers between devices: 29.1 us -> 31.6 us
    ppermute x33, waiting for transfers between devices: 38.2 us -> 29.7 us  [along_dev(): lax.ppermute(block, 'dev', [(source(i) % size, i) for i in range(size)])]
    ppermute x4, waiting for transfers between devices: 2.27 us -> 5.5 us  [from_group(): lax.ppermute(block, 'grp', [((i + step) % size, i) for i in range(size)])]
    ppermute x33, starting transfers between devices: 24 us -> 26.2 us  [along_dev(): lax.ppermute(block, 'dev', [(source(i) % size, i) for i in range(size)])]
  transfers between devices with their start and end apart: 37 -> 37, of which waited for: 21 -> 19; matrix products, arithmetic and copies ran while one was open for 1% -> 3% of each run, Pallas kernels for 29% -> 30%
where the time goes in v9:
time: 107 us
  Pallas kernels  35.3 us (33%)
  waiting for transfers between devices  35.2 us (33%)
  starting transfers between devices  31.6 us (30%)
  local copies, waits for them, and re-layouts  3.84 us (4%)
    pallas_call x17, Pallas kernels, call(): pl.pallas_call(kernel, in_specs=specs, out_shape=out_shape, scratch_shape...  35.3 us
    ppermute x33, waiting for transfers between devices, along_dev(): lax.ppermute(block, 'dev', [(source(i) % size, i) for i in range(size)])  29.7 us
    ppermute x33, starting transfers between devices, along_dev(): lax.ppermute(block, 'dev', [(source(i) % size, i) for i in range(size)])  26.2 us
    ppermute x4, waiting for transfers between devices, from_group(): lax.ppermute(block, 'grp', [((i + step) % size, i) for i in range(size)])  5.5 us
    ppermute x4, starting transfers between devices, from_group(): lax.ppermute(block, 'grp', [((i + step) % size, i) for i in range(size)])  5.41 us
  transfers between devices with their start and end apart: 37, of which 19 were waited for; matrix products, arithmetic and copies ran while one was open for 3% of the time, Pallas kernels for 30%

profile of v9, /device:TPU:0, one launch (start us, length us, event | category | flops | bytes accessed | tf_op | source)
XLA Modules:
  0.0 107.0 jit_solution(493879788889909067)
XLA Ops:
  0.0 5.0 %collective-permute-start.4 = (bf16[384,768]{1,0:T(8,128)(2,1)}, bf16[384,768]{1,0:T(8,128)(2,1)S(1)}, u32[]{:S(2)}, u32[]{:S(2)}) collective-permute-start(bf16[384,768]{1,0:T(8,128)(2,1)} %own.3), channel_id=1, source_target_pairs={{4,0},{5,1},{6,2},{7,3},{8,4},{9,5},{10,6},{11,7},{12,8},{13,9},{1... | collective-permute-start | bytes 1769480 | tf_op jit(solution)/shard_map/ppermute | solution.py:23
  5.0 1.7 %slice.6 = bf16[192,768]{1,0:T(8,128)(2,1)} slice(bf16[384,768]{1,0:T(8,128)(2,1)} %own.3), slice={[0:192], [0:768]} | slice | bytes 589824 | tf_op jit(solution)/shard_map/slice | solution.py:343
  6.8 1.5 %collective-permute-start = (bf16[192,768]{1,0:T(8,128)(2,1)}, bf16[192,768]{1,0:T(8,128)(2,1)S(1)}, u32[]{:S(2)}, u32[]{:S(2)}) collective-permute-start(bf16[192,768]{1,0:T(8,128)(2,1)} %slice.6), channel_id=1, source_target_pairs={{2,0},{3,1},{0,2},{1,3},{6,4},{7,5},{4,6},{5,7},{10,8},{11,9},{8,1... | collective-permute-start | bytes 884744 | tf_op jit(solution)/shard_map/ppermute | solution.py:23
  13.2 3.2 %collective-permute-done.side_a.side = bf16[192,768]{1,0:T(8,128)(2,1)S(1)} collective-permute-done((bf16[192,768]{1,0:T(8,128)(2,1)}, bf16[192,768]{1,0:T(8,128)(2,1)S(1)}, u32[]{:S(2)}, u32[]{:S(2)}) %collective-permute-start) | collective-permute-done | bytes 294944 | tf_op jit(solution)/shard_map/ppermute | solution.py:23
  16.4 1.5 %collective-permute-start.8 = (bf16[384,768]{1,0:T(8,128)(2,1)}, bf16[384,768]{1,0:T(8,128)(2,1)}, u32[]{:S(2)}, u32[]{:S(2)}) collective-permute-start(bf16[384,768]{1,0:T(8,128)(2,1)} %own.3), channel_id=1, source_target_pairs={{16,0},{0,16},{17,1},{1,17},{18,2},{2,18},{19,3},{3,19},{20,4},{4,... | collective-permute-start | bytes 1769480 | tf_op jit(solution)/shard_map/ppermute | solution.py:44
  19.0 1.6 %collective-permute-done.5.p2 = bf16[384,224]{1,0:T(8,128)(2,1)S(1)} collective-permute-done((bf16[384,224]{1,0:T(8,128)(2,1)S(1)}, bf16[384,224]{1,0:T(8,128)(2,1)S(1)}, u32[]{:S(2)}, u32[]{:S(2)}) %collective-permute-start.5) | collective-permute-done | bytes 172064 | tf_op jit(solution)/shard_map/ppermute | solution.py:23
  21.1 1.9 %collective-permute-done.6.p3 = bf16[384,224]{1,0:T(8,128)(2,1)S(1)} collective-permute-done((bf16[384,224]{1,0:T(8,128)(2,1)S(1)}, bf16[384,224]{1,0:T(8,128)(2,1)S(1)}, u32[]{:S(2)}, u32[]{:S(2)}) %collective-permute-start.6) | collective-permute-done | bytes 172064 | tf_op jit(solution)/shard_map/ppermute | solution.py:23
  24.8 1.4 %collective-permute-start.2 = (bf16[192,768]{1,0:T(8,128)(2,1)S(1)}, bf16[192,768]{1,0:T(8,128)(2,1)}, u32[]{:S(2)}, u32[]{:S(2)}) collective-permute-start(bf16[192,768]{1,0:T(8,128)(2,1)S(1)} %collective-permute-done.side_a.side), channel_id=1, source_target_pairs={{1,0},{0,1},{3,2},{2,3},{5,4},{4,5},{7,6},{6,7},{9,8},{8,9},{11,10... | collective-permute-start | bytes 884744 | tf_op jit(solution)/shard_map/ppermute | solution.py:23
  26.2 2.4 %collective-permute-done.9.side_a = bf16[192,768]{1,0:T(8,128)(2,1)} collective-permute-done((bf16[192,768]{1,0:T(8,128)(2,1)S(1)}, bf16[192,768]{1,0:T(8,128)(2,1)}, u32[]{:S(2)}, u32[]{:S(2)}) %collective-permute-start.9) | collective-permute-done | bytes 294944 | tf_op jit(solution)/shard_map/ppermute | solution.py:23
  29.7 2.3 %collective-permute-start.13 = (bf16[384,896]{1,0:T(8,128)(2,1)S(1)}, bf16[384,896]{1,0:T(8,128)(2,1)S(1)}, u32[]{:S(2)}, u32[]{:S(2)}) collective-permute-start(bf16[384,896]{1,0:T(8,128)(2,1)S(1)} %pack.3.seed.own), channel_id=1, source_target_pairs={{4,0},{5,1},{6,2},{7,3},{8,4},{9,5},{10,6},{11,7},{12,8},{13,9},{1... | collective-permute-start | bytes 2064392 | tf_op jit(solution)/shard_map/ppermute | solution.py:23
  31.9 1.8 %cross.1.t0 = bf16[384,384]{1,0:T(8,128)(2,1)S(1)} custom-call(bf16[384,768]{1,0:T(8,128)(2,1)S(1)} %copy-done, bf16[384,768]{1,0:T(8,128)(2,1)} %collective-permute-done.8.rest_0_), custom_call_target="tpu_custom_call" | custom-call | tf_op jit(solution)/shard_map/cross/pallas_call | solution.py:59
  34.6 2.0 %stage_own.1 = (bf16[1536,768]{1,0:T(8,128)(2,1)S(1)}, bf16[1536,224]{1,0:T(8,128)(2,1)S(1)}) custom-call(s32[4]{0:T(128)S(1)} %pad_add_fusion.1.clusters, bf16[384,768]{1,0:T(8,128)(2,1)S(1)} %copy-done, bf16[192,768]{1,0:T(8,128)(2,1)S(1)} %collective-permute-done.side_a.side, bf16[384,768]{1,0:T(8,128)(2,1)} %collective-permute-done.1.core, ...), custom_call_target="tpu_custom_call" | custom-call | tf_op jit(solution)/shard_map/stage_own/pallas_call | solution.py:59
  36.6 3.3 %collective-permute-done.7.side_b = bf16[384,768]{1,0:T(8,128)(2,1)S(1)} collective-permute-done((bf16[384,768]{1,0:T(8,128)(2,1)}, bf16[384,768]{1,0:T(8,128)(2,1)S(1)}, u32[]{:S(2)}, u32[]{:S(2)}) %collective-permute-start.7) | collective-permute-done | bytes 589856 | tf_op jit(solution)/shard_map/ppermute | solution.py:23
  40.3 1.7 %stage_up.1.up_in = bf16[1536,768]{1,0:T(8,128)(2,1)S(1)} custom-call(s32[4]{0:T(128)S(1)} %pad_add_fusion.1.clusters, bf16[384,768]{1,0:T(8,128)(2,1)S(1)} %collective-permute-done.4.up.own, bf16[192,768]{1,0:T(8,128)(2,1)} %collective-permute-done.9.side_a, bf16[384,768]{1,0:T(8,128)(2,1)S(1)} %collective-permute-done.11.core, ...), custom_call_target="tpu_custom_call" | custom-call | tf_op jit(solution)/shard_map/stage_up/pallas_call | solution.py:59
  42.1 4.7 %far.1 = (bf16[1536,768]{1,0:T(8,128)(2,1)S(1)}, bf16[1536,768]{1,0:T(8,128)(2,1)S(1)}, bf16[1536,1536]{1,0:T(8,128)(2,1)S(1)}, bf16[384,896]{1,0:T(8,128)(2,1)S(1)}) custom-call(s32[4]{0:T(128)S(1)} %pad_add_fusion.1.clusters, bf16[1536,768]{1,0:T(8,128)(2,1)S(1)} %get-tuple-element.50.units_in, ...), custom_call_target="tpu_custom_call", output_to_operand_aliasing={{0}: (1, {}), {1}: (2, {})} | custom-call | tf_op jit(solution)/shard_map/far/pallas_call | solution.py:59
  47.4 3.8 %collective-permute-done.14.rest_0_.rest_5_ = bf16[384,896]{1,0:T(8,128)(2,1)S(1)} collective-permute-done((bf16[384,896]{1,0:T(8,128)(2,1)S(1)}, bf16[384,896]{1,0:T(8,128)(2,1)S(1)}, u32[]{:S(2)}, u32[]{:S(2)}) %collective-permute-start.14) | collective-permute-done | bytes 688160 | tf_op jit(solution)/shard_map/ppermute | solution.py:44
  51.3 2.0 %collective-permute-start.15 = (bf16[384,384]{1,0:T(8,128)(2,1)S(1)}, bf16[384,384]{1,0:T(8,128)(2,1)S(1)}, u32[]{:S(2)}, u32[]{:S(2)}) collective-permute-start(bf16[384,384]{1,0:T(8,128)(2,1)S(1)} %cross.1.t0), channel_id=1, source_target_pairs={{2,0},{3,1},{0,2},{1,3},{6,4},{7,5},{4,6},{5,7},{10,8},{11,9},{8,1... | collective-permute-start | bytes 884744 | tf_op jit(solution)/shard_map/ppermute | solution.py:23
  53.3 3.9 %near.1 = bf16[1536,1536]{1,0:T(8,128)(2,1)S(1)} custom-call(bf16[1536,768]{1,0:T(8,128)(2,1)S(1)} %get-tuple-element.58.units), custom_call_target="tpu_custom_call" | custom-call | tf_op jit(solution)/shard_map/near/pallas_call | solution.py:59
  57.2 2.7 %collective-permute-done.15.t1 = bf16[384,384]{1,0:T(8,128)(2,1)S(1)} collective-permute-done((bf16[384,384]{1,0:T(8,128)(2,1)S(1)}, bf16[384,384]{1,0:T(8,128)(2,1)S(1)}, u32[]{:S(2)}, u32[]{:S(2)}) %collective-permute-start.15) | collective-permute-done | bytes 294944 | tf_op jit(solution)/shard_map/ppermute | solution.py:23
  59.9 1.6 %collective-permute-done.17.t3 = bf16[384,384]{1,0:T(8,128)(2,1)S(1)} collective-permute-done((bf16[384,384]{1,0:T(8,128)(2,1)S(1)}, bf16[384,384]{1,0:T(8,128)(2,1)S(1)}, u32[]{:S(2)}, u32[]{:S(2)}) %collective-permute-start.17) | collective-permute-done | bytes 294944 | tf_op jit(solution)/shard_map/ppermute | solution.py:23
  61.4 3.7 %gather.1.kept = f32[384,896]{1,0:T(8,128)S(1)} custom-call(s32[4]{0:T(128)S(1)} %pad_add_fusion.1.clusters, bf16[1536,1536]{1,0:T(8,128)(2,1)S(1)} %near.1, bf16[1536,1536]{1,0:T(8,128)(2,1)S(1)} %get-tuple-element.56.far, bf16[384,384]{1,0:T(8,128)(2,1)S(1)} %cross.1.t0, bf16[384,384]{1,0:T(8,128)(2,1)S(1)} %collective-permute-done.15.t1, ...), custom_call_target="tpu_custom_call" | custom-call | tf_op jit(solution)/shard_map/gather/pallas_call | solution.py:59
  67.6 1.6 %collective-permute-start.26 = (bf16[320,896]{1,0:T(8,128)(2,1)S(1)}, bf16[320,896]{1,0:T(8,128)(2,1)S(1)}, u32[]{:S(2)}, u32[]{:S(2)}) collective-permute-start(bf16[320,896]{1,0:T(8,128)(2,1)S(1)} %get-tuple-element.66), channel_id=1, source_target_pairs={{16,0},{0,16},{17,1},{1,17},{18,2},{2,18},{19,3},{3,19},{20,4},{4,... | collective-permute-start | bytes 1720328 | tf_op jit(solution)/shard_map/ppermute | solution.py:44
  71.0 1.8 %collective-permute-done.20.s2 = f32[8,384]{1,0:T(8,128)S(1)} collective-permute-done((f32[8,384]{1,0:T(8,128)S(1)}, f32[8,384]{1,0:T(8,128)S(1)}, u32[]{:S(2)}, u32[]{:S(2)}) %collective-permute-start.20) | collective-permute-done | bytes 12320 | tf_op jit(solution)/shard_map/ppermute | solution.py:23
  73.3 3.5 %mix.1 = (bf16[80,896]{1,0:T(8,128)(2,1)S(1)}, bf16[384,896]{1,0:T(8,128)(2,1)}, bf16[1536,224]{1,0:T(8,128)(2,1)S(1)}, bf16[192,896]{1,0:T(8,128)(2,1)S(1)}, bf...) custom-call(s32[2]{0:T(128)S(1)} %pad_add_fusion.scalars, ...), custom_call_target="tpu_custom_call" | custom-call | tf_op jit(solution)/shard_map/mix/pallas_call | solution.py:59
  80.4 2.4 %collective-permute-done.24.p2 = bf16[192,224]{1,0:T(8,128)(2,1)S(1)} collective-permute-done((bf16[192,224]{1,0:T(8,128)(2,1)S(1)}, bf16[192,224]{1,0:T(8,128)(2,1)S(1)}, u32[]{:S(2)}, u32[]{:S(2)}) %collective-permute-start.24) | collective-permute-done | bytes 86048 | tf_op jit(solution)/shard_map/ppermute | solution.py:23
  82.7 1.4 %collective-permute-start.28 = (bf16[80,896]{1,0:T(8,128)(2,1)S(1)}, bf16[80,896]{1,0:T(8,128)(2,1)S(1)}, u32[]{:S(2)}, u32[]{:S(2)}) collective-permute-start(bf16[80,896]{1,0:T(8,128)(2,1)S(1)} %get-tuple-element.71), channel_id=1, source_target_pairs={{16,0},{0,16},{17,1},{1,17},{18,2},{2,18},{19,3},{3,19},{20,4},{4,... | collective-permute-start | bytes 430088 | tf_op jit(solution)/shard_map/ppermute | solution.py:44
  86.2 1.6 %collective-permute-done.28.rest_4_ = bf16[80,896]{1,0:T(8,128)(2,1)S(1)} collective-permute-done((bf16[80,896]{1,0:T(8,128)(2,1)S(1)}, bf16[80,896]{1,0:T(8,128)(2,1)S(1)}, u32[]{:S(2)}, u32[]{:S(2)}) %collective-permute-start.28) | collective-permute-done | bytes 143392 | tf_op jit(solution)/shard_map/ppermute | solution.py:44
  87.8 2.0 %collective-permute-start.32 = (bf16[192,896]{1,0:T(8,128)(2,1)S(1)}, bf16[192,896]{1,0:T(8,128)(2,1)S(1)}, u32[]{:S(2)}, u32[]{:S(2)}) collective-permute-start(bf16[192,896]{1,0:T(8,128)(2,1)S(1)} %pack.4), channel_id=1, source_target_pairs={{12,0},{13,1},{14,2},{15,3},{0,4},{1,5},{2,6},{3,7},{4,8},{5,9},{6... | collective-permute-start | bytes 1032200 | tf_op jit(solution)/shard_map/ppermute | solution.py:23
  89.8 3.6 %gather_mixed.1 = (f32[1536,224]{1,0:T(8,128)S(1)}, f32[192,896]{1,0:T(8,128)S(1)}, bf16[192,896]{1,0:T(8,128)(2,1)S(1)}, bf16[192,224]{1,0:T(8,128)(2,1)S(1)}, ...) custom-call(s32[4]{0:T(128)S(1)} %pad_add_fusion.1.clusters, ...), custom_call_target="tpu_custom_call", output_to_operand_aliasing={{0}: (6, {})} | custom-call | tf_op jit(solution)/shard_map/gather_mixed/pallas_call | solution.py:59
  95.3 1.5 %collective-permute-done.33.sent = bf16[192,896]{1,0:T(8,128)(2,1)S(1)} collective-permute-done((bf16[192,896]{1,0:T(8,128)(2,1)S(1)}, bf16[192,896]{1,0:T(8,128)(2,1)S(1)}, u32[]{:S(2)}, u32[]{:S(2)}) %collective-permute-start.33) | collective-permute-done | bytes 344096 | tf_op jit(solution)/shard_map/ppermute | solution.py:23
  101.2 2.4 %collective-permute-done.35.p2 = bf16[192,224]{1,0:T(8,128)(2,1)S(1)} collective-permute-done((bf16[192,224]{1,0:T(8,128)(2,1)S(1)}, bf16[192,224]{1,0:T(8,128)(2,1)S(1)}, u32[]{:S(2)}, u32[]{:S(2)}) %collective-permute-start.35) | collective-permute-done | bytes 86048 | tf_op jit(solution)/shard_map/ppermute | solution.py:23
  104.8 2.2 %finish.1 = bf16[384,896]{1,0:T(8,128)(2,1)} custom-call(s32[2]{0:T(128)S(1)} %pad_add_fusion.scalars, bf16[192,896]{1,0:T(8,128)(2,1)S(1)} %pack.5.kept_a, bf16[192,896]{1,0:T(8,128)(2,1)S(1)} %collective-permute-done.32.sent_a, bf16[192,896]{1,0:T(8,128)(2,1)S(1)} %get-tuple-element.81.sums_b, bf16[192,224]{1,0:T(8,128)(2,1)S(1)} %collective-permute-done.34.p1, ...), custom_call_target="tpu_custom_call" | custom-call | tf_op jit(solution)/shard_map/finish/pallas_call | solution.py:59
  (67 shorter events, 28.5 us)
Async XLA Ops:
  0.0 22.9 %collective-permute-start.4 = (bf16[384,768]{1,0:T(8,128)(2,1)}, bf16[384,768]{1,0:T(8,128)(2,1)S(1)}, u32[]{:S(2)}, u32[]{:S(2)}) collective-permute-start(bf16[384,768]{1,0:T(8,128)(2,1)} %own.3), channel_id=1, source_target_pairs={{4,0},{5,1},{6,2},{7,3},{8,4},{9,5},{10,6},{11,7},{12,8},{13,9},{1... | collective-permute-start | bytes 1769480 | tf_op jit(solution)/shard_map/ppermute | solution.py:23
  6.8 9.6 %collective-permute-start = (bf16[192,768]{1,0:T(8,128)(2,1)}, bf16[192,768]{1,0:T(8,128)(2,1)S(1)}, u32[]{:S(2)}, u32[]{:S(2)}) collective-permute-start(bf16[192,768]{1,0:T(8,128)(2,1)} %slice.6), channel_id=1, source_target_pairs={{2,0},{3,1},{0,2},{1,3},{6,4},{7,5},{4,6},{5,7},{10,8},{11,9},{8,1... | collective-permute-start | bytes 884744 | tf_op jit(solution)/shard_map/ppermute | solution.py:23
  11.3 7.7 %collective-permute-start.3 = (bf16[384,224]{1,0:T(8,128)(2,1)S(1)}, bf16[384,224]{1,0:T(8,128)(2,1)S(1)}, u32[]{:S(2)}, u32[]{:S(2)}) collective-permute-start(bf16[384,224]{1,0:T(8,128)(2,1)S(1)} %get-tuple-element.46), channel_id=1, source_target_pairs={{1,0},{0,1},{3,2},{2,3},{5,4},{4,5},{7,6},{6,7},{9,8},{8,9},{11,10... | collective-permute-start | bytes 516104 | tf_op jit(solution)/shard_map/ppermute | solution.py:23
  11.3 9.3 %collective-permute-start.5 = (bf16[384,224]{1,0:T(8,128)(2,1)S(1)}, bf16[384,224]{1,0:T(8,128)(2,1)S(1)}, u32[]{:S(2)}, u32[]{:S(2)}) collective-permute-start(bf16[384,224]{1,0:T(8,128)(2,1)S(1)} %get-tuple-element.48), channel_id=1, source_target_pairs={{2,0},{3,1},{0,2},{1,3},{6,4},{7,5},{4,6},{5,7},{10,8},{11,9},{8,1... | collective-permute-start | bytes 516104 | tf_op jit(solution)/shard_map/ppermute | solution.py:23
  11.8 11.1 %collective-permute-start.6 = (bf16[384,224]{1,0:T(8,128)(2,1)S(1)}, bf16[384,224]{1,0:T(8,128)(2,1)S(1)}, u32[]{:S(2)}, u32[]{:S(2)}) collective-permute-start(bf16[384,224]{1,0:T(8,128)(2,1)S(1)} %get-tuple-element.49), channel_id=1, source_target_pairs={{3,0},{2,1},{1,2},{0,3},{7,4},{6,5},{5,6},{4,7},{11,8},{10,9},{9,1... | collective-permute-start | bytes 516104 | tf_op jit(solution)/shard_map/ppermute | solution.py:23
  16.4 13.2 %collective-permute-start.8 = (bf16[384,768]{1,0:T(8,128)(2,1)}, bf16[384,768]{1,0:T(8,128)(2,1)}, u32[]{:S(2)}, u32[]{:S(2)}) collective-permute-start(bf16[384,768]{1,0:T(8,128)(2,1)} %own.3), channel_id=1, source_target_pairs={{16,0},{0,16},{17,1},{1,17},{18,2},{2,18},{19,3},{3,19},{20,4},{4,... | collective-permute-start | bytes 1769480 | tf_op jit(solution)/shard_map/ppermute | solution.py:44
  19.0 15.7 %collective-permute-start.1 = (bf16[384,768]{1,0:T(8,128)(2,1)}, bf16[384,768]{1,0:T(8,128)(2,1)}, u32[]{:S(2)}, u32[]{:S(2)}) collective-permute-start(bf16[384,768]{1,0:T(8,128)(2,1)} %own.3), channel_id=1, source_target_pairs={{1,0},{0,1},{3,2},{2,3},{5,4},{4,5},{7,6},{6,7},{9,8},{8,9},{11,10... | collective-permute-start | bytes 1769480 | tf_op jit(solution)/shard_map/ppermute | solution.py:23
  20.6 7.9 %collective-permute-start.9 = (bf16[192,768]{1,0:T(8,128)(2,1)S(1)}, bf16[192,768]{1,0:T(8,128)(2,1)}, u32[]{:S(2)}, u32[]{:S(2)}) collective-permute-start(bf16[192,768]{1,0:T(8,128)(2,1)S(1)} %collective-permute-done.side_a.side), channel_id=1, source_target_pairs={{4,0},{5,1},{6,2},{7,3},{8,4},{9,5},{10,6},{11,7},{12,8},{13,9},{1... | collective-permute-start | bytes 884744 | tf_op jit(solution)/shard_map/ppermute | solution.py:23
  23.8 16.2 %collective-permute-start.7 = (bf16[384,768]{1,0:T(8,128)(2,1)}, bf16[384,768]{1,0:T(8,128)(2,1)S(1)}, u32[]{:S(2)}, u32[]{:S(2)}) collective-permute-start(bf16[384,768]{1,0:T(8,128)(2,1)} %late.1), channel_id=1, source_target_pairs={{2,0},{3,1},{0,2},{1,3},{6,4},{7,5},{4,6},{5,7},{10,8},{11,9},{8,1... | collective-permute-start | bytes 1769480 | tf_op jit(solution)/shard_map/ppermute | solution.py:23
  24.8 9.0 %collective-permute-start.2 = (bf16[192,768]{1,0:T(8,128)(2,1)S(1)}, bf16[192,768]{1,0:T(8,128)(2,1)}, u32[]{:S(2)}, u32[]{:S(2)}) collective-permute-start(bf16[192,768]{1,0:T(8,128)(2,1)S(1)} %collective-permute-done.side_a.side), channel_id=1, source_target_pairs={{1,0},{0,1},{3,2},{2,3},{5,4},{4,5},{7,6},{6,7},{9,8},{8,9},{11,10... | collective-permute-start | bytes 884744 | tf_op jit(solution)/shard_map/ppermute | solution.py:23
  28.6 8.1 %collective-permute-start.10 = (bf16[192,768]{1,0:T(8,128)(2,1)}, bf16[192,768]{1,0:T(8,128)(2,1)}, u32[]{:S(2)}, u32[]{:S(2)}) collective-permute-start(bf16[192,768]{1,0:T(8,128)(2,1)} %collective-permute-done.9.side_a), channel_id=1, source_target_pairs={{1,0},{0,1},{3,2},{2,3},{5,4},{4,5},{7,6},{6,7},{9,8},{8,9},{11,10... | collective-permute-start | bytes 884744 | tf_op jit(solution)/shard_map/ppermute | solution.py:23
  29.7 17.8 %collective-permute-start.13 = (bf16[384,896]{1,0:T(8,128)(2,1)S(1)}, bf16[384,896]{1,0:T(8,128)(2,1)S(1)}, u32[]{:S(2)}, u32[]{:S(2)}) collective-permute-start(bf16[384,896]{1,0:T(8,128)(2,1)S(1)} %pack.3.seed.own), channel_id=1, source_target_pairs={{4,0},{5,1},{6,2},{7,3},{8,4},{9,5},{10,6},{11,7},{12,8},{13,9},{1... | collective-permute-start | bytes 2064392 | tf_op jit(solution)/shard_map/ppermute | solution.py:23
  33.7 17.6 %collective-permute-start.14 = (bf16[384,896]{1,0:T(8,128)(2,1)S(1)}, bf16[384,896]{1,0:T(8,128)(2,1)S(1)}, u32[]{:S(2)}, u32[]{:S(2)}) collective-permute-start(bf16[384,896]{1,0:T(8,128)(2,1)S(1)} %pack.3.seed.own), channel_id=1, source_target_pairs={{16,0},{0,16},{17,1},{1,17},{18,2},{2,18},{19,3},{3,19},{20,4},{4,... | collective-permute-start | bytes 2064392 | tf_op jit(solution)/shard_map/ppermute | solution.py:44
  34.6 5.7 %collective-permute-start.11 = (bf16[384,768]{1,0:T(8,128)(2,1)S(1)}, bf16[384,768]{1,0:T(8,128)(2,1)S(1)}, u32[]{:S(2)}, u32[]{:S(2)}) collective-permute-start(bf16[384,768]{1,0:T(8,128)(2,1)S(1)} %collective-permute-done.4.up.own), channel_id=1, source_target_pairs={{1,0},{0,1},{3,2},{2,3},{5,4},{4,5},{7,6},{6,7},{9,8},{8,9},{11,10... | collective-permute-start | bytes 1769480 | tf_op jit(solution)/shard_map/ppermute | solution.py:23
  46.8 19.6 %collective-permute-start.18 = (bf16[384,896]{1,0:T(8,128)(2,1)S(1)}, bf16[384,896]{1,0:T(8,128)(2,1)S(1)}, u32[]{:S(2)}, u32[]{:S(2)}) collective-permute-start(bf16[384,896]{1,0:T(8,128)(2,1)S(1)} %get-tuple-element.60), channel_id=1, source_target_pairs={{12,0},{13,1},{14,2},{15,3},{0,4},{1,5},{2,6},{3,7},{4,8},{5,9},{6... | collective-permute-start | bytes 2064392 | tf_op jit(solution)/shard_map/ppermute | solution.py:23
  51.3 8.6 %collective-permute-start.15 = (bf16[384,384]{1,0:T(8,128)(2,1)S(1)}, bf16[384,384]{1,0:T(8,128)(2,1)S(1)}, u32[]{:S(2)}, u32[]{:S(2)}) collective-permute-start(bf16[384,384]{1,0:T(8,128)(2,1)S(1)} %cross.1.t0), channel_id=1, source_target_pairs={{2,0},{3,1},{0,2},{1,3},{6,4},{7,5},{4,6},{5,7},{10,8},{11,9},{8,1... | collective-permute-start | bytes 884744 | tf_op jit(solution)/shard_map/ppermute | solution.py:23
  53.3 6.6 %collective-permute-start.16 = (bf16[384,384]{1,0:T(8,128)(2,1)S(1)}, bf16[384,384]{1,0:T(8,128)(2,1)S(1)}, u32[]{:S(2)}, u32[]{:S(2)}) collective-permute-start(bf16[384,384]{1,0:T(8,128)(2,1)S(1)} %cross.1.t0), channel_id=1, source_target_pairs={{1,0},{0,1},{3,2},{2,3},{5,4},{4,5},{7,6},{6,7},{9,8},{8,9},{11,10... | collective-permute-start | bytes 884744 | tf_op jit(solution)/shard_map/ppermute | solution.py:23
  67.6 20.3 %collective-permute-start.23 = (bf16[320,896]{1,0:T(8,128)(2,1)S(1)}, bf16[320,896]{1,0:T(8,128)(2,1)S(1)}, u32[]{:S(2)}, u32[]{:S(2)}) collective-permute-start(bf16[320,896]{1,0:T(8,128)(2,1)S(1)} %get-tuple-element.66), channel_id=1, source_target_pairs={{4,0},{5,1},{6,2},{7,3},{8,4},{9,5},{10,6},{11,7},{12,8},{13,9},{1... | collective-permute-start | bytes 1720328 | tf_op jit(solution)/shard_map/ppermute | solution.py:23
  67.6 20.2 %collective-permute-start.26 = (bf16[320,896]{1,0:T(8,128)(2,1)S(1)}, bf16[320,896]{1,0:T(8,128)(2,1)S(1)}, u32[]{:S(2)}, u32[]{:S(2)}) collective-permute-start(bf16[320,896]{1,0:T(8,128)(2,1)S(1)} %get-tuple-element.66), channel_id=1, source_target_pairs={{16,0},{0,16},{17,1},{1,17},{18,2},{2,18},{19,3},{3,19},{20,4},{4,... | collective-permute-start | bytes 1720328 | tf_op jit(solution)/shard_map/ppermute | solution.py:44
  69.2 3.7 %collective-permute-start.20 = (f32[8,384]{1,0:T(8,128)S(1)}, f32[8,384]{1,0:T(8,128)S(1)}, u32[]{:S(2)}, u32[]{:S(2)}) collective-permute-start(f32[8,384]{1,0:T(8,128)S(1)} %get-tuple-element.62.s0), channel_id=1, source_target_pairs={{2,0},{3,1},{0,2},{1,3},{6,4},{7,5},{4,6},{5,7},{10,8},{11,9},{8,1... | collective-permute-start | bytes 36872 | tf_op jit(solution)/shard_map/ppermute | solution.py:23
  70.2 3.1 %collective-permute-start.21 = (f32[8,384]{1,0:T(8,128)S(1)}, f32[8,384]{1,0:T(8,128)S(1)}, u32[]{:S(2)}, u32[]{:S(2)}) collective-permute-start(f32[8,384]{1,0:T(8,128)S(1)} %get-tuple-element.62.s0), channel_id=1, source_target_pairs={{3,0},{2,1},{1,2},{0,3},{7,4},{6,5},{5,6},{4,7},{11,8},{10,9},{9,1... | collective-permute-start | bytes 36872 | tf_op jit(solution)/shard_map/ppermute | solution.py:23
  77.2 5.5 %collective-permute-start.24 = (bf16[192,224]{1,0:T(8,128)(2,1)S(1)}, bf16[192,224]{1,0:T(8,128)(2,1)S(1)}, u32[]{:S(2)}, u32[]{:S(2)}) collective-permute-start(bf16[192,224]{1,0:T(8,128)(2,1)S(1)} %get-tuple-element.68), channel_id=1, source_target_pairs={{2,0},{3,1},{0,2},{1,3},{6,4},{7,5},{4,6},{5,7},{10,8},{11,9},{8,1... | collective-permute-start | bytes 258056 | tf_op jit(solution)/shard_map/ppermute | solution.py:23
  78.3 5.9 %collective-permute-start.25 = (bf16[192,224]{1,0:T(8,128)(2,1)S(1)}, bf16[192,224]{1,0:T(8,128)(2,1)S(1)}, u32[]{:S(2)}, u32[]{:S(2)}) collective-permute-start(bf16[192,224]{1,0:T(8,128)(2,1)S(1)} %get-tuple-element.69), channel_id=1, source_target_pairs={{3,0},{2,1},{1,2},{0,3},{7,4},{6,5},{5,6},{4,7},{11,8},{10,9},{9,1... | collective-permute-start | bytes 258056 | tf_op jit(solution)/shard_map/ppermute | solution.py:23
  78.6 7.5 %collective-permute-start.27 = (bf16[80,896]{1,0:T(8,128)(2,1)S(1)}, bf16[80,896]{1,0:T(8,128)(2,1)S(1)}, u32[]{:S(2)}, u32[]{:S(2)}) collective-permute-start(bf16[80,896]{1,0:T(8,128)(2,1)S(1)} %get-tuple-element.71), channel_id=1, source_target_pairs={{4,0},{5,1},{6,2},{7,3},{8,4},{9,5},{10,6},{11,7},{12,8},{13,9},{1... | collective-permute-start | bytes 430088 | tf_op jit(solution)/shard_map/ppermute | solution.py:23
  82.7 5.1 %collective-permute-start.28 = (bf16[80,896]{1,0:T(8,128)(2,1)S(1)}, bf16[80,896]{1,0:T(8,128)(2,1)S(1)}, u32[]{:S(2)}, u32[]{:S(2)}) collective-permute-start(bf16[80,896]{1,0:T(8,128)(2,1)S(1)} %get-tuple-element.71), channel_id=1, source_target_pairs={{16,0},{0,16},{17,1},{1,17},{18,2},{2,18},{19,3},{3,19},{20,4},{4,... | collective-permute-start | bytes 430088 | tf_op jit(solution)/shard_map/ppermute | solution.py:44
  84.1 12.7 %collective-permute-start.33 = (bf16[192,896]{1,0:T(8,128)(2,1)S(1)}, bf16[192,896]{1,0:T(8,128)(2,1)S(1)}, u32[]{:S(2)}, u32[]{:S(2)}) collective-permute-start(bf16[192,896]{1,0:T(8,128)(2,1)S(1)} %get-tuple-element.80), channel_id=1, source_target_pairs={{12,0},{13,1},{14,2},{15,3},{0,4},{1,5},{2,6},{3,7},{4,8},{5,9},{6... | collective-permute-start | bytes 1032200 | tf_op jit(solution)/shard_map/ppermute | solution.py:23
  87.8 17.0 %collective-permute-start.32 = (bf16[192,896]{1,0:T(8,128)(2,1)S(1)}, bf16[192,896]{1,0:T(8,128)(2,1)S(1)}, u32[]{:S(2)}, u32[]{:S(2)}) collective-permute-start(bf16[192,896]{1,0:T(8,128)(2,1)S(1)} %pack.4), channel_id=1, source_target_pairs={{12,0},{13,1},{14,2},{15,3},{0,4},{1,5},{2,6},{3,7},{4,8},{5,9},{6... | collective-permute-start | bytes 1032200 | tf_op jit(solution)/shard_map/ppermute | solution.py:23
  93.5 5.7 %collective-permute-start.30 = (bf16[192,224]{1,0:T(8,128)(2,1)S(1)}, bf16[192,224]{1,0:T(8,128)(2,1)S(1)}, u32[]{:S(2)}, u32[]{:S(2)}) collective-permute-start(bf16[192,224]{1,0:T(8,128)(2,1)S(1)} %get-tuple-element.76), channel_id=1, source_target_pairs={{2,0},{3,1},{0,2},{1,3},{6,4},{7,5},{4,6},{5,7},{10,8},{11,9},{8,1... | collective-permute-start | bytes 258056 | tf_op jit(solution)/shard_map/ppermute | solution.py:23
  94.4 5.9 %collective-permute-start.31 = (bf16[192,224]{1,0:T(8,128)(2,1)S(1)}, bf16[192,224]{1,0:T(8,128)(2,1)S(1)}, u32[]{:S(2)}, u32[]{:S(2)}) collective-permute-start(bf16[192,224]{1,0:T(8,128)(2,1)S(1)} %get-tuple-element.77), channel_id=1, source_target_pairs={{3,0},{2,1},{1,2},{0,3},{7,4},{6,5},{5,6},{4,7},{11,8},{10,9},{9,1... | collective-permute-start | bytes 258056 | tf_op jit(solution)/shard_map/ppermute | solution.py:23
  97.8 3.4 %collective-permute-start.34 = (bf16[192,224]{1,0:T(8,128)(2,1)S(1)}, bf16[192,224]{1,0:T(8,128)(2,1)S(1)}, u32[]{:S(2)}, u32[]{:S(2)}) collective-permute-start(bf16[192,224]{1,0:T(8,128)(2,1)S(1)} %get-tuple-element.82), channel_id=1, source_target_pairs={{1,0},{0,1},{3,2},{2,3},{5,4},{4,5},{7,6},{6,7},{9,8},{8,9},{11,10... | collective-permute-start | bytes 258056 | tf_op jit(solution)/shard_map/ppermute | solution.py:23
  97.9 5.7 %collective-permute-start.35 = (bf16[192,224]{1,0:T(8,128)(2,1)S(1)}, bf16[192,224]{1,0:T(8,128)(2,1)S(1)}, u32[]{:S(2)}, u32[]{:S(2)}) collective-permute-start(bf16[192,224]{1,0:T(8,128)(2,1)S(1)} %get-tuple-element.83), channel_id=1, source_target_pairs={{2,0},{3,1},{0,2},{1,3},{6,4},{7,5},{4,6},{5,7},{10,8},{11,9},{8,1... | collective-permute-start | bytes 258056 | tf_op jit(solution)/shard_map/ppermute | solution.py:23
  99.1 5.6 %collective-permute-start.36 = (bf16[192,224]{1,0:T(8,128)(2,1)S(1)}, bf16[192,224]{1,0:T(8,128)(2,1)S(1)}, u32[]{:S(2)}, u32[]{:S(2)}) collective-permute-start(bf16[192,224]{1,0:T(8,128)(2,1)S(1)} %get-tuple-element.84), channel_id=1, source_target_pairs={{3,0},{2,1},{1,2},{0,3},{7,4},{6,5},{5,6},{4,7},{11,8},{10,9},{9,1... | collective-permute-start | bytes 258056 | tf_op jit(solution)/shard_map/ppermute | solution.py:23
  (7 other events, 29.2 us)

commit v10 on v9

--- a/solution.py
+++ b/solution.py
@@ -354,9 +354,6 @@
     packed_seed = call(pack_kernel, "pack", (scalars, seed, *received), packed)
     seed_up = from_up(packed_seed)
     seed_cross = [from_group(packed_seed, step) for step in steps]
-    cross0 = call(
-        functools.partial(cross_kernel, weight), "cross", (embeddings, *cross_own), like((len(steps) * rows, rows), BF16)
-    )
     across_a = from_core(side_a)
     unit_stack = like((QUAD * rows, depth), BF16)
     units, seed_stack = call(
@@ -364,6 +361,9 @@
         "stage_own",
         (clusters, embeddings, side_a, own_core, across_a, packed_seed),
         (unit_stack, like((QUAD * rows, classes // QUAD), BF16)),
+    )
+    cross0 = call(
+        functools.partial(cross_kernel, weight), "cross", (after(embeddings, units), *cross_own), like((len(steps) * rows, rows), BF16)
     )
     up_core, up_across_a = from_core(own_up), from_core(up_side_a)
     side_b = after(side_b, (cross0, units, up_across_a))

time: 107 us -> 107 us (level)
    ppermute x4, waiting for transfers between devices: 5.5 us -> 3.6 us  [from_group(): lax.ppermute(block, 'grp', [((i + step) % size, i) for i in range(size)])]
    ppermute x33, waiting for transfers between devices: 29.7 us -> 31.2 us  [along_dev(): lax.ppermute(block, 'dev', [(source(i) % size, i) for i in range(size)])]
where the time goes in v10:
time: 107 us
  Pallas kernels  35.3 us (33%)
  waiting for transfers between devices  34.8 us (33%)
  starting transfers between devices  31.9 us (30%)
  local copies, waits for them, and re-layouts  3.81 us (4%)
    pallas_call x17, Pallas kernels, call(): pl.pallas_call(kernel, in_specs=specs, out_shape=out_shape, scratch_shape...  35.3 us
    ppermute x33, waiting for transfers between devices, along_dev(): lax.ppermute(block, 'dev', [(source(i) % size, i) for i in range(size)])  31.2 us
    ppermute x33, starting transfers between devices, along_dev(): lax.ppermute(block, 'dev', [(source(i) % size, i) for i in range(size)])  26.5 us
    ppermute x4, starting transfers between devices, from_group(): lax.ppermute(block, 'grp', [((i + step) % size, i) for i in range(size)])  5.41 us
    ppermute x4, waiting for transfers between devices, from_group(): lax.ppermute(block, 'grp', [((i + step) % size, i) for i in range(size)])  3.6 us
  transfers between devices with their start and end apart: 37, of which 19 were waited for; matrix products, arithmetic and copies ran while one was open for 3% of the time, Pallas kernels for 30%

profile of v10, /device:TPU:0, one launch (start us, length us, event | category | flops | bytes accessed | tf_op | source)
XLA Modules:
  0.0 106.9 jit_solution(9811227787048760156)
XLA Ops:
  0.0 5.0 %collective-permute-start.4 = (bf16[384,768]{1,0:T(8,128)(2,1)}, bf16[384,768]{1,0:T(8,128)(2,1)S(1)}, u32[]{:S(2)}, u32[]{:S(2)}) collective-permute-start(bf16[384,768]{1,0:T(8,128)(2,1)} %own.2), channel_id=1, source_target_pairs={{4,0},{5,1},{6,2},{7,3},{8,4},{9,5},{10,6},{11,7},{12,8},{13,9},{1... | collective-permute-start | bytes 1769480 | tf_op jit(solution)/shard_map/ppermute | solution.py:23
  5.0 1.7 %slice.6 = bf16[192,768]{1,0:T(8,128)(2,1)} slice(bf16[384,768]{1,0:T(8,128)(2,1)} %own.2), slice={[0:192], [0:768]} | slice | bytes 589824 | tf_op jit(solution)/shard_map/slice | solution.py:343
  6.8 1.5 %collective-permute-start = (bf16[192,768]{1,0:T(8,128)(2,1)}, bf16[192,768]{1,0:T(8,128)(2,1)S(1)}, u32[]{:S(2)}, u32[]{:S(2)}) collective-permute-start(bf16[192,768]{1,0:T(8,128)(2,1)} %slice.6), channel_id=1, source_target_pairs={{2,0},{3,1},{0,2},{1,3},{6,4},{7,5},{4,6},{5,7},{10,8},{11,9},{8,1... | collective-permute-start | bytes 884744 | tf_op jit(solution)/shard_map/ppermute | solution.py:23
  13.2 3.2 %collective-permute-done.side_a.side = bf16[192,768]{1,0:T(8,128)(2,1)S(1)} collective-permute-done((bf16[192,768]{1,0:T(8,128)(2,1)}, bf16[192,768]{1,0:T(8,128)(2,1)S(1)}, u32[]{:S(2)}, u32[]{:S(2)}) %collective-permute-start) | collective-permute-done | bytes 294944 | tf_op jit(solution)/shard_map/ppermute | solution.py:23
  17.4 1.6 %collective-permute-start.8 = (bf16[384,768]{1,0:T(8,128)(2,1)}, bf16[384,768]{1,0:T(8,128)(2,1)}, u32[]{:S(2)}, u32[]{:S(2)}) collective-permute-start(bf16[384,768]{1,0:T(8,128)(2,1)} %own.2), channel_id=1, source_target_pairs={{16,0},{0,16},{17,1},{1,17},{18,2},{2,18},{19,3},{3,19},{20,4},{4,... | collective-permute-start | bytes 1769480 | tf_op jit(solution)/shard_map/ppermute | solution.py:44
  19.0 1.6 %collective-permute-done.5.p2 = bf16[384,224]{1,0:T(8,128)(2,1)S(1)} collective-permute-done((bf16[384,224]{1,0:T(8,128)(2,1)S(1)}, bf16[384,224]{1,0:T(8,128)(2,1)S(1)}, u32[]{:S(2)}, u32[]{:S(2)}) %collective-permute-start.5) | collective-permute-done | bytes 172064 | tf_op jit(solution)/shard_map/ppermute | solution.py:23
  21.1 1.9 %collective-permute-done.6.p3 = bf16[384,224]{1,0:T(8,128)(2,1)S(1)} collective-permute-done((bf16[384,224]{1,0:T(8,128)(2,1)S(1)}, bf16[384,224]{1,0:T(8,128)(2,1)S(1)}, u32[]{:S(2)}, u32[]{:S(2)}) %collective-permute-start.6) | collective-permute-done | bytes 172064 | tf_op jit(solution)/shard_map/ppermute | solution.py:23
  24.8 1.4 %collective-permute-start.2 = (bf16[192,768]{1,0:T(8,128)(2,1)S(1)}, bf16[192,768]{1,0:T(8,128)(2,1)}, u32[]{:S(2)}, u32[]{:S(2)}) collective-permute-start(bf16[192,768]{1,0:T(8,128)(2,1)S(1)} %collective-permute-done.side_a.side), channel_id=1, source_target_pairs={{1,0},{0,1},{3,2},{2,3},{5,4},{4,5},{7,6},{6,7},{9,8},{8,9},{11,10... | collective-permute-start | bytes 884744 | tf_op jit(solution)/shard_map/ppermute | solution.py:23
  26.2 2.1 %collective-permute-done.9.side_a = bf16[192,768]{1,0:T(8,128)(2,1)} collective-permute-done((bf16[192,768]{1,0:T(8,128)(2,1)S(1)}, bf16[192,768]{1,0:T(8,128)(2,1)}, u32[]{:S(2)}, u32[]{:S(2)}) %collective-permute-start.9) | collective-permute-done | bytes 294944 | tf_op jit(solution)/shard_map/ppermute | solution.py:23
  29.3 2.3 %collective-permute-start.13 = (bf16[384,896]{1,0:T(8,128)(2,1)S(1)}, bf16[384,896]{1,0:T(8,128)(2,1)S(1)}, u32[]{:S(2)}, u32[]{:S(2)}) collective-permute-start(bf16[384,896]{1,0:T(8,128)(2,1)S(1)} %pack.3.seed.own), channel_id=1, source_target_pairs={{4,0},{5,1},{6,2},{7,3},{8,4},{9,5},{10,6},{11,7},{12,8},{13,9},{1... | collective-permute-start | bytes 2064392 | tf_op jit(solution)/shard_map/ppermute | solution.py:23
  32.7 2.0 %stage_own.1 = (bf16[1536,768]{1,0:T(8,128)(2,1)S(1)}, bf16[1536,224]{1,0:T(8,128)(2,1)S(1)}) custom-call(s32[4]{0:T(128)S(1)} %pad_add_fusion.1.clusters, bf16[384,768]{1,0:T(8,128)(2,1)S(1)} %copy-done, bf16[192,768]{1,0:T(8,128)(2,1)S(1)} %collective-permute-done.side_a.side, bf16[384,768]{1,0:T(8,128)(2,1)} %collective-permute-done.1.core, ...), custom_call_target="tpu_custom_call" | custom-call | tf_op jit(solution)/shard_map/stage_own/pallas_call | solution.py:59
  34.9 1.8 %cross.1.t0 = bf16[384,384]{1,0:T(8,128)(2,1)S(1)} custom-call(bf16[384,768]{1,0:T(8,128)(2,1)S(1)} %copy-done, bf16[384,768]{1,0:T(8,128)(2,1)} %collective-permute-done.8.rest_0_), custom_call_target="tpu_custom_call" | custom-call | tf_op jit(solution)/shard_map/cross/pallas_call | solution.py:59
  36.7 3.3 %collective-permute-done.7.side_b = bf16[384,768]{1,0:T(8,128)(2,1)S(1)} collective-permute-done((bf16[384,768]{1,0:T(8,128)(2,1)}, bf16[384,768]{1,0:T(8,128)(2,1)S(1)}, u32[]{:S(2)}, u32[]{:S(2)}) %collective-permute-start.7) | collective-permute-done | bytes 589856 | tf_op jit(solution)/shard_map/ppermute | solution.py:23
  40.3 1.7 %stage_up.1.up_in = bf16[1536,768]{1,0:T(8,128)(2,1)S(1)} custom-call(s32[4]{0:T(128)S(1)} %pad_add_fusion.1.clusters, bf16[384,768]{1,0:T(8,128)(2,1)S(1)} %collective-permute-done.4.up.own, bf16[192,768]{1,0:T(8,128)(2,1)} %collective-permute-done.9.side_a, bf16[384,768]{1,0:T(8,128)(2,1)S(1)} %collective-permute-done.11.core, ...), custom_call_target="tpu_custom_call" | custom-call | tf_op jit(solution)/shard_map/stage_up/pallas_call | solution.py:59
  42.1 4.7 %far.1 = (bf16[1536,768]{1,0:T(8,128)(2,1)S(1)}, bf16[1536,768]{1,0:T(8,128)(2,1)S(1)}, bf16[1536,1536]{1,0:T(8,128)(2,1)S(1)}, bf16[384,896]{1,0:T(8,128)(2,1)S(1)}) custom-call(s32[4]{0:T(128)S(1)} %pad_add_fusion.1.clusters, bf16[1536,768]{1,0:T(8,128)(2,1)S(1)} %get-tuple-element.51.units_in, ...), custom_call_target="tpu_custom_call", output_to_operand_aliasing={{0}: (1, {}), {1}: (2, {})} | custom-call | tf_op jit(solution)/shard_map/far/pallas_call | solution.py:59
  47.1 2.0 %collective-permute-done.14.rest_0_.rest_5_ = bf16[384,896]{1,0:T(8,128)(2,1)S(1)} collective-permute-done((bf16[384,896]{1,0:T(8,128)(2,1)S(1)}, bf16[384,896]{1,0:T(8,128)(2,1)S(1)}, u32[]{:S(2)}, u32[]{:S(2)}) %collective-permute-start.14) | collective-permute-done | bytes 688160 | tf_op jit(solution)/shard_map/ppermute | solution.py:44
  49.1 2.0 %collective-permute-start.15 = (bf16[384,384]{1,0:T(8,128)(2,1)S(1)}, bf16[384,384]{1,0:T(8,128)(2,1)S(1)}, u32[]{:S(2)}, u32[]{:S(2)}) collective-permute-start(bf16[384,384]{1,0:T(8,128)(2,1)S(1)} %cross.1.t0), channel_id=1, source_target_pairs={{2,0},{3,1},{0,2},{1,3},{6,4},{7,5},{4,6},{5,7},{10,8},{11,9},{8,1... | collective-permute-start | bytes 884744 | tf_op jit(solution)/shard_map/ppermute | solution.py:23
  51.1 3.9 %near.1 = bf16[1536,1536]{1,0:T(8,128)(2,1)S(1)} custom-call(bf16[1536,768]{1,0:T(8,128)(2,1)S(1)} %get-tuple-element.60.units), custom_call_target="tpu_custom_call" | custom-call | tf_op jit(solution)/shard_map/near/pallas_call | solution.py:59
  55.0 2.7 %collective-permute-done.15.t1 = bf16[384,384]{1,0:T(8,128)(2,1)S(1)} collective-permute-done((bf16[384,384]{1,0:T(8,128)(2,1)S(1)}, bf16[384,384]{1,0:T(8,128)(2,1)S(1)}, u32[]{:S(2)}, u32[]{:S(2)}) %collective-permute-start.15) | collective-permute-done | bytes 294944 | tf_op jit(solution)/shard_map/ppermute | solution.py:23
  57.7 1.6 %collective-permute-done.17.t3 = bf16[384,384]{1,0:T(8,128)(2,1)S(1)} collective-permute-done((bf16[384,384]{1,0:T(8,128)(2,1)S(1)}, bf16[384,384]{1,0:T(8,128)(2,1)S(1)}, u32[]{:S(2)}, u32[]{:S(2)}) %collective-permute-start.17) | collective-permute-done | bytes 294944 | tf_op jit(solution)/shard_map/ppermute | solution.py:23
  59.3 3.7 %gather.1.kept = f32[384,896]{1,0:T(8,128)S(1)} custom-call(s32[4]{0:T(128)S(1)} %pad_add_fusion.1.clusters, bf16[1536,1536]{1,0:T(8,128)(2,1)S(1)} %near.1, bf16[1536,1536]{1,0:T(8,128)(2,1)S(1)} %get-tuple-element.58.far, bf16[384,384]{1,0:T(8,128)(2,1)S(1)} %cross.1.t0, bf16[384,384]{1,0:T(8,128)(2,1)S(1)} %collective-permute-done.15.t1, ...), custom_call_target="tpu_custom_call" | custom-call | tf_op jit(solution)/shard_map/gather/pallas_call | solution.py:59
  62.9 3.5 %collective-permute-done.18.sent = bf16[384,896]{1,0:T(8,128)(2,1)S(1)} collective-permute-done((bf16[384,896]{1,0:T(8,128)(2,1)S(1)}, bf16[384,896]{1,0:T(8,128)(2,1)S(1)}, u32[]{:S(2)}, u32[]{:S(2)}) %collective-permute-start.18) | collective-permute-done | bytes 688160 | tf_op jit(solution)/shard_map/ppermute | solution.py:23
  67.6 1.6 %collective-permute-start.26 = (bf16[320,896]{1,0:T(8,128)(2,1)S(1)}, bf16[320,896]{1,0:T(8,128)(2,1)S(1)}, u32[]{:S(2)}, u32[]{:S(2)}) collective-permute-start(bf16[320,896]{1,0:T(8,128)(2,1)S(1)} %get-tuple-element.68), channel_id=1, source_target_pairs={{16,0},{0,16},{17,1},{1,17},{18,2},{2,18},{19,3},{3,19},{20,4},{4,... | collective-permute-start | bytes 1720328 | tf_op jit(solution)/shard_map/ppermute | solution.py:44
  71.0 1.8 %collective-permute-done.20.s2 = f32[8,384]{1,0:T(8,128)S(1)} collective-permute-done((f32[8,384]{1,0:T(8,128)S(1)}, f32[8,384]{1,0:T(8,128)S(1)}, u32[]{:S(2)}, u32[]{:S(2)}) %collective-permute-start.20) | collective-permute-done | bytes 12320 | tf_op jit(solution)/shard_map/ppermute | solution.py:23
  73.3 3.5 %mix.1 = (bf16[80,896]{1,0:T(8,128)(2,1)S(1)}, bf16[384,896]{1,0:T(8,128)(2,1)}, bf16[1536,224]{1,0:T(8,128)(2,1)S(1)}, bf16[192,896]{1,0:T(8,128)(2,1)S(1)}, bf...) custom-call(s32[2]{0:T(128)S(1)} %pad_add_fusion.scalars, ...), custom_call_target="tpu_custom_call" | custom-call | tf_op jit(solution)/shard_map/mix/pallas_call | solution.py:59
  80.3 2.4 %collective-permute-done.24.p2 = bf16[192,224]{1,0:T(8,128)(2,1)S(1)} collective-permute-done((bf16[192,224]{1,0:T(8,128)(2,1)S(1)}, bf16[192,224]{1,0:T(8,128)(2,1)S(1)}, u32[]{:S(2)}, u32[]{:S(2)}) %collective-permute-start.24) | collective-permute-done | bytes 86048 | tf_op jit(solution)/shard_map/ppermute | solution.py:23
  83.8 1.5 %collective-permute-start.33 = (bf16[192,896]{1,0:T(8,128)(2,1)S(1)}, bf16[192,896]{1,0:T(8,128)(2,1)S(1)}, u32[]{:S(2)}, u32[]{:S(2)}) collective-permute-start(bf16[192,896]{1,0:T(8,128)(2,1)S(1)} %get-tuple-element.82), channel_id=1, source_target_pairs={{12,0},{13,1},{14,2},{15,3},{0,4},{1,5},{2,6},{3,7},{4,8},{5,9},{6... | collective-permute-start | bytes 1032200 | tf_op jit(solution)/shard_map/ppermute | solution.py:23
  86.2 1.6 %collective-permute-done.28.rest_4_ = bf16[80,896]{1,0:T(8,128)(2,1)S(1)} collective-permute-done((bf16[80,896]{1,0:T(8,128)(2,1)S(1)}, bf16[80,896]{1,0:T(8,128)(2,1)S(1)}, u32[]{:S(2)}, u32[]{:S(2)}) %collective-permute-start.28) | collective-permute-done | bytes 143392 | tf_op jit(solution)/shard_map/ppermute | solution.py:44
  87.8 2.0 %collective-permute-start.32 = (bf16[192,896]{1,0:T(8,128)(2,1)S(1)}, bf16[192,896]{1,0:T(8,128)(2,1)S(1)}, u32[]{:S(2)}, u32[]{:S(2)}) collective-permute-start(bf16[192,896]{1,0:T(8,128)(2,1)S(1)} %pack.4), channel_id=1, source_target_pairs={{12,0},{13,1},{14,2},{15,3},{0,4},{1,5},{2,6},{3,7},{4,8},{5,9},{6... | collective-permute-start | bytes 1032200 | tf_op jit(solution)/shard_map/ppermute | solution.py:23
  89.8 3.6 %gather_mixed.1 = (f32[1536,224]{1,0:T(8,128)S(1)}, f32[192,896]{1,0:T(8,128)S(1)}, bf16[192,896]{1,0:T(8,128)(2,1)S(1)}, bf16[192,224]{1,0:T(8,128)(2,1)S(1)}, ...) custom-call(s32[4]{0:T(128)S(1)} %pad_add_fusion.1.clusters, ...), custom_call_target="tpu_custom_call", output_to_operand_aliasing={{0}: (6, {})} | custom-call | tf_op jit(solution)/shard_map/gather_mixed/pallas_call | solution.py:59
  101.2 2.0 %collective-permute-done.35.p2 = bf16[192,224]{1,0:T(8,128)(2,1)S(1)} collective-permute-done((bf16[192,224]{1,0:T(8,128)(2,1)S(1)}, bf16[192,224]{1,0:T(8,128)(2,1)S(1)}, u32[]{:S(2)}, u32[]{:S(2)}) %collective-permute-start.35) | collective-permute-done | bytes 86048 | tf_op jit(solution)/shard_map/ppermute | solution.py:23
  104.6 2.2 %finish.1 = bf16[384,896]{1,0:T(8,128)(2,1)} custom-call(s32[2]{0:T(128)S(1)} %pad_add_fusion.scalars, bf16[192,896]{1,0:T(8,128)(2,1)S(1)} %pack.5.kept_a, bf16[192,896]{1,0:T(8,128)(2,1)S(1)} %collective-permute-done.32.sent_a, bf16[192,896]{1,0:T(8,128)(2,1)S(1)} %get-tuple-element.83.sums_b, bf16[192,224]{1,0:T(8,128)(2,1)S(1)} %collective-permute-done.34.p1, ...), custom_call_target="tpu_custom_call" | custom-call | tf_op jit(solution)/shard_map/finish/pallas_call | solution.py:59
  (67 shorter events, 28.6 us)
Async XLA Ops:
  0.0 22.9 %collective-permute-start.4 = (bf16[384,768]{1,0:T(8,128)(2,1)}, bf16[384,768]{1,0:T(8,128)(2,1)S(1)}, u32[]{:S(2)}, u32[]{:S(2)}) collective-permute-start(bf16[384,768]{1,0:T(8,128)(2,1)} %own.2), channel_id=1, source_target_pairs={{4,0},{5,1},{6,2},{7,3},{8,4},{9,5},{10,6},{11,7},{12,8},{13,9},{1... | collective-permute-start | bytes 1769480 | tf_op jit(solution)/shard_map/ppermute | solution.py:23
  6.8 9.6 %collective-permute-start = (bf16[192,768]{1,0:T(8,128)(2,1)}, bf16[192,768]{1,0:T(8,128)(2,1)S(1)}, u32[]{:S(2)}, u32[]{:S(2)}) collective-permute-start(bf16[192,768]{1,0:T(8,128)(2,1)} %slice.6), channel_id=1, source_target_pairs={{2,0},{3,1},{0,2},{1,3},{6,4},{7,5},{4,6},{5,7},{10,8},{11,9},{8,1... | collective-permute-start | bytes 884744 | tf_op jit(solution)/shard_map/ppermute | solution.py:23
  11.3 6.1 %collective-permute-start.3 = (bf16[384,224]{1,0:T(8,128)(2,1)S(1)}, bf16[384,224]{1,0:T(8,128)(2,1)S(1)}, u32[]{:S(2)}, u32[]{:S(2)}) collective-permute-start(bf16[384,224]{1,0:T(8,128)(2,1)S(1)} %get-tuple-element.47), channel_id=1, source_target_pairs={{1,0},{0,1},{3,2},{2,3},{5,4},{4,5},{7,6},{6,7},{9,8},{8,9},{11,10... | collective-permute-start | bytes 516104 | tf_op jit(solution)/shard_map/ppermute | solution.py:23
  11.3 9.3 %collective-permute-start.5 = (bf16[384,224]{1,0:T(8,128)(2,1)S(1)}, bf16[384,224]{1,0:T(8,128)(2,1)S(1)}, u32[]{:S(2)}, u32[]{:S(2)}) collective-permute-start(bf16[384,224]{1,0:T(8,128)(2,1)S(1)} %get-tuple-element.49), channel_id=1, source_target_pairs={{2,0},{3,1},{0,2},{1,3},{6,4},{7,5},{4,6},{5,7},{10,8},{11,9},{8,1... | collective-permute-start | bytes 516104 | tf_op jit(solution)/shard_map/ppermute | solution.py:23
  11.8 11.1 %collective-permute-start.6 = (bf16[384,224]{1,0:T(8,128)(2,1)S(1)}, bf16[384,224]{1,0:T(8,128)(2,1)S(1)}, u32[]{:S(2)}, u32[]{:S(2)}) collective-permute-start(bf16[384,224]{1,0:T(8,128)(2,1)S(1)} %get-tuple-element.50), channel_id=1, source_target_pairs={{3,0},{2,1},{1,2},{0,3},{7,4},{6,5},{5,6},{4,7},{11,8},{10,9},{9,1... | collective-permute-start | bytes 516104 | tf_op jit(solution)/shard_map/ppermute | solution.py:23
  16.4 15.2 %collective-permute-start.1 = (bf16[384,768]{1,0:T(8,128)(2,1)}, bf16[384,768]{1,0:T(8,128)(2,1)}, u32[]{:S(2)}, u32[]{:S(2)}) collective-permute-start(bf16[384,768]{1,0:T(8,128)(2,1)} %own.2), channel_id=1, source_target_pairs={{1,0},{0,1},{3,2},{2,3},{5,4},{4,5},{7,6},{6,7},{9,8},{8,9},{11,10... | collective-permute-start | bytes 1769480 | tf_op jit(solution)/shard_map/ppermute | solution.py:23
  17.4 17.4 %collective-permute-start.8 = (bf16[384,768]{1,0:T(8,128)(2,1)}, bf16[384,768]{1,0:T(8,128)(2,1)}, u32[]{:S(2)}, u32[]{:S(2)}) collective-permute-start(bf16[384,768]{1,0:T(8,128)(2,1)} %own.2), channel_id=1, source_target_pairs={{16,0},{0,16},{17,1},{1,17},{18,2},{2,18},{19,3},{3,19},{20,4},{4,... | collective-permute-start | bytes 1769480 | tf_op jit(solution)/shard_map/ppermute | solution.py:44
  20.6 7.6 %collective-permute-start.9 = (bf16[192,768]{1,0:T(8,128)(2,1)S(1)}, bf16[192,768]{1,0:T(8,128)(2,1)}, u32[]{:S(2)}, u32[]{:S(2)}) collective-permute-start(bf16[192,768]{1,0:T(8,128)(2,1)S(1)} %collective-permute-done.side_a.side), channel_id=1, source_target_pairs={{4,0},{5,1},{6,2},{7,3},{8,4},{9,5},{10,6},{11,7},{12,8},{13,9},{1... | collective-permute-start | bytes 884744 | tf_op jit(solution)/shard_map/ppermute | solution.py:23
  23.8 16.2 %collective-permute-start.7 = (bf16[384,768]{1,0:T(8,128)(2,1)}, bf16[384,768]{1,0:T(8,128)(2,1)S(1)}, u32[]{:S(2)}, u32[]{:S(2)}) collective-permute-start(bf16[384,768]{1,0:T(8,128)(2,1)} %late.1), channel_id=1, source_target_pairs={{2,0},{3,1},{0,2},{1,3},{6,4},{7,5},{4,6},{5,7},{10,8},{11,9},{8,1... | collective-permute-start | bytes 1769480 | tf_op jit(solution)/shard_map/ppermute | solution.py:23
  24.8 4.5 %collective-permute-start.2 = (bf16[192,768]{1,0:T(8,128)(2,1)S(1)}, bf16[192,768]{1,0:T(8,128)(2,1)}, u32[]{:S(2)}, u32[]{:S(2)}) collective-permute-start(bf16[192,768]{1,0:T(8,128)(2,1)S(1)} %collective-permute-done.side_a.side), channel_id=1, source_target_pairs={{1,0},{0,1},{3,2},{2,3},{5,4},{4,5},{7,6},{6,7},{9,8},{8,9},{11,10... | collective-permute-start | bytes 884744 | tf_op jit(solution)/shard_map/ppermute | solution.py:23
  28.2 8.4 %collective-permute-start.10 = (bf16[192,768]{1,0:T(8,128)(2,1)}, bf16[192,768]{1,0:T(8,128)(2,1)}, u32[]{:S(2)}, u32[]{:S(2)}) collective-permute-start(bf16[192,768]{1,0:T(8,128)(2,1)} %collective-permute-done.9.side_a), channel_id=1, source_target_pairs={{1,0},{0,1},{3,2},{2,3},{5,4},{4,5},{7,6},{6,7},{9,8},{8,9},{11,10... | collective-permute-start | bytes 884744 | tf_op jit(solution)/shard_map/ppermute | solution.py:23
  29.3 17.8 %collective-permute-start.13 = (bf16[384,896]{1,0:T(8,128)(2,1)S(1)}, bf16[384,896]{1,0:T(8,128)(2,1)S(1)}, u32[]{:S(2)}, u32[]{:S(2)}) collective-permute-start(bf16[384,896]{1,0:T(8,128)(2,1)S(1)} %pack.3.seed.own), channel_id=1, source_target_pairs={{4,0},{5,1},{6,2},{7,3},{8,4},{9,5},{10,6},{11,7},{12,8},{13,9},{1... | collective-permute-start | bytes 2064392 | tf_op jit(solution)/shard_map/ppermute | solution.py:23
  31.6 17.5 %collective-permute-start.14 = (bf16[384,896]{1,0:T(8,128)(2,1)S(1)}, bf16[384,896]{1,0:T(8,128)(2,1)S(1)}, u32[]{:S(2)}, u32[]{:S(2)}) collective-permute-start(bf16[384,896]{1,0:T(8,128)(2,1)S(1)} %pack.3.seed.own), channel_id=1, source_target_pairs={{16,0},{0,16},{17,1},{1,17},{18,2},{2,18},{19,3},{3,19},{20,4},{4,... | collective-permute-start | bytes 2064392 | tf_op jit(solution)/shard_map/ppermute | solution.py:44
  34.8 5.5 %collective-permute-start.11 = (bf16[384,768]{1,0:T(8,128)(2,1)S(1)}, bf16[384,768]{1,0:T(8,128)(2,1)S(1)}, u32[]{:S(2)}, u32[]{:S(2)}) collective-permute-start(bf16[384,768]{1,0:T(8,128)(2,1)S(1)} %collective-permute-done.4.up.own), channel_id=1, source_target_pairs={{1,0},{0,1},{3,2},{2,3},{5,4},{4,5},{7,6},{6,7},{9,8},{8,9},{11,10... | collective-permute-start | bytes 1769480 | tf_op jit(solution)/shard_map/ppermute | solution.py:23
  46.8 19.6 %collective-permute-start.18 = (bf16[384,896]{1,0:T(8,128)(2,1)S(1)}, bf16[384,896]{1,0:T(8,128)(2,1)S(1)}, u32[]{:S(2)}, u32[]{:S(2)}) collective-permute-start(bf16[384,896]{1,0:T(8,128)(2,1)S(1)} %get-tuple-element.62), channel_id=1, source_target_pairs={{12,0},{13,1},{14,2},{15,3},{0,4},{1,5},{2,6},{3,7},{4,8},{5,9},{6... | collective-permute-start | bytes 2064392 | tf_op jit(solution)/shard_map/ppermute | solution.py:23
  49.1 8.6 %collective-permute-start.15 = (bf16[384,384]{1,0:T(8,128)(2,1)S(1)}, bf16[384,384]{1,0:T(8,128)(2,1)S(1)}, u32[]{:S(2)}, u32[]{:S(2)}) collective-permute-start(bf16[384,384]{1,0:T(8,128)(2,1)S(1)} %cross.1.t0), channel_id=1, source_target_pairs={{2,0},{3,1},{0,2},{1,3},{6,4},{7,5},{4,6},{5,7},{10,8},{11,9},{8,1... | collective-permute-start | bytes 884744 | tf_op jit(solution)/shard_map/ppermute | solution.py:23
  51.1 6.6 %collective-permute-start.16 = (bf16[384,384]{1,0:T(8,128)(2,1)S(1)}, bf16[384,384]{1,0:T(8,128)(2,1)S(1)}, u32[]{:S(2)}, u32[]{:S(2)}) collective-permute-start(bf16[384,384]{1,0:T(8,128)(2,1)S(1)} %cross.1.t0), channel_id=1, source_target_pairs={{1,0},{0,1},{3,2},{2,3},{5,4},{4,5},{7,6},{6,7},{9,8},{8,9},{11,10... | collective-permute-start | bytes 884744 | tf_op jit(solution)/shard_map/ppermute | solution.py:23
  67.6 20.3 %collective-permute-start.23 = (bf16[320,896]{1,0:T(8,128)(2,1)S(1)}, bf16[320,896]{1,0:T(8,128)(2,1)S(1)}, u32[]{:S(2)}, u32[]{:S(2)}) collective-permute-start(bf16[320,896]{1,0:T(8,128)(2,1)S(1)} %get-tuple-element.68), channel_id=1, source_target_pairs={{4,0},{5,1},{6,2},{7,3},{8,4},{9,5},{10,6},{11,7},{12,8},{13,9},{1... | collective-permute-start | bytes 1720328 | tf_op jit(solution)/shard_map/ppermute | solution.py:23
  67.6 20.2 %collective-permute-start.26 = (bf16[320,896]{1,0:T(8,128)(2,1)S(1)}, bf16[320,896]{1,0:T(8,128)(2,1)S(1)}, u32[]{:S(2)}, u32[]{:S(2)}) collective-permute-start(bf16[320,896]{1,0:T(8,128)(2,1)S(1)} %get-tuple-element.68), channel_id=1, source_target_pairs={{16,0},{0,16},{17,1},{1,17},{18,2},{2,18},{19,3},{3,19},{20,4},{4,... | collective-permute-start | bytes 1720328 | tf_op jit(solution)/shard_map/ppermute | solution.py:44
  69.2 3.7 %collective-permute-start.20 = (f32[8,384]{1,0:T(8,128)S(1)}, f32[8,384]{1,0:T(8,128)S(1)}, u32[]{:S(2)}, u32[]{:S(2)}) collective-permute-start(f32[8,384]{1,0:T(8,128)S(1)} %get-tuple-element.64.s0), channel_id=1, source_target_pairs={{2,0},{3,1},{0,2},{1,3},{6,4},{7,5},{4,6},{5,7},{10,8},{11,9},{8,1... | collective-permute-start | bytes 36872 | tf_op jit(solution)/shard_map/ppermute | solution.py:23
  70.2 3.1 %collective-permute-start.21 = (f32[8,384]{1,0:T(8,128)S(1)}, f32[8,384]{1,0:T(8,128)S(1)}, u32[]{:S(2)}, u32[]{:S(2)}) collective-permute-start(f32[8,384]{1,0:T(8,128)S(1)} %get-tuple-element.64.s0), channel_id=1, source_target_pairs={{3,0},{2,1},{1,2},{0,3},{7,4},{6,5},{5,6},{4,7},{11,8},{10,9},{9,1... | collective-permute-start | bytes 36872 | tf_op jit(solution)/shard_map/ppermute | solution.py:23
  77.2 5.5 %collective-permute-start.24 = (bf16[192,224]{1,0:T(8,128)(2,1)S(1)}, bf16[192,224]{1,0:T(8,128)(2,1)S(1)}, u32[]{:S(2)}, u32[]{:S(2)}) collective-permute-start(bf16[192,224]{1,0:T(8,128)(2,1)S(1)} %get-tuple-element.70), channel_id=1, source_target_pairs={{2,0},{3,1},{0,2},{1,3},{6,4},{7,5},{4,6},{5,7},{10,8},{11,9},{8,1... | collective-permute-start | bytes 258056 | tf_op jit(solution)/shard_map/ppermute | solution.py:23
  78.3 5.6 %collective-permute-start.25 = (bf16[192,224]{1,0:T(8,128)(2,1)S(1)}, bf16[192,224]{1,0:T(8,128)(2,1)S(1)}, u32[]{:S(2)}, u32[]{:S(2)}) collective-permute-start(bf16[192,224]{1,0:T(8,128)(2,1)S(1)} %get-tuple-element.71), channel_id=1, source_target_pairs={{3,0},{2,1},{1,2},{0,3},{7,4},{6,5},{5,6},{4,7},{11,8},{10,9},{9,1... | collective-permute-start | bytes 258056 | tf_op jit(solution)/shard_map/ppermute | solution.py:23
  78.6 7.5 %collective-permute-start.27 = (bf16[80,896]{1,0:T(8,128)(2,1)S(1)}, bf16[80,896]{1,0:T(8,128)(2,1)S(1)}, u32[]{:S(2)}, u32[]{:S(2)}) collective-permute-start(bf16[80,896]{1,0:T(8,128)(2,1)S(1)} %get-tuple-element.73), channel_id=1, source_target_pairs={{4,0},{5,1},{6,2},{7,3},{8,4},{9,5},{10,6},{11,7},{12,8},{13,9},{1... | collective-permute-start | bytes 430088 | tf_op jit(solution)/shard_map/ppermute | solution.py:23
  82.7 5.1 %collective-permute-start.28 = (bf16[80,896]{1,0:T(8,128)(2,1)S(1)}, bf16[80,896]{1,0:T(8,128)(2,1)S(1)}, u32[]{:S(2)}, u32[]{:S(2)}) collective-permute-start(bf16[80,896]{1,0:T(8,128)(2,1)S(1)} %get-tuple-element.73), channel_id=1, source_target_pairs={{16,0},{0,16},{17,1},{1,17},{18,2},{2,18},{19,3},{3,19},{20,4},{4,... | collective-permute-start | bytes 430088 | tf_op jit(solution)/shard_map/ppermute | solution.py:44
  83.8 12.7 %collective-permute-start.33 = (bf16[192,896]{1,0:T(8,128)(2,1)S(1)}, bf16[192,896]{1,0:T(8,128)(2,1)S(1)}, u32[]{:S(2)}, u32[]{:S(2)}) collective-permute-start(bf16[192,896]{1,0:T(8,128)(2,1)S(1)} %get-tuple-element.82), channel_id=1, source_target_pairs={{12,0},{13,1},{14,2},{15,3},{0,4},{1,5},{2,6},{3,7},{4,8},{5,9},{6... | collective-permute-start | bytes 1032200 | tf_op jit(solution)/shard_map/ppermute | solution.py:23
  87.8 16.8 %collective-permute-start.32 = (bf16[192,896]{1,0:T(8,128)(2,1)S(1)}, bf16[192,896]{1,0:T(8,128)(2,1)S(1)}, u32[]{:S(2)}, u32[]{:S(2)}) collective-permute-start(bf16[192,896]{1,0:T(8,128)(2,1)S(1)} %pack.4), channel_id=1, source_target_pairs={{12,0},{13,1},{14,2},{15,3},{0,4},{1,5},{2,6},{3,7},{4,8},{5,9},{6... | collective-permute-start | bytes 1032200 | tf_op jit(solution)/shard_map/ppermute | solution.py:23
  93.5 5.7 %collective-permute-start.30 = (bf16[192,224]{1,0:T(8,128)(2,1)S(1)}, bf16[192,224]{1,0:T(8,128)(2,1)S(1)}, u32[]{:S(2)}, u32[]{:S(2)}) collective-permute-start(bf16[192,224]{1,0:T(8,128)(2,1)S(1)} %get-tuple-element.78), channel_id=1, source_target_pairs={{2,0},{3,1},{0,2},{1,3},{6,4},{7,5},{4,6},{5,7},{10,8},{11,9},{8,1... | collective-permute-start | bytes 258056 | tf_op jit(solution)/shard_map/ppermute | solution.py:23
  94.4 5.9 %collective-permute-start.31 = (bf16[192,224]{1,0:T(8,128)(2,1)S(1)}, bf16[192,224]{1,0:T(8,128)(2,1)S(1)}, u32[]{:S(2)}, u32[]{:S(2)}) collective-permute-start(bf16[192,224]{1,0:T(8,128)(2,1)S(1)} %get-tuple-element.79), channel_id=1, source_target_pairs={{3,0},{2,1},{1,2},{0,3},{7,4},{6,5},{5,6},{4,7},{11,8},{10,9},{9,1... | collective-permute-start | bytes 258056 | tf_op jit(solution)/shard_map/ppermute | solution.py:23
  97.5 3.7 %collective-permute-start.34 = (bf16[192,224]{1,0:T(8,128)(2,1)S(1)}, bf16[192,224]{1,0:T(8,128)(2,1)S(1)}, u32[]{:S(2)}, u32[]{:S(2)}) collective-permute-start(bf16[192,224]{1,0:T(8,128)(2,1)S(1)} %get-tuple-element.84), channel_id=1, source_target_pairs={{1,0},{0,1},{3,2},{2,3},{5,4},{4,5},{7,6},{6,7},{9,8},{8,9},{11,10... | collective-permute-start | bytes 258056 | tf_op jit(solution)/shard_map/ppermute | solution.py:23
  97.6 5.7 %collective-permute-start.35 = (bf16[192,224]{1,0:T(8,128)(2,1)S(1)}, bf16[192,224]{1,0:T(8,128)(2,1)S(1)}, u32[]{:S(2)}, u32[]{:S(2)}) collective-permute-start(bf16[192,224]{1,0:T(8,128)(2,1)S(1)} %get-tuple-element.85), channel_id=1, source_target_pairs={{2,0},{3,1},{0,2},{1,3},{6,4},{7,5},{4,6},{5,7},{10,8},{11,9},{8,1... | collective-permute-start | bytes 258056 | tf_op jit(solution)/shard_map/ppermute | solution.py:23
  99.1 5.5 %collective-permute-start.36 = (bf16[192,224]{1,0:T(8,128)(2,1)S(1)}, bf16[192,224]{1,0:T(8,128)(2,1)S(1)}, u32[]{:S(2)}, u32[]{:S(2)}) collective-permute-start(bf16[192,224]{1,0:T(8,128)(2,1)S(1)} %get-tuple-element.86), channel_id=1, source_target_pairs={{3,0},{2,1},{1,2},{0,3},{7,4},{6,5},{5,6},{4,7},{11,8},{10,9},{9,1... | collective-permute-start | bytes 258056 | tf_op jit(solution)/shard_map/ppermute | solution.py:23
  (7 other events, 30.0 us)

commit v11 on v9

--- a/solution.py
+++ b/solution.py
@@ -401,14 +401,16 @@
 
     head_up = from_up(head)
     head_cross = [from_group(head, step) for step in steps]
-    half, half_piece = like((half_rows, classes), BF16), like((half_rows, classes // QUAD), BF16)
+    last_rows = rows * 11 // 24 // 16 * 16
+    part_a, part_b = like((rows - last_rows, classes), BF16), like((last_rows, classes), BF16)
+    piece_a, piece_b = (like((p.shape[0], classes // QUAD), BF16) for p in (part_a, part_b))
     tail, _, current_stack, sums_b, sums_a, *pieces = call(
         mix_kernel,
         "mix",
         (scalars, far, summed, squares, *exchange([squares] * 3), packed_seed),
         (
             tail, packed, like((QUAD * rows, classes // QUAD), BF16),
-            half, half, half_piece, half_piece, half_piece,
+            part_b, part_a, piece_a, piece_a, piece_a,
         ),
     )
     received = exchange(pieces)
@@ -421,7 +423,7 @@
     tail_up = from_up(tail)
     tail_cross = [from_group(after(tail, near_total), step) for step in steps]
     sent_b = from_down(sums_b)
-    sums_a = call(pack_kernel, "pack", (scalars, sums_a, *received), half)
+    sums_a = call(pack_kernel, "pack", (scalars, sums_a, *received), part_a)
     sums_a = after(sums_a, (head_up, head_cross, tail_up, tail_cross))
     sent_a = from_down(sums_a)
     head_up = after(head_up, sums_a)
@@ -434,20 +436,20 @@
         (clusters, far, *crosses, near_total, *triples),
         (
             like((QUAD * rows, classes // QUAD), F32),
-            like(half.shape, F32), half, half_piece, half_piece, half_piece,
+            like(part_b.shape, F32), part_a, piece_a, piece_a, piece_a,
         ),
         [pltpu.VMEM(labels.shape, BF16), stack],
         aliases={6: 0},
     )
     received = exchange(pieces)
-    sums_b, *pieces = call(add_kernel, "add", (scalars, after(kept_b, received[0]), sent_b), (half, half_piece, half_piece, half_piece))
-    kept_a = call(pack_kernel, "pack", (scalars, kept_a, *received), half)
+    sums_b, *pieces = call(add_kernel, "add", (scalars, after(kept_b, received[0]), sent_b), (part_b, piece_b, piece_b, piece_b))
+    kept_a = call(pack_kernel, "pack", (scalars, kept_a, *received), part_a)
     return call(
         finish_kernel,
         "finish",
         (scalars, kept_a, sent_a, sums_b, *exchange(pieces), seed),
         packed,
-        [pltpu.VMEM(half.shape, BF16)],
+        [pltpu.VMEM(part_b.shape, BF16)],
     )
 
 

time: 107 us -> 109 us (1.019)
  waiting for transfers between devices: 35.2 us -> 37.6 us
    ppermute x33, waiting for transfers between devices: 29.7 us -> 33.7 us  [along_dev(): lax.ppermute(block, 'dev', [(source(i) % size, i) for i in range(size)])]
    ppermute x4, waiting for transfers between devices: 5.5 us -> 3.88 us  [from_group(): lax.ppermute(block, 'grp', [((i + step) % size, i) for i in range(size)])]
  transfers between devices with their start and end apart: 37 -> 37, of which waited for: 19 -> 17; matrix products, arithmetic and copies ran while one was open for 3% -> 3% of each run, Pallas kernels for 30% -> 29%
where the time goes in v11:
time: 109 us
  waiting for transfers between devices  37.6 us (34%)
  Pallas kernels  35.4 us (32%)
  starting transfers between devices  31 us (28%)
  local copies, waits for them, and re-layouts  3.84 us (4%)
    pallas_call x17, Pallas kernels, call(): pl.pallas_call(kernel, in_specs=specs, out_shape=out_shape, scratch_shape...  35.4 us
    ppermute x33, waiting for transfers between devices, along_dev(): lax.ppermute(block, 'dev', [(source(i) % size, i) for i in range(size)])  33.7 us
    ppermute x33, starting transfers between devices, along_dev(): lax.ppermute(block, 'dev', [(source(i) % size, i) for i in range(size)])  25.7 us
    ppermute x4, starting transfers between devices, from_group(): lax.ppermute(block, 'grp', [((i + step) % size, i) for i in range(size)])  5.24 us
    ppermute x4, waiting for transfers between devices, from_group(): lax.ppermute(block, 'grp', [((i + step) % size, i) for i in range(size)])  3.88 us
  transfers between devices with their start and end apart: 37, of which 17 were waited for; matrix products, arithmetic and copies ran while one was open for 3% of the time, Pallas kernels for 29%

profile of v11, /device:TPU:0, one launch (start us, length us, event | category | flops | bytes accessed | tf_op | source)
XLA Modules:
  0.0 108.9 jit_solution(12095147621756410204)
XLA Ops:
  0.0 5.0 %collective-permute-start.4 = (bf16[384,768]{1,0:T(8,128)(2,1)}, bf16[384,768]{1,0:T(8,128)(2,1)S(1)}, u32[]{:S(2)}, u32[]{:S(2)}) collective-permute-start(bf16[384,768]{1,0:T(8,128)(2,1)} %own.3), channel_id=1, source_target_pairs={{4,0},{5,1},{6,2},{7,3},{8,4},{9,5},{10,6},{11,7},{12,8},{13,9},{1... | collective-permute-start | bytes 1769480 | tf_op jit(solution)/shard_map/ppermute | solution.py:23
  5.0 1.7 %slice.6 = bf16[192,768]{1,0:T(8,128)(2,1)} slice(bf16[384,768]{1,0:T(8,128)(2,1)} %own.3), slice={[0:192], [0:768]} | slice | bytes 589824 | tf_op jit(solution)/shard_map/slice | solution.py:343
  6.8 1.5 %collective-permute-start = (bf16[192,768]{1,0:T(8,128)(2,1)}, bf16[192,768]{1,0:T(8,128)(2,1)S(1)}, u32[]{:S(2)}, u32[]{:S(2)}) collective-permute-start(bf16[192,768]{1,0:T(8,128)(2,1)} %slice.6), channel_id=1, source_target_pairs={{2,0},{3,1},{0,2},{1,3},{6,4},{7,5},{4,6},{5,7},{10,8},{11,9},{8,1... | collective-permute-start | bytes 884744 | tf_op jit(solution)/shard_map/ppermute | solution.py:23
  11.8 1.4 %collective-permute-start.6 = (bf16[384,224]{1,0:T(8,128)(2,1)S(1)}, bf16[384,224]{1,0:T(8,128)(2,1)S(1)}, u32[]{:S(2)}, u32[]{:S(2)}) collective-permute-start(bf16[384,224]{1,0:T(8,128)(2,1)S(1)} %get-tuple-element.49), channel_id=1, source_target_pairs={{3,0},{2,1},{1,2},{0,3},{7,4},{6,5},{5,6},{4,7},{11,8},{10,9},{9,1... | collective-permute-start | bytes 516104 | tf_op jit(solution)/shard_map/ppermute | solution.py:23
  13.2 3.2 %collective-permute-done.side_a.side = bf16[192,768]{1,0:T(8,128)(2,1)S(1)} collective-permute-done((bf16[192,768]{1,0:T(8,128)(2,1)}, bf16[192,768]{1,0:T(8,128)(2,1)S(1)}, u32[]{:S(2)}, u32[]{:S(2)}) %collective-permute-start) | collective-permute-done | bytes 294944 | tf_op jit(solution)/shard_map/ppermute | solution.py:23
  16.4 1.5 %collective-permute-start.8 = (bf16[384,768]{1,0:T(8,128)(2,1)}, bf16[384,768]{1,0:T(8,128)(2,1)}, u32[]{:S(2)}, u32[]{:S(2)}) collective-permute-start(bf16[384,768]{1,0:T(8,128)(2,1)} %own.3), channel_id=1, source_target_pairs={{16,0},{0,16},{17,1},{1,17},{18,2},{2,18},{19,3},{3,19},{20,4},{4,... | collective-permute-start | bytes 1769480 | tf_op jit(solution)/shard_map/ppermute | solution.py:44
  19.0 1.6 %collective-permute-done.5.p2 = bf16[384,224]{1,0:T(8,128)(2,1)S(1)} collective-permute-done((bf16[384,224]{1,0:T(8,128)(2,1)S(1)}, bf16[384,224]{1,0:T(8,128)(2,1)S(1)}, u32[]{:S(2)}, u32[]{:S(2)}) %collective-permute-start.5) | collective-permute-done | bytes 172064 | tf_op jit(solution)/shard_map/ppermute | solution.py:23
  21.1 1.9 %collective-permute-done.6.p3 = bf16[384,224]{1,0:T(8,128)(2,1)S(1)} collective-permute-done((bf16[384,224]{1,0:T(8,128)(2,1)S(1)}, bf16[384,224]{1,0:T(8,128)(2,1)S(1)}, u32[]{:S(2)}, u32[]{:S(2)}) %collective-permute-start.6) | collective-permute-done | bytes 172064 | tf_op jit(solution)/shard_map/ppermute | solution.py:23
  24.8 1.4 %collective-permute-start.2 = (bf16[192,768]{1,0:T(8,128)(2,1)S(1)}, bf16[192,768]{1,0:T(8,128)(2,1)}, u32[]{:S(2)}, u32[]{:S(2)}) collective-permute-start(bf16[192,768]{1,0:T(8,128)(2,1)S(1)} %collective-permute-done.side_a.side), channel_id=1, source_target_pairs={{1,0},{0,1},{3,2},{2,3},{5,4},{4,5},{7,6},{6,7},{9,8},{8,9},{11,10... | collective-permute-start | bytes 884744 | tf_op jit(solution)/shard_map/ppermute | solution.py:23
  26.2 2.4 %collective-permute-done.9.side_a = bf16[192,768]{1,0:T(8,128)(2,1)} collective-permute-done((bf16[192,768]{1,0:T(8,128)(2,1)S(1)}, bf16[192,768]{1,0:T(8,128)(2,1)}, u32[]{:S(2)}, u32[]{:S(2)}) %collective-permute-start.9) | collective-permute-done | bytes 294944 | tf_op jit(solution)/shard_map/ppermute | solution.py:23
  29.7 2.3 %collective-permute-start.13 = (bf16[384,896]{1,0:T(8,128)(2,1)S(1)}, bf16[384,896]{1,0:T(8,128)(2,1)S(1)}, u32[]{:S(2)}, u32[]{:S(2)}) collective-permute-start(bf16[384,896]{1,0:T(8,128)(2,1)S(1)} %pack.3.seed.own), channel_id=1, source_target_pairs={{4,0},{5,1},{6,2},{7,3},{8,4},{9,5},{10,6},{11,7},{12,8},{13,9},{1... | collective-permute-start | bytes 2064392 | tf_op jit(solution)/shard_map/ppermute | solution.py:23
  31.9 1.8 %cross.1.t0 = bf16[384,384]{1,0:T(8,128)(2,1)S(1)} custom-call(bf16[384,768]{1,0:T(8,128)(2,1)S(1)} %copy-done, bf16[384,768]{1,0:T(8,128)(2,1)} %collective-permute-done.8.rest_0_), custom_call_target="tpu_custom_call" | custom-call | tf_op jit(solution)/shard_map/cross/pallas_call | solution.py:59
  34.6 2.0 %stage_own.1 = (bf16[1536,768]{1,0:T(8,128)(2,1)S(1)}, bf16[1536,224]{1,0:T(8,128)(2,1)S(1)}) custom-call(s32[4]{0:T(128)S(1)} %pad_add_fusion.1.clusters, bf16[384,768]{1,0:T(8,128)(2,1)S(1)} %copy-done, bf16[192,768]{1,0:T(8,128)(2,1)S(1)} %collective-permute-done.side_a.side, bf16[384,768]{1,0:T(8,128)(2,1)} %collective-permute-done.1.core, ...), custom_call_target="tpu_custom_call" | custom-call | tf_op jit(solution)/shard_map/stage_own/pallas_call | solution.py:59
  36.7 3.3 %collective-permute-done.7.side_b = bf16[384,768]{1,0:T(8,128)(2,1)S(1)} collective-permute-done((bf16[384,768]{1,0:T(8,128)(2,1)}, bf16[384,768]{1,0:T(8,128)(2,1)S(1)}, u32[]{:S(2)}, u32[]{:S(2)}) %collective-permute-start.7) | collective-permute-done | bytes 589856 | tf_op jit(solution)/shard_map/ppermute | solution.py:23
  40.3 1.7 %stage_up.1.up_in = bf16[1536,768]{1,0:T(8,128)(2,1)S(1)} custom-call(s32[4]{0:T(128)S(1)} %pad_add_fusion.1.clusters, bf16[384,768]{1,0:T(8,128)(2,1)S(1)} %collective-permute-done.4.up.own, bf16[192,768]{1,0:T(8,128)(2,1)} %collective-permute-done.9.side_a, bf16[384,768]{1,0:T(8,128)(2,1)S(1)} %collective-permute-done.11.core, ...), custom_call_target="tpu_custom_call" | custom-call | tf_op jit(solution)/shard_map/stage_up/pallas_call | solution.py:59
  42.1 4.7 %far.1 = (bf16[1536,768]{1,0:T(8,128)(2,1)S(1)}, bf16[1536,768]{1,0:T(8,128)(2,1)S(1)}, bf16[1536,1536]{1,0:T(8,128)(2,1)S(1)}, bf16[384,896]{1,0:T(8,128)(2,1)S(1)}) custom-call(s32[4]{0:T(128)S(1)} %pad_add_fusion.1.clusters, bf16[1536,768]{1,0:T(8,128)(2,1)S(1)} %get-tuple-element.50.units_in, ...), custom_call_target="tpu_custom_call", output_to_operand_aliasing={{0}: (1, {}), {1}: (2, {})} | custom-call | tf_op jit(solution)/shard_map/far/pallas_call | solution.py:59
  47.4 3.8 %collective-permute-done.14.rest_0_.rest_5_ = bf16[384,896]{1,0:T(8,128)(2,1)S(1)} collective-permute-done((bf16[384,896]{1,0:T(8,128)(2,1)S(1)}, bf16[384,896]{1,0:T(8,128)(2,1)S(1)}, u32[]{:S(2)}, u32[]{:S(2)}) %collective-permute-start.14) | collective-permute-done | bytes 688160 | tf_op jit(solution)/shard_map/ppermute | solution.py:44
  51.3 2.0 %collective-permute-start.15 = (bf16[384,384]{1,0:T(8,128)(2,1)S(1)}, bf16[384,384]{1,0:T(8,128)(2,1)S(1)}, u32[]{:S(2)}, u32[]{:S(2)}) collective-permute-start(bf16[384,384]{1,0:T(8,128)(2,1)S(1)} %cross.1.t0), channel_id=1, source_target_pairs={{2,0},{3,1},{0,2},{1,3},{6,4},{7,5},{4,6},{5,7},{10,8},{11,9},{8,1... | collective-permute-start | bytes 884744 | tf_op jit(solution)/shard_map/ppermute | solution.py:23
  53.3 3.9 %near.1 = bf16[1536,1536]{1,0:T(8,128)(2,1)S(1)} custom-call(bf16[1536,768]{1,0:T(8,128)(2,1)S(1)} %get-tuple-element.58.units), custom_call_target="tpu_custom_call" | custom-call | tf_op jit(solution)/shard_map/near/pallas_call | solution.py:59
  57.2 2.7 %collective-permute-done.15.t1 = bf16[384,384]{1,0:T(8,128)(2,1)S(1)} collective-permute-done((bf16[384,384]{1,0:T(8,128)(2,1)S(1)}, bf16[384,384]{1,0:T(8,128)(2,1)S(1)}, u32[]{:S(2)}, u32[]{:S(2)}) %collective-permute-start.15) | collective-permute-done | bytes 294944 | tf_op jit(solution)/shard_map/ppermute | solution.py:23
  59.9 1.6 %collective-permute-done.17.t3 = bf16[384,384]{1,0:T(8,128)(2,1)S(1)} collective-permute-done((bf16[384,384]{1,0:T(8,128)(2,1)S(1)}, bf16[384,384]{1,0:T(8,128)(2,1)S(1)}, u32[]{:S(2)}, u32[]{:S(2)}) %collective-permute-start.17) | collective-permute-done | bytes 294944 | tf_op jit(solution)/shard_map/ppermute | solution.py:23
  61.4 3.7 %gather.1.kept = f32[384,896]{1,0:T(8,128)S(1)} custom-call(s32[4]{0:T(128)S(1)} %pad_add_fusion.1.clusters, bf16[1536,1536]{1,0:T(8,128)(2,1)S(1)} %near.1, bf16[1536,1536]{1,0:T(8,128)(2,1)S(1)} %get-tuple-element.56.far, bf16[384,384]{1,0:T(8,128)(2,1)S(1)} %cross.1.t0, bf16[384,384]{1,0:T(8,128)(2,1)S(1)} %collective-permute-done.15.t1, ...), custom_call_target="tpu_custom_call" | custom-call | tf_op jit(solution)/shard_map/gather/pallas_call | solution.py:59
  67.6 1.6 %collective-permute-start.26 = (bf16[320,896]{1,0:T(8,128)(2,1)S(1)}, bf16[320,896]{1,0:T(8,128)(2,1)S(1)}, u32[]{:S(2)}, u32[]{:S(2)}) collective-permute-start(bf16[320,896]{1,0:T(8,128)(2,1)S(1)} %get-tuple-element.66), channel_id=1, source_target_pairs={{16,0},{0,16},{17,1},{1,17},{18,2},{2,18},{19,3},{3,19},{20,4},{4,... | collective-permute-start | bytes 1720328 | tf_op jit(solution)/shard_map/ppermute | solution.py:44
  71.0 1.8 %collective-permute-done.20.s2 = f32[8,384]{1,0:T(8,128)S(1)} collective-permute-done((f32[8,384]{1,0:T(8,128)S(1)}, f32[8,384]{1,0:T(8,128)S(1)}, u32[]{:S(2)}, u32[]{:S(2)}) %collective-permute-start.20) | collective-permute-done | bytes 12320 | tf_op jit(solution)/shard_map/ppermute | solution.py:23
  73.3 3.5 %mix.1 = (bf16[80,896]{1,0:T(8,128)(2,1)S(1)}, bf16[384,896]{1,0:T(8,128)(2,1)}, bf16[1536,224]{1,0:T(8,128)(2,1)S(1)}, bf16[176,896]{1,0:T(8,128)(2,1)S(1)}, bf...) custom-call(s32[2]{0:T(128)S(1)} %pad_add_fusion.scalars, ...), custom_call_target="tpu_custom_call" | custom-call | tf_op jit(solution)/shard_map/mix/pallas_call | solution.py:59
  78.3 1.4 %near_products.1.total_in = f32[1536,224]{1,0:T(8,128)S(1)} custom-call(bf16[1536,1536]{1,0:T(8,128)(2,1)S(1)} %near.1, bf16[1536,224]{1,0:T(8,128)(2,1)S(1)} %get-tuple-element.65.stack), custom_call_target="tpu_custom_call" | custom-call | tf_op jit(solution)/shard_map/near_products/pallas_call | solution.py:59
  82.2 4.8 %collective-permute-done.25.p3 = bf16[208,224]{1,0:T(8,128)(2,1)S(1)} collective-permute-done((bf16[208,224]{1,0:T(8,128)(2,1)S(1)}, bf16[208,224]{1,0:T(8,128)(2,1)S(1)}, u32[]{:S(2)}, u32[]{:S(2)}) %collective-permute-start.25) | collective-permute-done | bytes 93216 | tf_op jit(solution)/shard_map/ppermute | solution.py:23
  87.0 2.0 %collective-permute-start.33 = (bf16[176,896]{1,0:T(8,128)(2,1)S(1)}, bf16[176,896]{1,0:T(8,128)(2,1)S(1)}, u32[]{:S(2)}, u32[]{:S(2)}) collective-permute-start(bf16[176,896]{1,0:T(8,128)(2,1)S(1)} %get-tuple-element.80), channel_id=1, source_target_pairs={{12,0},{13,1},{14,2},{15,3},{0,4},{1,5},{2,6},{3,7},{4,8},{5,9},{6... | collective-permute-start | bytes 946184 | tf_op jit(solution)/shard_map/ppermute | solution.py:23
  90.2 3.6 %gather_mixed.1 = (f32[1536,224]{1,0:T(8,128)S(1)}, f32[176,896]{1,0:T(8,128)S(1)}, bf16[208,896]{1,0:T(8,128)(2,1)S(1)}, bf16[208,224]{1,0:T(8,128)(2,1)S(1)}, ...) custom-call(s32[4]{0:T(128)S(1)} %pad_add_fusion.1.clusters, ...), custom_call_target="tpu_custom_call", output_to_operand_aliasing={{0}: (6, {})} | custom-call | tf_op jit(solution)/shard_map/gather_mixed/pallas_call | solution.py:59
  95.8 3.4 %collective-permute-done.33.sent = bf16[176,896]{1,0:T(8,128)(2,1)S(1)} collective-permute-done((bf16[176,896]{1,0:T(8,128)(2,1)S(1)}, bf16[176,896]{1,0:T(8,128)(2,1)S(1)}, u32[]{:S(2)}, u32[]{:S(2)}) %collective-permute-start.33) | collective-permute-done | bytes 315424 | tf_op jit(solution)/shard_map/ppermute | solution.py:23
  102.9 2.7 %collective-permute-done.35.p2 = bf16[176,224]{1,0:T(8,128)(2,1)S(1)} collective-permute-done((bf16[176,224]{1,0:T(8,128)(2,1)S(1)}, bf16[176,224]{1,0:T(8,128)(2,1)S(1)}, u32[]{:S(2)}, u32[]{:S(2)}) %collective-permute-start.35) | collective-permute-done | bytes 78880 | tf_op jit(solution)/shard_map/ppermute | solution.py:23
  106.7 2.2 %finish.1 = bf16[384,896]{1,0:T(8,128)(2,1)} custom-call(s32[2]{0:T(128)S(1)} %pad_add_fusion.scalars, bf16[208,896]{1,0:T(8,128)(2,1)S(1)} %pack.5.kept_a, bf16[208,896]{1,0:T(8,128)(2,1)S(1)} %collective-permute-done.32.sent_a, bf16[176,896]{1,0:T(8,128)(2,1)S(1)} %get-tuple-element.81.sums_b, bf16[176,224]{1,0:T(8,128)(2,1)S(1)} %collective-permute-done.34.p1, ...), custom_call_target="tpu_custom_call" | custom-call | tf_op jit(solution)/shard_map/finish/pallas_call | solution.py:59
  (67 shorter events, 25.9 us)
Async XLA Ops:
  0.0 22.9 %collective-permute-start.4 = (bf16[384,768]{1,0:T(8,128)(2,1)}, bf16[384,768]{1,0:T(8,128)(2,1)S(1)}, u32[]{:S(2)}, u32[]{:S(2)}) collective-permute-start(bf16[384,768]{1,0:T(8,128)(2,1)} %own.3), channel_id=1, source_target_pairs={{4,0},{5,1},{6,2},{7,3},{8,4},{9,5},{10,6},{11,7},{12,8},{13,9},{1... | collective-permute-start | bytes 1769480 | tf_op jit(solution)/shard_map/ppermute | solution.py:23
  6.8 9.6 %collective-permute-start = (bf16[192,768]{1,0:T(8,128)(2,1)}, bf16[192,768]{1,0:T(8,128)(2,1)S(1)}, u32[]{:S(2)}, u32[]{:S(2)}) collective-permute-start(bf16[192,768]{1,0:T(8,128)(2,1)} %slice.6), channel_id=1, source_target_pairs={{2,0},{3,1},{0,2},{1,3},{6,4},{7,5},{4,6},{5,7},{10,8},{11,9},{8,1... | collective-permute-start | bytes 884744 | tf_op jit(solution)/shard_map/ppermute | solution.py:23
  11.3 7.7 %collective-permute-start.3 = (bf16[384,224]{1,0:T(8,128)(2,1)S(1)}, bf16[384,224]{1,0:T(8,128)(2,1)S(1)}, u32[]{:S(2)}, u32[]{:S(2)}) collective-permute-start(bf16[384,224]{1,0:T(8,128)(2,1)S(1)} %get-tuple-element.46), channel_id=1, source_target_pairs={{1,0},{0,1},{3,2},{2,3},{5,4},{4,5},{7,6},{6,7},{9,8},{8,9},{11,10... | collective-permute-start | bytes 516104 | tf_op jit(solution)/shard_map/ppermute | solution.py:23
  11.3 9.3 %collective-permute-start.5 = (bf16[384,224]{1,0:T(8,128)(2,1)S(1)}, bf16[384,224]{1,0:T(8,128)(2,1)S(1)}, u32[]{:S(2)}, u32[]{:S(2)}) collective-permute-start(bf16[384,224]{1,0:T(8,128)(2,1)S(1)} %get-tuple-element.48), channel_id=1, source_target_pairs={{2,0},{3,1},{0,2},{1,3},{6,4},{7,5},{4,6},{5,7},{10,8},{11,9},{8,1... | collective-permute-start | bytes 516104 | tf_op jit(solution)/shard_map/ppermute | solution.py:23
  11.8 11.1 %collective-permute-start.6 = (bf16[384,224]{1,0:T(8,128)(2,1)S(1)}, bf16[384,224]{1,0:T(8,128)(2,1)S(1)}, u32[]{:S(2)}, u32[]{:S(2)}) collective-permute-start(bf16[384,224]{1,0:T(8,128)(2,1)S(1)} %get-tuple-element.49), channel_id=1, source_target_pairs={{3,0},{2,1},{1,2},{0,3},{7,4},{6,5},{5,6},{4,7},{11,8},{10,9},{9,1... | collective-permute-start | bytes 516104 | tf_op jit(solution)/shard_map/ppermute | solution.py:23
  16.4 13.2 %collective-permute-start.8 = (bf16[384,768]{1,0:T(8,128)(2,1)}, bf16[384,768]{1,0:T(8,128)(2,1)}, u32[]{:S(2)}, u32[]{:S(2)}) collective-permute-start(bf16[384,768]{1,0:T(8,128)(2,1)} %own.3), channel_id=1, source_target_pairs={{16,0},{0,16},{17,1},{1,17},{18,2},{2,18},{19,3},{3,19},{20,4},{4,... | collective-permute-start | bytes 1769480 | tf_op jit(solution)/shard_map/ppermute | solution.py:44
  19.0 15.7 %collective-permute-start.1 = (bf16[384,768]{1,0:T(8,128)(2,1)}, bf16[384,768]{1,0:T(8,128)(2,1)}, u32[]{:S(2)}, u32[]{:S(2)}) collective-permute-start(bf16[384,768]{1,0:T(8,128)(2,1)} %own.3), channel_id=1, source_target_pairs={{1,0},{0,1},{3,2},{2,3},{5,4},{4,5},{7,6},{6,7},{9,8},{8,9},{11,10... | collective-permute-start | bytes 1769480 | tf_op jit(solution)/shard_map/ppermute | solution.py:23
  20.6 7.9 %collective-permute-start.9 = (bf16[192,768]{1,0:T(8,128)(2,1)S(1)}, bf16[192,768]{1,0:T(8,128)(2,1)}, u32[]{:S(2)}, u32[]{:S(2)}) collective-permute-start(bf16[192,768]{1,0:T(8,128)(2,1)S(1)} %collective-permute-done.side_a.side), channel_id=1, source_target_pairs={{4,0},{5,1},{6,2},{7,3},{8,4},{9,5},{10,6},{11,7},{12,8},{13,9},{1... | collective-permute-start | bytes 884744 | tf_op jit(solution)/shard_map/ppermute | solution.py:23
  23.8 16.2 %collective-permute-start.7 = (bf16[384,768]{1,0:T(8,128)(2,1)}, bf16[384,768]{1,0:T(8,128)(2,1)S(1)}, u32[]{:S(2)}, u32[]{:S(2)}) collective-permute-start(bf16[384,768]{1,0:T(8,128)(2,1)} %late.1), channel_id=1, source_target_pairs={{2,0},{3,1},{0,2},{1,3},{6,4},{7,5},{4,6},{5,7},{10,8},{11,9},{8,1... | collective-permute-start | bytes 1769480 | tf_op jit(solution)/shard_map/ppermute | solution.py:23
  24.8 9.0 %collective-permute-start.2 = (bf16[192,768]{1,0:T(8,128)(2,1)S(1)}, bf16[192,768]{1,0:T(8,128)(2,1)}, u32[]{:S(2)}, u32[]{:S(2)}) collective-permute-start(bf16[192,768]{1,0:T(8,128)(2,1)S(1)} %collective-permute-done.side_a.side), channel_id=1, source_target_pairs={{1,0},{0,1},{3,2},{2,3},{5,4},{4,5},{7,6},{6,7},{9,8},{8,9},{11,10... | collective-permute-start | bytes 884744 | tf_op jit(solution)/shard_map/ppermute | solution.py:23
  28.6 8.1 %collective-permute-start.10 = (bf16[192,768]{1,0:T(8,128)(2,1)}, bf16[192,768]{1,0:T(8,128)(2,1)}, u32[]{:S(2)}, u32[]{:S(2)}) collective-permute-start(bf16[192,768]{1,0:T(8,128)(2,1)} %collective-permute-done.9.side_a), channel_id=1, source_target_pairs={{1,0},{0,1},{3,2},{2,3},{5,4},{4,5},{7,6},{6,7},{9,8},{8,9},{11,10... | collective-permute-start | bytes 884744 | tf_op jit(solution)/shard_map/ppermute | solution.py:23
  29.7 17.8 %collective-permute-start.13 = (bf16[384,896]{1,0:T(8,128)(2,1)S(1)}, bf16[384,896]{1,0:T(8,128)(2,1)S(1)}, u32[]{:S(2)}, u32[]{:S(2)}) collective-permute-start(bf16[384,896]{1,0:T(8,128)(2,1)S(1)} %pack.3.seed.own), channel_id=1, source_target_pairs={{4,0},{5,1},{6,2},{7,3},{8,4},{9,5},{10,6},{11,7},{12,8},{13,9},{1... | collective-permute-start | bytes 2064392 | tf_op jit(solution)/shard_map/ppermute | solution.py:23
  33.7 17.6 %collective-permute-start.14 = (bf16[384,896]{1,0:T(8,128)(2,1)S(1)}, bf16[384,896]{1,0:T(8,128)(2,1)S(1)}, u32[]{:S(2)}, u32[]{:S(2)}) collective-permute-start(bf16[384,896]{1,0:T(8,128)(2,1)S(1)} %pack.3.seed.own), channel_id=1, source_target_pairs={{16,0},{0,16},{17,1},{1,17},{18,2},{2,18},{19,3},{3,19},{20,4},{4,... | collective-permute-start | bytes 2064392 | tf_op jit(solution)/shard_map/ppermute | solution.py:44
  34.6 5.7 %collective-permute-start.11 = (bf16[384,768]{1,0:T(8,128)(2,1)S(1)}, bf16[384,768]{1,0:T(8,128)(2,1)S(1)}, u32[]{:S(2)}, u32[]{:S(2)}) collective-permute-start(bf16[384,768]{1,0:T(8,128)(2,1)S(1)} %collective-permute-done.4.up.own), channel_id=1, source_target_pairs={{1,0},{0,1},{3,2},{2,3},{5,4},{4,5},{7,6},{6,7},{9,8},{8,9},{11,10... | collective-permute-start | bytes 1769480 | tf_op jit(solution)/shard_map/ppermute | solution.py:23
  46.8 19.6 %collective-permute-start.18 = (bf16[384,896]{1,0:T(8,128)(2,1)S(1)}, bf16[384,896]{1,0:T(8,128)(2,1)S(1)}, u32[]{:S(2)}, u32[]{:S(2)}) collective-permute-start(bf16[384,896]{1,0:T(8,128)(2,1)S(1)} %get-tuple-element.60), channel_id=1, source_target_pairs={{12,0},{13,1},{14,2},{15,3},{0,4},{1,5},{2,6},{3,7},{4,8},{5,9},{6... | collective-permute-start | bytes 2064392 | tf_op jit(solution)/shard_map/ppermute | solution.py:23
  51.3 8.6 %collective-permute-start.15 = (bf16[384,384]{1,0:T(8,128)(2,1)S(1)}, bf16[384,384]{1,0:T(8,128)(2,1)S(1)}, u32[]{:S(2)}, u32[]{:S(2)}) collective-permute-start(bf16[384,384]{1,0:T(8,128)(2,1)S(1)} %cross.1.t0), channel_id=1, source_target_pairs={{2,0},{3,1},{0,2},{1,3},{6,4},{7,5},{4,6},{5,7},{10,8},{11,9},{8,1... | collective-permute-start | bytes 884744 | tf_op jit(solution)/shard_map/ppermute | solution.py:23
  53.3 6.6 %collective-permute-start.16 = (bf16[384,384]{1,0:T(8,128)(2,1)S(1)}, bf16[384,384]{1,0:T(8,128)(2,1)S(1)}, u32[]{:S(2)}, u32[]{:S(2)}) collective-permute-start(bf16[384,384]{1,0:T(8,128)(2,1)S(1)} %cross.1.t0), channel_id=1, source_target_pairs={{1,0},{0,1},{3,2},{2,3},{5,4},{4,5},{7,6},{6,7},{9,8},{8,9},{11,10... | collective-permute-start | bytes 884744 | tf_op jit(solution)/shard_map/ppermute | solution.py:23
  67.6 22.3 %collective-permute-start.23 = (bf16[320,896]{1,0:T(8,128)(2,1)S(1)}, bf16[320,896]{1,0:T(8,128)(2,1)S(1)}, u32[]{:S(2)}, u32[]{:S(2)}) collective-permute-start(bf16[320,896]{1,0:T(8,128)(2,1)S(1)} %get-tuple-element.66), channel_id=1, source_target_pairs={{4,0},{5,1},{6,2},{7,3},{8,4},{9,5},{10,6},{11,7},{12,8},{13,9},{1... | collective-permute-start | bytes 1720328 | tf_op jit(solution)/shard_map/ppermute | solution.py:23
  67.6 22.3 %collective-permute-start.26 = (bf16[320,896]{1,0:T(8,128)(2,1)S(1)}, bf16[320,896]{1,0:T(8,128)(2,1)S(1)}, u32[]{:S(2)}, u32[]{:S(2)}) collective-permute-start(bf16[320,896]{1,0:T(8,128)(2,1)S(1)} %get-tuple-element.66), channel_id=1, source_target_pairs={{16,0},{0,16},{17,1},{1,17},{18,2},{2,18},{19,3},{3,19},{20,4},{4,... | collective-permute-start | bytes 1720328 | tf_op jit(solution)/shard_map/ppermute | solution.py:44
  69.2 3.7 %collective-permute-start.20 = (f32[8,384]{1,0:T(8,128)S(1)}, f32[8,384]{1,0:T(8,128)S(1)}, u32[]{:S(2)}, u32[]{:S(2)}) collective-permute-start(f32[8,384]{1,0:T(8,128)S(1)} %get-tuple-element.62.s0), channel_id=1, source_target_pairs={{2,0},{3,1},{0,2},{1,3},{6,4},{7,5},{4,6},{5,7},{10,8},{11,9},{8,1... | collective-permute-start | bytes 36872 | tf_op jit(solution)/shard_map/ppermute | solution.py:23
  70.2 3.1 %collective-permute-start.21 = (f32[8,384]{1,0:T(8,128)S(1)}, f32[8,384]{1,0:T(8,128)S(1)}, u32[]{:S(2)}, u32[]{:S(2)}) collective-permute-start(f32[8,384]{1,0:T(8,128)S(1)} %get-tuple-element.62.s0), channel_id=1, source_target_pairs={{3,0},{2,1},{1,2},{0,3},{7,4},{6,5},{5,6},{4,7},{11,8},{10,9},{9,1... | collective-permute-start | bytes 36872 | tf_op jit(solution)/shard_map/ppermute | solution.py:23
  77.2 5.0 %collective-permute-start.24 = (bf16[208,224]{1,0:T(8,128)(2,1)S(1)}, bf16[208,224]{1,0:T(8,128)(2,1)S(1)}, u32[]{:S(2)}, u32[]{:S(2)}) collective-permute-start(bf16[208,224]{1,0:T(8,128)(2,1)S(1)} %get-tuple-element.68), channel_id=1, source_target_pairs={{2,0},{3,1},{0,2},{1,3},{6,4},{7,5},{4,6},{5,7},{10,8},{11,9},{8,1... | collective-permute-start | bytes 279560 | tf_op jit(solution)/shard_map/ppermute | solution.py:23
  78.3 11.5 %collective-permute-start.27 = (bf16[80,896]{1,0:T(8,128)(2,1)S(1)}, bf16[80,896]{1,0:T(8,128)(2,1)S(1)}, u32[]{:S(2)}, u32[]{:S(2)}) collective-permute-start(bf16[80,896]{1,0:T(8,128)(2,1)S(1)} %get-tuple-element.71), channel_id=1, source_target_pairs={{4,0},{5,1},{6,2},{7,3},{8,4},{9,5},{10,6},{11,7},{12,8},{13,9},{1... | collective-permute-start | bytes 430088 | tf_op jit(solution)/shard_map/ppermute | solution.py:23
  79.7 10.2 %collective-permute-start.28 = (bf16[80,896]{1,0:T(8,128)(2,1)S(1)}, bf16[80,896]{1,0:T(8,128)(2,1)S(1)}, u32[]{:S(2)}, u32[]{:S(2)}) collective-permute-start(bf16[80,896]{1,0:T(8,128)(2,1)S(1)} %get-tuple-element.71), channel_id=1, source_target_pairs={{16,0},{0,16},{17,1},{1,17},{18,2},{2,18},{19,3},{3,19},{20,4},{4,... | collective-permute-start | bytes 430088 | tf_op jit(solution)/shard_map/ppermute | solution.py:44
  82.2 4.8 %collective-permute-start.25 = (bf16[208,224]{1,0:T(8,128)(2,1)S(1)}, bf16[208,224]{1,0:T(8,128)(2,1)S(1)}, u32[]{:S(2)}, u32[]{:S(2)}) collective-permute-start(bf16[208,224]{1,0:T(8,128)(2,1)S(1)} %get-tuple-element.69), channel_id=1, source_target_pairs={{3,0},{2,1},{1,2},{0,3},{7,4},{6,5},{5,6},{4,7},{11,8},{10,9},{9,1... | collective-permute-start | bytes 279560 | tf_op jit(solution)/shard_map/ppermute | solution.py:23
  87.0 12.1 %collective-permute-start.33 = (bf16[176,896]{1,0:T(8,128)(2,1)S(1)}, bf16[176,896]{1,0:T(8,128)(2,1)S(1)}, u32[]{:S(2)}, u32[]{:S(2)}) collective-permute-start(bf16[176,896]{1,0:T(8,128)(2,1)S(1)} %get-tuple-element.80), channel_id=1, source_target_pairs={{12,0},{13,1},{14,2},{15,3},{0,4},{1,5},{2,6},{3,7},{4,8},{5,9},{6... | collective-permute-start | bytes 946184 | tf_op jit(solution)/shard_map/ppermute | solution.py:23
  89.9 16.8 %collective-permute-start.32 = (bf16[208,896]{1,0:T(8,128)(2,1)S(1)}, bf16[208,896]{1,0:T(8,128)(2,1)S(1)}, u32[]{:S(2)}, u32[]{:S(2)}) collective-permute-start(bf16[208,896]{1,0:T(8,128)(2,1)S(1)} %pack.4), channel_id=1, source_target_pairs={{12,0},{13,1},{14,2},{15,3},{0,4},{1,5},{2,6},{3,7},{4,8},{5,9},{6... | collective-permute-start | bytes 1118216 | tf_op jit(solution)/shard_map/ppermute | solution.py:23
  93.9 7.3 %collective-permute-start.30 = (bf16[208,224]{1,0:T(8,128)(2,1)S(1)}, bf16[208,224]{1,0:T(8,128)(2,1)S(1)}, u32[]{:S(2)}, u32[]{:S(2)}) collective-permute-start(bf16[208,224]{1,0:T(8,128)(2,1)S(1)} %get-tuple-element.76), channel_id=1, source_target_pairs={{2,0},{3,1},{0,2},{1,3},{6,4},{7,5},{4,6},{5,7},{10,8},{11,9},{8,1... | collective-permute-start | bytes 279560 | tf_op jit(solution)/shard_map/ppermute | solution.py:23
  94.8 7.2 %collective-permute-start.31 = (bf16[208,224]{1,0:T(8,128)(2,1)S(1)}, bf16[208,224]{1,0:T(8,128)(2,1)S(1)}, u32[]{:S(2)}, u32[]{:S(2)}) collective-permute-start(bf16[208,224]{1,0:T(8,128)(2,1)S(1)} %get-tuple-element.77), channel_id=1, source_target_pairs={{3,0},{2,1},{1,2},{0,3},{7,4},{6,5},{5,6},{4,7},{11,8},{10,9},{9,1... | collective-permute-start | bytes 279560 | tf_op jit(solution)/shard_map/ppermute | solution.py:23
  100.1 2.8 %collective-permute-start.34 = (bf16[176,224]{1,0:T(8,128)(2,1)S(1)}, bf16[176,224]{1,0:T(8,128)(2,1)S(1)}, u32[]{:S(2)}, u32[]{:S(2)}) collective-permute-start(bf16[176,224]{1,0:T(8,128)(2,1)S(1)} %get-tuple-element.82), channel_id=1, source_target_pairs={{1,0},{0,1},{3,2},{2,3},{5,4},{4,5},{7,6},{6,7},{9,8},{8,9},{11,10... | collective-permute-start | bytes 236552 | tf_op jit(solution)/shard_map/ppermute | solution.py:23
  100.2 5.5 %collective-permute-start.35 = (bf16[176,224]{1,0:T(8,128)(2,1)S(1)}, bf16[176,224]{1,0:T(8,128)(2,1)S(1)}, u32[]{:S(2)}, u32[]{:S(2)}) collective-permute-start(bf16[176,224]{1,0:T(8,128)(2,1)S(1)} %get-tuple-element.83), channel_id=1, source_target_pairs={{2,0},{3,1},{0,2},{1,3},{6,4},{7,5},{4,6},{5,7},{10,8},{11,9},{8,1... | collective-permute-start | bytes 236552 | tf_op jit(solution)/shard_map/ppermute | solution.py:23
  101.2 5.5 %collective-permute-start.36 = (bf16[176,224]{1,0:T(8,128)(2,1)S(1)}, bf16[176,224]{1,0:T(8,128)(2,1)S(1)}, u32[]{:S(2)}, u32[]{:S(2)}) collective-permute-start(bf16[176,224]{1,0:T(8,128)(2,1)S(1)} %get-tuple-element.84), channel_id=1, source_target_pairs={{3,0},{2,1},{1,2},{0,3},{7,4},{6,5},{5,6},{4,7},{11,8},{10,9},{9,1... | collective-permute-start | bytes 236552 | tf_op jit(solution)/shard_map/ppermute | solution.py:23
  (7 other events, 28.8 us)
